TPU v7x, 32 devices: a whole 2x2x4 slice. The times are simulated.
32 devices in a mesh: section: 4 (over y, x), slab: 8 (over z, core).
Axes of the slice: x: 2, y: 2, z: 4, core: 2. Of those that a mesh axis runs over, the one named last changes fastest.
Arguments:
- features: bfloat16 [4, 8, 16, 2, 8, 256], P('section', None, 'slab'), may hold values from -40 to 40
- vae_weight: bfloat16 [3, 3, 3, 256, 256], replicated, may hold values from -0.078125 to 0.078125
- vae_gain: float32 [256], replicated, may hold values from 0.25 to 1.75
- vae_shift: float32 [256], replicated, may hold values from -3 to 3
- vae_bias: float32 [256], replicated, may hold values from -3 to 3
- latent_weight: bfloat16 [256, 16], replicated, may hold values from -0.375 to 0.375
- latent_bias: float32 [16], replicated, may hold values from -3 to 3
- slot_clips: int32 [4, 8], replicated, may hold values from 0 to 7, each once within a row
- row_offsets: int32 [4, 8], replicated, may hold values from 0 to 120
- in_weight: bfloat16 [3, 3, 16, 320], replicated, may hold values from -0.5 to 0.5
- in_bias: float32 [320], replicated, may hold values from -3 to 3
- pos_table: bfloat16 [128, 320], replicated, may hold values from -3 to 3
- unet_gain: float32 [4, 320], P('section'), may hold values from 0.25 to 1.75
- unet_shift: float32 [4, 320], P('section'), may hold values from -3 to 3
- unet_weight: bfloat16 [4, 3, 3, 320, 320], P('section'), may hold values from -0.109375 to 0.109375
- unet_bias: float32 [4, 320], P('section'), may hold values from -3 to 3
Outputs:
- layer_outputs: bfloat16 [4, 4, 8, 8, 2, 1280], P('section', None, 'slab')
Inputs may be any that keep to these rules, and one draw needn't show every extreme that they name: Each row of slot_clips is a permutation of 0 to 7.
All inputs are finite; a program needn't handle non-finite values.
Results may differ from a plain program's by a relative error of at most 0.025.
Values may be sent and summed in bfloat16 or wider, within the bound.
No kernel may reach another device: no remote copies, remote signals or barrier semaphores. Data moves between devices by JAX's collectives and lax.ppermute only.
A program may use at most 64 MiB of HBM per device.

v0:
```python
import jax
import jax.numpy as jnp
from jax import lax
from jax.sharding import PartitionSpec as P

GROUPS = 32


norm_eps = 1e-06


def from_behind(value, axis, steps):
    count = lax.axis_size(axis)
    initial, last = (max(0, -steps), min(count, count - steps))
    return lax.ppermute(value, axis, [(source, source + steps) for source in range(initial, last)])


def group_stats(values, groups):
    full_shape = values.shape
    grouped = values.reshape(full_shape[0], -1, groups, full_shape[-1] // groups)
    return (jnp.sum(grouped, axis=(1, 3)), jnp.sum(grouped * grouped, axis=(1, 3)))


def normalize(values, sums, squares, cell_count, gain, shift, groups):
    mean_value = sums / cell_count
    variance = squares / cell_count - mean_value * mean_value
    inverse = lax.rsqrt(variance + norm_eps)
    full_shape = values.shape
    grouped = values.reshape(full_shape[0], -1, groups, full_shape[-1] // groups)
    normed = (grouped - mean_value[:, None, :, None]) * inverse[:, None, :, None]
    return normed.reshape(full_shape) * gain + shift


def keep_stats(stats_pair):
    return stats_pair


def zero_rows(active):
    return jnp.pad(active, ((0, 0), (1, 1), (0, 0), (0, 0), (0, 0)))


def encode(features, rows_total, reduce_stats, extend_rows, encoder):
    vae_weight, vae_gain, vae_shift, vae_bias, latent_weight, latent_bias = encoder
    clip_count, rows_here, frame_count, col_count, channels = features.shape
    values = features.astype(jnp.float32)
    sums, squares = reduce_stats(group_stats(values, GROUPS))
    cell_count = rows_total * frame_count * col_count * (channels // GROUPS)
    normed = normalize(values, sums, squares, cell_count, vae_gain, vae_shift, GROUPS)
    active = jax.nn.silu(normed).astype(jnp.bfloat16)
    extended = extend_rows(active)
    first_frame = extended[:, :, :1]
    timed = jnp.concatenate([first_frame, first_frame, extended], axis=2)
    padded = jnp.pad(timed, ((0, 0), (0, 0), (0, 0), (1, 1), (0, 0)))
    mixed = jnp.zeros((clip_count * rows_here * frame_count * col_count, channels), jnp.float32)
    for time_tap in range(3):
        for row_tap in range(3):
            for col_tap in range(3):
                window = padded[
                    :,
                    row_tap : row_tap + rows_here,
                    time_tap : time_tap + frame_count,
                    col_tap : col_tap + col_count,
                    :,
                ]
                mixed = mixed + jnp.dot(
                    window.reshape(-1, channels),
                    vae_weight[time_tap, row_tap, col_tap],
                    preferred_element_type=jnp.float32,
                )
    summed = values + mixed.reshape(values.shape) + vae_bias
    pooled = (
        summed.reshape(clip_count, rows_here // 2, 2, frame_count, col_count // 2, 2, channels)
        .mean(axis=(2, 5))
        .astype(jnp.bfloat16)
    )
    latent = (
        jnp.dot(pooled.reshape(-1, channels), latent_weight, preferred_element_type=jnp.float32)
        + latent_bias
    )
    return latent.astype(jnp.bfloat16).reshape(
        clip_count, rows_here // 2, frame_count, col_count // 2, -1
    )


def spatial_conv(active, weight):
    clip_count, row_count, frame_count, col_count, channels = active.shape
    padded = jnp.pad(active, ((0, 0), (1, 1), (0, 0), (1, 1), (0, 0)))
    total = jnp.zeros(
        (clip_count * row_count * frame_count * col_count, weight.shape[-1]), jnp.float32
    )
    for row_tap in range(3):
        for col_tap in range(3):
            window = padded[:, row_tap : row_tap + row_count, :, col_tap : col_tap + col_count, :]
            total = total + jnp.dot(
                window.reshape(-1, channels),
                weight[row_tap, col_tap],
                preferred_element_type=jnp.float32,
            )
    return total.reshape(clip_count, row_count, frame_count, col_count, -1)


def embed(latent, offsets_now, in_weight, in_bias, pos_table):
    projected = spatial_conv(latent, in_weight) + in_bias
    row_count = latent.shape[1]
    table_rows = pos_table.shape[0]
    wanted = offsets_now[:, None] + jnp.arange(row_count, dtype=jnp.int32)[None, :]
    one_hot = (wanted[:, :, None] == jnp.arange(table_rows, dtype=jnp.int32)[None, None, :]).astype(
        jnp.bfloat16
    )
    placed = jnp.dot(one_hot.reshape(-1, table_rows), pos_table, preferred_element_type=jnp.float32)
    placed = placed.reshape(latent.shape[0], row_count, 1, 1, -1)
    return (projected + placed).astype(jnp.bfloat16)


def unet_layer(state, gain, shift, weight, bias):
    values = state.astype(jnp.float32)
    sums, squares = group_stats(values, GROUPS)
    cell_count = values.shape[1] * values.shape[2] * values.shape[3] * (values.shape[4] // GROUPS)
    normed = normalize(values, sums, squares, cell_count, gain, shift, GROUPS)
    active = jax.nn.silu(normed).astype(jnp.bfloat16)
    return (values + spatial_conv(active, weight) + bias).astype(jnp.bfloat16)


def per_device(
    features,
    vae_weight,
    vae_gain,
    vae_shift,
    vae_bias,
    latent_weight,
    latent_bias,
    slot_clips,
    row_offsets,
    in_weight,
    in_bias,
    pos_table,
    unet_gain,
    unet_shift,
    unet_weight,
    unet_bias,
):
    section_index = lax.axis_index("section")
    section_count = lax.axis_size("section")
    slab_index = lax.axis_index("slab")
    slab_count = lax.axis_size("slab")
    local_clips = features[0]
    clip_total = local_clips.shape[0]
    owned_count = clip_total // slab_count
    slab_rows = local_clips.shape[1]
    order = lax.dynamic_index_in_dim(slot_clips, section_index, 0, keepdims=False)
    encoder = (vae_weight, vae_gain, vae_shift, vae_bias, latent_weight, latent_bias)
    ordered = jnp.take(local_clips, order, axis=0)
    col_count = local_clips.shape[3]
    channels = local_clips.shape[4]
    shaped = ordered.reshape(
        slab_count, owned_count, slab_rows, ordered.shape[2], col_count * channels
    )
    whole = lax.all_to_all(shaped, "slab", split_axis=0, concat_axis=2, tiled=True)[0]
    item_count = whole.shape[0]
    full_rows = whole.shape[1]
    frame_count = whole.shape[2]
    whole = whole.reshape(item_count, full_rows, frame_count, col_count, channels)
    owned = encode(whole, full_rows, keep_stats, zero_rows, encoder)
    slot_offsets = jnp.take_along_axis(row_offsets, slot_clips, axis=1)
    my_offsets = lax.dynamic_slice_in_dim(slot_offsets, slab_index * owned_count, owned_count, 1)
    lat_rows, frame_count, lat_cols = (owned.shape[1], owned.shape[2], owned.shape[3])
    width = unet_weight.shape[-1]
    stored = jnp.zeros(
        (section_count, owned_count, lat_rows, frame_count, lat_cols, width), jnp.bfloat16
    )
    arriving = jnp.zeros((owned_count, lat_rows, frame_count, lat_cols, width), jnp.bfloat16)

    def tick_step(tick_index, state_tuple):
        arriving_now, conveyor, stored_now = state_tuple
        feed_index = jnp.minimum(tick_index, section_count - 1)
        current = conveyor
        offsets_now = lax.dynamic_index_in_dim(my_offsets, feed_index, 0, keepdims=False)
        embedded = embed(current, offsets_now, in_weight, in_bias, pos_table)
        layer_input = jnp.where(section_index == 0, embedded, arriving_now)
        result = unet_layer(layer_input, unet_gain[0], unet_shift[0], unet_weight[0], unet_bias[0])
        micro_index = tick_index - section_index
        in_range = jnp.logical_and(micro_index >= 0, micro_index < section_count)
        position = jnp.clip(micro_index, 0, section_count - 1)
        previous = lax.dynamic_index_in_dim(stored_now, position, 0, keepdims=False)
        stored_now = lax.dynamic_update_index_in_dim(
            stored_now, jnp.where(in_range, result, previous), position, 0
        )
        arriving_now = from_behind(result, "section", 1)
        conveyor = from_behind(conveyor, "section", -1)
        return (arriving_now, conveyor, stored_now)

    final_tuple = lax.fori_loop(0, 2 * section_count - 1, tick_step, (arriving, owned, stored))
    stored = final_tuple[2]
    return stored.reshape(1, section_count, owned_count, lat_rows, frame_count, lat_cols * width)


def solution(mesh):
    return jax.shard_map(
        per_device,
        mesh=mesh,
        in_specs=(
            P("section", None, "slab", None, None, None),
            P(),
            P(),
            P(),
            P(),
            P(),
            P(),
            P(),
            P(),
            P(),
            P(),
            P(),
            P("section", None),
            P("section", None),
            P("section", None, None, None, None),
            P("section", None),
        ),
        out_specs=P("section", None, "slab", None, None, None),
        check_vma=False,
    )
```

profile of v0, /device:TPU:0, one launch (start us, length us, event | category | flops | bytes accessed | tf_op | source)
XLA Modules:
  0.0 142.5 jit_solution(7506867494145057589)
XLA Ops:
  2.9 6.3 %all-to-all-start = ((bf16[8,1,2,2,2048]{4,3,2,1,0:T(2,128)(2,1)}), bf16[8,1,2,2,2048]{4,3,2,1,0:T(2,128)(2,1)S(1)}, u32[]{:S(2)}, u32[]{:S(2)}) async-start(bf16[8,1,2,2,2048]{4,3,2,1,0:T(2,128)(2,1)} %broadcast_select_fusion), calls=%async_computation | async-start | bytes 262144 | tf_op jit(solution)/shard_map/all_to_all | solution.py:158
  11.3 1.4 %gather_fusion.1 = s32[32]{0:T(128)S(1)} fusion(s32[4,8]{1,0:T(4,128)} %param.26, s32[32]{0:T(128)S(1)} %reshape.745), kind=kCustom, calls=%fused_computation.1 | custom fusion | bytes 512 | tf_op jit(solution)/shard_map/jit(take_along_axis)/gather | solution.py:164
  13.6 2.3 %all-to-all-done = bf16[8,1,2,2,2048]{4,3,2,1,0:T(2,128)(2,1)S(1)} async-done(((bf16[8,1,2,2,2048]{4,3,2,1,0:T(2,128)(2,1)}), bf16[8,1,2,2,2048]{4,3,2,1,0:T(2,128)(2,1)S(1)}, u32[]{:S(2)}, u32[]{:S(2)}) %all-to-all-start) | async-done | bytes 131104 | tf_op jit(solution)/shard_map/all_to_all | solution.py:158
  16.0 3.6 %reshape.736 = f32[1,256,32,8]{3,2,1,0:T(8,128)} reshape(bf16[8,1,2,2,2048]{4,3,2,1,0:T(2,128)(2,1)S(1)} %all-to-all-done) | data formatting | bytes 393216 | tf_op jit(solution)/shard_map/convert_element_type | solution.py:45
  19.6 3.0 %fusion.98 = (f32[32]{0:T(128)S(1)}, f32[32]{0:T(128)S(1)}) fusion(f32[1,256,32,8]{3,2,1,0:T(8,128)} %reshape.736), kind=kLoop, calls=%fused_computation.218 | loop fusion | flops 196544 | bytes 262400 | tf_op jit(solution)/shard_map/reduce_sum | solution.py:21
  25.5 1.6 %convert_element_type.157 = bf16[256,256]{1,0:T(8,128)(2,1)} reshape(bf16[8,1,2,2,2048]{4,3,2,1,0:T(2,128)(2,1)} %fusion.37) | data formatting | bytes 262144 | tf_op jit(solution)/shard_map/convert_element_type | solution.py:49
  27.1 1.3 fusion.68
  29.6 1.2 convolution_add_fusion.40
  30.7 1.1 convolution_add_fusion.39
  31.8 1.1 convolution_add_fusion.38
  38.5 103.1 %while.19 = (s32[]{:T(128)}, bf16[1,8,2,4,320]{4,3,2,1,0:T(4,128)(2,1)S(1)}, bf16[1,8,2,4,16]{4,3,2,1,0:T(4,128)(2,1)S(1)}, bf16[4,1,8,2,4,320]{5,4,3,2,1,0:T(4,...) while((s32[]{:T(128)}, ...), condition=%wide.region_8.9_spmd, body=%wide.region_3.8_spmd.sunk | while | flops 125318256 | bytes 8348378 | solution.py:192
  44.4 3.4 %collective-permute-start = (bf16[1,8,2,4,320]{4,3,2,1,0:T(4,128)(2,1)S(1)}, bf16[1,8,2,4,320]{4,3,2,1,0:T(4,128)(2,1)S(1)}, u32[]{:S(2)}, u32[]{:S(2)}) collective-permute-start(bf16[1,8,2,4,320]{4,3,2,1,0:T(4,128)(2,1)S(1)} %get-tuple-element.572), channel_id=1, source_target_pairs={{0,8},{8,16},{16,24},{1,9},{9,17},{17,25},{2,10},{10,18},{18,26},{... | collective-permute-start | bytes 122888 | tf_op jit(solution)/shard_map/while/body/eval_jaxpr/ppermute | solution.py:15
  47.8 1.3 collective-permute-start.1
  49.1 4.3 %collective-permute-done.1 = bf16[1,8,2,4,16]{4,3,2,1,0:T(4,128)(2,1)S(1)} collective-permute-done((bf16[1,8,2,4,16]{4,3,2,1,0:T(4,128)(2,1)S(1)}, bf16[1,8,2,4,16]{4,3,2,1,0:T(4,128)(2,1)S(1)}, u32[]{:S(2)}, u32[]{:S(2)}) %collective-permute-start.1) | collective-permute-done | bytes 2080 | tf_op jit(solution)/shard_map/while/body/eval_jaxpr/ppermute | solution.py:15
  59.3 4.3 %collective-permute-start = (bf16[1,8,2,4,320]{4,3,2,1,0:T(4,128)(2,1)S(1)}, bf16[1,8,2,4,320]{4,3,2,1,0:T(4,128)(2,1)S(1)}, u32[]{:S(2)}, u32[]{:S(2)}) collective-permute-start(bf16[1,8,2,4,320]{4,3,2,1,0:T(4,128)(2,1)S(1)} %get-tuple-element.572), channel_id=1, source_target_pairs={{0,8},{8,16},{16,24},{1,9},{9,17},{17,25},{2,10},{10,18},{18,26},{... | collective-permute-start | bytes 122888 | tf_op jit(solution)/shard_map/while/body/eval_jaxpr/ppermute | solution.py:15
  63.6 1.3 collective-permute-start.1
  64.9 4.3 %collective-permute-done.1 = bf16[1,8,2,4,16]{4,3,2,1,0:T(4,128)(2,1)S(1)} collective-permute-done((bf16[1,8,2,4,16]{4,3,2,1,0:T(4,128)(2,1)S(1)}, bf16[1,8,2,4,16]{4,3,2,1,0:T(4,128)(2,1)S(1)}, u32[]{:S(2)}, u32[]{:S(2)}) %collective-permute-start.1) | collective-permute-done | bytes 2080 | tf_op jit(solution)/shard_map/while/body/eval_jaxpr/ppermute | solution.py:15
  75.1 3.5 %collective-permute-start = (bf16[1,8,2,4,320]{4,3,2,1,0:T(4,128)(2,1)S(1)}, bf16[1,8,2,4,320]{4,3,2,1,0:T(4,128)(2,1)S(1)}, u32[]{:S(2)}, u32[]{:S(2)}) collective-permute-start(bf16[1,8,2,4,320]{4,3,2,1,0:T(4,128)(2,1)S(1)} %get-tuple-element.572), channel_id=1, source_target_pairs={{0,8},{8,16},{16,24},{1,9},{9,17},{17,25},{2,10},{10,18},{18,26},{... | collective-permute-start | bytes 122888 | tf_op jit(solution)/shard_map/while/body/eval_jaxpr/ppermute | solution.py:15
  78.6 1.3 collective-permute-start.1
  79.9 4.3 %collective-permute-done.1 = bf16[1,8,2,4,16]{4,3,2,1,0:T(4,128)(2,1)S(1)} collective-permute-done((bf16[1,8,2,4,16]{4,3,2,1,0:T(4,128)(2,1)S(1)}, bf16[1,8,2,4,16]{4,3,2,1,0:T(4,128)(2,1)S(1)}, u32[]{:S(2)}, u32[]{:S(2)}) %collective-permute-start.1) | collective-permute-done | bytes 2080 | tf_op jit(solution)/shard_map/while/body/eval_jaxpr/ppermute | solution.py:15
  90.1 2.8 %collective-permute-start = (bf16[1,8,2,4,320]{4,3,2,1,0:T(4,128)(2,1)S(1)}, bf16[1,8,2,4,320]{4,3,2,1,0:T(4,128)(2,1)S(1)}, u32[]{:S(2)}, u32[]{:S(2)}) collective-permute-start(bf16[1,8,2,4,320]{4,3,2,1,0:T(4,128)(2,1)S(1)} %get-tuple-element.572), channel_id=1, source_target_pairs={{0,8},{8,16},{16,24},{1,9},{9,17},{17,25},{2,10},{10,18},{18,26},{... | collective-permute-start | bytes 122888 | tf_op jit(solution)/shard_map/while/body/eval_jaxpr/ppermute | solution.py:15
  92.9 1.3 collective-permute-start.1
  94.2 4.3 %collective-permute-done.1 = bf16[1,8,2,4,16]{4,3,2,1,0:T(4,128)(2,1)S(1)} collective-permute-done((bf16[1,8,2,4,16]{4,3,2,1,0:T(4,128)(2,1)S(1)}, bf16[1,8,2,4,16]{4,3,2,1,0:T(4,128)(2,1)S(1)}, u32[]{:S(2)}, u32[]{:S(2)}) %collective-permute-start.1) | collective-permute-done | bytes 2080 | tf_op jit(solution)/shard_map/while/body/eval_jaxpr/ppermute | solution.py:15
  104.5 2.8 %collective-permute-start = (bf16[1,8,2,4,320]{4,3,2,1,0:T(4,128)(2,1)S(1)}, bf16[1,8,2,4,320]{4,3,2,1,0:T(4,128)(2,1)S(1)}, u32[]{:S(2)}, u32[]{:S(2)}) collective-permute-start(bf16[1,8,2,4,320]{4,3,2,1,0:T(4,128)(2,1)S(1)} %get-tuple-element.572), channel_id=1, source_target_pairs={{0,8},{8,16},{16,24},{1,9},{9,17},{17,25},{2,10},{10,18},{18,26},{... | collective-permute-start | bytes 122888 | tf_op jit(solution)/shard_map/while/body/eval_jaxpr/ppermute | solution.py:15
  107.3 1.3 collective-permute-start.1
  108.6 4.3 %collective-permute-done.1 = bf16[1,8,2,4,16]{4,3,2,1,0:T(4,128)(2,1)S(1)} collective-permute-done((bf16[1,8,2,4,16]{4,3,2,1,0:T(4,128)(2,1)S(1)}, bf16[1,8,2,4,16]{4,3,2,1,0:T(4,128)(2,1)S(1)}, u32[]{:S(2)}, u32[]{:S(2)}) %collective-permute-start.1) | collective-permute-done | bytes 2080 | tf_op jit(solution)/shard_map/while/body/eval_jaxpr/ppermute | solution.py:15
  118.8 2.8 %collective-permute-start = (bf16[1,8,2,4,320]{4,3,2,1,0:T(4,128)(2,1)S(1)}, bf16[1,8,2,4,320]{4,3,2,1,0:T(4,128)(2,1)S(1)}, u32[]{:S(2)}, u32[]{:S(2)}) collective-permute-start(bf16[1,8,2,4,320]{4,3,2,1,0:T(4,128)(2,1)S(1)} %get-tuple-element.572), channel_id=1, source_target_pairs={{0,8},{8,16},{16,24},{1,9},{9,17},{17,25},{2,10},{10,18},{18,26},{... | collective-permute-start | bytes 122888 | tf_op jit(solution)/shard_map/while/body/eval_jaxpr/ppermute | solution.py:15
  121.6 1.3 collective-permute-start.1
  122.9 4.3 %collective-permute-done.1 = bf16[1,8,2,4,16]{4,3,2,1,0:T(4,128)(2,1)S(1)} collective-permute-done((bf16[1,8,2,4,16]{4,3,2,1,0:T(4,128)(2,1)S(1)}, bf16[1,8,2,4,16]{4,3,2,1,0:T(4,128)(2,1)S(1)}, u32[]{:S(2)}, u32[]{:S(2)}) %collective-permute-start.1) | collective-permute-done | bytes 2080 | tf_op jit(solution)/shard_map/while/body/eval_jaxpr/ppermute | solution.py:15
  133.1 2.8 %collective-permute-start = (bf16[1,8,2,4,320]{4,3,2,1,0:T(4,128)(2,1)S(1)}, bf16[1,8,2,4,320]{4,3,2,1,0:T(4,128)(2,1)S(1)}, u32[]{:S(2)}, u32[]{:S(2)}) collective-permute-start(bf16[1,8,2,4,320]{4,3,2,1,0:T(4,128)(2,1)S(1)} %get-tuple-element.572), channel_id=1, source_target_pairs={{0,8},{8,16},{16,24},{1,9},{9,17},{17,25},{2,10},{10,18},{18,26},{... | collective-permute-start | bytes 122888 | tf_op jit(solution)/shard_map/while/body/eval_jaxpr/ppermute | solution.py:15
  136.0 1.3 collective-permute-start.1
  137.3 4.3 %collective-permute-done.1 = bf16[1,8,2,4,16]{4,3,2,1,0:T(4,128)(2,1)S(1)} collective-permute-done((bf16[1,8,2,4,16]{4,3,2,1,0:T(4,128)(2,1)S(1)}, bf16[1,8,2,4,16]{4,3,2,1,0:T(4,128)(2,1)S(1)}, u32[]{:S(2)}, u32[]{:S(2)}) %collective-permute-start.1) | collective-permute-done | bytes 2080 | tf_op jit(solution)/shard_map/while/body/eval_jaxpr/ppermute | solution.py:15
  (460 shorter events, 55.2 us)
Async XLA Ops:
  0.0 1.4 %copy-start = (bf16[1,8,2,2,8,256]{5,4,3,2,1,0:T(8,128)(2,1)S(1)}, bf16[1,8,2,2,8,256]{5,4,3,2,1,0:T(8,128)(2,1)}, u32[]{:S(2)}) copy-start(bf16[1,8,2,2,8,256]{5,4,3,2,1,0:T(8,128)(2,1)} %param.18) | copy-start | bytes 393220
  2.9 13.1 %all-to-all-start = ((bf16[8,1,2,2,2048]{4,3,2,1,0:T(2,128)(2,1)}), bf16[8,1,2,2,2048]{4,3,2,1,0:T(2,128)(2,1)S(1)}, u32[]{:S(2)}, u32[]{:S(2)}) async-start(bf16[8,1,2,2,2048]{4,3,2,1,0:T(2,128)(2,1)} %broadcast_select_fusion), calls=%async_computation | async-start | bytes 262144 | tf_op jit(solution)/shard_map/all_to_all | solution.py:158
  13.6 9.4 %copy-start.9 = (f32[256]{0:T(256)S(1)}, f32[256]{0:T(256)}, u32[]{:S(2)}) copy-start(f32[256]{0:T(256)} %param.21) | copy-start | bytes 3076
  13.6 9.4 %copy-start.10 = (f32[256]{0:T(256)S(1)}, f32[256]{0:T(256)}, u32[]{:S(2)}) copy-start(f32[256]{0:T(256)} %param.20) | copy-start | bytes 3076
  27.1 5.8 %copy-start.2 = (bf16[3,3,3,256,256]{4,3,2,1,0:T(8,128)(2,1)S(1)}, bf16[3,3,3,256,256]{4,3,2,1,0:T(8,128)(2,1)}, u32[]{:S(2)}) copy-start(bf16[3,3,3,256,256]{4,3,2,1,0:T(8,128)(2,1)} %param.19) | copy-start | bytes 10616836
  34.5 1.9 %copy-start.4 = (bf16[256,256]{1,0:T(8,128)(2,1)S(1)}, bf16[256,256]{1,0:T(8,128)(2,1)}, u32[]{:S(2)}) copy-start(bf16[256,256]{1,0:T(8,128)(2,1)} %convert_element_type.157) | copy-start | bytes 393220
  35.7 2.0 %copy-start.11 = (f32[256]{0:T(256)S(1)}, f32[256]{0:T(256)}, u32[]{:S(2)}) copy-start(f32[256]{0:T(256)} %param.22) | copy-start | bytes 3076
  35.9 2.2 %copy-start.13 = (bf16[256,16]{0,1:T(8,128)(2,1)S(1)}, bf16[256,16]{0,1:T(8,128)(2,1)}, u32[]{:S(2)}) copy-start(bf16[256,16]{0,1:T(8,128)(2,1)} %param.23) | copy-start | bytes 24580
  35.9 2.2 %copy-start.14 = (f32[16]{0:T(128)S(1)}, f32[16]{0:T(128)}, u32[]{:S(2)}) copy-start(f32[16]{0:T(128)} %param.24) | copy-start | bytes 196
  36.1 2.4 %copy-start.1 = (bf16[1,3,3,320,320]{4,3,2,1,0:T(8,128)(2,1)S(1)}, bf16[1,3,3,320,320]{4,3,2,1,0:T(8,128)(2,1)}, u32[]{:S(2)}) copy-start(bf16[1,3,3,320,320]{4,3,2,1,0:T(8,128)(2,1)} %param.32) | copy-start | bytes 5529604
  36.1 2.4 %copy-start.3 = (bf16[3,3,16,320]{3,2,1,0:T(8,128)(2,1)S(1)}, bf16[3,3,16,320]{3,2,1,0:T(8,128)(2,1)}, u32[]{:S(2)}) copy-start(bf16[3,3,16,320]{3,2,1,0:T(8,128)(2,1)} %param.27) | copy-start | bytes 276484
  36.1 2.4 %copy-start.5 = (f32[320]{0:T(512)S(1)}, f32[320]{0:T(512)}, u32[]{:S(2)}) copy-start(f32[320]{0:T(512)} %param.28) | copy-start | bytes 3844
  36.1 2.4 %copy-start.6 = (f32[1,320]{1,0:T(1,128)S(1)}, f32[1,320]{1,0:T(1,128)}, u32[]{:S(2)}) copy-start(f32[1,320]{1,0:T(1,128)} %param.30) | copy-start | bytes 3844
  36.1 2.3 %copy-start.7 = (f32[1,320]{1,0:T(1,128)S(1)}, f32[1,320]{1,0:T(1,128)}, u32[]{:S(2)}) copy-start(f32[1,320]{1,0:T(1,128)} %param.31) | copy-start | bytes 3844
  36.2 2.3 %copy-start.8 = (f32[1,320]{1,0:T(1,128)S(1)}, f32[1,320]{1,0:T(1,128)}, u32[]{:S(2)}) copy-start(f32[1,320]{1,0:T(1,128)} %param.33) | copy-start | bytes 3844
  36.2 2.3 %copy-start.12 = (bf16[128,320]{0,1:T(8,128)(2,1)S(1)}, bf16[128,320]{0,1:T(8,128)(2,1)}, u32[]{:S(2)}) copy-start(bf16[128,320]{0,1:T(8,128)(2,1)} %param.29) | copy-start | bytes 245764
  44.4 9.0 %collective-permute-start = (bf16[1,8,2,4,320]{4,3,2,1,0:T(4,128)(2,1)S(1)}, bf16[1,8,2,4,320]{4,3,2,1,0:T(4,128)(2,1)S(1)}, u32[]{:S(2)}, u32[]{:S(2)}) collective-permute-start(bf16[1,8,2,4,320]{4,3,2,1,0:T(4,128)(2,1)S(1)} %get-tuple-element.572), channel_id=1, source_target_pairs={{0,8},{8,16},{16,24},{1,9},{9,17},{17,25},{2,10},{10,18},{18,26},{... | collective-permute-start | bytes 122888 | tf_op jit(solution)/shard_map/while/body/eval_jaxpr/ppermute | solution.py:15
  47.8 5.6 %collective-permute-start.1 = (bf16[1,8,2,4,16]{4,3,2,1,0:T(4,128)(2,1)S(1)}, bf16[1,8,2,4,16]{4,3,2,1,0:T(4,128)(2,1)S(1)}, u32[]{:S(2)}, u32[]{:S(2)}) collective-permute-start(bf16[1,8,2,4,16]{4,3,2,1,0:T(4,128)(2,1)S(1)} %copy.35), channel_id=1, source_target_pairs={{8,0},{16,8},{24,16},{9,1},{17,9},{25,17},{10,2},{18,10},{26,18},{... | collective-permute-start | bytes 6152 | tf_op jit(solution)/shard_map/while/body/eval_jaxpr/ppermute | solution.py:15
  59.3 9.9 %collective-permute-start = (bf16[1,8,2,4,320]{4,3,2,1,0:T(4,128)(2,1)S(1)}, bf16[1,8,2,4,320]{4,3,2,1,0:T(4,128)(2,1)S(1)}, u32[]{:S(2)}, u32[]{:S(2)}) collective-permute-start(bf16[1,8,2,4,320]{4,3,2,1,0:T(4,128)(2,1)S(1)} %get-tuple-element.572), channel_id=1, source_target_pairs={{0,8},{8,16},{16,24},{1,9},{9,17},{17,25},{2,10},{10,18},{18,26},{... | collective-permute-start | bytes 122888 | tf_op jit(solution)/shard_map/while/body/eval_jaxpr/ppermute | solution.py:15
  63.6 5.6 %collective-permute-start.1 = (bf16[1,8,2,4,16]{4,3,2,1,0:T(4,128)(2,1)S(1)}, bf16[1,8,2,4,16]{4,3,2,1,0:T(4,128)(2,1)S(1)}, u32[]{:S(2)}, u32[]{:S(2)}) collective-permute-start(bf16[1,8,2,4,16]{4,3,2,1,0:T(4,128)(2,1)S(1)} %copy.35), channel_id=1, source_target_pairs={{8,0},{16,8},{24,16},{9,1},{17,9},{25,17},{10,2},{18,10},{26,18},{... | collective-permute-start | bytes 6152 | tf_op jit(solution)/shard_map/while/body/eval_jaxpr/ppermute | solution.py:15
  75.1 9.1 %collective-permute-start = (bf16[1,8,2,4,320]{4,3,2,1,0:T(4,128)(2,1)S(1)}, bf16[1,8,2,4,320]{4,3,2,1,0:T(4,128)(2,1)S(1)}, u32[]{:S(2)}, u32[]{:S(2)}) collective-permute-start(bf16[1,8,2,4,320]{4,3,2,1,0:T(4,128)(2,1)S(1)} %get-tuple-element.572), channel_id=1, source_target_pairs={{0,8},{8,16},{16,24},{1,9},{9,17},{17,25},{2,10},{10,18},{18,26},{... | collective-permute-start | bytes 122888 | tf_op jit(solution)/shard_map/while/body/eval_jaxpr/ppermute | solution.py:15
  78.6 5.6 %collective-permute-start.1 = (bf16[1,8,2,4,16]{4,3,2,1,0:T(4,128)(2,1)S(1)}, bf16[1,8,2,4,16]{4,3,2,1,0:T(4,128)(2,1)S(1)}, u32[]{:S(2)}, u32[]{:S(2)}) collective-permute-start(bf16[1,8,2,4,16]{4,3,2,1,0:T(4,128)(2,1)S(1)} %copy.35), channel_id=1, source_target_pairs={{8,0},{16,8},{24,16},{9,1},{17,9},{25,17},{10,2},{18,10},{26,18},{... | collective-permute-start | bytes 6152 | tf_op jit(solution)/shard_map/while/body/eval_jaxpr/ppermute | solution.py:15
  90.1 8.5 %collective-permute-start = (bf16[1,8,2,4,320]{4,3,2,1,0:T(4,128)(2,1)S(1)}, bf16[1,8,2,4,320]{4,3,2,1,0:T(4,128)(2,1)S(1)}, u32[]{:S(2)}, u32[]{:S(2)}) collective-permute-start(bf16[1,8,2,4,320]{4,3,2,1,0:T(4,128)(2,1)S(1)} %get-tuple-element.572), channel_id=1, source_target_pairs={{0,8},{8,16},{16,24},{1,9},{9,17},{17,25},{2,10},{10,18},{18,26},{... | collective-permute-start | bytes 122888 | tf_op jit(solution)/shard_map/while/body/eval_jaxpr/ppermute | solution.py:15
  92.9 5.6 %collective-permute-start.1 = (bf16[1,8,2,4,16]{4,3,2,1,0:T(4,128)(2,1)S(1)}, bf16[1,8,2,4,16]{4,3,2,1,0:T(4,128)(2,1)S(1)}, u32[]{:S(2)}, u32[]{:S(2)}) collective-permute-start(bf16[1,8,2,4,16]{4,3,2,1,0:T(4,128)(2,1)S(1)} %copy.35), channel_id=1, source_target_pairs={{8,0},{16,8},{24,16},{9,1},{17,9},{25,17},{10,2},{18,10},{26,18},{... | collective-permute-start | bytes 6152 | tf_op jit(solution)/shard_map/while/body/eval_jaxpr/ppermute | solution.py:15
  104.5 8.5 %collective-permute-start = (bf16[1,8,2,4,320]{4,3,2,1,0:T(4,128)(2,1)S(1)}, bf16[1,8,2,4,320]{4,3,2,1,0:T(4,128)(2,1)S(1)}, u32[]{:S(2)}, u32[]{:S(2)}) collective-permute-start(bf16[1,8,2,4,320]{4,3,2,1,0:T(4,128)(2,1)S(1)} %get-tuple-element.572), channel_id=1, source_target_pairs={{0,8},{8,16},{16,24},{1,9},{9,17},{17,25},{2,10},{10,18},{18,26},{... | collective-permute-start | bytes 122888 | tf_op jit(solution)/shard_map/while/body/eval_jaxpr/ppermute | solution.py:15
  107.3 5.6 %collective-permute-start.1 = (bf16[1,8,2,4,16]{4,3,2,1,0:T(4,128)(2,1)S(1)}, bf16[1,8,2,4,16]{4,3,2,1,0:T(4,128)(2,1)S(1)}, u32[]{:S(2)}, u32[]{:S(2)}) collective-permute-start(bf16[1,8,2,4,16]{4,3,2,1,0:T(4,128)(2,1)S(1)} %copy.35), channel_id=1, source_target_pairs={{8,0},{16,8},{24,16},{9,1},{17,9},{25,17},{10,2},{18,10},{26,18},{... | collective-permute-start | bytes 6152 | tf_op jit(solution)/shard_map/while/body/eval_jaxpr/ppermute | solution.py:15
  118.8 8.5 %collective-permute-start = (bf16[1,8,2,4,320]{4,3,2,1,0:T(4,128)(2,1)S(1)}, bf16[1,8,2,4,320]{4,3,2,1,0:T(4,128)(2,1)S(1)}, u32[]{:S(2)}, u32[]{:S(2)}) collective-permute-start(bf16[1,8,2,4,320]{4,3,2,1,0:T(4,128)(2,1)S(1)} %get-tuple-element.572), channel_id=1, source_target_pairs={{0,8},{8,16},{16,24},{1,9},{9,17},{17,25},{2,10},{10,18},{18,26},{... | collective-permute-start | bytes 122888 | tf_op jit(solution)/shard_map/while/body/eval_jaxpr/ppermute | solution.py:15
  121.6 5.6 %collective-permute-start.1 = (bf16[1,8,2,4,16]{4,3,2,1,0:T(4,128)(2,1)S(1)}, bf16[1,8,2,4,16]{4,3,2,1,0:T(4,128)(2,1)S(1)}, u32[]{:S(2)}, u32[]{:S(2)}) collective-permute-start(bf16[1,8,2,4,16]{4,3,2,1,0:T(4,128)(2,1)S(1)} %copy.35), channel_id=1, source_target_pairs={{8,0},{16,8},{24,16},{9,1},{17,9},{25,17},{10,2},{18,10},{26,18},{... | collective-permute-start | bytes 6152 | tf_op jit(solution)/shard_map/while/body/eval_jaxpr/ppermute | solution.py:15
  133.1 8.5 %collective-permute-start = (bf16[1,8,2,4,320]{4,3,2,1,0:T(4,128)(2,1)S(1)}, bf16[1,8,2,4,320]{4,3,2,1,0:T(4,128)(2,1)S(1)}, u32[]{:S(2)}, u32[]{:S(2)}) collective-permute-start(bf16[1,8,2,4,320]{4,3,2,1,0:T(4,128)(2,1)S(1)} %get-tuple-element.572), channel_id=1, source_target_pairs={{0,8},{8,16},{16,24},{1,9},{9,17},{17,25},{2,10},{10,18},{18,26},{... | collective-permute-start | bytes 122888 | tf_op jit(solution)/shard_map/while/body/eval_jaxpr/ppermute | solution.py:15
  136.0 5.6 %collective-permute-start.1 = (bf16[1,8,2,4,16]{4,3,2,1,0:T(4,128)(2,1)S(1)}, bf16[1,8,2,4,16]{4,3,2,1,0:T(4,128)(2,1)S(1)}, u32[]{:S(2)}, u32[]{:S(2)}) collective-permute-start(bf16[1,8,2,4,16]{4,3,2,1,0:T(4,128)(2,1)S(1)} %copy.35), channel_id=1, source_target_pairs={{8,0},{16,8},{24,16},{9,1},{17,9},{25,17},{10,2},{18,10},{26,18},{... | collective-permute-start | bytes 6152 | tf_op jit(solution)/shard_map/while/body/eval_jaxpr/ppermute | solution.py:15
where the time goes:
time: 143 us
  starting transfers between devices  37.8 us (26%)
  waiting for transfers between devices  32.7 us (23%)
  matrix products  29.7 us (21%)
  local copies, waits for them, and re-layouts  23 us (16%)
  other arithmetic  16.9 us (12%)
  loops' own time  1.98 us (1%)
    ppermute x14, starting transfers between devices, from_behind(): lax.ppermute(value, axis, [(source, source + steps) for source in range(i...  31.4 us
    ppermute x14, waiting for transfers between devices, from_behind(): lax.ppermute(value, axis, [(source, source + steps) for source in range(i...  30.3 us
    dot_general x126, matrix products, spatial_conv(): jnp.dot(window.reshape(-1, channels), weight[row_tap, col_tap], preferred...  18.5 us
    dot_general x27, matrix products, encode(): jnp.dot(window.reshape(-1, channels), vae_weight[time_tap, row_tap, col_t...  9.88 us
    all_to_all x1, starting transfers between devices, per_device(): lax.all_to_all(shaped, 'slab', split_axis=0, concat_axis=2, tiled=True)[0]  6.33 us
    reduce_sum x15, other arithmetic, group_stats(): jnp.sum(grouped, axis=(1, 3))  4.55 us
    add x7, other arithmetic, embed(): offsets_now[:, None] + jnp.arange(row_count, dtype=jnp.int32)[None, :]  4.53 us
    convert_element_type x3, local copies, waits for them, and re-layouts, encode(): values = features.astype(jnp.float32)  3.81 us
  transfers between devices with their start and end apart: 15, of which 8 were waited for; matrix products, arithmetic and copies ran while one was open for 3% of the time, Pallas kernels for 0%

commit v1 on v0

v1 whole, which is shorter than its diff:
```python
import functools

import jax
import jax.numpy as jnp
from jax import lax
from jax.experimental import pallas as pl
from jax.experimental.pallas import tpu as pltpu
from jax.sharding import PartitionSpec as P

GROUPS = 32
LANES = 128
EPS = 1e-06
VMEM_LIMIT = 48 * 1024 * 1024
F32 = jnp.float32
BF16 = jnp.bfloat16


def vmem():
    return pl.BlockSpec(memory_space=pltpu.VMEM)


def smem():
    return pl.BlockSpec(memory_space=pltpu.SMEM)


def params():
    return pltpu.CompilerParams(vmem_limit_bytes=VMEM_LIMIT)


def group_sums(rows, channels):
    size = channels // GROUPS
    count = rows.shape[0]

    def group_of(axis):
        index = lax.broadcasted_iota(jnp.int32, (channels, channels), axis).astype(F32)
        return jnp.floor((index + 0.5) * (1.0 / size))

    same = (group_of(0) == group_of(1)).astype(BF16)
    high = rows.astype(BF16)
    rest = rows - high.astype(F32)
    middle = rest.astype(BF16)
    low = (rest - middle.astype(F32)).astype(BF16)
    total = jnp.dot(high, same, preferred_element_type=F32)
    total += jnp.dot(middle, same, preferred_element_type=F32)
    total += jnp.dot(low, same, preferred_element_type=F32)
    return total.reshape(count, channels)


def silu(value):
    return value / (1.0 + jnp.exp(-value))


def encode_kernel(
    x_ref, weight_ref, gain_ref, shift_ref, bias_ref, lat_weight_ref, lat_bias_ref,
    out_ref, dup_ref, act_ref, pool_ref,
):
    row_count, frames, cols, channels = x_ref.shape[1:]
    plane = frames * cols
    size = row_count * plane
    lat_rows, lat_cols = row_count // 2, cols // 2
    for item in range(x_ref.shape[0]):
        x = x_ref[item].astype(F32).reshape(size, channels)
        sums = jnp.concatenate(
            [jnp.sum(x, axis=0, keepdims=True), jnp.sum(x * x, axis=0, keepdims=True)]
            + [jnp.zeros((6, channels), F32)],
            axis=0,
        )
        sums = group_sums(sums, channels) * (1.0 / (size * (channels // GROUPS)))
        mean = sums[0:1]
        inverse = lax.rsqrt(sums[1:2] - mean * mean + EPS)
        act = silu((x - mean) * inverse * gain_ref[...] + shift_ref[...])
        column = lax.broadcasted_iota(jnp.int32, (size, 1), 0) & (cols - 1)
        for tap in range(3):
            if tap == 0:
                moved = jnp.where(column == 0, 0.0, pltpu.roll(act, 1, 0))
            elif tap == 2:
                moved = jnp.where(column == cols - 1, 0.0, pltpu.roll(act, size - 1, 0))
            else:
                moved = act
            lanes = pl.ds(tap * channels, channels)
            first = moved.reshape(row_count, frames, cols, channels)[:, 0:1]
            first = jnp.broadcast_to(first, (row_count, frames, cols, channels))
            act_ref[pl.ds(plane, size), lanes] = moved.astype(BF16)
            dup_ref[pl.ds(plane, size), lanes] = first.reshape(size, channels).astype(BF16)
        for ref in (act_ref, dup_ref):
            ref[pl.ds(0, plane), :] = jnp.zeros((plane, 3 * channels), BF16)
            ref[pl.ds(plane + size, plane), :] = jnp.zeros((plane, 3 * channels), BF16)
        total = x + bias_ref[...]
        for time_tap in range(3):
            source = act_ref if time_tap == 2 else dup_ref
            for row_tap in range(3):
                weight = weight_ref[time_tap, row_tap].reshape(3 * channels, channels)
                window = source[pl.ds(row_tap * plane, size), :]
                total += jnp.dot(window, weight, preferred_element_type=F32)
        paired = total.reshape(lat_rows, 2, plane, channels)
        merged = (paired[:, 0] + paired[:, 1]).reshape(lat_rows * plane, channels)
        halves = []
        for part in range(channels // LANES):
            pool_ref[part] = merged[:, part * LANES : (part + 1) * LANES]
            picked = []
            for col in range(lat_cols):
                left = pool_ref[part, pl.ds(2 * col, lat_rows * frames, stride=cols), :]
                right = pool_ref[part, pl.ds(2 * col + 1, lat_rows * frames, stride=cols), :]
                picked.append((left + right) * 0.25)
            halves.append(jnp.concatenate(picked, axis=0))
        pooled = jnp.concatenate(halves, axis=1).astype(BF16)
        latent = jnp.dot(pooled, lat_weight_ref[...], preferred_element_type=F32)
        out_ref[item] = (latent + lat_bias_ref[...]).astype(BF16)


def encode(clips, vae_weight, gain, shift, bias, lat_weight, lat_bias):
    items, row_count, frames, cols, channels = clips.shape
    plane = frames * cols
    lat_rows, lat_cols = row_count // 2, cols // 2
    padded = pltpu.VMEM(((row_count + 2) * plane, 3 * channels), BF16)
    return pl.pallas_call(
        encode_kernel,
        out_shape=jax.ShapeDtypeStruct(
            (items, lat_cols * lat_rows * frames, lat_weight.shape[1]), BF16
        ),
        in_specs=[vmem()] * 7,
        out_specs=vmem(),
        scratch_shapes=[padded, padded, pltpu.VMEM((channels // LANES, lat_rows * plane, LANES), F32)],
        compiler_params=params(),
        name="encode",
    )(
        clips, vae_weight, gain.reshape(1, -1), shift.reshape(1, -1), bias.reshape(1, -1),
        lat_weight, lat_bias.reshape(1, -1),
    )


def fill_taps(value, taps_ref, block, frames):
    size, channels = value.shape
    unit = block[1]
    edge = block[0] * unit
    place = lax.broadcasted_iota(jnp.int32, (size, 1), 0) & (unit - 1)
    for tap in range(3):
        if tap == 0:
            moved = jnp.where(place < frames, 0.0, pltpu.roll(value, frames, 0))
        elif tap == 2:
            moved = jnp.where(place >= unit - frames, 0.0, pltpu.roll(value, size - frames, 0))
        else:
            moved = value
        taps_ref[tap, pl.ds(edge, size), :] = moved.astype(BF16)
        taps_ref[tap, pl.ds(0, edge), :] = jnp.zeros((edge, channels), BF16)
        taps_ref[tap, pl.ds(edge + size, edge), :] = jnp.zeros((edge, channels), BF16)


def conv_taps(total, taps_ref, weight_ref, block):
    size = total.shape[0]
    edge = block[0] * block[1]
    for row_tap in range(3):
        for col_tap in range(3):
            window = taps_ref[row_tap, pl.ds(col_tap * edge, size), :]
            total += jnp.dot(window, weight_ref[row_tap, col_tap], preferred_element_type=F32)
    return total


def unet_layer(state, weight_ref, gain, shift, bias, taps_ref, block, frames):
    streams, unit = block
    size, channels = state.shape
    cols = size // (streams * unit)
    values = state.reshape(cols, streams, unit, channels)
    rows = []
    for item in range(streams):
        own = values[:, item].reshape(cols * unit, channels)
        rows.append(jnp.sum(own, axis=0, keepdims=True))
        rows.append(jnp.sum(own * own, axis=0, keepdims=True))
    rows.extend([jnp.zeros((1, channels), F32)] * (-len(rows) % 8))
    sums = group_sums(jnp.concatenate(rows, axis=0), channels)
    sums = sums * (1.0 / (cols * unit * (channels // GROUPS)))
    normed = []
    for item in range(streams):
        mean = sums[2 * item : 2 * item + 1]
        inverse = lax.rsqrt(sums[2 * item + 1 : 2 * item + 2] - mean * mean + EPS)
        normed.append((values[:, item : item + 1] - mean) * inverse * gain + shift)
    act = silu(jnp.concatenate(normed, axis=1).reshape(size, channels))
    fill_taps(act, taps_ref, block, frames)
    return conv_taps(state + bias, taps_ref, weight_ref, block).astype(BF16)


def write_output(out_ref, state, block):
    streams, unit = block
    channels = state.shape[1]
    cols = state.shape[0] // (streams * unit)
    values = state.reshape(cols, streams, unit, channels)
    for item in range(streams):
        for col in range(cols):
            out_ref[item, :, pl.ds(col * channels, channels)] = values[col, item]


def first_kernel(
    block, frames, slab, owned, section_axis,
    *refs,
):
    streams, unit = block
    latent_refs = refs[: streams // owned]
    (
        clips_ref, offsets_ref, in_weight_ref, in_bias_ref, table_ref, weight_ref, gain_ref, shift_ref, bias_ref,
        state_ref, out_ref, lat_taps_ref, taps_ref,
    ) = refs[streams // owned :]
    table_rows, width = table_ref.shape

    @pl.when(lax.axis_index(section_axis) == 0)
    def _():
        cols = state_ref.shape[0] // (streams * unit)
        first = lax.axis_index(slab) * owned
        parts = []
        for col in range(cols):
            for ref in latent_refs:
                for item in range(owned):
                    parts.append(ref[item, pl.ds(col * unit, unit), :])
        fill_taps(jnp.concatenate(parts, axis=0).astype(F32), lat_taps_ref, block, frames)
        size = cols * streams * unit
        total = jnp.broadcast_to(in_bias_ref[...], (size, width))
        total = conv_taps(total, lat_taps_ref, in_weight_ref, block)
        row = lax.broadcasted_iota(jnp.int32, (unit, table_rows), 0)
        row = lax.div(row, frames)
        wanted = lax.broadcasted_iota(jnp.int32, (unit, table_rows), 1)
        hot = []
        for item in range(streams):
            micro = item // owned
            offset = offsets_ref[micro, clips_ref[micro, first + item % owned]]
            hot.append((wanted - row == offset).astype(F32))
        placed = jnp.dot(
            jnp.concatenate(hot, axis=0).astype(BF16), table_ref[...], preferred_element_type=F32
        )
        placed = placed.reshape(1, streams * unit, width)
        total = (total.reshape(cols, streams * unit, width) + placed).reshape(size, width)
        state = total.astype(BF16).astype(F32)
        state = unet_layer(
            state, weight_ref, gain_ref[...], shift_ref[...], bias_ref[...], taps_ref, block, frames
        )
        state_ref[...] = state
        write_output(out_ref, state, block)


def later_kernel(
    stage, block, frames, section_axis,
    before_ref, out_in_ref, weight_ref, gain_ref, shift_ref, bias_ref, state_ref, out_ref, taps_ref,
):
    del out_in_ref

    @pl.when(lax.axis_index(section_axis) == stage)
    def _():
        state = unet_layer(
            before_ref[...].astype(F32), weight_ref, gain_ref[...], shift_ref[...], bias_ref[...],
            taps_ref, block, frames,
        )
        state_ref[...] = state
        write_output(out_ref, state, block)


def select_kernel(section_axis, clips_ref, features_ref, out_ref):
    section = lax.axis_index(section_axis)
    for slot in range(out_ref.shape[0]):
        out_ref[slot] = features_ref[clips_ref[section, slot]]


def per_device(
    features, vae_weight, vae_gain, vae_shift, vae_bias, latent_weight, latent_bias, slot_clips, row_offsets,
    in_weight, in_bias, pos_table, unet_gain, unet_shift, unet_weight, unet_bias,
):
    section_count = lax.axis_size("section")
    slab_count = lax.axis_size("slab")
    _, clip_total, slab_rows, frames, cols, channels = features.shape
    owned = clip_total // slab_count
    row_total = slab_rows * slab_count
    width = unet_weight.shape[-1]

    ordered = pl.pallas_call(
        functools.partial(select_kernel, "section"),
        out_shape=jax.ShapeDtypeStruct(features.shape[1:], BF16),
        in_specs=[smem(), vmem()],
        out_specs=vmem(),
        name="select",
    )(slot_clips, features[0])
    shaped = ordered.reshape(slab_count, owned, slab_rows, frames, cols, channels)
    whole = lax.all_to_all(shaped, "slab", split_axis=0, concat_axis=0)
    whole = jnp.swapaxes(whole, 0, 1).reshape(owned, row_total, frames, cols, channels)
    latent = encode(
        whole, vae_weight, vae_gain, vae_shift, vae_bias, latent_weight, latent_bias
    )

    latents = [latent]
    for other in range(1, section_count):
        latents.append(lax.ppermute(latent, "section", [(other, 0)]))

    lat_rows, lat_cols = row_total // 2, cols // 2
    unit = lat_rows * frames
    streams = section_count * owned
    block = (streams, unit)
    size = lat_cols * streams * unit
    taps = pltpu.VMEM((3, size + 2 * streams * unit, width), BF16)
    lat_taps = pltpu.VMEM((3, size + 2 * streams * unit, latent.shape[-1]), BF16)
    result_shapes = [
        jax.ShapeDtypeStruct((size, width), BF16),
        jax.ShapeDtypeStruct((streams, unit, lat_cols * width), BF16),
    ]
    weight = unet_weight[0]
    state, out = pl.pallas_call(
        functools.partial(first_kernel, block, frames, "slab", owned, "section"),
        out_shape=result_shapes,
        in_specs=[vmem()] * section_count + [smem()] * 2 + [vmem()] * 7,
        out_specs=[vmem()] * 2,
        scratch_shapes=[lat_taps, taps],
        compiler_params=params(),
        name="first_block",
    )(
        *latents, slot_clips, row_offsets, in_weight, in_bias.reshape(1, -1), pos_table,
        weight, unet_gain, unet_shift, unet_bias,
    )
    for stage in range(1, section_count):
        arrived = lax.ppermute(state, "section", [(stage - 1, stage)])
        state, out = pl.pallas_call(
            functools.partial(later_kernel, stage, block, frames, "section"),
            out_shape=result_shapes,
            in_specs=[vmem()] * 6,
            out_specs=[vmem()] * 2,
            scratch_shapes=[taps],
            input_output_aliases={1: 1},
            compiler_params=params(),
            name="later_block",
        )(arrived, out, weight, unet_gain, unet_shift, unet_bias)
    return out.reshape(1, section_count, owned, lat_rows, frames, lat_cols * width)


def solution(mesh):
    return jax.shard_map(
        per_device,
        mesh=mesh,
        in_specs=(
            P("section", None, "slab", None, None, None),
            P(),
            P(),
            P(),
            P(),
            P(),
            P(),
            P(),
            P(),
            P(),
            P(),
            P(),
            P("section", None),
            P("section", None),
            P("section", None, None, None, None),
            P("section", None),
        ),
        out_specs=P("section", None, "slab", None, None, None),
        check_vma=False,
    )
```

time: 143 us -> 56.1 us (0.39)
  the two profiles are of different devices: /device:TPU:0 before, /device:TPU:6 now
where the time goes in v1:
time: 56.1 us; the launch traced here: 55.6 us
  waiting for transfers between devices  30.9 us (55%)
  starting transfers between devices  11.2 us (20%)
  Pallas kernels  6.83 us (12%)
  local copies, waits for them, and re-layouts  6.41 us (11%)
    ppermute x3, waiting for transfers between devices, per_device(): arrived = lax.ppermute(state, 'section', [(stage - 1, stage)])  25 us
    all_to_all x1, waiting for transfers between devices, per_device(): whole = lax.all_to_all(shaped, 'slab', split_axis=0, concat_axis=0)  5.96 us
    unnamed x30, local copies, waits for them, and re-layouts  5.67 us
    all_to_all x1, starting transfers between devices, per_device(): whole = lax.all_to_all(shaped, 'slab', split_axis=0, concat_axis=0)  4.88 us
    ppermute x3, starting transfers between devices, per_device(): latents.append(lax.ppermute(latent, 'section', [(other, 0)]))  3.71 us
    ppermute x3, starting transfers between devices, per_device(): arrived = lax.ppermute(state, 'section', [(stage - 1, stage)])  2.64 us
    pallas_call x3, Pallas kernels, per_device(): pl.pallas_call(functools.partial(later_kernel, stage, block, frames, 'sec...  2.44 us
    pallas_call x1, Pallas kernels, encode(): pl.pallas_call(encode_kernel, out_shape=jax.ShapeDtypeStruct((items, lat_...  2.04 us
  transfers between devices with their start and end apart: 7, of which 2 were waited for; matrix products, arithmetic and copies ran while one was open for 2% of the time, Pallas kernels for 0%

profile of v1, /device:TPU:6, one launch (start us, length us, event | category | flops | bytes accessed | tf_op | source)
XLA Modules:
  0.0 55.6 jit_solution(6136158815676384217)
XLA Ops:
  0.0 1.7 %select.1 = bf16[8,2,2,8,256]{4,3,2,1,0:T(8,128)(2,1)} custom-call(s32[4,8]{1,0:T(4,128)} %refs_4_.1, bf16[8,2,2,8,256]{4,3,2,1,0:T(8,128)(2,1)} %bitcast.21), custom_call_target="tpu_custom_call" | custom-call | tf_op jit(solution)/shard_map/select/pallas_call | solution.py:271
  1.7 4.9 %all-to-all-start = ((bf16[8,1,2,2,8,256]{5,4,3,2,1,0:T(8,128)(2,1)}), bf16[8,1,2,2,8,256]{5,4,3,2,1,0:T(8,128)(2,1)S(1)}, u32[]{:S(2)}, u32[]{:S(2)}) async-start(bf16[8,1,2,2,8,256]{5,4,3,2,1,0:T(8,128)(2,1)} %bitcast.20), calls=%async_computation | async-start | bytes 262144 | tf_op jit(solution)/shard_map/all_to_all | solution.py:279
  6.6 0.8 %copy.24.lat_weight_ref = bf16[256,16]{1,0:T(8,128)(2,1)S(1)} copy(bf16[256,16]{0,1:T(8,128)(2,1)} %param.21) | data formatting | bytes 16384 | tf_op args[5]
  7.4 6.0 %all-to-all-done = bf16[8,1,2,2,8,256]{5,4,3,2,1,0:T(8,128)(2,1)S(1)} async-done(((bf16[8,1,2,2,8,256]{5,4,3,2,1,0:T(8,128)(2,1)}), bf16[8,1,2,2,8,256]{5,4,3,2,1,0:T(8,128)(2,1)S(1)}, u32[]{:S(2)}, u32[]{:S(2)}) %all-to-all-start) | async-done | bytes 131104 | tf_op jit(solution)/shard_map/all_to_all | solution.py:279
  13.4 2.0 %copy-done.1 = bf16[3,3,3,256,256]{4,3,2,1,0:T(8,128)(2,1)S(1)} copy-done((bf16[3,3,3,256,256]{4,3,2,1,0:T(8,128)(2,1)S(1)}, bf16[3,3,3,256,256]{4,3,2,1,0:T(8,128)(2,1)}, u32[]{:S(2)}) %copy-start.1) | copy-done | bytes 3538968
  15.4 0.7 %copy-done.8 = f32[256]{0:T(256)S(1)} copy-done((f32[256]{0:T(256)S(1)}, f32[256]{0:T(256)}, u32[]{:S(2)}) %copy-start.8) | copy-done | bytes 1048
  16.1 0.7 %copy-done.9 = f32[256]{0:T(256)S(1)} copy-done((f32[256]{0:T(256)S(1)}, f32[256]{0:T(256)}, u32[]{:S(2)}) %copy-start.9) | copy-done | bytes 1048
  16.8 0.7 %copy-done.10 = f32[256]{0:T(256)S(1)} copy-done((f32[256]{0:T(256)S(1)}, f32[256]{0:T(256)}, u32[]{:S(2)}) %copy-start.10) | copy-done | bytes 1048
  17.4 0.7 %copy-done.11 = f32[16]{0:T(128)S(1)} copy-done((f32[16]{0:T(128)S(1)}, f32[16]{0:T(128)}, u32[]{:S(2)}) %copy-start.11) | copy-done | bytes 88
  18.1 0.0 copy-start.4
  18.1 0.0 copy-start.5
  18.1 0.0 copy-start.6
  18.1 0.0 copy-start.7
  18.2 2.0 %encode.1.refs_0_ = bf16[1,64,16]{2,1,0:T(8,128)(2,1)S(1)} custom-call(bf16[1,16,2,8,256]{4,3,2,1,0:T(8,128)(2,1)S(1)} %bitcast.15, bf16[3,3,3,256,256]{4,3,2,1,0:T(8,128)(2,1)S(1)} %copy-done.1, f32[1,256]{1,0:T(1,128)S(1)} %bitcast.16, f32[1,256]{1,0:T(1,128)S(1)} %bitcast.17, f32[1,256]{1,0:T(1,128)S(1)} %bitcast.18, ...), custom_call_target="tpu_custom_call" | custom-call | tf_op jit(solution)/shard_map/encode/pallas_call | solution.py:116
  20.2 2.4 %collective-permute-start.2 = (bf16[1,64,16]{2,1,0:T(8,128)(2,1)S(1)}, bf16[1,64,16]{2,1,0:T(8,128)(2,1)S(1)}, u32[]{:S(2)}, u32[]{:S(2)}) collective-permute-start(bf16[1,64,16]{2,1,0:T(8,128)(2,1)S(1)} %encode.1.refs_0_), channel_id=1, source_target_pairs={{24,0},{25,1},{26,2},{27,3},{28,4},{29,5},{30,6},{31,7}} | collective-permute-start | bytes 6152 | tf_op jit(solution)/shard_map/ppermute | solution.py:287
  22.6 0.7 %collective-permute-start.1 = (bf16[1,64,16]{2,1,0:T(8,128)(2,1)S(1)}, bf16[1,64,16]{2,1,0:T(8,128)(2,1)S(1)}, u32[]{:S(2)}, u32[]{:S(2)}) collective-permute-start(bf16[1,64,16]{2,1,0:T(8,128)(2,1)S(1)} %encode.1.refs_0_), channel_id=1, source_target_pairs={{16,0},{17,1},{18,2},{19,3},{20,4},{21,5},{22,6},{23,7}} | collective-permute-start | bytes 6152 | tf_op jit(solution)/shard_map/ppermute | solution.py:287
  23.3 0.7 %collective-permute-start = (bf16[1,64,16]{2,1,0:T(8,128)(2,1)S(1)}, bf16[1,64,16]{2,1,0:T(8,128)(2,1)S(1)}, u32[]{:S(2)}, u32[]{:S(2)}) collective-permute-start(bf16[1,64,16]{2,1,0:T(8,128)(2,1)S(1)} %encode.1.refs_0_), channel_id=1, source_target_pairs={{8,0},{9,1},{10,2},{11,3},{12,4},{13,5},{14,6},{15,7}} | collective-permute-start | bytes 6152 | tf_op jit(solution)/shard_map/ppermute | solution.py:287
  23.9 0.0 copy-done.13
  24.0 0.0 copy-done.12
  24.0 0.1 copy.25.refs_8_
  24.1 0.0 collective-permute-done.2.refs_3_
  24.1 0.0 collective-permute-done.1.refs_2_
  24.1 0.0 collective-permute-done.refs_1_
  24.2 0.6 %first_block.1 = (bf16[256,320]{1,0:T(8,128)(2,1)S(1)}, bf16[4,16,1280]{2,1,0:T(8,128)(2,1)S(1)}) custom-call(bf16[1,64,16]{2,1,0:T(8,128)(2,1)S(1)} %encode.1.refs_0_, bf16[1,64,16]{2,1,0:T(8,128)(2,1)S(1)} %collective-permute-done.refs_1_, bf16[1,64,16]{2,1,0:T(8,128)(2,1)S(1)} %collective-permute-done.1.refs_2_, ...), custom_call_target="tpu_custom_call" | custom-call | tf_op jit(solution)/shard_map/first_block/pallas_call | solution.py:301
  24.8 0.7 %collective-permute-start.3 = (bf16[256,320]{1,0:T(8,128)(2,1)S(1)}, bf16[256,320]{1,0:T(8,128)(2,1)S(1)}, u32[]{:S(2)}, u32[]{:S(2)}) collective-permute-start(bf16[256,320]{1,0:T(8,128)(2,1)S(1)} %get-tuple-element.12), channel_id=1, source_target_pairs={{0,8},{1,9},{2,10},{3,11},{4,12},{5,13},{6,14},{7,15}} | collective-permute-start | bytes 491528 | tf_op jit(solution)/shard_map/ppermute | solution.py:314
  25.5 0.0 collective-permute-done.3.before_ref
  25.5 0.7 %collective-permute-start.4 = (bf16[256,320]{1,0:T(8,128)(2,1)S(1)}, bf16[256,320]{1,0:T(8,128)(2,1)S(1)}, u32[]{:S(2)}, u32[]{:S(2)}) collective-permute-start(bf16[256,320]{1,0:T(8,128)(2,1)S(1)} %get-tuple-element.14), channel_id=1, source_target_pairs={{8,16},{9,17},{10,18},{11,19},{12,20},{13,21},{14,22},{15,23}} | collective-permute-start | bytes 491528 | tf_op jit(solution)/shard_map/ppermute | solution.py:314
  26.2 0.0 collective-permute-done.4.before_ref
  26.2 1.3 %collective-permute-start.5 = (bf16[256,320]{1,0:T(8,128)(2,1)S(1)}, bf16[256,320]{1,0:T(8,128)(2,1)S(1)}, u32[]{:S(2)}, u32[]{:S(2)}) collective-permute-start(bf16[256,320]{1,0:T(8,128)(2,1)S(1)} %get-tuple-element.16), channel_id=1, source_target_pairs={{16,24},{17,25},{18,26},{19,27},{20,28},{21,29},{22,30},{23,31}} | collective-permute-start | bytes 491528 | tf_op jit(solution)/shard_map/ppermute | solution.py:314
  27.5 25.0 %collective-permute-done.5.before_ref = bf16[256,320]{1,0:T(8,128)(2,1)S(1)} collective-permute-done((bf16[256,320]{1,0:T(8,128)(2,1)S(1)}, bf16[256,320]{1,0:T(8,128)(2,1)S(1)}, u32[]{:S(2)}, u32[]{:S(2)}) %collective-permute-start.5) | collective-permute-done | bytes 163872 | tf_op jit(solution)/shard_map/ppermute | solution.py:314
  52.5 2.4 %later_block.5 = (bf16[256,320]{1,0:T(8,128)(2,1)}, bf16[4,16,1280]{2,1,0:T(8,128)(2,1)S(1)}) custom-call(bf16[256,320]{1,0:T(8,128)(2,1)S(1)} %collective-permute-done.5.before_ref, bf16[4,16,1280]{2,1,0:T(8,128)(2,1)S(1)} %get-tuple-element.17.out_in_ref, bf16[3,3,320,320]{3,2,1,0:T(8,128)(2,1)S(1)} %bitcast.14, ...), custom_call_target="tpu_custom_call", output_to_operand_aliasing={{1}: (1, {})} | custom-call | tf_op jit(solution)/shard_map/later_block/pallas_call | solution.py:315
  54.9 0.7 %reshape.27 = bf16[1,4,1,8,2,1280]{5,4,3,1,2,0:T(2,128)(2,1)} reshape(bf16[4,16,1280]{2,1,0:T(8,128)(2,1)S(1)} %get-tuple-element.18) | data formatting | bytes 327680 | tf_op jit(solution)/shard_map/reshape | solution.py:325
  (20 shorter events, 0.1 us)
Async XLA Ops:
  0.0 24.1 %copy-start = (bf16[1,3,3,320,320]{4,3,2,1,0:T(8,128)(2,1)S(1)}, bf16[1,3,3,320,320]{4,3,2,1,0:T(8,128)(2,1)}, u32[]{:S(2)}) copy-start(bf16[1,3,3,320,320]{4,3,2,1,0:T(8,128)(2,1)} %param.30) | copy-start | bytes 5529604
  1.7 11.7 %all-to-all-start = ((bf16[8,1,2,2,8,256]{5,4,3,2,1,0:T(8,128)(2,1)}), bf16[8,1,2,2,8,256]{5,4,3,2,1,0:T(8,128)(2,1)S(1)}, u32[]{:S(2)}, u32[]{:S(2)}) async-start(bf16[8,1,2,2,8,256]{5,4,3,2,1,0:T(8,128)(2,1)} %bitcast.20), calls=%async_computation | async-start | bytes 262144 | tf_op jit(solution)/shard_map/all_to_all | solution.py:279
  13.4 2.0 %copy-start.1 = (bf16[3,3,3,256,256]{4,3,2,1,0:T(8,128)(2,1)S(1)}, bf16[3,3,3,256,256]{4,3,2,1,0:T(8,128)(2,1)}, u32[]{:S(2)}) copy-start(bf16[3,3,3,256,256]{4,3,2,1,0:T(8,128)(2,1)} %weight_ref.1) | copy-start | bytes 10616836
  15.4 0.7 %copy-start.8 = (f32[256]{0:T(256)S(1)}, f32[256]{0:T(256)}, u32[]{:S(2)}) copy-start(f32[256]{0:T(256)} %param.18) | copy-start | bytes 3076
  16.1 0.7 %copy-start.9 = (f32[256]{0:T(256)S(1)}, f32[256]{0:T(256)}, u32[]{:S(2)}) copy-start(f32[256]{0:T(256)} %param.19) | copy-start | bytes 3076
  16.8 0.7 %copy-start.10 = (f32[256]{0:T(256)S(1)}, f32[256]{0:T(256)}, u32[]{:S(2)}) copy-start(f32[256]{0:T(256)} %param.20) | copy-start | bytes 3076
  17.4 0.7 %copy-start.11 = (f32[16]{0:T(128)S(1)}, f32[16]{0:T(128)}, u32[]{:S(2)}) copy-start(f32[16]{0:T(128)} %param.22) | copy-start | bytes 196
  18.1 5.8 %copy-start.13 = (f32[320]{0:T(512)S(1)}, f32[320]{0:T(512)}, u32[]{:S(2)}) copy-start(f32[320]{0:T(512)} %param.26) | copy-start | bytes 3844
  18.1 5.9 %copy-start.12 = (bf16[128,320]{0,1:T(8,128)(2,1)S(1)}, bf16[128,320]{0,1:T(8,128)(2,1)}, u32[]{:S(2)}) copy-start(bf16[128,320]{0,1:T(8,128)(2,1)} %param.27) | copy-start | bytes 245764
  18.1 6.0 %copy-start.2 = (bf16[3,3,16,320]{3,2,1,0:T(8,128)(2,1)S(1)}, bf16[3,3,16,320]{3,2,1,0:T(8,128)(2,1)}, u32[]{:S(2)}) copy-start(bf16[3,3,16,320]{3,2,1,0:T(8,128)(2,1)} %refs_6_.1) | copy-start | bytes 276484
  18.1 6.0 %copy-start.3 = (f32[1,320]{1,0:T(1,128)S(1)}, f32[1,320]{1,0:T(1,128)}, u32[]{:S(2)}) copy-start(f32[1,320]{1,0:T(1,128)} %gain_ref.5) | copy-start | bytes 3844
  18.1 6.0 %copy-start.4 = (f32[1,320]{1,0:T(1,128)S(1)}, f32[1,320]{1,0:T(1,128)}, u32[]{:S(2)}) copy-start(f32[1,320]{1,0:T(1,128)} %shift_ref.5) | copy-start | bytes 3844
  18.1 6.0 %copy-start.5 = (f32[1,320]{1,0:T(1,128)S(1)}, f32[1,320]{1,0:T(1,128)}, u32[]{:S(2)}) copy-start(f32[1,320]{1,0:T(1,128)} %bias_ref.5) | copy-start | bytes 3844
  18.1 6.0 %copy-start.6 = (s32[4,8]{1,0:T(4,128)S(1)}, s32[4,8]{1,0:T(4,128)}, u32[]{:S(2)}) copy-start(s32[4,8]{1,0:T(4,128)} %refs_4_.1) | copy-start | bytes 388
  18.1 6.0 %copy-start.7 = (s32[4,8]{1,0:T(4,128)S(1)}, s32[4,8]{1,0:T(4,128)}, u32[]{:S(2)}) copy-start(s32[4,8]{1,0:T(4,128)} %refs_5_.1) | copy-start | bytes 388
  20.2 3.9 %collective-permute-start.2 = (bf16[1,64,16]{2,1,0:T(8,128)(2,1)S(1)}, bf16[1,64,16]{2,1,0:T(8,128)(2,1)S(1)}, u32[]{:S(2)}, u32[]{:S(2)}) collective-permute-start(bf16[1,64,16]{2,1,0:T(8,128)(2,1)S(1)} %encode.1.refs_0_), channel_id=1, source_target_pairs={{24,0},{25,1},{26,2},{27,3},{28,4},{29,5},{30,6},{31,7}} | collective-permute-start | bytes 6152 | tf_op jit(solution)/shard_map/ppermute | solution.py:287
  22.6 1.5 %collective-permute-start.1 = (bf16[1,64,16]{2,1,0:T(8,128)(2,1)S(1)}, bf16[1,64,16]{2,1,0:T(8,128)(2,1)S(1)}, u32[]{:S(2)}, u32[]{:S(2)}) collective-permute-start(bf16[1,64,16]{2,1,0:T(8,128)(2,1)S(1)} %encode.1.refs_0_), channel_id=1, source_target_pairs={{16,0},{17,1},{18,2},{19,3},{20,4},{21,5},{22,6},{23,7}} | collective-permute-start | bytes 6152 | tf_op jit(solution)/shard_map/ppermute | solution.py:287
  23.3 0.9 %collective-permute-start = (bf16[1,64,16]{2,1,0:T(8,128)(2,1)S(1)}, bf16[1,64,16]{2,1,0:T(8,128)(2,1)S(1)}, u32[]{:S(2)}, u32[]{:S(2)}) collective-permute-start(bf16[1,64,16]{2,1,0:T(8,128)(2,1)S(1)} %encode.1.refs_0_), channel_id=1, source_target_pairs={{8,0},{9,1},{10,2},{11,3},{12,4},{13,5},{14,6},{15,7}} | collective-permute-start | bytes 6152 | tf_op jit(solution)/shard_map/ppermute | solution.py:287
  24.8 0.7 %collective-permute-start.3 = (bf16[256,320]{1,0:T(8,128)(2,1)S(1)}, bf16[256,320]{1,0:T(8,128)(2,1)S(1)}, u32[]{:S(2)}, u32[]{:S(2)}) collective-permute-start(bf16[256,320]{1,0:T(8,128)(2,1)S(1)} %get-tuple-element.12), channel_id=1, source_target_pairs={{0,8},{1,9},{2,10},{3,11},{4,12},{5,13},{6,14},{7,15}} | collective-permute-start | bytes 491528 | tf_op jit(solution)/shard_map/ppermute | solution.py:314
  25.5 0.7 %collective-permute-start.4 = (bf16[256,320]{1,0:T(8,128)(2,1)S(1)}, bf16[256,320]{1,0:T(8,128)(2,1)S(1)}, u32[]{:S(2)}, u32[]{:S(2)}) collective-permute-start(bf16[256,320]{1,0:T(8,128)(2,1)S(1)} %get-tuple-element.14), channel_id=1, source_target_pairs={{8,16},{9,17},{10,18},{11,19},{12,20},{13,21},{14,22},{15,23}} | collective-permute-start | bytes 491528 | tf_op jit(solution)/shard_map/ppermute | solution.py:314
  26.2 26.3 %collective-permute-start.5 = (bf16[256,320]{1,0:T(8,128)(2,1)S(1)}, bf16[256,320]{1,0:T(8,128)(2,1)S(1)}, u32[]{:S(2)}, u32[]{:S(2)}) collective-permute-start(bf16[256,320]{1,0:T(8,128)(2,1)S(1)} %get-tuple-element.16), channel_id=1, source_target_pairs={{16,24},{17,25},{18,26},{19,27},{20,28},{21,29},{22,30},{23,31}} | collective-permute-start | bytes 491528 | tf_op jit(solution)/shard_map/ppermute | solution.py:314

commit v2 on v1

v2 whole, which is shorter than its diff:
```python
import functools

import jax
import jax.numpy as jnp
from jax import lax
from jax.experimental import pallas as pl
from jax.experimental.pallas import tpu as pltpu
from jax.sharding import PartitionSpec as P

GROUPS = 32
LANES = 128
PLACE_FLOPS = 6_000_000_000
EPS = 1e-06
VMEM_LIMIT = 32 * 1024 * 1024
PLACE_VMEM = 8 * 1024 * 1024
F32 = jnp.float32
BF16 = jnp.bfloat16


def vmem():
    return pl.BlockSpec(memory_space=pltpu.VMEM)


def smem():
    return pl.BlockSpec(memory_space=pltpu.SMEM)


def params(limit=VMEM_LIMIT):
    return pltpu.CompilerParams(vmem_limit_bytes=limit)


def same_group(channels):
    size = channels // GROUPS

    def group_of(axis):
        index = lax.broadcasted_iota(jnp.int32, (channels, channels), axis).astype(F32)
        return jnp.floor((index + 0.5) * (1.0 / size))

    return jnp.where(group_of(0) == group_of(1), 1.0, 0.0).astype(BF16)


def group_sums(rows, same):
    high = rows.astype(BF16)
    rest = rows - high.astype(F32)
    middle = rest.astype(BF16)
    low = (rest - middle.astype(F32)).astype(BF16)
    total = jnp.dot(high, same, preferred_element_type=F32)
    total += jnp.dot(middle, same, preferred_element_type=F32)
    total += jnp.dot(low, same, preferred_element_type=F32)
    return total


def dot_last(left, right):
    return lax.dot_general(left, right, (((1,), (1,)), ((), ())), preferred_element_type=F32)


def silu(value):
    return value / (1.0 + jnp.exp(-value))


def encode_kernel(
    x_ref, weight_ref, gain_ref, shift_ref, bias_ref, lat_weight_ref, lat_bias_ref, after_ref,
    out_ref, dup_ref, act_ref, pool_ref,
):
    del after_ref
    row_count, frames, cols, channels = x_ref.shape[1:]
    plane = frames * cols
    size = row_count * plane
    lat_rows, lat_cols = row_count // 2, cols // 2
    same = same_group(channels)
    for item in range(x_ref.shape[0]):
        x = x_ref[item].astype(F32).reshape(size, channels)
        sums = jnp.concatenate(
            [jnp.sum(x, axis=0, keepdims=True), jnp.sum(x * x, axis=0, keepdims=True)]
            + [jnp.zeros((6, channels), F32)],
            axis=0,
        )
        sums = group_sums(sums, same) * (1.0 / (size * (channels // GROUPS)))
        mean = sums[0:1]
        inverse = lax.rsqrt(sums[1:2] - mean * mean + EPS)
        act = silu((x - mean) * inverse * gain_ref[...] + shift_ref[...])
        column = lax.broadcasted_iota(jnp.int32, (size, 1), 0) & (cols - 1)
        for tap in range(3):
            if tap == 0:
                moved = jnp.where(column == 0, 0.0, pltpu.roll(act, 1, 0))
            elif tap == 2:
                moved = jnp.where(column == cols - 1, 0.0, pltpu.roll(act, size - 1, 0))
            else:
                moved = act
            lanes = pl.ds(tap * channels, channels)
            first = moved.reshape(row_count, frames, cols, channels)[:, 0:1]
            first = jnp.broadcast_to(first, (row_count, frames, cols, channels))
            act_ref[pl.ds(plane, size), lanes] = moved.astype(BF16)
            dup_ref[pl.ds(plane, size), lanes] = first.reshape(size, channels).astype(BF16)
        for ref in (act_ref, dup_ref):
            ref[pl.ds(0, plane), :] = jnp.zeros((plane, 3 * channels), BF16)
            ref[pl.ds(plane + size, plane), :] = jnp.zeros((plane, 3 * channels), BF16)
        total = x + bias_ref[...]
        for time_tap in range(3):
            source = act_ref if time_tap == 2 else dup_ref
            for row_tap in range(3):
                weight = weight_ref[time_tap, row_tap].reshape(3 * channels, channels)
                window = source[pl.ds(row_tap * plane, size), :]
                total += jnp.dot(window, weight, preferred_element_type=F32)
        paired = total.reshape(lat_rows, 2, plane, channels)
        merged = (paired[:, 0] + paired[:, 1]).reshape(lat_rows * plane, channels)
        halves = []
        for part in range(channels // LANES):
            pool_ref[part] = merged[:, part * LANES : (part + 1) * LANES]
            picked = []
            for col in range(lat_cols):
                left = pool_ref[part, pl.ds(2 * col, lat_rows * frames, stride=cols), :]
                right = pool_ref[part, pl.ds(2 * col + 1, lat_rows * frames, stride=cols), :]
                picked.append((left + right) * 0.25)
            halves.append(jnp.concatenate(picked, axis=0))
        pooled = jnp.concatenate(halves, axis=1).astype(BF16)
        latent = dot_last(pooled, lat_weight_ref[...])
        out_ref[item] = (latent + lat_bias_ref[...]).astype(BF16)


def encode(clips, *operands):
    items, row_count, frames, cols, channels = clips.shape
    plane = frames * cols
    lat_rows, lat_cols = row_count // 2, cols // 2
    padded = pltpu.VMEM(((row_count + 2) * plane, 3 * channels), BF16)
    return pl.pallas_call(
        encode_kernel,
        out_shape=jax.ShapeDtypeStruct((items, lat_cols * lat_rows * frames, operands[-2].shape[1]), BF16),
        in_specs=[vmem()] * len(operands) + [pl.BlockSpec(memory_space=pl.ANY)],
        out_specs=vmem(),
        scratch_shapes=[
            padded,
            padded,
            pltpu.VMEM((channels // LANES, lat_rows * plane, LANES), F32),
        ],
        compiler_params=params(),
        name="encode",
    )(clips, *operands)


def shifted(value, unit, frames):
    size = value.shape[0]
    place = lax.broadcasted_iota(jnp.int32, (size, 1), 0) & (unit - 1)
    return (
        jnp.where(place < frames, 0.0, pltpu.roll(value, frames, 0)),
        value,
        jnp.where(place >= unit - frames, 0.0, pltpu.roll(value, size - frames, 0)),
    )


def conv3(value, weight_ref, taps_ref, block, frames):
    streams, unit = block
    size, channels = value.shape
    edge = streams * unit
    zeros = jnp.zeros((edge, channels), BF16)
    total = None
    for row_tap, moved in enumerate(shifted(value, unit, frames)):
        taps_ref[row_tap, pl.ds(edge, size), :] = moved.astype(BF16)
        taps_ref[row_tap, pl.ds(0, edge), :] = zeros
        taps_ref[row_tap, pl.ds(edge + size, edge), :] = zeros
        for col_tap in range(3):
            window = taps_ref[row_tap, pl.ds(col_tap * edge, size), :]
            term = jnp.dot(window, weight_ref[row_tap, col_tap], preferred_element_type=F32)
            total = term if total is None else total + term
    return total


def conv3_narrow(value, weight, block, frames):
    streams, unit = block
    size, channels = value.shape
    edge = streams * unit
    zeros = jnp.zeros((edge, channels), F32)
    windows = []
    for moved in shifted(value, unit, frames):
        padded = jnp.concatenate([zeros, moved, zeros], axis=0)
        for col_tap in range(3):
            windows.append(padded[col_tap * edge : col_tap * edge + size])
    window = jnp.concatenate(windows, axis=1).astype(BF16)
    return jnp.dot(window, weight, preferred_element_type=F32)


def unet_layer(state, operands, taps_ref, block, frames):
    weight_ref, gain_ref, shift_ref, bias_ref = operands
    streams, unit = block
    size, channels = state.shape
    cols = size // (streams * unit)
    values = state.reshape(cols, streams, unit, channels)
    rows = []
    for item in range(streams):
        own = values[:, item].reshape(cols * unit, channels)
        rows.append(jnp.sum(own, axis=0, keepdims=True))
        rows.append(jnp.sum(own * own, axis=0, keepdims=True))
    rows.extend([jnp.zeros((1, channels), F32)] * (-len(rows) % 8))
    sums = group_sums(jnp.concatenate(rows, axis=0), same_group(channels))
    sums = sums * (1.0 / (cols * unit * (channels // GROUPS)))
    normed = []
    for item in range(streams):
        mean = sums[2 * item : 2 * item + 1]
        inverse = lax.rsqrt(sums[2 * item + 1 : 2 * item + 2] - mean * mean + EPS)
        scaled = (values[:, item : item + 1] - mean) * inverse * gain_ref[...]
        normed.append(scaled + shift_ref[...])
    act = silu(jnp.concatenate(normed, axis=1).reshape(size, channels))
    total = conv3(act, weight_ref, taps_ref, block, frames)
    return (state + total + bias_ref[...]).astype(BF16)


def write_output(out_ref, state, first, block, frames):
    streams, unit = block
    channels = state.shape[1]
    cols = state.shape[0] // (streams * unit)
    values = state.astype(F32).reshape(cols, streams, unit, channels)
    for item in range(streams):
        wide = jnp.concatenate([values[col, item] for col in range(cols)], axis=1)
        wide = wide.astype(BF16).reshape(unit // frames, frames, cols * channels)
        out_ref[first + item] = wide


def place_kernel(slab, owned, frames, clips_ref, offsets_ref, table_ref, bias_ref, kept_ref, out_ref):
    del kept_ref
    streams, unit, _ = out_ref.shape
    first = lax.axis_index(slab) * owned
    table_rows = table_ref.shape[1]
    row = lax.broadcasted_iota(jnp.int32, (unit, table_rows), 0)
    row = lax.div(row, jnp.int32(frames))
    wanted = lax.broadcasted_iota(jnp.int32, (unit, table_rows), 1) - row
    for stream in range(streams):
        micro = stream // owned
        offset = offsets_ref[micro, clips_ref[micro, first + stream % owned]]
        hot = jnp.where(wanted == offset, 1.0, 0.0).astype(BF16)
        out_ref[stream] = dot_last(hot, table_ref[...]) + bias_ref[...]


def first_kernel(block, frames, count, chunk, section_axis, *refs):
    streams, unit = block
    latent_refs = refs[:count]
    place_ref, in_weight_ref, *operands = refs[count:-3]
    state_ref, out_ref, taps_ref = refs[-3:]

    @pl.when(lax.axis_index(section_axis) == 0)
    def _():
        size, width = state_ref.shape
        cols = size // (streams * unit)
        parts = []
        for col in range(cols):
            for ref in latent_refs:
                for item in range(ref.shape[0]):
                    parts.append(ref[item, pl.ds(col * unit, unit), :].astype(F32))
        total = conv3_narrow(jnp.concatenate(parts, axis=0), in_weight_ref[...], block, frames)
        placed = place_ref[pl.ds(chunk * streams, streams)].reshape(1, streams * unit, width)
        total = (total.reshape(cols, streams * unit, width) + placed).reshape(size, width)
        state = total.astype(BF16).astype(F32)
        state = unet_layer(state, operands, taps_ref, block, frames)
        state_ref[...] = state
        write_output(out_ref, state, 0, block, frames)


def later_kernel(
    stage_index, block, frames, section_axis,
    before_ref, out_in_ref, weight_ref, gain_ref, shift_ref, bias_ref, state_ref, out_ref, taps_ref,
):
    del out_in_ref

    @pl.when(lax.axis_index(section_axis) == stage_index)
    def _():
        state = unet_layer(
            before_ref[...].astype(F32), (weight_ref, gain_ref, shift_ref, bias_ref), taps_ref, block, frames
        )
        state_ref[...] = state
        write_output(out_ref, state, 0, block, frames)


def last_kernel(block, frames, section_axis, chunks, *refs):
    streams = block[0]
    before_ref = refs[0]
    parts = refs[1 : 1 + chunks]
    operands = refs[1 + chunks : -2]
    out_ref, taps_ref = refs[-2:]
    last = lax.axis_index(section_axis) == lax.axis_size(section_axis) - 1
    for chunk in range(chunks - 1):
        out_ref[pl.ds(chunk * streams, streams)] = parts[chunk][...]

    @pl.when(last)
    def _():
        state = unet_layer(before_ref[...].astype(F32), operands, taps_ref, block, frames)
        write_output(out_ref, state, (chunks - 1) * streams, block, frames)

    @pl.when(jnp.logical_not(last))
    def _():
        out_ref[pl.ds((chunks - 1) * streams, streams)] = parts[chunks - 1][...]


def select_kernel(section_axis, clips_ref, features_ref, out_ref):
    section = lax.axis_index(section_axis)
    for slot in range(out_ref.shape[0]):
        out_ref[slot] = features_ref[clips_ref[section, slot]]


def hop(value, source, target):
    count = lax.axis_size("section")
    if count & (count - 1):
        return lax.ppermute(value, "section", [(source, target)])
    return lax.ppermute(value, "section", [(s, s ^ source ^ target) for s in range(count)])


def gather_first(value):
    count = lax.axis_size("section")
    if count & (count - 1):
        return [value] + [hop(value, other, 0) for other in range(1, count)]
    parts = [value]
    step = 1
    while step < count:
        held = parts[0] if len(parts) == 1 else jnp.concatenate(parts, axis=0)
        parts.append(lax.ppermute(held, "section", [(s, s ^ step) for s in range(count)]))
        step *= 2
    return parts


def per_device(
    features, vae_weight, vae_gain, vae_shift, vae_bias, latent_weight, latent_bias, slot_clips, row_offsets,
    in_weight, in_bias, pos_table, unet_gain, unet_shift, unet_weight, unet_bias,
):
    section_count = lax.axis_size("section")
    slab_count = lax.axis_size("slab")
    _, clip_total, slab_rows, frames, cols, channels = features.shape
    owned = clip_total // slab_count
    row_total = slab_rows * slab_count
    width = unet_weight.shape[-1]
    lat_rows, lat_cols = row_total // 2, cols // 2
    unit = lat_rows * frames

    ordered = pl.pallas_call(
        functools.partial(select_kernel, "section"),
        out_shape=jax.ShapeDtypeStruct(features.shape[1:], BF16),
        in_specs=[smem(), vmem()],
        out_specs=vmem(),
        name="select",
    )(slot_clips, features[0])
    shaped = ordered.reshape(slab_count, owned, slab_rows, frames, cols, channels)
    whole = lax.all_to_all(shaped, "slab", split_axis=0, concat_axis=0)
    whole = jnp.swapaxes(whole, 0, 1).reshape(owned, row_total, frames, cols, channels)
    place = pl.pallas_call(
        functools.partial(place_kernel, "slab", owned, frames),
        out_shape=jax.ShapeDtypeStruct((section_count * owned, unit, width), F32),
        in_specs=[smem()] * 2 + [vmem()] * 2 + [pl.BlockSpec(memory_space=pl.ANY)],
        out_specs=vmem(),
        compiler_params=params(PLACE_VMEM),
        cost_estimate=pl.CostEstimate(flops=PLACE_FLOPS, bytes_accessed=0, transcendentals=0),
        name="place",
    )(slot_clips, row_offsets, pos_table.T, in_bias.reshape(1, -1), vae_weight)
    latent = encode(
        whole, vae_weight, vae_gain.reshape(1, -1), vae_shift.reshape(1, -1), vae_bias.reshape(1, -1),
        latent_weight.T, latent_bias.reshape(1, -1), place,
    )
    latents = gather_first(latent)

    chunks = 2 if section_count % 2 == 0 else 1
    per_chunk = section_count // chunks
    streams = per_chunk * owned
    block = (streams, unit)
    size = lat_cols * streams * unit
    taps = pltpu.VMEM((3, size + 2 * streams * unit, width), BF16)
    layer = [unet_weight[0], unet_gain, unet_shift, unet_bias]
    result_shapes = [
        jax.ShapeDtypeStruct((size, width), BF16),
        jax.ShapeDtypeStruct((streams, lat_rows, frames, lat_cols * width), BF16),
    ]
    arrived = [None] * chunks
    outs = [None] * chunks
    for chunk in range(chunks):
        mine = latents
        if chunks == 2:
            mine = latents[-1:] if chunk else latents[:-1]
        operands = mine + [place, in_weight.reshape(-1, width)] + layer
        state, outs[chunk] = pl.pallas_call(
            functools.partial(first_kernel, block, frames, len(mine), chunk, "section"),
            out_shape=result_shapes,
            in_specs=[vmem()] * len(operands),
            out_specs=[vmem()] * 2,
            scratch_shapes=[taps],
            compiler_params=params(),
            name="first_block",
        )(*operands)
        if section_count > 1:
            arrived[chunk] = hop(state, 0, 1)
    for index in range(1, section_count):
        for chunk in range(chunks):
            if index == section_count - 1 and chunk == chunks - 1:
                break
            state, outs[chunk] = pl.pallas_call(
                functools.partial(later_kernel, index, block, frames, "section"),
                out_shape=result_shapes,
                in_specs=[vmem()] * 6,
                out_specs=[vmem()] * 2,
                scratch_shapes=[taps],
                input_output_aliases={1: 1},
                compiler_params=params(),
                name="later_block",
            )(arrived[chunk], outs[chunk], *layer)
            if index < section_count - 1:
                arrived[chunk] = hop(state, index, index + 1)
    operands = [arrived[-1]] + outs + layer
    out = pl.pallas_call(
        functools.partial(last_kernel, block, frames, "section", chunks),
        out_shape=jax.ShapeDtypeStruct(
            (section_count * owned, lat_rows, frames, lat_cols * width), BF16
        ),
        in_specs=[vmem()] * len(operands),
        out_specs=vmem(),
        scratch_shapes=[taps],
        compiler_params=params(),
        name="last_block",
    )(*operands)
    return out.reshape(1, section_count, owned, lat_rows, frames, lat_cols * width)


def solution(mesh):
    return jax.shard_map(
        per_device,
        mesh=mesh,
        in_specs=(
            P("section", None, "slab", None, None, None),
            P(),
            P(),
            P(),
            P(),
            P(),
            P(),
            P(),
            P(),
            P(),
            P(),
            P(),
            P("section", None),
            P("section", None),
            P("section", None, None, None, None),
            P("section", None),
        ),
        out_specs=P("section", None, "slab", None, None, None),
        check_vma=False,
    )
```

time: 56.1 us -> 44.2 us (0.79)
  the two profiles are of different devices: /device:TPU:6 before, /device:TPU:4 now
where the time goes in v2:
time: 44.2 us; the launch traced here: 43.9 us
  starting transfers between devices  15 us (34%)
  waiting for transfers between devices  13.6 us (31%)
  Pallas kernels  8.07 us (18%)
  local copies, waits for them, and re-layouts  6.98 us (16%)
    ppermute x6, waiting for transfers between devices, hop(): lax.ppermute(value, 'section', [(s, s ^ source ^ target) for s in range(c...  8.59 us
    ppermute x6, starting transfers between devices, hop(): lax.ppermute(value, 'section', [(s, s ^ source ^ target) for s in range(c...  8.02 us
    unnamed x30, local copies, waits for them, and re-layouts  6.3 us
    all_to_all x1, starting transfers between devices, per_device(): whole = lax.all_to_all(shaped, 'slab', split_axis=0, concat_axis=0)  4.88 us
    ppermute x2, waiting for transfers between devices, gather_first(): lax.ppermute(held, 'section', [(s, s ^ step) for s in range(count)])  4.05 us
    pallas_call x5, Pallas kernels, per_device(): pl.pallas_call(functools.partial(later_kernel, index, block, frames, 'sec...  2.91 us
    ppermute x2, starting transfers between devices, gather_first(): lax.ppermute(held, 'section', [(s, s ^ step) for s in range(count)])  2.13 us
    pallas_call x1, Pallas kernels, encode(): pl.pallas_call(encode_kernel, out_shape=jax.ShapeDtypeStruct((items, lat_...  2.07 us
  transfers between devices with their start and end apart: 9, of which 9 were waited for; matrix products, arithmetic and copies ran while one was open for 2% of the time, Pallas kernels for 8%

profile of v2, /device:TPU:4, one launch (start us, length us, event | category | flops | bytes accessed | tf_op | source)
XLA Modules:
  0.0 43.9 jit_solution(7406149100210644024)
XLA Ops:
  0.0 1.6 %select.1 = bf16[8,2,2,8,256]{4,3,2,1,0:T(8,128)(2,1)} custom-call(s32[4,8]{1,0:T(4,128)} %clips_ref.3, bf16[8,2,2,8,256]{4,3,2,1,0:T(8,128)(2,1)} %bitcast.34), custom_call_target="tpu_custom_call" | custom-call | tf_op jit(solution)/shard_map/select/pallas_call | solution.py:331
  1.6 4.9 %all-to-all-start = ((bf16[8,1,2,2,8,256]{5,4,3,2,1,0:T(8,128)(2,1)}), bf16[8,1,2,2,8,256]{5,4,3,2,1,0:T(8,128)(2,1)S(1)}, u32[]{:S(2)}, u32[]{:S(2)}) async-start(bf16[8,1,2,2,8,256]{5,4,3,2,1,0:T(8,128)(2,1)} %bitcast.33), calls=%async_computation | async-start | bytes 262144 | tf_op jit(solution)/shard_map/all_to_all | solution.py:339
  6.5 0.7 %reshape.30.bias_ref = f32[1,320]{1,0:T(1,128)S(1)} reshape(f32[320]{0:T(512)} %param.26) | data formatting | bytes 2560 | tf_op jit(solution)/shard_map/reshape | solution.py:349
  7.2 2.0 %copy-done.1 = bf16[3,3,3,256,256]{4,3,2,1,0:T(8,128)(2,1)S(1)} copy-done((bf16[3,3,3,256,256]{4,3,2,1,0:T(8,128)(2,1)S(1)}, bf16[3,3,3,256,256]{4,3,2,1,0:T(8,128)(2,1)}, u32[]{:S(2)}) %copy-start.1) | copy-done | bytes 3538968
  9.2 0.7 %copy-done.8 = s32[4,8]{1,0:T(4,128)S(1)} copy-done((s32[4,8]{1,0:T(4,128)S(1)}, s32[4,8]{1,0:T(4,128)}, u32[]{:S(2)}) %copy-start.8) | copy-done | bytes 152
  9.8 0.9 %copy-done.13 = bf16[128,320]{0,1:T(8,128)(2,1)S(1)} copy-done((bf16[128,320]{0,1:T(8,128)(2,1)S(1)}, bf16[128,320]{0,1:T(8,128)(2,1)}, u32[]{:S(2)}) %copy-start.13) | copy-done | bytes 81944
  10.7 0.7 %copy-done.14 = s32[4,8]{1,0:T(4,128)S(1)} copy-done((s32[4,8]{1,0:T(4,128)S(1)}, s32[4,8]{1,0:T(4,128)}, u32[]{:S(2)}) %copy-start.14) | copy-done | bytes 152
  11.5 0.8 %place.1.after_ref.refs_1_.refs_2_ = f32[4,16,320]{2,1,0:T(8,128)S(1)} custom-call(s32[4,8]{1,0:T(4,128)S(1)} %copy-done.8, s32[4,8]{1,0:T(4,128)S(1)} %copy-done.14, bf16[320,128]{1,0:T(8,128)(2,1)S(1)} %bitcast.32, f32[1,320]{1,0:T(1,128)S(1)} %reshape.30.bias_ref, bf16[3,3,3,256,256]{4,3,2,1,0:T(8,128)(2,1)S(1)} %copy-done.1), custom_call_target="tpu_custom_call" | custom-call | flops 6000000000 | tf_op jit(solution)/shard_map/place/pallas_call | solution.py:341
  12.3 0.0 copy-start
  12.3 1.0 %all-to-all-done = bf16[8,1,2,2,8,256]{5,4,3,2,1,0:T(8,128)(2,1)S(1)} async-done(((bf16[8,1,2,2,8,256]{5,4,3,2,1,0:T(8,128)(2,1)}), bf16[8,1,2,2,8,256]{5,4,3,2,1,0:T(8,128)(2,1)S(1)}, u32[]{:S(2)}, u32[]{:S(2)}) %all-to-all-start) | async-done | bytes 131104 | tf_op jit(solution)/shard_map/all_to_all | solution.py:339
  13.3 2.0 %copy-done.2 = bf16[3,3,3,256,256]{4,3,2,1,0:T(8,128)(2,1)S(1)} copy-done((bf16[3,3,3,256,256]{4,3,2,1,0:T(8,128)(2,1)S(1)}, bf16[3,3,3,256,256]{4,3,2,1,0:T(8,128)(2,1)}, u32[]{:S(2)}) %copy-start.2) | copy-done | bytes 3538968
  15.3 2.1 %encode.1.refs_0_ = bf16[1,64,16]{2,1,0:T(8,128)(2,1)S(1)} custom-call(bf16[1,16,2,8,256]{4,3,2,1,0:T(8,128)(2,1)S(1)} %bitcast.24, bf16[3,3,3,256,256]{4,3,2,1,0:T(8,128)(2,1)S(1)} %copy-done.2, f32[1,256]{1,0:T(1,128)S(1)} %bitcast.28, f32[1,256]{1,0:T(1,128)S(1)} %bitcast.29, f32[1,256]{1,0:T(1,128)S(1)} %bitcast.30, bf16[16,256]{1,0:T(8,128)(2,1)S(1)} %bitcast.27, ...), custom_call_target="tpu_custom_call" | custom-call | tf_op jit(solution)/shard_map/encode/pallas_call | solution.py:126
  17.4 1.6 %collective-permute-start = (bf16[1,64,16]{2,1,0:T(8,128)(2,1)S(1)}, bf16[1,64,16]{2,1,0:T(8,128)(2,1)S(1)}, u32[]{:S(2)}, u32[]{:S(2)}) collective-permute-start(bf16[1,64,16]{2,1,0:T(8,128)(2,1)S(1)} %encode.1.refs_0_), channel_id=1, source_target_pairs={{0,8},{8,0},{16,24},{24,16},{1,9},{9,1},{17,25},{25,17},{2,10},{10... | collective-permute-start | bytes 6152 | tf_op jit(solution)/shard_map/ppermute | solution.py:313
  18.9 2.2 %collective-permute-done.refs_1_ = bf16[1,64,16]{2,1,0:T(8,128)(2,1)S(1)} collective-permute-done((bf16[1,64,16]{2,1,0:T(8,128)(2,1)S(1)}, bf16[1,64,16]{2,1,0:T(8,128)(2,1)S(1)}, u32[]{:S(2)}, u32[]{:S(2)}) %collective-permute-start) | collective-permute-done | bytes 2080 | tf_op jit(solution)/shard_map/ppermute | solution.py:313
  21.2 0.6 %collective-permute-start.1 = (bf16[2,64,16]{2,1,0:T(8,128)(2,1)S(1)}, bf16[2,64,16]{2,1,0:T(8,128)(2,1)S(1)}, u32[]{:S(2)}, u32[]{:S(2)}) collective-permute-start(bf16[2,64,16]{2,1,0:T(8,128)(2,1)S(1)} %pad_maximum_fusion), channel_id=1, source_target_pairs={{0,16},{8,24},{16,0},{24,8},{1,17},{9,25},{17,1},{25,9},{2,18},{10... | collective-permute-start | bytes 12296 | tf_op jit(solution)/shard_map/ppermute | solution.py:313
  21.8 1.6 %collective-permute-start.5 = (bf16[128,320]{1,0:T(8,128)(2,1)S(1)}, bf16[128,320]{1,0:T(8,128)(2,1)S(1)}, u32[]{:S(2)}, u32[]{:S(2)}) collective-permute-start(bf16[128,320]{1,0:T(8,128)(2,1)S(1)} %get-tuple-element.23), channel_id=1, source_target_pairs={{0,8},{8,0},{16,24},{24,16},{1,9},{9,1},{17,25},{25,17},{2,10},{10... | collective-permute-start | bytes 245768 | tf_op jit(solution)/shard_map/ppermute | solution.py:302
  23.4 1.8 %collective-permute-done.1.refs_0_ = bf16[2,64,16]{2,1,0:T(8,128)(2,1)S(1)} collective-permute-done((bf16[2,64,16]{2,1,0:T(8,128)(2,1)S(1)}, bf16[2,64,16]{2,1,0:T(8,128)(2,1)S(1)}, u32[]{:S(2)}, u32[]{:S(2)}) %collective-permute-start.1) | collective-permute-done | bytes 4128 | tf_op jit(solution)/shard_map/ppermute | solution.py:313
  25.2 1.5 %collective-permute-start.2 = (bf16[128,320]{1,0:T(8,128)(2,1)S(1)}, bf16[128,320]{1,0:T(8,128)(2,1)S(1)}, u32[]{:S(2)}, u32[]{:S(2)}) collective-permute-start(bf16[128,320]{1,0:T(8,128)(2,1)S(1)} %get-tuple-element.18), channel_id=1, source_target_pairs={{0,8},{8,0},{16,24},{24,16},{1,9},{9,1},{17,25},{25,17},{2,10},{10... | collective-permute-start | bytes 245768 | tf_op jit(solution)/shard_map/ppermute | solution.py:302
  26.7 0.6 %collective-permute-done.5.before_ref = bf16[128,320]{1,0:T(8,128)(2,1)S(1)} collective-permute-done((bf16[128,320]{1,0:T(8,128)(2,1)S(1)}, bf16[128,320]{1,0:T(8,128)(2,1)S(1)}, u32[]{:S(2)}, u32[]{:S(2)}) %collective-permute-start.5) | collective-permute-done | bytes 81952 | tf_op jit(solution)/shard_map/ppermute | solution.py:302
  27.3 3.0 %collective-permute-start.6 = (bf16[128,320]{1,0:T(8,128)(2,1)S(1)}, bf16[128,320]{1,0:T(8,128)(2,1)S(1)}, u32[]{:S(2)}, u32[]{:S(2)}) collective-permute-start(bf16[128,320]{1,0:T(8,128)(2,1)S(1)} %get-tuple-element.25), channel_id=1, source_target_pairs={{0,24},{8,16},{16,8},{24,0},{1,25},{9,17},{17,9},{25,1},{2,26},{10... | collective-permute-start | bytes 245768 | tf_op jit(solution)/shard_map/ppermute | solution.py:302
  30.3 0.5 %collective-permute-done.2.before_ref = bf16[128,320]{1,0:T(8,128)(2,1)S(1)} collective-permute-done((bf16[128,320]{1,0:T(8,128)(2,1)S(1)}, bf16[128,320]{1,0:T(8,128)(2,1)S(1)}, u32[]{:S(2)}, u32[]{:S(2)}) %collective-permute-start.2) | collective-permute-done | bytes 81952 | tf_op jit(solution)/shard_map/ppermute | solution.py:302
  30.8 1.6 %collective-permute-start.3 = (bf16[128,320]{1,0:T(8,128)(2,1)S(1)}, bf16[128,320]{1,0:T(8,128)(2,1)S(1)}, u32[]{:S(2)}, u32[]{:S(2)}) collective-permute-start(bf16[128,320]{1,0:T(8,128)(2,1)S(1)} %get-tuple-element.20), channel_id=1, source_target_pairs={{0,24},{8,16},{16,8},{24,0},{1,25},{9,17},{17,9},{25,1},{2,26},{10... | collective-permute-start | bytes 245768 | tf_op jit(solution)/shard_map/ppermute | solution.py:302
  32.4 0.8 %collective-permute-done.6.before_ref = bf16[128,320]{1,0:T(8,128)(2,1)S(1)} collective-permute-done((bf16[128,320]{1,0:T(8,128)(2,1)S(1)}, bf16[128,320]{1,0:T(8,128)(2,1)S(1)}, u32[]{:S(2)}, u32[]{:S(2)}) %collective-permute-start.6) | collective-permute-done | bytes 81952 | tf_op jit(solution)/shard_map/ppermute | solution.py:302
  33.2 1.1 %later_block.8 = (bf16[128,320]{1,0:T(8,128)(2,1)S(1)}, bf16[2,8,2,1280]{3,2,1,0:T(2,128)(2,1)S(1)}) custom-call(bf16[128,320]{1,0:T(8,128)(2,1)S(1)} %collective-permute-done.6.before_ref, bf16[2,8,2,1280]{3,2,1,0:T(2,128)(2,1)S(1)} %get-tuple-element.26.out_in_ref, bf16[3,3,320,320]{3,2,1,0:T(8,128)(2,1)S(1)} %bitcast.20, ...), custom_call_target="tpu_custom_call", output_to_operand_aliasing={{1}: (1, {})} | custom-call | tf_op jit(solution)/shard_map/later_block/pallas_call | solution.py:389
  34.4 0.1 collective-permute-start.7
  34.5 2.9 %collective-permute-done.3.before_ref = bf16[128,320]{1,0:T(8,128)(2,1)S(1)} collective-permute-done((bf16[128,320]{1,0:T(8,128)(2,1)S(1)}, bf16[128,320]{1,0:T(8,128)(2,1)S(1)}, u32[]{:S(2)}, u32[]{:S(2)}) %collective-permute-start.3) | collective-permute-done | bytes 81952 | tf_op jit(solution)/shard_map/ppermute | solution.py:302
  37.3 1.1 %later_block.6 = (bf16[128,320]{1,0:T(8,128)(2,1)S(1)}, bf16[2,8,2,1280]{3,2,1,0:T(2,128)(2,1)S(1)}) custom-call(bf16[128,320]{1,0:T(8,128)(2,1)S(1)} %collective-permute-done.3.before_ref, bf16[2,8,2,1280]{3,2,1,0:T(2,128)(2,1)S(1)} %get-tuple-element.21.out_in_ref, bf16[3,3,320,320]{3,2,1,0:T(8,128)(2,1)S(1)} %bitcast.21, ...), custom_call_target="tpu_custom_call", output_to_operand_aliasing={{1}: (1, {})} | custom-call | tf_op jit(solution)/shard_map/later_block/pallas_call | solution.py:389
  38.5 0.3 collective-permute-start.4
  38.8 0.3 collective-permute-done.7.before_ref
  39.1 0.6 %later_block.9 = (bf16[128,320]{1,0:T(8,128)(2,1)}, bf16[2,8,2,1280]{3,2,1,0:T(2,128)(2,1)S(1)}) custom-call(bf16[128,320]{1,0:T(8,128)(2,1)S(1)} %collective-permute-done.7.before_ref, bf16[2,8,2,1280]{3,2,1,0:T(2,128)(2,1)S(1)} %get-tuple-element.28.out_in_ref, bf16[3,3,320,320]{3,2,1,0:T(8,128)(2,1)S(1)} %bitcast.22, ...), custom_call_target="tpu_custom_call", output_to_operand_aliasing={{1}: (1, {})} | custom-call | tf_op jit(solution)/shard_map/later_block/pallas_call | solution.py:389
  39.7 3.5 %collective-permute-done.4.refs_0_ = bf16[128,320]{1,0:T(8,128)(2,1)S(1)} collective-permute-done((bf16[128,320]{1,0:T(8,128)(2,1)S(1)}, bf16[128,320]{1,0:T(8,128)(2,1)S(1)}, u32[]{:S(2)}, u32[]{:S(2)}) %collective-permute-start.4) | collective-permute-done | bytes 81952 | tf_op jit(solution)/shard_map/ppermute | solution.py:302
  43.2 0.7 %last_block.1 = bf16[4,8,2,1280]{3,2,1,0:T(2,128)(2,1)} custom-call(bf16[128,320]{1,0:T(8,128)(2,1)S(1)} %collective-permute-done.4.refs_0_, bf16[2,8,2,1280]{3,2,1,0:T(2,128)(2,1)S(1)} %get-tuple-element.29.refs_1_, bf16[2,8,2,1280]{3,2,1,0:T(2,128)(2,1)S(1)} %get-tuple-element.30.refs_2_, bf16[3,3,320,320]{3,2,1,0:T(8,128)(2,1)S(1)} %bitcast.23, ...), custom_call_target="tpu_custom_call" | custom-call | tf_op jit(solution)/shard_map/last_block/pallas_call | solution.py:402
  (29 shorter events, 0.1 us)
Async XLA Ops:
  1.6 11.7 %all-to-all-start = ((bf16[8,1,2,2,8,256]{5,4,3,2,1,0:T(8,128)(2,1)}), bf16[8,1,2,2,8,256]{5,4,3,2,1,0:T(8,128)(2,1)S(1)}, u32[]{:S(2)}, u32[]{:S(2)}) async-start(bf16[8,1,2,2,8,256]{5,4,3,2,1,0:T(8,128)(2,1)} %bitcast.33), calls=%async_computation | async-start | bytes 262144 | tf_op jit(solution)/shard_map/all_to_all | solution.py:339
  7.2 2.0 %copy-start.1 = (bf16[3,3,3,256,256]{4,3,2,1,0:T(8,128)(2,1)S(1)}, bf16[3,3,3,256,256]{4,3,2,1,0:T(8,128)(2,1)}, u32[]{:S(2)}) copy-start(bf16[3,3,3,256,256]{4,3,2,1,0:T(8,128)(2,1)} %weight_ref.1) | copy-start | bytes 10616836
  9.2 0.7 %copy-start.8 = (s32[4,8]{1,0:T(4,128)S(1)}, s32[4,8]{1,0:T(4,128)}, u32[]{:S(2)}) copy-start(s32[4,8]{1,0:T(4,128)} %clips_ref.3) | copy-start | bytes 388
  9.8 0.9 %copy-start.13 = (bf16[128,320]{0,1:T(8,128)(2,1)S(1)}, bf16[128,320]{0,1:T(8,128)(2,1)}, u32[]{:S(2)}) copy-start(bf16[128,320]{0,1:T(8,128)(2,1)} %param.27) | copy-start | bytes 245764
  10.7 0.7 %copy-start.14 = (s32[4,8]{1,0:T(4,128)S(1)}, s32[4,8]{1,0:T(4,128)}, u32[]{:S(2)}) copy-start(s32[4,8]{1,0:T(4,128)} %offsets_ref.1) | copy-start | bytes 388
  11.4 1.8 %copy-start.7 = (bf16[256,16]{0,1:T(8,128)(2,1)S(1)}, bf16[256,16]{0,1:T(8,128)(2,1)}, u32[]{:S(2)}) copy-start(bf16[256,16]{0,1:T(8,128)(2,1)} %param.21) | copy-start | bytes 24580
  11.4 1.8 %copy-start.9 = (f32[256]{0:T(256)S(1)}, f32[256]{0:T(256)}, u32[]{:S(2)}) copy-start(f32[256]{0:T(256)} %param.18) | copy-start | bytes 3076
  11.4 1.8 %copy-start.10 = (f32[256]{0:T(256)S(1)}, f32[256]{0:T(256)}, u32[]{:S(2)}) copy-start(f32[256]{0:T(256)} %param.19) | copy-start | bytes 3076
  11.4 1.9 %copy-start.11 = (f32[256]{0:T(256)S(1)}, f32[256]{0:T(256)}, u32[]{:S(2)}) copy-start(f32[256]{0:T(256)} %param.20) | copy-start | bytes 3076
  11.4 1.9 %copy-start.12 = (f32[16]{0:T(128)S(1)}, f32[16]{0:T(128)}, u32[]{:S(2)}) copy-start(f32[16]{0:T(128)} %param.22) | copy-start | bytes 196
  11.4 10.3 %copy-start.3 = (bf16[3,3,16,320]{3,2,1,0:T(8,128)(2,1)S(1)}, bf16[3,3,16,320]{3,2,1,0:T(8,128)(2,1)}, u32[]{:S(2)}) copy-start(bf16[3,3,16,320]{3,2,1,0:T(8,128)(2,1)} %param.25) | copy-start | bytes 276484
  11.4 10.3 %copy-start.4 = (f32[1,320]{1,0:T(1,128)S(1)}, f32[1,320]{1,0:T(1,128)}, u32[]{:S(2)}) copy-start(f32[1,320]{1,0:T(1,128)} %refs_4_.3) | copy-start | bytes 3844
  11.5 10.3 %copy-start.5 = (f32[1,320]{1,0:T(1,128)S(1)}, f32[1,320]{1,0:T(1,128)}, u32[]{:S(2)}) copy-start(f32[1,320]{1,0:T(1,128)} %refs_5_.5) | copy-start | bytes 3844
  11.5 10.3 %copy-start.6 = (f32[1,320]{1,0:T(1,128)S(1)}, f32[1,320]{1,0:T(1,128)}, u32[]{:S(2)}) copy-start(f32[1,320]{1,0:T(1,128)} %refs_6_.5) | copy-start | bytes 3844
  12.3 9.5 %copy-start = (bf16[1,3,3,320,320]{4,3,2,1,0:T(8,128)(2,1)S(1)}, bf16[1,3,3,320,320]{4,3,2,1,0:T(8,128)(2,1)}, u32[]{:S(2)}) copy-start(bf16[1,3,3,320,320]{4,3,2,1,0:T(8,128)(2,1)} %param.30) | copy-start | bytes 5529604
  13.3 2.0 %copy-start.2 = (bf16[3,3,3,256,256]{4,3,2,1,0:T(8,128)(2,1)S(1)}, bf16[3,3,3,256,256]{4,3,2,1,0:T(8,128)(2,1)}, u32[]{:S(2)}) copy-start(bf16[3,3,3,256,256]{4,3,2,1,0:T(8,128)(2,1)} %weight_ref.1) | copy-start | bytes 10616836
  17.4 3.8 %collective-permute-start = (bf16[1,64,16]{2,1,0:T(8,128)(2,1)S(1)}, bf16[1,64,16]{2,1,0:T(8,128)(2,1)S(1)}, u32[]{:S(2)}, u32[]{:S(2)}) collective-permute-start(bf16[1,64,16]{2,1,0:T(8,128)(2,1)S(1)} %encode.1.refs_0_), channel_id=1, source_target_pairs={{0,8},{8,0},{16,24},{24,16},{1,9},{9,1},{17,25},{25,17},{2,10},{10... | collective-permute-start | bytes 6152 | tf_op jit(solution)/shard_map/ppermute | solution.py:313
  21.2 4.0 %collective-permute-start.1 = (bf16[2,64,16]{2,1,0:T(8,128)(2,1)S(1)}, bf16[2,64,16]{2,1,0:T(8,128)(2,1)S(1)}, u32[]{:S(2)}, u32[]{:S(2)}) collective-permute-start(bf16[2,64,16]{2,1,0:T(8,128)(2,1)S(1)} %pad_maximum_fusion), channel_id=1, source_target_pairs={{0,16},{8,24},{16,0},{24,8},{1,17},{9,25},{17,1},{25,9},{2,18},{10... | collective-permute-start | bytes 12296 | tf_op jit(solution)/shard_map/ppermute | solution.py:313
  21.8 5.5 %collective-permute-start.5 = (bf16[128,320]{1,0:T(8,128)(2,1)S(1)}, bf16[128,320]{1,0:T(8,128)(2,1)S(1)}, u32[]{:S(2)}, u32[]{:S(2)}) collective-permute-start(bf16[128,320]{1,0:T(8,128)(2,1)S(1)} %get-tuple-element.23), channel_id=1, source_target_pairs={{0,8},{8,0},{16,24},{24,16},{1,9},{9,1},{17,25},{25,17},{2,10},{10... | collective-permute-start | bytes 245768 | tf_op jit(solution)/shard_map/ppermute | solution.py:302
  25.2 5.7 %collective-permute-start.2 = (bf16[128,320]{1,0:T(8,128)(2,1)S(1)}, bf16[128,320]{1,0:T(8,128)(2,1)S(1)}, u32[]{:S(2)}, u32[]{:S(2)}) collective-permute-start(bf16[128,320]{1,0:T(8,128)(2,1)S(1)} %get-tuple-element.18), channel_id=1, source_target_pairs={{0,8},{8,0},{16,24},{24,16},{1,9},{9,1},{17,25},{25,17},{2,10},{10... | collective-permute-start | bytes 245768 | tf_op jit(solution)/shard_map/ppermute | solution.py:302
  27.3 6.0 %collective-permute-start.6 = (bf16[128,320]{1,0:T(8,128)(2,1)S(1)}, bf16[128,320]{1,0:T(8,128)(2,1)S(1)}, u32[]{:S(2)}, u32[]{:S(2)}) collective-permute-start(bf16[128,320]{1,0:T(8,128)(2,1)S(1)} %get-tuple-element.25), channel_id=1, source_target_pairs={{0,24},{8,16},{16,8},{24,0},{1,25},{9,17},{17,9},{25,1},{2,26},{10... | collective-permute-start | bytes 245768 | tf_op jit(solution)/shard_map/ppermute | solution.py:302
  30.8 6.5 %collective-permute-start.3 = (bf16[128,320]{1,0:T(8,128)(2,1)S(1)}, bf16[128,320]{1,0:T(8,128)(2,1)S(1)}, u32[]{:S(2)}, u32[]{:S(2)}) collective-permute-start(bf16[128,320]{1,0:T(8,128)(2,1)S(1)} %get-tuple-element.20), channel_id=1, source_target_pairs={{0,24},{8,16},{16,8},{24,0},{1,25},{9,17},{17,9},{25,1},{2,26},{10... | collective-permute-start | bytes 245768 | tf_op jit(solution)/shard_map/ppermute | solution.py:302
  34.4 4.7 %collective-permute-start.7 = (bf16[128,320]{1,0:T(8,128)(2,1)S(1)}, bf16[128,320]{1,0:T(8,128)(2,1)S(1)}, u32[]{:S(2)}, u32[]{:S(2)}) collective-permute-start(bf16[128,320]{1,0:T(8,128)(2,1)S(1)} %get-tuple-element.27), channel_id=1, source_target_pairs={{0,8},{8,0},{16,24},{24,16},{1,9},{9,1},{17,25},{25,17},{2,10},{10... | collective-permute-start | bytes 245768 | tf_op jit(solution)/shard_map/ppermute | solution.py:302
  38.5 4.7 %collective-permute-start.4 = (bf16[128,320]{1,0:T(8,128)(2,1)S(1)}, bf16[128,320]{1,0:T(8,128)(2,1)S(1)}, u32[]{:S(2)}, u32[]{:S(2)}) collective-permute-start(bf16[128,320]{1,0:T(8,128)(2,1)S(1)} %get-tuple-element.22), channel_id=1, source_target_pairs={{0,8},{8,0},{16,24},{24,16},{1,9},{9,1},{17,25},{25,17},{2,10},{10... | collective-permute-start | bytes 245768 | tf_op jit(solution)/shard_map/ppermute | solution.py:302

commit v3 on v2

--- a/solution.py
+++ b/solution.py
@@ -9,10 +9,10 @@
 
 GROUPS = 32
 LANES = 128
-PLACE_FLOPS = 6_000_000_000
 EPS = 1e-06
 VMEM_LIMIT = 32 * 1024 * 1024
-PLACE_VMEM = 8 * 1024 * 1024
+GROUPS_VMEM = 4 * 1024 * 1024
+GROUPS_FLOPS = 12_000_000_000
 F32 = jnp.float32
 BF16 = jnp.bfloat16
 
@@ -37,6 +37,12 @@
         return jnp.floor((index + 0.5) * (1.0 / size))
 
     return jnp.where(group_of(0) == group_of(1), 1.0, 0.0).astype(BF16)
+
+
+def groups_kernel(after_ref, *out_refs):
+    del after_ref
+    for out_ref in out_refs:
+        out_ref[...] = same_group(out_ref.shape[0])
 
 
 def group_sums(rows, same):
@@ -59,15 +65,22 @@
 
 
 def encode_kernel(
-    x_ref, weight_ref, gain_ref, shift_ref, bias_ref, lat_weight_ref, lat_bias_ref, after_ref,
-    out_ref, dup_ref, act_ref, pool_ref,
+    slab_axis, *refs
 ):
-    del after_ref
+    (
+        weight_ref, gain_ref, shift_ref, bias_ref, lat_weight_ref, lat_bias_ref, same_ref,
+        out_ref, dup_ref, act_ref, pool_ref, x_ref,
+    ) = refs[-12:]
+    slab_rows = refs[0].shape[2]
+    for step, piece_ref in enumerate(refs[:-12]):
+        for half in range(2):
+            source = lax.axis_index(slab_axis) ^ (2 * step + half)
+            x_ref[:, pl.ds(source * slab_rows, slab_rows)] = piece_ref[half]
     row_count, frames, cols, channels = x_ref.shape[1:]
     plane = frames * cols
     size = row_count * plane
     lat_rows, lat_cols = row_count // 2, cols // 2
-    same = same_group(channels)
+    same = same_ref[...]
     for item in range(x_ref.shape[0]):
         x = x_ref[item].astype(F32).reshape(size, channels)
         sums = jnp.concatenate(
@@ -118,24 +131,26 @@
         out_ref[item] = (latent + lat_bias_ref[...]).astype(BF16)
 
 
-def encode(clips, *operands):
-    items, row_count, frames, cols, channels = clips.shape
+def encode(pieces, *operands):
+    _, items, slab_rows, frames, cols, channels = pieces[0].shape
+    row_count = 2 * len(pieces) * slab_rows
     plane = frames * cols
     lat_rows, lat_cols = row_count // 2, cols // 2
     padded = pltpu.VMEM(((row_count + 2) * plane, 3 * channels), BF16)
     return pl.pallas_call(
-        encode_kernel,
+        functools.partial(encode_kernel, "slab"),
         out_shape=jax.ShapeDtypeStruct((items, lat_cols * lat_rows * frames, operands[-2].shape[1]), BF16),
-        in_specs=[vmem()] * len(operands) + [pl.BlockSpec(memory_space=pl.ANY)],
+        in_specs=[vmem()] * (len(pieces) + len(operands)),
         out_specs=vmem(),
         scratch_shapes=[
             padded,
             padded,
             pltpu.VMEM((channels // LANES, lat_rows * plane, LANES), F32),
+            pltpu.VMEM((items, row_count, frames, cols, channels), BF16),
         ],
         compiler_params=params(),
         name="encode",
-    )(clips, *operands)
+    )(*pieces, *operands)
 
 
 def shifted(value, unit, frames):
@@ -180,7 +195,7 @@
 
 
 def unet_layer(state, operands, taps_ref, block, frames):
-    weight_ref, gain_ref, shift_ref, bias_ref = operands
+    weight_ref, gain_ref, shift_ref, bias_ref, same_ref = operands
     streams, unit = block
     size, channels = state.shape
     cols = size // (streams * unit)
@@ -191,7 +206,7 @@
         rows.append(jnp.sum(own, axis=0, keepdims=True))
         rows.append(jnp.sum(own * own, axis=0, keepdims=True))
     rows.extend([jnp.zeros((1, channels), F32)] * (-len(rows) % 8))
-    sums = group_sums(jnp.concatenate(rows, axis=0), same_group(channels))
+    sums = group_sums(jnp.concatenate(rows, axis=0), same_ref[...])
     sums = sums * (1.0 / (cols * unit * (channels // GROUPS)))
     normed = []
     for item in range(streams):
@@ -215,28 +230,25 @@
         out_ref[first + item] = wide
 
 
-def place_kernel(slab, owned, frames, clips_ref, offsets_ref, table_ref, bias_ref, kept_ref, out_ref):
-    del kept_ref
+def place_rows(clips_ref, offsets_ref, table, bias, out_ref, slab, owned, frames):
     streams, unit, _ = out_ref.shape
-    first = lax.axis_index(slab) * owned
-    table_rows = table_ref.shape[1]
-    row = lax.broadcasted_iota(jnp.int32, (unit, table_rows), 0)
-    row = lax.div(row, jnp.int32(frames))
+    table_rows = table.shape[1]
+    row = lax.div(lax.broadcasted_iota(jnp.int32, (unit, table_rows), 0), jnp.int32(frames))
     wanted = lax.broadcasted_iota(jnp.int32, (unit, table_rows), 1) - row
     for stream in range(streams):
         micro = stream // owned
-        offset = offsets_ref[micro, clips_ref[micro, first + stream % owned]]
+        offset = offsets_ref[micro, clips_ref[micro, slab * owned + stream % owned]]
         hot = jnp.where(wanted == offset, 1.0, 0.0).astype(BF16)
-        out_ref[stream] = dot_last(hot, table_ref[...]) + bias_ref[...]
-
-
-def first_kernel(block, frames, count, chunk, section_axis, *refs):
+        out_ref[stream] = dot_last(hot, table) + bias
+
+
+def first_kernel(block, frames, count, chunk, *refs):
     streams, unit = block
     latent_refs = refs[:count]
     place_ref, in_weight_ref, *operands = refs[count:-3]
     state_ref, out_ref, taps_ref = refs[-3:]
 
-    @pl.when(lax.axis_index(section_axis) == 0)
+    @pl.when(lax.axis_index("section") == 0)
     def _():
         size, width = state_ref.shape
         cols = size // (streams * unit)
@@ -246,7 +258,8 @@
                 for item in range(ref.shape[0]):
                     parts.append(ref[item, pl.ds(col * unit, unit), :].astype(F32))
         total = conv3_narrow(jnp.concatenate(parts, axis=0), in_weight_ref[...], block, frames)
-        placed = place_ref[pl.ds(chunk * streams, streams)].reshape(1, streams * unit, width)
+        placed = place_ref[pl.ds(chunk * streams, streams)]
+        placed = placed.reshape(1, streams * unit, width)
         total = (total.reshape(cols, streams * unit, width) + placed).reshape(size, width)
         state = total.astype(BF16).astype(F32)
         state = unet_layer(state, operands, taps_ref, block, frames)
@@ -256,14 +269,15 @@
 
 def later_kernel(
     stage_index, block, frames, section_axis,
-    before_ref, out_in_ref, weight_ref, gain_ref, shift_ref, bias_ref, state_ref, out_ref, taps_ref,
+    before_ref, out_in_ref, *refs
 ):
     del out_in_ref
+    *operands, state_ref, out_ref, taps_ref = refs
 
     @pl.when(lax.axis_index(section_axis) == stage_index)
     def _():
         state = unet_layer(
-            before_ref[...].astype(F32), (weight_ref, gain_ref, shift_ref, bias_ref), taps_ref, block, frames
+            before_ref[...].astype(F32), operands, taps_ref, block, frames
         )
         state_ref[...] = state
         write_output(out_ref, state, 0, block, frames)
@@ -289,14 +303,51 @@
         out_ref[pl.ds((chunks - 1) * streams, streams)] = parts[chunks - 1][...]
 
 
-def select_kernel(section_axis, clips_ref, features_ref, out_ref):
+def select_kernel(
+    section_axis, slab_axis, owned,
+    clips_ref, offsets_ref, features_ref, table_ref, bias_ref, keep_ref, give_ref, place_ref,
+):
     section = lax.axis_index(section_axis)
-    for slot in range(out_ref.shape[0]):
-        out_ref[slot] = features_ref[clips_ref[section, slot]]
+    slab = lax.axis_index(slab_axis)
+    for step in range(keep_ref.shape[0]):
+        for half, out_ref in enumerate((keep_ref, give_ref)):
+            for item in range(owned):
+                slot = (slab ^ (2 * step + half)) * owned + item
+                out_ref[step, item] = features_ref[clips_ref[section, slot]]
+    bias = bias_ref[...].reshape(1, -1)
+    frames = features_ref.shape[2]
+    place_rows(clips_ref, offsets_ref, table_ref[...], bias, place_ref, slab, owned, frames)
+
+
+def exchange(features, slot_clips, row_offsets, table, bias, place_shape, slab_count, owned):
+    steps = slab_count // 2
+    shape = jax.ShapeDtypeStruct((steps, owned) + features.shape[1:], BF16)
+    keep, give, place = pl.pallas_call(
+        functools.partial(select_kernel, "section", "slab", owned),
+        out_shape=[shape, shape, jax.ShapeDtypeStruct(place_shape, F32)],
+        in_specs=[smem()] * 2 + [vmem()] * 3,
+        out_specs=[vmem()] * 3,
+        name="select",
+    )(slot_clips, row_offsets, features, table, bias)
+    got = lax.ppermute(give, "slab", [(slab, slab ^ 1) for slab in range(slab_count)])
+    pieces = [jnp.stack([keep[step], got[step]]) for step in range(steps)]
+    for step in range(1, steps):
+        pairs = [(slab, slab ^ (2 * step)) for slab in range(slab_count)]
+        pieces[step] = lax.ppermute(pieces[step], "slab", pairs)
+    return pieces, got, place
+
+
+CYCLES = {
+    (0, 1): ((0, 1), (1, 3), (3, 2), (2, 0)),
+    (1, 2): ((1, 2), (2, 0), (0, 3), (3, 1)),
+    (2, 3): ((2, 3),),
+}
 
 
 def hop(value, source, target):
     count = lax.axis_size("section")
+    if count == 4 and (source, target) in CYCLES:
+        return lax.ppermute(value, "section", list(CYCLES[source, target]))
     if count & (count - 1):
         return lax.ppermute(value, "section", [(source, target)])
     return lax.ppermute(value, "section", [(s, s ^ source ^ target) for s in range(count)])
@@ -328,28 +379,22 @@
     lat_rows, lat_cols = row_total // 2, cols // 2
     unit = lat_rows * frames
 
-    ordered = pl.pallas_call(
-        functools.partial(select_kernel, "section"),
-        out_shape=jax.ShapeDtypeStruct(features.shape[1:], BF16),
-        in_specs=[smem(), vmem()],
-        out_specs=vmem(),
-        name="select",
-    )(slot_clips, features[0])
-    shaped = ordered.reshape(slab_count, owned, slab_rows, frames, cols, channels)
-    whole = lax.all_to_all(shaped, "slab", split_axis=0, concat_axis=0)
-    whole = jnp.swapaxes(whole, 0, 1).reshape(owned, row_total, frames, cols, channels)
-    place = pl.pallas_call(
-        functools.partial(place_kernel, "slab", owned, frames),
-        out_shape=jax.ShapeDtypeStruct((section_count * owned, unit, width), F32),
-        in_specs=[smem()] * 2 + [vmem()] * 2 + [pl.BlockSpec(memory_space=pl.ANY)],
-        out_specs=vmem(),
-        compiler_params=params(PLACE_VMEM),
-        cost_estimate=pl.CostEstimate(flops=PLACE_FLOPS, bytes_accessed=0, transcendentals=0),
-        name="place",
-    )(slot_clips, row_offsets, pos_table.T, in_bias.reshape(1, -1), vae_weight)
+    place_shape = (section_count * owned, unit, width)
+    pieces, got, place = exchange(
+        features[0], slot_clips, row_offsets, pos_table.T, in_bias, place_shape, slab_count, owned
+    )
+    vae_same, unet_same = pl.pallas_call(
+        groups_kernel,
+        out_shape=[jax.ShapeDtypeStruct((size, size), BF16) for size in (channels, width)],
+        in_specs=[pl.BlockSpec(memory_space=pl.ANY)],
+        out_specs=[vmem()] * 2,
+        compiler_params=params(GROUPS_VMEM),
+        cost_estimate=pl.CostEstimate(flops=GROUPS_FLOPS, bytes_accessed=0, transcendentals=0),
+        name="groups",
+    )(got)
     latent = encode(
-        whole, vae_weight, vae_gain.reshape(1, -1), vae_shift.reshape(1, -1), vae_bias.reshape(1, -1),
-        latent_weight.T, latent_bias.reshape(1, -1), place,
+        pieces, vae_weight, vae_gain.reshape(1, -1), vae_shift.reshape(1, -1), vae_bias.reshape(1, -1),
+        latent_weight.T, latent_bias.reshape(1, -1), vae_same,
     )
     latents = gather_first(latent)
 
@@ -359,7 +404,7 @@
     block = (streams, unit)
     size = lat_cols * streams * unit
     taps = pltpu.VMEM((3, size + 2 * streams * unit, width), BF16)
-    layer = [unet_weight[0], unet_gain, unet_shift, unet_bias]
+    layer = [unet_weight[0], unet_gain, unet_shift, unet_bias, unet_same]
     result_shapes = [
         jax.ShapeDtypeStruct((size, width), BF16),
         jax.ShapeDtypeStruct((streams, lat_rows, frames, lat_cols * width), BF16),
@@ -372,7 +417,7 @@
             mine = latents[-1:] if chunk else latents[:-1]
         operands = mine + [place, in_weight.reshape(-1, width)] + layer
         state, outs[chunk] = pl.pallas_call(
-            functools.partial(first_kernel, block, frames, len(mine), chunk, "section"),
+            functools.partial(first_kernel, block, frames, len(mine), chunk),
             out_shape=result_shapes,
             in_specs=[vmem()] * len(operands),
             out_specs=[vmem()] * 2,
@@ -389,7 +434,7 @@
             state, outs[chunk] = pl.pallas_call(
                 functools.partial(later_kernel, index, block, frames, "section"),
                 out_shape=result_shapes,
-                in_specs=[vmem()] * 6,
+                in_specs=[vmem()] * (2 + len(layer)),
                 out_specs=[vmem()] * 2,
                 scratch_shapes=[taps],
                 input_output_aliases={1: 1},

time: 44.2 us -> 41.2 us (0.932)
  the two profiles are of different devices: /device:TPU:4 before, /device:TPU:22 now
where the time goes in v3:
time: 41.2 us; the launch traced here: 40.9 us
  waiting for transfers between devices  18.8 us (46%)
  starting transfers between devices  13.5 us (33%)
  Pallas kernels  7.44 us (18%)
  local copies, waits for them, and re-layouts  0.85 us (2%)
    ppermute x6, waiting for transfers between devices, hop(): return lax.ppermute(value, 'section', list(CYCLES[source, target]))  8.26 us
    ppermute x6, starting transfers between devices, hop(): return lax.ppermute(value, 'section', list(CYCLES[source, target]))  8.25 us
    ppermute x2, waiting for transfers between devices, gather_first(): lax.ppermute(held, 'section', [(s, s ^ step) for s in range(count)])  6.21 us
    ppermute x3, starting transfers between devices, exchange(): pieces[step] = lax.ppermute(pieces[step], 'slab', pairs)  4.07 us
    ppermute x3, waiting for transfers between devices, exchange(): pieces[step] = lax.ppermute(pieces[step], 'slab', pairs)  3.69 us
    pallas_call x1, Pallas kernels, encode(): pl.pallas_call(functools.partial(encode_kernel, 'slab'), out_shape=jax.Sh...  1.99 us
    pallas_call x1, Pallas kernels, exchange(): pl.pallas_call(functools.partial(select_kernel, 'section', 'slab', owned)...  1.81 us
    pallas_call x1, Pallas kernels, per_device(): pl.pallas_call(functools.partial(last_kernel, block, frames, 'section', c...  1.77 us
  transfers between devices with their start and end apart: 12, of which 11 were waited for; matrix products, arithmetic and copies ran while one was open for 2% of the time, Pallas kernels for 5%

profile of v3, /device:TPU:22, one launch (start us, length us, event | category | flops | bytes accessed | tf_op | source)
XLA Modules:
  0.0 40.9 jit_solution(16552340487760511983)
XLA Ops:
  0.0 1.8 %select.1 = (bf16[4,1,2,2,8,256]{5,4,3,2,1,0:T(8,128)(2,1)}, bf16[4,1,2,2,8,256]{5,4,3,2,1,0:T(8,128)(2,1)}, f32[4,16,320]{2,1,0:T(8,128)}) custom-call(s32[4,8]{1,0:T(4,128)} %clips_ref.1, s32[4,8]{1,0:T(4,128)} %offsets_ref.1, bf16[8,2,2,8,256]{4,3,2,1,0:T(8,128)(2,1)} %bitcast.27, bf16[320,128]{1,0:T(8,128)(2,1)} %bitcast.28, f32[320]{0:T(512)} %bias_ref.1), custom_call_target="tpu_custom_call" | custom-call | tf_op jit(solution)/shard_map/select/pallas_call | solution.py:325
  1.8 0.8 %fusion = (bf16[1,1,2,2,8,256]{5,4,3,2,1,0:T(8,128)(2,1)S(1)}, bf16[1,1,2,2,8,256]{5,4,3,2,1,0:T(8,128)(2,1)S(1)}, bf16[1,1,2,2,8,256]{5,4,3,2,1,0:T(8,128)(2,1)S(1)}, bf16[1,1,2,2,8,256]{5,4,3,2,1,0:T(8,128)(2,1)S(1)}) fusion(bf16[4,1,2,2,8,256]{5,4,3,2,1,0:T(8,128)(2,1)} %get-tuple-element.23), kind=kLoop, calls=%fused_computation.5 | loop fusion | bytes 131072 | tf_op jit(solution)/shard_map/slice | solution.py:333
  2.6 0.7 %collective-permute-done.after_ref = bf16[4,1,2,2,8,256]{5,4,3,2,1,0:T(8,128)(2,1)S(1)} collective-permute-done((bf16[4,1,2,2,8,256]{5,4,3,2,1,0:T(8,128)(2,1)}, bf16[4,1,2,2,8,256]{5,4,3,2,1,0:T(8,128)(2,1)S(1)}, u32[]{:S(2)}, u32[]{:S(2)}) %collective-permute-start) | collective-permute-done | bytes 65568 | tf_op jit(solution)/shard_map/ppermute | solution.py:332
  3.3 0.5 %collective-permute-start.3 = (bf16[2,1,2,2,8,256]{5,4,3,2,1,0:T(8,128)(2,1)S(1)}, bf16[2,1,2,2,8,256]{5,4,3,2,1,0:T(8,128)(2,1)S(1)}, u32[]{:S(2)}, u32[]{:S(2)}) collective-permute-start(bf16[2,1,2,2,8,256]{5,4,3,2,1,0:T(8,128)(2,1)S(1)} %pad_maximum_fusion.3), channel_id=1, source_target_pairs={{0,6},{1,7},{2,4},{3,5},{4,2},{5,3},{6,0},{7,1},{8,14},{9,15},{10,... | collective-permute-start | bytes 98312 | tf_op jit(solution)/shard_map/ppermute | solution.py:336
  3.8 3.5 %collective-permute-start.2 = (bf16[2,1,2,2,8,256]{5,4,3,2,1,0:T(8,128)(2,1)S(1)}, bf16[2,1,2,2,8,256]{5,4,3,2,1,0:T(8,128)(2,1)S(1)}, u32[]{:S(2)}, u32[]{:S(2)}) collective-permute-start(bf16[2,1,2,2,8,256]{5,4,3,2,1,0:T(8,128)(2,1)S(1)} %pad_maximum_fusion.2), channel_id=1, source_target_pairs={{0,4},{1,5},{2,6},{3,7},{4,0},{5,1},{6,2},{7,3},{8,12},{9,13},{10,... | collective-permute-start | bytes 98312 | tf_op jit(solution)/shard_map/ppermute | solution.py:336
  7.3 0.0 copy-start.10
  7.4 0.0 copy-start.11
  7.4 0.1 collective-permute-start.1
  7.4 0.1 groups.1
  7.6 0.0 copy-start.2
  7.6 0.0 copy-start.3
  7.7 2.1 %collective-permute-done.2.refs_2_ = bf16[2,1,2,2,8,256]{5,4,3,2,1,0:T(8,128)(2,1)S(1)} collective-permute-done((bf16[2,1,2,2,8,256]{5,4,3,2,1,0:T(8,128)(2,1)S(1)}, bf16[2,1,2,2,8,256]{5,4,3,2,1,0:T(8,128)(2,1)S(1)}, u32[]{:S(2)}, u32[]{:S(2)}) %collective-permute-start.2) | collective-permute-done | bytes 32800 | tf_op jit(solution)/shard_map/ppermute | solution.py:336
  9.8 1.6 %collective-permute-done.1.refs_1_ = bf16[2,1,2,2,8,256]{5,4,3,2,1,0:T(8,128)(2,1)S(1)} collective-permute-done((bf16[2,1,2,2,8,256]{5,4,3,2,1,0:T(8,128)(2,1)S(1)}, bf16[2,1,2,2,8,256]{5,4,3,2,1,0:T(8,128)(2,1)S(1)}, u32[]{:S(2)}, u32[]{:S(2)}) %collective-permute-start.1) | collective-permute-done | bytes 32800 | tf_op jit(solution)/shard_map/ppermute | solution.py:336
  11.4 2.0 %encode.1.refs_0_ = bf16[1,64,16]{2,1,0:T(8,128)(2,1)S(1)} custom-call(bf16[2,1,2,2,8,256]{5,4,3,2,1,0:T(8,128)(2,1)S(1)} %pad_maximum_fusion.refs_0_, bf16[2,1,2,2,8,256]{5,4,3,2,1,0:T(8,128)(2,1)S(1)} %collective-permute-done.1.refs_1_, bf16[2,1,2,2,8,256]{5,4,3,2,1,0:T(8,128)(2,1)S(1)} %collective-permute-done.2.refs_2_, ...), custom_call_target="tpu_custom_call" | custom-call | tf_op jit(solution)/shard_map/encode/pallas_call | solution.py:140
  13.4 0.6 %collective-permute-start.4 = (bf16[1,64,16]{2,1,0:T(8,128)(2,1)S(1)}, bf16[1,64,16]{2,1,0:T(8,128)(2,1)S(1)}, u32[]{:S(2)}, u32[]{:S(2)}) collective-permute-start(bf16[1,64,16]{2,1,0:T(8,128)(2,1)S(1)} %encode.1.refs_0_), channel_id=1, source_target_pairs={{0,8},{8,0},{16,24},{24,16},{1,9},{9,1},{17,25},{25,17},{2,10},{10... | collective-permute-start | bytes 6152 | tf_op jit(solution)/shard_map/ppermute | solution.py:364
  14.0 3.2 %collective-permute-done.4.refs_1_ = bf16[1,64,16]{2,1,0:T(8,128)(2,1)S(1)} collective-permute-done((bf16[1,64,16]{2,1,0:T(8,128)(2,1)S(1)}, bf16[1,64,16]{2,1,0:T(8,128)(2,1)S(1)}, u32[]{:S(2)}, u32[]{:S(2)}) %collective-permute-start.4) | collective-permute-done | bytes 2080 | tf_op jit(solution)/shard_map/ppermute | solution.py:364
  17.2 0.6 %collective-permute-start.5 = (bf16[2,64,16]{2,1,0:T(8,128)(2,1)S(1)}, bf16[2,64,16]{2,1,0:T(8,128)(2,1)S(1)}, u32[]{:S(2)}, u32[]{:S(2)}) collective-permute-start(bf16[2,64,16]{2,1,0:T(8,128)(2,1)S(1)} %pad_maximum_fusion.4), channel_id=1, source_target_pairs={{0,16},{8,24},{16,0},{24,8},{1,17},{9,25},{17,1},{25,9},{2,18},{10... | collective-permute-start | bytes 12296 | tf_op jit(solution)/shard_map/ppermute | solution.py:364
  17.8 0.6 %collective-permute-start.9 = (bf16[128,320]{1,0:T(8,128)(2,1)S(1)}, bf16[128,320]{1,0:T(8,128)(2,1)S(1)}, u32[]{:S(2)}, u32[]{:S(2)}) collective-permute-start(bf16[128,320]{1,0:T(8,128)(2,1)S(1)} %get-tuple-element.33), channel_id=1, source_target_pairs={{0,8},{8,24},{24,16},{16,0},{1,9},{9,25},{25,17},{17,1},{2,10},{10... | collective-permute-start | bytes 245768 | tf_op jit(solution)/shard_map/ppermute | solution.py:350
  18.4 3.0 %collective-permute-done.5.refs_0_ = bf16[2,64,16]{2,1,0:T(8,128)(2,1)S(1)} collective-permute-done((bf16[2,64,16]{2,1,0:T(8,128)(2,1)S(1)}, bf16[2,64,16]{2,1,0:T(8,128)(2,1)S(1)}, u32[]{:S(2)}, u32[]{:S(2)}) %collective-permute-start.5) | collective-permute-done | bytes 4128 | tf_op jit(solution)/shard_map/ppermute | solution.py:364
  21.4 0.3 collective-permute-start.6
  21.7 0.8 %collective-permute-done.9.before_ref = bf16[128,320]{1,0:T(8,128)(2,1)S(1)} collective-permute-done((bf16[128,320]{1,0:T(8,128)(2,1)S(1)}, bf16[128,320]{1,0:T(8,128)(2,1)S(1)}, u32[]{:S(2)}, u32[]{:S(2)}) %collective-permute-start.9) | collective-permute-done | bytes 81952 | tf_op jit(solution)/shard_map/ppermute | solution.py:350
  22.5 3.5 %collective-permute-start.10 = (bf16[128,320]{1,0:T(8,128)(2,1)S(1)}, bf16[128,320]{1,0:T(8,128)(2,1)S(1)}, u32[]{:S(2)}, u32[]{:S(2)}) collective-permute-start(bf16[128,320]{1,0:T(8,128)(2,1)S(1)} %get-tuple-element.35), channel_id=1, source_target_pairs={{8,16},{16,0},{0,24},{24,8},{9,17},{17,1},{1,25},{25,9},{10,18},{1... | collective-permute-start | bytes 245768 | tf_op jit(solution)/shard_map/ppermute | solution.py:350
  26.0 1.1 %collective-permute-done.6.before_ref = bf16[128,320]{1,0:T(8,128)(2,1)S(1)} collective-permute-done((bf16[128,320]{1,0:T(8,128)(2,1)S(1)}, bf16[128,320]{1,0:T(8,128)(2,1)S(1)}, u32[]{:S(2)}, u32[]{:S(2)}) %collective-permute-start.6) | collective-permute-done | bytes 81952 | tf_op jit(solution)/shard_map/ppermute | solution.py:350
  27.1 1.3 %collective-permute-start.7 = (bf16[128,320]{1,0:T(8,128)(2,1)S(1)}, bf16[128,320]{1,0:T(8,128)(2,1)S(1)}, u32[]{:S(2)}, u32[]{:S(2)}) collective-permute-start(bf16[128,320]{1,0:T(8,128)(2,1)S(1)} %get-tuple-element.30), channel_id=1, source_target_pairs={{8,16},{16,0},{0,24},{24,8},{9,17},{17,1},{1,25},{25,9},{10,18},{1... | collective-permute-start | bytes 245768 | tf_op jit(solution)/shard_map/ppermute | solution.py:350
  28.4 0.5 %collective-permute-done.10.before_ref = bf16[128,320]{1,0:T(8,128)(2,1)S(1)} collective-permute-done((bf16[128,320]{1,0:T(8,128)(2,1)S(1)}, bf16[128,320]{1,0:T(8,128)(2,1)S(1)}, u32[]{:S(2)}, u32[]{:S(2)}) %collective-permute-start.10) | collective-permute-done | bytes 81952 | tf_op jit(solution)/shard_map/ppermute | solution.py:350
  28.9 1.3 %collective-permute-start.11 = (bf16[128,320]{1,0:T(8,128)(2,1)S(1)}, bf16[128,320]{1,0:T(8,128)(2,1)S(1)}, u32[]{:S(2)}, u32[]{:S(2)}) collective-permute-start(bf16[128,320]{1,0:T(8,128)(2,1)S(1)} %get-tuple-element.37), channel_id=1, source_target_pairs={{16,24},{17,25},{18,26},{19,27},{20,28},{21,29},{22,30},{23,31}} | collective-permute-start | bytes 245768 | tf_op jit(solution)/shard_map/ppermute | solution.py:350
  30.2 2.4 %collective-permute-done.7.before_ref = bf16[128,320]{1,0:T(8,128)(2,1)S(1)} collective-permute-done((bf16[128,320]{1,0:T(8,128)(2,1)S(1)}, bf16[128,320]{1,0:T(8,128)(2,1)S(1)}, u32[]{:S(2)}, u32[]{:S(2)}) %collective-permute-start.7) | collective-permute-done | bytes 81952 | tf_op jit(solution)/shard_map/ppermute | solution.py:350
  32.6 1.3 %collective-permute-start.8 = (bf16[128,320]{1,0:T(8,128)(2,1)S(1)}, bf16[128,320]{1,0:T(8,128)(2,1)S(1)}, u32[]{:S(2)}, u32[]{:S(2)}) collective-permute-start(bf16[128,320]{1,0:T(8,128)(2,1)S(1)} %get-tuple-element.32), channel_id=1, source_target_pairs={{16,24},{17,25},{18,26},{19,27},{20,28},{21,29},{22,30},{23,31}} | collective-permute-start | bytes 245768 | tf_op jit(solution)/shard_map/ppermute | solution.py:350
  33.9 1.5 %collective-permute-done.11.before_ref = bf16[128,320]{1,0:T(8,128)(2,1)S(1)} collective-permute-done((bf16[128,320]{1,0:T(8,128)(2,1)S(1)}, bf16[128,320]{1,0:T(8,128)(2,1)S(1)}, u32[]{:S(2)}, u32[]{:S(2)}) %collective-permute-start.11) | collective-permute-done | bytes 81952 | tf_op jit(solution)/shard_map/ppermute | solution.py:350
  35.4 1.7 %later_block.9 = (bf16[128,320]{1,0:T(8,128)(2,1)}, bf16[2,8,2,1280]{3,2,1,0:T(2,128)(2,1)S(1)}) custom-call(bf16[128,320]{1,0:T(8,128)(2,1)S(1)} %collective-permute-done.11.before_ref, bf16[2,8,2,1280]{3,2,1,0:T(2,128)(2,1)S(1)} %get-tuple-element.38.out_in_ref, bf16[3,3,320,320]{3,2,1,0:T(8,128)(2,1)S(1)} %bitcast.18, ...), custom_call_target="tpu_custom_call", output_to_operand_aliasing={{1}: (1, {})} | custom-call | tf_op jit(solution)/shard_map/later_block/pallas_call | solution.py:434
  37.1 2.0 %collective-permute-done.8.refs_0_ = bf16[128,320]{1,0:T(8,128)(2,1)S(1)} collective-permute-done((bf16[128,320]{1,0:T(8,128)(2,1)S(1)}, bf16[128,320]{1,0:T(8,128)(2,1)S(1)}, u32[]{:S(2)}, u32[]{:S(2)}) %collective-permute-start.8) | collective-permute-done | bytes 81952 | tf_op jit(solution)/shard_map/ppermute | solution.py:350
  39.1 1.8 %last_block.1 = bf16[4,8,2,1280]{3,2,1,0:T(2,128)(2,1)} custom-call(bf16[128,320]{1,0:T(8,128)(2,1)S(1)} %collective-permute-done.8.refs_0_, bf16[2,8,2,1280]{3,2,1,0:T(2,128)(2,1)S(1)} %get-tuple-element.39.refs_1_, bf16[2,8,2,1280]{3,2,1,0:T(2,128)(2,1)S(1)} %get-tuple-element.40.refs_2_, bf16[3,3,320,320]{3,2,1,0:T(8,128)(2,1)S(1)} %bitcast.19, ...), custom_call_target="tpu_custom_call" | custom-call | tf_op jit(solution)/shard_map/last_block/pallas_call | solution.py:447
  (34 shorter events, 0.1 us)
Async XLA Ops:
  1.8 1.5 %collective-permute-start = (bf16[4,1,2,2,8,256]{5,4,3,2,1,0:T(8,128)(2,1)}, bf16[4,1,2,2,8,256]{5,4,3,2,1,0:T(8,128)(2,1)S(1)}, u32[]{:S(2)}, u32[]{:S(2)}) collective-permute-start(bf16[4,1,2,2,8,256]{5,4,3,2,1,0:T(8,128)(2,1)} %get-tuple-element.24), channel_id=1, source_target_pairs={{0,1},{1,0},{2,3},{3,2},{4,5},{5,4},{6,7},{7,6},{8,9},{9,8},{10,11... | collective-permute-start | bytes 196616 | tf_op jit(solution)/shard_map/ppermute | solution.py:332
  3.3 4.4 %collective-permute-start.3 = (bf16[2,1,2,2,8,256]{5,4,3,2,1,0:T(8,128)(2,1)S(1)}, bf16[2,1,2,2,8,256]{5,4,3,2,1,0:T(8,128)(2,1)S(1)}, u32[]{:S(2)}, u32[]{:S(2)}) collective-permute-start(bf16[2,1,2,2,8,256]{5,4,3,2,1,0:T(8,128)(2,1)S(1)} %pad_maximum_fusion.3), channel_id=1, source_target_pairs={{0,6},{1,7},{2,4},{3,5},{4,2},{5,3},{6,0},{7,1},{8,14},{9,15},{10,... | collective-permute-start | bytes 98312 | tf_op jit(solution)/shard_map/ppermute | solution.py:336
  3.8 6.0 %collective-permute-start.2 = (bf16[2,1,2,2,8,256]{5,4,3,2,1,0:T(8,128)(2,1)S(1)}, bf16[2,1,2,2,8,256]{5,4,3,2,1,0:T(8,128)(2,1)S(1)}, u32[]{:S(2)}, u32[]{:S(2)}) collective-permute-start(bf16[2,1,2,2,8,256]{5,4,3,2,1,0:T(8,128)(2,1)S(1)} %pad_maximum_fusion.2), channel_id=1, source_target_pairs={{0,4},{1,5},{2,6},{3,7},{4,0},{5,1},{6,2},{7,3},{8,12},{9,13},{10,... | collective-permute-start | bytes 98312 | tf_op jit(solution)/shard_map/ppermute | solution.py:336
  7.3 4.0 %copy-start.1 = (bf16[3,3,3,256,256]{4,3,2,1,0:T(8,128)(2,1)S(1)}, bf16[3,3,3,256,256]{4,3,2,1,0:T(8,128)(2,1)}, u32[]{:S(2)}) copy-start(bf16[3,3,3,256,256]{4,3,2,1,0:T(8,128)(2,1)} %refs_4_.3) | copy-start | bytes 10616836
  7.3 4.0 %copy-start.7 = (bf16[256,16]{0,1:T(8,128)(2,1)S(1)}, bf16[256,16]{0,1:T(8,128)(2,1)}, u32[]{:S(2)}) copy-start(bf16[256,16]{0,1:T(8,128)(2,1)} %param.21) | copy-start | bytes 24580
  7.3 4.0 %copy-start.8 = (f32[256]{0:T(256)S(1)}, f32[256]{0:T(256)}, u32[]{:S(2)}) copy-start(f32[256]{0:T(256)} %param.18) | copy-start | bytes 3076
  7.3 4.0 %copy-start.9 = (f32[256]{0:T(256)S(1)}, f32[256]{0:T(256)}, u32[]{:S(2)}) copy-start(f32[256]{0:T(256)} %param.19) | copy-start | bytes 3076
  7.3 4.0 %copy-start.10 = (f32[256]{0:T(256)S(1)}, f32[256]{0:T(256)}, u32[]{:S(2)}) copy-start(f32[256]{0:T(256)} %param.20) | copy-start | bytes 3076
  7.4 4.0 %copy-start.11 = (f32[16]{0:T(128)S(1)}, f32[16]{0:T(128)}, u32[]{:S(2)}) copy-start(f32[16]{0:T(128)} %param.22) | copy-start | bytes 196
  7.4 4.0 %collective-permute-start.1 = (bf16[2,1,2,2,8,256]{5,4,3,2,1,0:T(8,128)(2,1)S(1)}, bf16[2,1,2,2,8,256]{5,4,3,2,1,0:T(8,128)(2,1)S(1)}, u32[]{:S(2)}, u32[]{:S(2)}) collective-permute-start(bf16[2,1,2,2,8,256]{5,4,3,2,1,0:T(8,128)(2,1)S(1)} %pad_maximum_fusion.1), channel_id=1, source_target_pairs={{0,2},{1,3},{2,0},{3,1},{4,6},{5,7},{6,4},{7,5},{8,10},{9,11},{10,... | collective-permute-start | bytes 98312 | tf_op jit(solution)/shard_map/ppermute | solution.py:336
  7.6 10.2 %copy-start = (bf16[1,3,3,320,320]{4,3,2,1,0:T(8,128)(2,1)S(1)}, bf16[1,3,3,320,320]{4,3,2,1,0:T(8,128)(2,1)}, u32[]{:S(2)}) copy-start(bf16[1,3,3,320,320]{4,3,2,1,0:T(8,128)(2,1)} %param.30) | copy-start | bytes 5529604
  7.6 10.2 %copy-start.2 = (bf16[3,3,16,320]{3,2,1,0:T(8,128)(2,1)S(1)}, bf16[3,3,16,320]{3,2,1,0:T(8,128)(2,1)}, u32[]{:S(2)}) copy-start(bf16[3,3,16,320]{3,2,1,0:T(8,128)(2,1)} %param.25) | copy-start | bytes 276484
  7.6 10.2 %copy-start.3 = (f32[4,16,320]{2,1,0:T(8,128)S(1)}, f32[4,16,320]{2,1,0:T(8,128)}, u32[]{:S(2)}) copy-start(f32[4,16,320]{2,1,0:T(8,128)} %get-tuple-element.26.refs_1_.refs_2_) | copy-start | bytes 245764
  7.6 10.2 %copy-start.4 = (f32[1,320]{1,0:T(1,128)S(1)}, f32[1,320]{1,0:T(1,128)}, u32[]{:S(2)}) copy-start(f32[1,320]{1,0:T(1,128)} %refs_4_.5) | copy-start | bytes 3844
  7.6 10.2 %copy-start.5 = (f32[1,320]{1,0:T(1,128)S(1)}, f32[1,320]{1,0:T(1,128)}, u32[]{:S(2)}) copy-start(f32[1,320]{1,0:T(1,128)} %refs_5_.5) | copy-start | bytes 3844
  7.6 10.2 %copy-start.6 = (f32[1,320]{1,0:T(1,128)S(1)}, f32[1,320]{1,0:T(1,128)}, u32[]{:S(2)}) copy-start(f32[1,320]{1,0:T(1,128)} %refs_6_.5) | copy-start | bytes 3844
  13.4 3.8 %collective-permute-start.4 = (bf16[1,64,16]{2,1,0:T(8,128)(2,1)S(1)}, bf16[1,64,16]{2,1,0:T(8,128)(2,1)S(1)}, u32[]{:S(2)}, u32[]{:S(2)}) collective-permute-start(bf16[1,64,16]{2,1,0:T(8,128)(2,1)S(1)} %encode.1.refs_0_), channel_id=1, source_target_pairs={{0,8},{8,0},{16,24},{24,16},{1,9},{9,1},{17,25},{25,17},{2,10},{10... | collective-permute-start | bytes 6152 | tf_op jit(solution)/shard_map/ppermute | solution.py:364
  17.2 4.2 %collective-permute-start.5 = (bf16[2,64,16]{2,1,0:T(8,128)(2,1)S(1)}, bf16[2,64,16]{2,1,0:T(8,128)(2,1)S(1)}, u32[]{:S(2)}, u32[]{:S(2)}) collective-permute-start(bf16[2,64,16]{2,1,0:T(8,128)(2,1)S(1)} %pad_maximum_fusion.4), channel_id=1, source_target_pairs={{0,16},{8,24},{16,0},{24,8},{1,17},{9,25},{17,1},{25,9},{2,18},{10... | collective-permute-start | bytes 12296 | tf_op jit(solution)/shard_map/ppermute | solution.py:364
  17.8 4.7 %collective-permute-start.9 = (bf16[128,320]{1,0:T(8,128)(2,1)S(1)}, bf16[128,320]{1,0:T(8,128)(2,1)S(1)}, u32[]{:S(2)}, u32[]{:S(2)}) collective-permute-start(bf16[128,320]{1,0:T(8,128)(2,1)S(1)} %get-tuple-element.33), channel_id=1, source_target_pairs={{0,8},{8,24},{24,16},{16,0},{1,9},{9,25},{25,17},{17,1},{2,10},{10... | collective-permute-start | bytes 245768 | tf_op jit(solution)/shard_map/ppermute | solution.py:350
  21.4 5.7 %collective-permute-start.6 = (bf16[128,320]{1,0:T(8,128)(2,1)S(1)}, bf16[128,320]{1,0:T(8,128)(2,1)S(1)}, u32[]{:S(2)}, u32[]{:S(2)}) collective-permute-start(bf16[128,320]{1,0:T(8,128)(2,1)S(1)} %get-tuple-element.28), channel_id=1, source_target_pairs={{0,8},{8,24},{24,16},{16,0},{1,9},{9,25},{25,17},{17,1},{2,10},{10... | collective-permute-start | bytes 245768 | tf_op jit(solution)/shard_map/ppermute | solution.py:350
  22.5 6.4 %collective-permute-start.10 = (bf16[128,320]{1,0:T(8,128)(2,1)S(1)}, bf16[128,320]{1,0:T(8,128)(2,1)S(1)}, u32[]{:S(2)}, u32[]{:S(2)}) collective-permute-start(bf16[128,320]{1,0:T(8,128)(2,1)S(1)} %get-tuple-element.35), channel_id=1, source_target_pairs={{8,16},{16,0},{0,24},{24,8},{9,17},{17,1},{1,25},{25,9},{10,18},{1... | collective-permute-start | bytes 245768 | tf_op jit(solution)/shard_map/ppermute | solution.py:350
  27.1 5.5 %collective-permute-start.7 = (bf16[128,320]{1,0:T(8,128)(2,1)S(1)}, bf16[128,320]{1,0:T(8,128)(2,1)S(1)}, u32[]{:S(2)}, u32[]{:S(2)}) collective-permute-start(bf16[128,320]{1,0:T(8,128)(2,1)S(1)} %get-tuple-element.30), channel_id=1, source_target_pairs={{8,16},{16,0},{0,24},{24,8},{9,17},{17,1},{1,25},{25,9},{10,18},{1... | collective-permute-start | bytes 245768 | tf_op jit(solution)/shard_map/ppermute | solution.py:350
  28.9 6.5 %collective-permute-start.11 = (bf16[128,320]{1,0:T(8,128)(2,1)S(1)}, bf16[128,320]{1,0:T(8,128)(2,1)S(1)}, u32[]{:S(2)}, u32[]{:S(2)}) collective-permute-start(bf16[128,320]{1,0:T(8,128)(2,1)S(1)} %get-tuple-element.37), channel_id=1, source_target_pairs={{16,24},{17,25},{18,26},{19,27},{20,28},{21,29},{22,30},{23,31}} | collective-permute-start | bytes 245768 | tf_op jit(solution)/shard_map/ppermute | solution.py:350
  32.6 6.5 %collective-permute-start.8 = (bf16[128,320]{1,0:T(8,128)(2,1)S(1)}, bf16[128,320]{1,0:T(8,128)(2,1)S(1)}, u32[]{:S(2)}, u32[]{:S(2)}) collective-permute-start(bf16[128,320]{1,0:T(8,128)(2,1)S(1)} %get-tuple-element.32), channel_id=1, source_target_pairs={{16,24},{17,25},{18,26},{19,27},{20,28},{21,29},{22,30},{23,31}} | collective-permute-start | bytes 245768 | tf_op jit(solution)/shard_map/ppermute | solution.py:350

commit v4 on v3

--- a/solution.py
+++ b/solution.py
@@ -61,65 +61,64 @@
 
 
 def silu(value):
-    return value / (1.0 + jnp.exp(-value))
-
-
-def encode_kernel(
-    slab_axis, *refs
-):
+    return 0.5 * value * (1.0 + jnp.tanh(0.5 * value))
+
+
+def encode_kernel(slab_axis, *refs):
     (
         weight_ref, gain_ref, shift_ref, bias_ref, lat_weight_ref, lat_bias_ref, same_ref,
-        out_ref, dup_ref, act_ref, pool_ref, x_ref,
-    ) = refs[-12:]
-    slab_rows = refs[0].shape[2]
-    for step, piece_ref in enumerate(refs[:-12]):
+        out_ref, x_ref, pool_ref,
+    ) = refs[-10:]
+    pieces = refs[:-10]
+    slab_rows = pieces[0].shape[2]
+    items, frames, row_count, cols, channels = x_ref.shape
+    for step, piece_ref in enumerate(pieces[::-1]):
         for half in range(2):
             source = lax.axis_index(slab_axis) ^ (2 * step + half)
-            x_ref[:, pl.ds(source * slab_rows, slab_rows)] = piece_ref[half]
-    row_count, frames, cols, channels = x_ref.shape[1:]
-    plane = frames * cols
-    size = row_count * plane
+            for item in range(items):
+                for frame in range(frames):
+                    piece = piece_ref[half, item, :, frame].astype(F32)
+                    x_ref[item, frame, pl.ds(source * slab_rows, slab_rows)] = piece
+    size = frames * row_count * cols
+    plane = row_count * cols
     lat_rows, lat_cols = row_count // 2, cols // 2
-    same = same_ref[...]
-    for item in range(x_ref.shape[0]):
-        x = x_ref[item].astype(F32).reshape(size, channels)
+    for item in range(items):
+        x = x_ref[item].reshape(size, channels)
         sums = jnp.concatenate(
             [jnp.sum(x, axis=0, keepdims=True), jnp.sum(x * x, axis=0, keepdims=True)]
             + [jnp.zeros((6, channels), F32)],
             axis=0,
         )
-        sums = group_sums(sums, same) * (1.0 / (size * (channels // GROUPS)))
+        sums = group_sums(sums, same_ref[...]) * (1.0 / (size * (channels // GROUPS)))
         mean = sums[0:1]
         inverse = lax.rsqrt(sums[1:2] - mean * mean + EPS)
         act = silu((x - mean) * inverse * gain_ref[...] + shift_ref[...])
         column = lax.broadcasted_iota(jnp.int32, (size, 1), 0) & (cols - 1)
-        for tap in range(3):
-            if tap == 0:
-                moved = jnp.where(column == 0, 0.0, pltpu.roll(act, 1, 0))
-            elif tap == 2:
-                moved = jnp.where(column == cols - 1, 0.0, pltpu.roll(act, size - 1, 0))
-            else:
-                moved = act
-            lanes = pl.ds(tap * channels, channels)
-            first = moved.reshape(row_count, frames, cols, channels)[:, 0:1]
-            first = jnp.broadcast_to(first, (row_count, frames, cols, channels))
-            act_ref[pl.ds(plane, size), lanes] = moved.astype(BF16)
-            dup_ref[pl.ds(plane, size), lanes] = first.reshape(size, channels).astype(BF16)
-        for ref in (act_ref, dup_ref):
-            ref[pl.ds(0, plane), :] = jnp.zeros((plane, 3 * channels), BF16)
-            ref[pl.ds(plane + size, plane), :] = jnp.zeros((plane, 3 * channels), BF16)
-        total = x + bias_ref[...]
-        for time_tap in range(3):
-            source = act_ref if time_tap == 2 else dup_ref
-            for row_tap in range(3):
-                weight = weight_ref[time_tap, row_tap].reshape(3 * channels, channels)
-                window = source[pl.ds(row_tap * plane, size), :]
-                total += jnp.dot(window, weight, preferred_element_type=F32)
-        paired = total.reshape(lat_rows, 2, plane, channels)
-        merged = (paired[:, 0] + paired[:, 1]).reshape(lat_rows * plane, channels)
+        taps = [
+            jnp.where(column == 0, 0.0, pltpu.roll(act, 1, 0)),
+            act,
+            jnp.where(column == cols - 1, 0.0, pltpu.roll(act, size - 1, 0)),
+        ]
+        wide = jnp.concatenate(taps, axis=1).reshape(frames, row_count, cols, 3 * channels)
+        edge = jnp.zeros((frames, 1, cols, 3 * channels), F32)
+        wide = jnp.concatenate([edge, wide, edge], axis=1)
+        total, still = x + bias_ref[...], None
+        for row_tap in range(3):
+            window = wide[:, row_tap : row_tap + row_count].reshape(size, 3 * channels).astype(BF16)
+            weights = [weight_ref[time, row_tap].reshape(3 * channels, channels) for time in range(3)]
+            total += jnp.dot(window, weights[2], preferred_element_type=F32)
+            for weight in weights[:2]:
+                term = jnp.dot(window[:plane], weight, preferred_element_type=F32)
+                still = term if still is None else still + term
+        paired = total.reshape(frames, lat_rows, 2, cols, channels)
+        paired = paired + still.reshape(1, lat_rows, 2, cols, channels)
+        merged = paired[:, :, 0] + paired[:, :, 1]
         halves = []
         for part in range(channels // LANES):
-            pool_ref[part] = merged[:, part * LANES : (part + 1) * LANES]
+            for row in range(lat_rows):
+                for frame in range(frames):
+                    block = merged[frame, row, :, part * LANES : (part + 1) * LANES]
+                    pool_ref[part, pl.ds((row * frames + frame) * cols, cols), :] = block
             picked = []
             for col in range(lat_cols):
                 left = pool_ref[part, pl.ds(2 * col, lat_rows * frames, stride=cols), :]
@@ -134,23 +133,19 @@
 def encode(pieces, *operands):
     _, items, slab_rows, frames, cols, channels = pieces[0].shape
     row_count = 2 * len(pieces) * slab_rows
-    plane = frames * cols
     lat_rows, lat_cols = row_count // 2, cols // 2
-    padded = pltpu.VMEM(((row_count + 2) * plane, 3 * channels), BF16)
     return pl.pallas_call(
         functools.partial(encode_kernel, "slab"),
         out_shape=jax.ShapeDtypeStruct((items, lat_cols * lat_rows * frames, operands[-2].shape[1]), BF16),
         in_specs=[vmem()] * (len(pieces) + len(operands)),
         out_specs=vmem(),
         scratch_shapes=[
-            padded,
-            padded,
-            pltpu.VMEM((channels // LANES, lat_rows * plane, LANES), F32),
-            pltpu.VMEM((items, row_count, frames, cols, channels), BF16),
+            pltpu.VMEM((items, frames, row_count, cols, channels), F32),
+            pltpu.VMEM((channels // LANES, lat_rows * frames * cols, LANES), F32),
         ],
         compiler_params=params(),
         name="encode",
-    )(*pieces, *operands)
+    )(*pieces[::-1], *operands)
 
 
 def shifted(value, unit, frames):
@@ -163,21 +158,17 @@
     )
 
 
-def conv3(value, weight_ref, taps_ref, block, frames):
+def conv3(value, weight_ref, block, frames):
     streams, unit = block
-    size, channels = value.shape
     edge = streams * unit
-    zeros = jnp.zeros((edge, channels), BF16)
-    total = None
-    for row_tap, moved in enumerate(shifted(value, unit, frames)):
-        taps_ref[row_tap, pl.ds(edge, size), :] = moved.astype(BF16)
-        taps_ref[row_tap, pl.ds(0, edge), :] = zeros
-        taps_ref[row_tap, pl.ds(edge + size, edge), :] = zeros
-        for col_tap in range(3):
-            window = taps_ref[row_tap, pl.ds(col_tap * edge, size), :]
-            term = jnp.dot(window, weight_ref[row_tap, col_tap], preferred_element_type=F32)
-            total = term if total is None else total + term
-    return total
+    wide = jnp.concatenate(shifted(value, unit, frames), axis=1).astype(BF16)
+    terms = []
+    for col_tap, window in enumerate((wide[:-edge], wide, wide[edge:])):
+        weight = jnp.concatenate([weight_ref[row_tap, col_tap] for row_tap in range(3)], axis=0)
+        terms.append(jnp.dot(window, weight, preferred_element_type=F32))
+    left, total, right = terms
+    zeros = jnp.zeros((edge, total.shape[1]), F32)
+    return total + jnp.concatenate([zeros, left], axis=0) + jnp.concatenate([right, zeros], axis=0)
 
 
 def conv3_narrow(value, weight, block, frames):
@@ -194,7 +185,7 @@
     return jnp.dot(window, weight, preferred_element_type=F32)
 
 
-def unet_layer(state, operands, taps_ref, block, frames):
+def unet_layer(state, operands, block, frames):
     weight_ref, gain_ref, shift_ref, bias_ref, same_ref = operands
     streams, unit = block
     size, channels = state.shape
@@ -215,7 +206,7 @@
         scaled = (values[:, item : item + 1] - mean) * inverse * gain_ref[...]
         normed.append(scaled + shift_ref[...])
     act = silu(jnp.concatenate(normed, axis=1).reshape(size, channels))
-    total = conv3(act, weight_ref, taps_ref, block, frames)
+    total = conv3(act, weight_ref, block, frames)
     return (state + total + bias_ref[...]).astype(BF16)
 
 
@@ -245,8 +236,8 @@
 def first_kernel(block, frames, count, chunk, *refs):
     streams, unit = block
     latent_refs = refs[:count]
-    place_ref, in_weight_ref, *operands = refs[count:-3]
-    state_ref, out_ref, taps_ref = refs[-3:]
+    place_ref, in_weight_ref, *operands = refs[count:-1]
+    state_ref = refs[-1]
 
     @pl.when(lax.axis_index("section") == 0)
     def _():
@@ -262,45 +253,46 @@
         placed = placed.reshape(1, streams * unit, width)
         total = (total.reshape(cols, streams * unit, width) + placed).reshape(size, width)
         state = total.astype(BF16).astype(F32)
-        state = unet_layer(state, operands, taps_ref, block, frames)
-        state_ref[...] = state
-        write_output(out_ref, state, 0, block, frames)
-
-
-def later_kernel(
-    stage_index, block, frames, section_axis,
-    before_ref, out_in_ref, *refs
-):
-    del out_in_ref
-    *operands, state_ref, out_ref, taps_ref = refs
-
-    @pl.when(lax.axis_index(section_axis) == stage_index)
+        state_ref[...] = unet_layer(state, operands, block, frames)
+
+
+def later_kernel(index, block, frames, before_ref, kept_ref, *refs):
+    del kept_ref
+    *operands, state_ref = refs
+
+    @pl.when(lax.axis_index("section") == index)
     def _():
-        state = unet_layer(
-            before_ref[...].astype(F32), operands, taps_ref, block, frames
-        )
-        state_ref[...] = state
-        write_output(out_ref, state, 0, block, frames)
-
-
-def last_kernel(block, frames, section_axis, chunks, *refs):
+        state_ref[...] = unet_layer(before_ref[...].astype(F32), operands, block, frames)
+
+
+def last_kernel(block, frames, chunk, chunks, before_ref, *refs):
     streams = block[0]
-    before_ref = refs[0]
-    parts = refs[1 : 1 + chunks]
-    operands = refs[1 + chunks : -2]
-    out_ref, taps_ref = refs[-2:]
-    last = lax.axis_index(section_axis) == lax.axis_size(section_axis) - 1
-    for chunk in range(chunks - 1):
-        out_ref[pl.ds(chunk * streams, streams)] = parts[chunk][...]
+    kept = refs[:chunks] if chunk == 0 else []
+    operands = refs[chunks:-4] if chunk == 0 else refs[1:-4]
+    out_ref, wide_ref, store_sem, _ = refs[-4:]
+    last = lax.axis_index("section") == lax.axis_size("section") - 1
+
+    def store(part, sem):
+        rows = pl.ds(part * streams, streams)
+        return pltpu.make_async_copy(wide_ref.at[rows], out_ref.at[rows], sem)
 
     @pl.when(last)
     def _():
-        state = unet_layer(before_ref[...].astype(F32), operands, taps_ref, block, frames)
-        write_output(out_ref, state, (chunks - 1) * streams, block, frames)
-
-    @pl.when(jnp.logical_not(last))
-    def _():
-        out_ref[pl.ds((chunks - 1) * streams, streams)] = parts[chunks - 1][...]
+        state = unet_layer(before_ref[...].astype(F32), operands, block, frames)
+        write_output(wide_ref, state, chunk * streams, block, frames)
+        copy = store(chunk, store_sem)
+        copy.start()
+        copy.wait()
+
+    if chunk == 0:
+
+        @pl.when(jnp.logical_not(last))
+        def _():
+            for part in range(chunks):
+                write_output(wide_ref, kept[part][...], part * streams, block, frames)
+                copy = store(part, store_sem)
+                copy.start()
+                copy.wait()
 
 
 def select_kernel(
@@ -340,7 +332,7 @@
 CYCLES = {
     (0, 1): ((0, 1), (1, 3), (3, 2), (2, 0)),
     (1, 2): ((1, 2), (2, 0), (0, 3), (3, 1)),
-    (2, 3): ((2, 3),),
+    (2, 3): ((0, 1), (1, 0), (2, 3), (3, 2)),
 }
 
 
@@ -357,6 +349,8 @@
     count = lax.axis_size("section")
     if count & (count - 1):
         return [value] + [hop(value, other, 0) for other in range(1, count)]
+    if count == 4:
+        return [value] + [lax.ppermute(value, "section", [(s, s ^ k) for s in range(4)]) for k in (1, 2, 3)]
     parts = [value]
     step = 1
     while step < count:
@@ -402,59 +396,59 @@
     per_chunk = section_count // chunks
     streams = per_chunk * owned
     block = (streams, unit)
-    size = lat_cols * streams * unit
-    taps = pltpu.VMEM((3, size + 2 * streams * unit, width), BF16)
+    state_shape = jax.ShapeDtypeStruct((lat_cols * streams * unit, width), BF16)
     layer = [unet_weight[0], unet_gain, unet_shift, unet_bias, unet_same]
-    result_shapes = [
-        jax.ShapeDtypeStruct((size, width), BF16),
-        jax.ShapeDtypeStruct((streams, lat_rows, frames, lat_cols * width), BF16),
-    ]
+    states = [None] * chunks
     arrived = [None] * chunks
-    outs = [None] * chunks
     for chunk in range(chunks):
         mine = latents
         if chunks == 2:
-            mine = latents[-1:] if chunk else latents[:-1]
+            cut = len(latents) // 2 if section_count == 4 else -1
+            mine = latents[cut:] if chunk else latents[:cut]
         operands = mine + [place, in_weight.reshape(-1, width)] + layer
-        state, outs[chunk] = pl.pallas_call(
+        states[chunk] = pl.pallas_call(
             functools.partial(first_kernel, block, frames, len(mine), chunk),
-            out_shape=result_shapes,
+            out_shape=state_shape,
             in_specs=[vmem()] * len(operands),
-            out_specs=[vmem()] * 2,
-            scratch_shapes=[taps],
+            out_specs=vmem(),
             compiler_params=params(),
             name="first_block",
         )(*operands)
-        if section_count > 1:
-            arrived[chunk] = hop(state, 0, 1)
-    for index in range(1, section_count):
+        arrived[chunk] = hop(states[chunk], 0, 1)
+    for index in range(1, section_count - 1):
         for chunk in range(chunks):
-            if index == section_count - 1 and chunk == chunks - 1:
-                break
-            state, outs[chunk] = pl.pallas_call(
-                functools.partial(later_kernel, index, block, frames, "section"),
-                out_shape=result_shapes,
+            states[chunk] = pl.pallas_call(
+                functools.partial(later_kernel, index, block, frames),
+                out_shape=state_shape,
                 in_specs=[vmem()] * (2 + len(layer)),
-                out_specs=[vmem()] * 2,
-                scratch_shapes=[taps],
-                input_output_aliases={1: 1},
+                out_specs=vmem(),
+                input_output_aliases={1: 0},
                 compiler_params=params(),
                 name="later_block",
-            )(arrived[chunk], outs[chunk], *layer)
-            if index < section_count - 1:
-                arrived[chunk] = hop(state, index, index + 1)
-    operands = [arrived[-1]] + outs + layer
-    out = pl.pallas_call(
-        functools.partial(last_kernel, block, frames, "section", chunks),
-        out_shape=jax.ShapeDtypeStruct(
-            (section_count * owned, lat_rows, frames, lat_cols * width), BF16
-        ),
-        in_specs=[vmem()] * len(operands),
-        out_specs=vmem(),
-        scratch_shapes=[taps],
-        compiler_params=params(),
-        name="last_block",
-    )(*operands)
+            )(arrived[chunk], states[chunk], *layer)
+            arrived[chunk] = hop(states[chunk], index, index + 1)
+    hbm = pl.BlockSpec(memory_space=pltpu.HBM)
+    out_shape = jax.ShapeDtypeStruct((section_count * owned, lat_rows, frames, lat_cols * width), BF16)
+    out = None
+    for chunk in range(chunks):
+        operands = [arrived[chunk]] + (states if chunk == 0 else [out]) + layer
+        specs = [vmem()] * len(operands)
+        if chunk:
+            specs[1] = hbm
+        out = pl.pallas_call(
+            functools.partial(last_kernel, block, frames, chunk, chunks),
+            out_shape=out_shape,
+            in_specs=specs,
+            out_specs=hbm,
+            scratch_shapes=[
+                pltpu.VMEM(out_shape.shape, BF16),
+                pltpu.SemaphoreType.DMA,
+                pltpu.SemaphoreType.DMA,
+            ],
+            input_output_aliases={1: 0} if chunk else {},
+            compiler_params=params(),
+            name="last_block",
+        )(*operands)
     return out.reshape(1, section_count, owned, lat_rows, frames, lat_cols * width)
 
 

time: 41.2 us -> 37.3 us (0.905)
  the two profiles are of different devices: /device:TPU:22 before, /device:TPU:4 now
where the time goes in v4:
time: 37.3 us; the launch traced here: 36.9 us
  starting transfers between devices  17.7 us (47%)
  waiting for transfers between devices  11.6 us (31%)
  Pallas kernels  6.37 us (17%)
  local copies, waits for them, and re-layouts  0.86 us (2%)
    ppermute x6, starting transfers between devices, hop(): return lax.ppermute(value, 'section', list(CYCLES[source, target]))  9.69 us
    ppermute x6, waiting for transfers between devices, hop(): return lax.ppermute(value, 'section', list(CYCLES[source, target]))  6.35 us
    ppermute x3, starting transfers between devices, exchange(): pieces[step] = lax.ppermute(pieces[step], 'slab', pairs)  4.49 us
    ppermute x3, waiting for transfers between devices, exchange(): pieces[step] = lax.ppermute(pieces[step], 'slab', pairs)  3.7 us
    ppermute x3, starting transfers between devices, gather_first(): lax.ppermute(value, 'section', [(s, s ^ k) for s in range(4)])  3.55 us
    pallas_call x1, Pallas kernels, exchange(): pl.pallas_call(functools.partial(select_kernel, 'section', 'slab', owned)...  1.81 us
    pallas_call x4, Pallas kernels, per_device(): pl.pallas_call(functools.partial(later_kernel, index, block, frames), out...  1.75 us
    pallas_call x2, Pallas kernels, per_device(): pl.pallas_call(functools.partial(last_kernel, block, frames, chunk, chunk...  1.5 us
  transfers between devices with their start and end apart: 13, of which 9 were waited for; matrix products, arithmetic and copies ran while one was open for 2% of the time, Pallas kernels for 9%

profile of v4, /device:TPU:4, one launch (start us, length us, event | category | flops | bytes accessed | tf_op | source)
XLA Modules:
  0.0 36.9 jit_solution(15491931764961384460)
XLA Ops:
  0.0 1.8 %select.1 = (bf16[4,1,2,2,8,256]{5,4,3,2,1,0:T(8,128)(2,1)}, bf16[4,1,2,2,8,256]{5,4,3,2,1,0:T(8,128)(2,1)}, f32[4,16,320]{2,1,0:T(8,128)}) custom-call(s32[4,8]{1,0:T(4,128)} %clips_ref.1, s32[4,8]{1,0:T(4,128)} %offsets_ref.1, bf16[8,2,2,8,256]{4,3,2,1,0:T(8,128)(2,1)} %bitcast.27, bf16[320,128]{1,0:T(8,128)(2,1)} %bitcast.28, f32[320]{0:T(512)} %bias_ref.1), custom_call_target="tpu_custom_call" | custom-call | tf_op jit(solution)/shard_map/select/pallas_call | solution.py:317
  1.8 0.8 %fusion = (bf16[1,1,2,2,8,256]{5,4,3,2,1,0:T(8,128)(2,1)S(1)}, bf16[1,1,2,2,8,256]{5,4,3,2,1,0:T(8,128)(2,1)S(1)}, bf16[1,1,2,2,8,256]{5,4,3,2,1,0:T(8,128)(2,1)S(1)}, bf16[1,1,2,2,8,256]{5,4,3,2,1,0:T(8,128)(2,1)S(1)}) fusion(bf16[4,1,2,2,8,256]{5,4,3,2,1,0:T(8,128)(2,1)} %get-tuple-element.10), kind=kLoop, calls=%fused_computation.4 | loop fusion | bytes 131072 | tf_op jit(solution)/shard_map/slice | solution.py:325
  2.6 0.7 %collective-permute-done.after_ref = bf16[4,1,2,2,8,256]{5,4,3,2,1,0:T(8,128)(2,1)S(1)} collective-permute-done((bf16[4,1,2,2,8,256]{5,4,3,2,1,0:T(8,128)(2,1)}, bf16[4,1,2,2,8,256]{5,4,3,2,1,0:T(8,128)(2,1)S(1)}, u32[]{:S(2)}, u32[]{:S(2)}) %collective-permute-start) | collective-permute-done | bytes 65568 | tf_op jit(solution)/shard_map/ppermute | solution.py:324
  3.3 3.7 %collective-permute-start.1 = (bf16[2,1,2,2,8,256]{5,4,3,2,1,0:T(8,128)(2,1)S(1)}, bf16[2,1,2,2,8,256]{5,4,3,2,1,0:T(8,128)(2,1)S(1)}, u32[]{:S(2)}, u32[]{:S(2)}) collective-permute-start(bf16[2,1,2,2,8,256]{5,4,3,2,1,0:T(8,128)(2,1)S(1)} %pad_maximum_fusion), channel_id=1, source_target_pairs={{0,6},{1,7},{2,4},{3,5},{4,2},{5,3},{6,0},{7,1},{8,14},{9,15},{10,... | collective-permute-start | bytes 98312 | tf_op jit(solution)/shard_map/ppermute | solution.py:328
  7.0 0.0 copy-start.1
  7.0 0.0 copy-start.9
  7.0 0.0 copy-start.10
  7.1 0.8 %collective-permute-start.3 = (bf16[2,1,2,2,8,256]{5,4,3,2,1,0:T(8,128)(2,1)S(1)}, bf16[2,1,2,2,8,256]{5,4,3,2,1,0:T(8,128)(2,1)S(1)}, u32[]{:S(2)}, u32[]{:S(2)}) collective-permute-start(bf16[2,1,2,2,8,256]{5,4,3,2,1,0:T(8,128)(2,1)S(1)} %pad_maximum_fusion.2), channel_id=1, source_target_pairs={{0,2},{1,3},{2,0},{3,1},{4,6},{5,7},{6,4},{7,5},{8,10},{9,11},{10,... | collective-permute-start | bytes 98312 | tf_op jit(solution)/shard_map/ppermute | solution.py:328
  7.9 0.1 groups.1
  8.0 0.0 copy-start.3
  8.1 1.0 %collective-permute-done.1.refs_0_ = bf16[2,1,2,2,8,256]{5,4,3,2,1,0:T(8,128)(2,1)S(1)} collective-permute-done((bf16[2,1,2,2,8,256]{5,4,3,2,1,0:T(8,128)(2,1)S(1)}, bf16[2,1,2,2,8,256]{5,4,3,2,1,0:T(8,128)(2,1)S(1)}, u32[]{:S(2)}, u32[]{:S(2)}) %collective-permute-start.1) | collective-permute-done | bytes 32800 | tf_op jit(solution)/shard_map/ppermute | solution.py:328
  9.1 2.7 %collective-permute-done.2.refs_1_ = bf16[2,1,2,2,8,256]{5,4,3,2,1,0:T(8,128)(2,1)S(1)} collective-permute-done((bf16[2,1,2,2,8,256]{5,4,3,2,1,0:T(8,128)(2,1)S(1)}, bf16[2,1,2,2,8,256]{5,4,3,2,1,0:T(8,128)(2,1)S(1)}, u32[]{:S(2)}, u32[]{:S(2)}) %collective-permute-start.2) | collective-permute-done | bytes 32800 | tf_op jit(solution)/shard_map/ppermute | solution.py:328
  11.8 1.2 %encode.1.refs_0_ = bf16[1,64,16]{2,1,0:T(8,128)(2,1)S(1)} custom-call(bf16[2,1,2,2,8,256]{5,4,3,2,1,0:T(8,128)(2,1)S(1)} %collective-permute-done.1.refs_0_, bf16[2,1,2,2,8,256]{5,4,3,2,1,0:T(8,128)(2,1)S(1)} %collective-permute-done.2.refs_1_, bf16[2,1,2,2,8,256]{5,4,3,2,1,0:T(8,128)(2,1)S(1)} %collective-permute-done.3.refs_2_, ...), custom_call_target="tpu_custom_call" | custom-call | tf_op jit(solution)/shard_map/encode/pallas_call | solution.py:137
  13.0 1.6 %collective-permute-start.9 = (bf16[1,64,16]{2,1,0:T(8,128)(2,1)S(1)}, bf16[1,64,16]{2,1,0:T(8,128)(2,1)S(1)}, u32[]{:S(2)}, u32[]{:S(2)}) collective-permute-start(bf16[1,64,16]{2,1,0:T(8,128)(2,1)S(1)} %encode.1.refs_0_), channel_id=1, source_target_pairs={{0,8},{8,0},{16,24},{24,16},{1,9},{9,1},{17,25},{25,17},{2,10},{10... | collective-permute-start | bytes 6152 | tf_op jit(solution)/shard_map/ppermute | solution.py:353
  14.6 0.5 %collective-permute-start.5 = (bf16[1,64,16]{2,1,0:T(8,128)(2,1)S(1)}, bf16[1,64,16]{2,1,0:T(8,128)(2,1)S(1)}, u32[]{:S(2)}, u32[]{:S(2)}) collective-permute-start(bf16[1,64,16]{2,1,0:T(8,128)(2,1)S(1)} %encode.1.refs_0_), channel_id=1, source_target_pairs={{0,24},{8,16},{16,8},{24,0},{1,25},{9,17},{17,9},{25,1},{2,26},{10... | collective-permute-start | bytes 6152 | tf_op jit(solution)/shard_map/ppermute | solution.py:353
  15.1 1.5 %collective-permute-start.4 = (bf16[1,64,16]{2,1,0:T(8,128)(2,1)S(1)}, bf16[1,64,16]{2,1,0:T(8,128)(2,1)S(1)}, u32[]{:S(2)}, u32[]{:S(2)}) collective-permute-start(bf16[1,64,16]{2,1,0:T(8,128)(2,1)S(1)} %encode.1.refs_0_), channel_id=1, source_target_pairs={{0,16},{8,24},{16,0},{24,8},{1,17},{9,25},{17,1},{25,9},{2,18},{10... | collective-permute-start | bytes 6152 | tf_op jit(solution)/shard_map/ppermute | solution.py:353
  16.6 0.2 collective-permute-done.9.refs_1_
  16.9 1.7 %collective-permute-start.10 = (bf16[128,320]{1,0:T(8,128)(2,1)S(1)}, bf16[128,320]{1,0:T(8,128)(2,1)S(1)}, u32[]{:S(2)}, u32[]{:S(2)}) collective-permute-start(bf16[128,320]{1,0:T(8,128)(2,1)S(1)} %first_block.3.kept_ref), channel_id=1, source_target_pairs={{0,8},{8,24},{24,16},{16,0},{1,9},{9,25},{25,17},{17,1},{2,10},{10... | collective-permute-start | bytes 245768 | tf_op jit(solution)/shard_map/ppermute | solution.py:342
  18.6 0.6 %collective-permute-done.5.refs_1_ = bf16[1,64,16]{2,1,0:T(8,128)(2,1)S(1)} collective-permute-done((bf16[1,64,16]{2,1,0:T(8,128)(2,1)S(1)}, bf16[1,64,16]{2,1,0:T(8,128)(2,1)S(1)}, u32[]{:S(2)}, u32[]{:S(2)}) %collective-permute-start.5) | collective-permute-done | bytes 2080 | tf_op jit(solution)/shard_map/ppermute | solution.py:353
  19.2 2.4 %collective-permute-start.6 = (bf16[128,320]{1,0:T(8,128)(2,1)S(1)}, bf16[128,320]{1,0:T(8,128)(2,1)S(1)}, u32[]{:S(2)}, u32[]{:S(2)}) collective-permute-start(bf16[128,320]{1,0:T(8,128)(2,1)S(1)} %first_block.2.kept_ref), channel_id=1, source_target_pairs={{0,8},{8,24},{24,16},{16,0},{1,9},{9,25},{25,17},{17,1},{2,10},{10... | collective-permute-start | bytes 245768 | tf_op jit(solution)/shard_map/ppermute | solution.py:342
  21.7 0.0 collective-permute-done.10.before_ref
  21.7 2.5 %collective-permute-start.11 = (bf16[128,320]{1,0:T(8,128)(2,1)S(1)}, bf16[128,320]{1,0:T(8,128)(2,1)S(1)}, u32[]{:S(2)}, u32[]{:S(2)}) collective-permute-start(bf16[128,320]{1,0:T(8,128)(2,1)S(1)} %later_block.6.kept_ref), channel_id=1, source_target_pairs={{8,16},{16,0},{0,24},{24,8},{9,17},{17,1},{1,25},{25,9},{10,18},{1... | collective-permute-start | bytes 245768 | tf_op jit(solution)/shard_map/ppermute | solution.py:342
  24.2 2.5 %collective-permute-start.7 = (bf16[128,320]{1,0:T(8,128)(2,1)S(1)}, bf16[128,320]{1,0:T(8,128)(2,1)S(1)}, u32[]{:S(2)}, u32[]{:S(2)}) collective-permute-start(bf16[128,320]{1,0:T(8,128)(2,1)S(1)} %later_block.4.kept_ref), channel_id=1, source_target_pairs={{8,16},{16,0},{0,24},{24,8},{9,17},{17,1},{1,25},{25,9},{10,18},{1... | collective-permute-start | bytes 245768 | tf_op jit(solution)/shard_map/ppermute | solution.py:342
  26.7 1.2 %collective-permute-done.11.before_ref = bf16[128,320]{1,0:T(8,128)(2,1)S(1)} collective-permute-done((bf16[128,320]{1,0:T(8,128)(2,1)S(1)}, bf16[128,320]{1,0:T(8,128)(2,1)S(1)}, u32[]{:S(2)}, u32[]{:S(2)}) %collective-permute-start.11) | collective-permute-done | bytes 81952 | tf_op jit(solution)/shard_map/ppermute | solution.py:342
  27.9 0.9 %later_block.7.refs_0_ = bf16[128,320]{1,0:T(8,128)(2,1)S(1)} custom-call(bf16[128,320]{1,0:T(8,128)(2,1)S(1)} %collective-permute-done.11.before_ref, bf16[128,320]{1,0:T(8,128)(2,1)S(1)} %later_block.6.kept_ref, bf16[3,3,320,320]{3,2,1,0:T(8,128)(2,1)S(1)} %bitcast.16, f32[1,320]{1,0:T(1,128)S(1)} %copy-done.4, ...), custom_call_target="tpu_custom_call", output_to_operand_aliasing={{}: (1, {})} | custom-call | tf_op jit(solution)/shard_map/later_block/pallas_call | solution.py:420
  28.8 0.6 %collective-permute-start.12 = (bf16[128,320]{1,0:T(8,128)(2,1)S(1)}, bf16[128,320]{1,0:T(8,128)(2,1)S(1)}, u32[]{:S(2)}, u32[]{:S(2)}) collective-permute-start(bf16[128,320]{1,0:T(8,128)(2,1)S(1)} %later_block.7.refs_0_), channel_id=1, source_target_pairs={{0,8},{8,0},{16,24},{24,16},{1,9},{9,1},{17,25},{25,17},{2,10},{10... | collective-permute-start | bytes 245768 | tf_op jit(solution)/shard_map/ppermute | solution.py:342
  29.3 2.0 %collective-permute-done.7.before_ref = bf16[128,320]{1,0:T(8,128)(2,1)S(1)} collective-permute-done((bf16[128,320]{1,0:T(8,128)(2,1)S(1)}, bf16[128,320]{1,0:T(8,128)(2,1)S(1)}, u32[]{:S(2)}, u32[]{:S(2)}) %collective-permute-start.7) | collective-permute-done | bytes 81952 | tf_op jit(solution)/shard_map/ppermute | solution.py:342
  31.3 0.9 %later_block.5.refs_1_ = bf16[128,320]{1,0:T(8,128)(2,1)S(1)} custom-call(bf16[128,320]{1,0:T(8,128)(2,1)S(1)} %collective-permute-done.7.before_ref, bf16[128,320]{1,0:T(8,128)(2,1)S(1)} %later_block.4.kept_ref, bf16[3,3,320,320]{3,2,1,0:T(8,128)(2,1)S(1)} %bitcast.17, f32[1,320]{1,0:T(1,128)S(1)} %copy-done.4, ...), custom_call_target="tpu_custom_call", output_to_operand_aliasing={{}: (1, {})} | custom-call | tf_op jit(solution)/shard_map/later_block/pallas_call | solution.py:420
  32.2 0.1 collective-permute-start.8
  32.3 1.2 %collective-permute-done.12.before_ref = bf16[128,320]{1,0:T(8,128)(2,1)S(1)} collective-permute-done((bf16[128,320]{1,0:T(8,128)(2,1)S(1)}, bf16[128,320]{1,0:T(8,128)(2,1)S(1)}, u32[]{:S(2)}, u32[]{:S(2)}) %collective-permute-start.12) | collective-permute-done | bytes 81952 | tf_op jit(solution)/shard_map/ppermute | solution.py:342
  33.5 1.5 %last_block.2.refs_0_ = bf16[4,8,2,1280]{3,2,1,0:T(2,128)(2,1)} custom-call(bf16[128,320]{1,0:T(8,128)(2,1)S(1)} %collective-permute-done.12.before_ref, bf16[128,320]{1,0:T(8,128)(2,1)S(1)} %later_block.7.refs_0_, bf16[128,320]{1,0:T(8,128)(2,1)S(1)} %later_block.5.refs_1_, bf16[3,3,320,320]{3,2,1,0:T(8,128)(2,1)S(1)} %bitcast.18, f32[1,320]{1,0:T(1,128)S(1)} %copy-done.4, ...), custom_call_target="tpu_custom_call" | custom-call | tf_op jit(solution)/shard_map/last_block/pallas_call | solution.py:438
  34.9 1.9 %collective-permute-done.8.before_ref = bf16[128,320]{1,0:T(8,128)(2,1)S(1)} collective-permute-done((bf16[128,320]{1,0:T(8,128)(2,1)S(1)}, bf16[128,320]{1,0:T(8,128)(2,1)S(1)}, u32[]{:S(2)}, u32[]{:S(2)}) %collective-permute-start.8) | collective-permute-done | bytes 81952 | tf_op jit(solution)/shard_map/ppermute | solution.py:342
  (35 shorter events, 0.1 us)
Async XLA Ops:
  1.8 1.5 %collective-permute-start = (bf16[4,1,2,2,8,256]{5,4,3,2,1,0:T(8,128)(2,1)}, bf16[4,1,2,2,8,256]{5,4,3,2,1,0:T(8,128)(2,1)S(1)}, u32[]{:S(2)}, u32[]{:S(2)}) collective-permute-start(bf16[4,1,2,2,8,256]{5,4,3,2,1,0:T(8,128)(2,1)} %get-tuple-element.11), channel_id=1, source_target_pairs={{0,1},{1,0},{2,3},{3,2},{4,5},{5,4},{6,7},{7,6},{8,9},{9,8},{10,11... | collective-permute-start | bytes 196616 | tf_op jit(solution)/shard_map/ppermute | solution.py:324
  3.3 5.8 %collective-permute-start.1 = (bf16[2,1,2,2,8,256]{5,4,3,2,1,0:T(8,128)(2,1)S(1)}, bf16[2,1,2,2,8,256]{5,4,3,2,1,0:T(8,128)(2,1)S(1)}, u32[]{:S(2)}, u32[]{:S(2)}) collective-permute-start(bf16[2,1,2,2,8,256]{5,4,3,2,1,0:T(8,128)(2,1)S(1)} %pad_maximum_fusion), channel_id=1, source_target_pairs={{0,6},{1,7},{2,4},{3,5},{4,2},{5,3},{6,0},{7,1},{8,14},{9,15},{10,... | collective-permute-start | bytes 98312 | tf_op jit(solution)/shard_map/ppermute | solution.py:328
  7.0 4.8 %collective-permute-start.2 = (bf16[2,1,2,2,8,256]{5,4,3,2,1,0:T(8,128)(2,1)S(1)}, bf16[2,1,2,2,8,256]{5,4,3,2,1,0:T(8,128)(2,1)S(1)}, u32[]{:S(2)}, u32[]{:S(2)}) collective-permute-start(bf16[2,1,2,2,8,256]{5,4,3,2,1,0:T(8,128)(2,1)S(1)} %pad_maximum_fusion.1), channel_id=1, source_target_pairs={{0,4},{1,5},{2,6},{3,7},{4,0},{5,1},{6,2},{7,3},{8,12},{9,13},{10,... | collective-permute-start | bytes 98312 | tf_op jit(solution)/shard_map/ppermute | solution.py:328
  7.0 4.8 %copy-start.1 = (bf16[3,3,3,256,256]{4,3,2,1,0:T(8,128)(2,1)S(1)}, bf16[3,3,3,256,256]{4,3,2,1,0:T(8,128)(2,1)}, u32[]{:S(2)}) copy-start(bf16[3,3,3,256,256]{4,3,2,1,0:T(8,128)(2,1)} %refs_4_.3) | copy-start | bytes 10616836
  7.0 4.8 %copy-start.7 = (bf16[256,16]{0,1:T(8,128)(2,1)S(1)}, bf16[256,16]{0,1:T(8,128)(2,1)}, u32[]{:S(2)}) copy-start(bf16[256,16]{0,1:T(8,128)(2,1)} %param.21) | copy-start | bytes 24580
  7.0 4.8 %copy-start.8 = (f32[256]{0:T(256)S(1)}, f32[256]{0:T(256)}, u32[]{:S(2)}) copy-start(f32[256]{0:T(256)} %param.18) | copy-start | bytes 3076
  7.0 4.8 %copy-start.9 = (f32[256]{0:T(256)S(1)}, f32[256]{0:T(256)}, u32[]{:S(2)}) copy-start(f32[256]{0:T(256)} %param.19) | copy-start | bytes 3076
  7.0 4.8 %copy-start.10 = (f32[256]{0:T(256)S(1)}, f32[256]{0:T(256)}, u32[]{:S(2)}) copy-start(f32[256]{0:T(256)} %param.20) | copy-start | bytes 3076
  7.0 4.8 %copy-start.11 = (f32[16]{0:T(128)S(1)}, f32[16]{0:T(128)}, u32[]{:S(2)}) copy-start(f32[16]{0:T(128)} %param.22) | copy-start | bytes 196
  7.1 4.7 %collective-permute-start.3 = (bf16[2,1,2,2,8,256]{5,4,3,2,1,0:T(8,128)(2,1)S(1)}, bf16[2,1,2,2,8,256]{5,4,3,2,1,0:T(8,128)(2,1)S(1)}, u32[]{:S(2)}, u32[]{:S(2)}) collective-permute-start(bf16[2,1,2,2,8,256]{5,4,3,2,1,0:T(8,128)(2,1)S(1)} %pad_maximum_fusion.2), channel_id=1, source_target_pairs={{0,2},{1,3},{2,0},{3,1},{4,6},{5,7},{6,4},{7,5},{8,10},{9,11},{10,... | collective-permute-start | bytes 98312 | tf_op jit(solution)/shard_map/ppermute | solution.py:328
  8.0 8.8 %copy-start = (bf16[1,3,3,320,320]{4,3,2,1,0:T(8,128)(2,1)S(1)}, bf16[1,3,3,320,320]{4,3,2,1,0:T(8,128)(2,1)}, u32[]{:S(2)}) copy-start(bf16[1,3,3,320,320]{4,3,2,1,0:T(8,128)(2,1)} %param.30) | copy-start | bytes 5529604
  8.0 8.8 %copy-start.2 = (bf16[3,3,16,320]{3,2,1,0:T(8,128)(2,1)S(1)}, bf16[3,3,16,320]{3,2,1,0:T(8,128)(2,1)}, u32[]{:S(2)}) copy-start(bf16[3,3,16,320]{3,2,1,0:T(8,128)(2,1)} %param.25) | copy-start | bytes 276484
  8.0 8.8 %copy-start.3 = (f32[4,16,320]{2,1,0:T(8,128)S(1)}, f32[4,16,320]{2,1,0:T(8,128)}, u32[]{:S(2)}) copy-start(f32[4,16,320]{2,1,0:T(8,128)} %get-tuple-element.13.refs_2_) | copy-start | bytes 245764
  8.0 8.8 %copy-start.4 = (f32[1,320]{1,0:T(1,128)S(1)}, f32[1,320]{1,0:T(1,128)}, u32[]{:S(2)}) copy-start(f32[1,320]{1,0:T(1,128)} %refs_2_.9) | copy-start | bytes 3844
  8.0 8.8 %copy-start.5 = (f32[1,320]{1,0:T(1,128)S(1)}, f32[1,320]{1,0:T(1,128)}, u32[]{:S(2)}) copy-start(f32[1,320]{1,0:T(1,128)} %refs_3_.11) | copy-start | bytes 3844
  8.1 8.8 %copy-start.6 = (f32[1,320]{1,0:T(1,128)S(1)}, f32[1,320]{1,0:T(1,128)}, u32[]{:S(2)}) copy-start(f32[1,320]{1,0:T(1,128)} %refs_4_.5) | copy-start | bytes 3844
  13.0 3.8 %collective-permute-start.9 = (bf16[1,64,16]{2,1,0:T(8,128)(2,1)S(1)}, bf16[1,64,16]{2,1,0:T(8,128)(2,1)S(1)}, u32[]{:S(2)}, u32[]{:S(2)}) collective-permute-start(bf16[1,64,16]{2,1,0:T(8,128)(2,1)S(1)} %encode.1.refs_0_), channel_id=1, source_target_pairs={{0,8},{8,0},{16,24},{24,16},{1,9},{9,1},{17,25},{25,17},{2,10},{10... | collective-permute-start | bytes 6152 | tf_op jit(solution)/shard_map/ppermute | solution.py:353
  14.6 4.6 %collective-permute-start.5 = (bf16[1,64,16]{2,1,0:T(8,128)(2,1)S(1)}, bf16[1,64,16]{2,1,0:T(8,128)(2,1)S(1)}, u32[]{:S(2)}, u32[]{:S(2)}) collective-permute-start(bf16[1,64,16]{2,1,0:T(8,128)(2,1)S(1)} %encode.1.refs_0_), channel_id=1, source_target_pairs={{0,24},{8,16},{16,8},{24,0},{1,25},{9,17},{17,9},{25,1},{2,26},{10... | collective-permute-start | bytes 6152 | tf_op jit(solution)/shard_map/ppermute | solution.py:353
  15.1 4.2 %collective-permute-start.4 = (bf16[1,64,16]{2,1,0:T(8,128)(2,1)S(1)}, bf16[1,64,16]{2,1,0:T(8,128)(2,1)S(1)}, u32[]{:S(2)}, u32[]{:S(2)}) collective-permute-start(bf16[1,64,16]{2,1,0:T(8,128)(2,1)S(1)} %encode.1.refs_0_), channel_id=1, source_target_pairs={{0,16},{8,24},{16,0},{24,8},{1,17},{9,25},{17,1},{25,9},{2,18},{10... | collective-permute-start | bytes 6152 | tf_op jit(solution)/shard_map/ppermute | solution.py:353
  16.9 4.8 %collective-permute-start.10 = (bf16[128,320]{1,0:T(8,128)(2,1)S(1)}, bf16[128,320]{1,0:T(8,128)(2,1)S(1)}, u32[]{:S(2)}, u32[]{:S(2)}) collective-permute-start(bf16[128,320]{1,0:T(8,128)(2,1)S(1)} %first_block.3.kept_ref), channel_id=1, source_target_pairs={{0,8},{8,24},{24,16},{16,0},{1,9},{9,25},{25,17},{17,1},{2,10},{10... | collective-permute-start | bytes 245768 | tf_op jit(solution)/shard_map/ppermute | solution.py:342
  19.2 5.0 %collective-permute-start.6 = (bf16[128,320]{1,0:T(8,128)(2,1)S(1)}, bf16[128,320]{1,0:T(8,128)(2,1)S(1)}, u32[]{:S(2)}, u32[]{:S(2)}) collective-permute-start(bf16[128,320]{1,0:T(8,128)(2,1)S(1)} %first_block.2.kept_ref), channel_id=1, source_target_pairs={{0,8},{8,24},{24,16},{16,0},{1,9},{9,25},{25,17},{17,1},{2,10},{10... | collective-permute-start | bytes 245768 | tf_op jit(solution)/shard_map/ppermute | solution.py:342
  21.7 6.2 %collective-permute-start.11 = (bf16[128,320]{1,0:T(8,128)(2,1)S(1)}, bf16[128,320]{1,0:T(8,128)(2,1)S(1)}, u32[]{:S(2)}, u32[]{:S(2)}) collective-permute-start(bf16[128,320]{1,0:T(8,128)(2,1)S(1)} %later_block.6.kept_ref), channel_id=1, source_target_pairs={{8,16},{16,0},{0,24},{24,8},{9,17},{17,1},{1,25},{25,9},{10,18},{1... | collective-permute-start | bytes 245768 | tf_op jit(solution)/shard_map/ppermute | solution.py:342
  24.2 7.1 %collective-permute-start.7 = (bf16[128,320]{1,0:T(8,128)(2,1)S(1)}, bf16[128,320]{1,0:T(8,128)(2,1)S(1)}, u32[]{:S(2)}, u32[]{:S(2)}) collective-permute-start(bf16[128,320]{1,0:T(8,128)(2,1)S(1)} %later_block.4.kept_ref), channel_id=1, source_target_pairs={{8,16},{16,0},{0,24},{24,8},{9,17},{17,1},{1,25},{25,9},{10,18},{1... | collective-permute-start | bytes 245768 | tf_op jit(solution)/shard_map/ppermute | solution.py:342
  28.8 4.7 %collective-permute-start.12 = (bf16[128,320]{1,0:T(8,128)(2,1)S(1)}, bf16[128,320]{1,0:T(8,128)(2,1)S(1)}, u32[]{:S(2)}, u32[]{:S(2)}) collective-permute-start(bf16[128,320]{1,0:T(8,128)(2,1)S(1)} %later_block.7.refs_0_), channel_id=1, source_target_pairs={{0,8},{8,0},{16,24},{24,16},{1,9},{9,1},{17,25},{25,17},{2,10},{10... | collective-permute-start | bytes 245768 | tf_op jit(solution)/shard_map/ppermute | solution.py:342
  32.2 4.7 %collective-permute-start.8 = (bf16[128,320]{1,0:T(8,128)(2,1)S(1)}, bf16[128,320]{1,0:T(8,128)(2,1)S(1)}, u32[]{:S(2)}, u32[]{:S(2)}) collective-permute-start(bf16[128,320]{1,0:T(8,128)(2,1)S(1)} %later_block.5.refs_1_), channel_id=1, source_target_pairs={{0,8},{8,0},{16,24},{24,16},{1,9},{9,1},{17,25},{25,17},{2,10},{10... | collective-permute-start | bytes 245768 | tf_op jit(solution)/shard_map/ppermute | solution.py:342

commit v5 on v4

--- a/solution.py
+++ b/solution.py
@@ -267,8 +267,8 @@
 
 def last_kernel(block, frames, chunk, chunks, before_ref, *refs):
     streams = block[0]
-    kept = refs[:chunks] if chunk == 0 else []
-    operands = refs[chunks:-4] if chunk == 0 else refs[1:-4]
+    count = 2 * chunks if chunk == 0 else 1
+    kept, operands = refs[:count], refs[count:-4]
     out_ref, wide_ref, store_sem, _ = refs[-4:]
     last = lax.axis_index("section") == lax.axis_size("section") - 1
 
@@ -288,15 +288,17 @@
 
         @pl.when(jnp.logical_not(last))
         def _():
+            early = lax.axis_index("section") < 2
             for part in range(chunks):
-                write_output(wide_ref, kept[part][...], part * streams, block, frames)
+                state = jnp.where(early, kept[chunks + part][...].astype(F32), kept[part][...].astype(F32))
+                write_output(wide_ref, state, part * streams, block, frames)
                 copy = store(part, store_sem)
                 copy.start()
                 copy.wait()
 
 
 def select_kernel(
-    section_axis, slab_axis, owned,
+    section_axis, slab_axis, owned, crossed,
     clips_ref, offsets_ref, features_ref, table_ref, bias_ref, keep_ref, give_ref, place_ref,
 ):
     section = lax.axis_index(section_axis)
@@ -308,20 +310,21 @@
                 out_ref[step, item] = features_ref[clips_ref[section, slot]]
     bias = bias_ref[...].reshape(1, -1)
     frames = features_ref.shape[2]
-    place_rows(clips_ref, offsets_ref, table_ref[...], bias, place_ref, slab, owned, frames)
+    worker = slab ^ 1 if crossed else slab
+    place_rows(clips_ref, offsets_ref, table_ref[...], bias, place_ref, worker, owned, frames)
 
 
 def exchange(features, slot_clips, row_offsets, table, bias, place_shape, slab_count, owned):
     steps = slab_count // 2
     shape = jax.ShapeDtypeStruct((steps, owned) + features.shape[1:], BF16)
     keep, give, place = pl.pallas_call(
-        functools.partial(select_kernel, "section", "slab", owned),
+        functools.partial(select_kernel, "section", "slab", owned, crosses()),
         out_shape=[shape, shape, jax.ShapeDtypeStruct(place_shape, F32)],
         in_specs=[smem()] * 2 + [vmem()] * 3,
         out_specs=[vmem()] * 3,
         name="select",
     )(slot_clips, row_offsets, features, table, bias)
-    got = lax.ppermute(give, "slab", [(slab, slab ^ 1) for slab in range(slab_count)])
+    got = swap_cores(give)
     pieces = [jnp.stack([keep[step], got[step]]) for step in range(steps)]
     for step in range(1, steps):
         pairs = [(slab, slab ^ (2 * step)) for slab in range(slab_count)]
@@ -336,10 +339,26 @@
 }
 
 
+def crosses():
+    return lax.axis_size("section") == 4 and lax.axis_size("slab") % 2 == 0
+
+
+def send(value, pairs, cross):
+    if not cross:
+        return lax.ppermute(value, "section", pairs)
+    slabs = lax.axis_size("slab")
+    joint = [(s * slabs + slab, t * slabs + (slab ^ 1)) for s, t in pairs for slab in range(slabs)]
+    return lax.ppermute(value, ("section", "slab"), joint)
+
+
+def swap_cores(value):
+    return lax.ppermute(value, "slab", [(slab, slab ^ 1) for slab in range(lax.axis_size("slab"))])
+
+
 def hop(value, source, target):
     count = lax.axis_size("section")
     if count == 4 and (source, target) in CYCLES:
-        return lax.ppermute(value, "section", list(CYCLES[source, target]))
+        return send(value, CYCLES[source, target], crosses() and source == 1)
     if count & (count - 1):
         return lax.ppermute(value, "section", [(source, target)])
     return lax.ppermute(value, "section", [(s, s ^ source ^ target) for s in range(count)])
@@ -350,7 +369,8 @@
     if count & (count - 1):
         return [value] + [hop(value, other, 0) for other in range(1, count)]
     if count == 4:
-        return [value] + [lax.ppermute(value, "section", [(s, s ^ k) for s in range(4)]) for k in (1, 2, 3)]
+        own = swap_cores(value) if crosses() else value
+        return [own] + [send(value, [(s, s ^ k) for s in range(4)], crosses()) for k in (1, 2, 3)]
     parts = [value]
     step = 1
     while step < count:
@@ -430,8 +450,9 @@
     hbm = pl.BlockSpec(memory_space=pltpu.HBM)
     out_shape = jax.ShapeDtypeStruct((section_count * owned, lat_rows, frames, lat_cols * width), BF16)
     out = None
+    early = [swap_cores(state) if crosses() else state for state in states]
     for chunk in range(chunks):
-        operands = [arrived[chunk]] + (states if chunk == 0 else [out]) + layer
+        operands = [arrived[chunk]] + (states + early if chunk == 0 else [out]) + layer
         specs = [vmem()] * len(operands)
         if chunk:
             specs[1] = hbm

time: 37.3 us -> 37.2 us (level)
  the two profiles are of different devices: /device:TPU:4 before, /device:TPU:0 now
where the time goes in v5:
time: 37.2 us; the launch traced here: 36.9 us
  waiting for transfers between devices  16.6 us (45%)
  starting transfers between devices  12.3 us (33%)
  Pallas kernels  6.89 us (19%)
  local copies, waits for them, and re-layouts  0.85 us (2%)
    ppermute x4, waiting for transfers between devices, send(): return lax.ppermute(value, 'section', pairs)  7.17 us
    ppermute x3, starting transfers between devices, exchange(): pieces[step] = lax.ppermute(pieces[step], 'slab', pairs)  5.7 us
    ppermute x5, waiting for transfers between devices, send(): return lax.ppermute(value, ('section', 'slab'), joint)  5.22 us
    ppermute x3, waiting for transfers between devices, exchange(): pieces[step] = lax.ppermute(pieces[step], 'slab', pairs)  3.84 us
    ppermute x4, starting transfers between devices, send(): return lax.ppermute(value, 'section', pairs)  2.71 us
    pallas_call x2, Pallas kernels, per_device(): pl.pallas_call(functools.partial(first_kernel, block, frames, len(mine),...  2.27 us
    ppermute x5, starting transfers between devices, send(): return lax.ppermute(value, ('section', 'slab'), joint)  2.06 us
    pallas_call x1, Pallas kernels, exchange(): pl.pallas_call(functools.partial(select_kernel, 'section', 'slab', owned,...  1.81 us
  transfers between devices with their start and end apart: 16, of which 11 were waited for; matrix products, arithmetic and copies ran while one was open for 2% of the time, Pallas kernels for 10%

profile of v5, /device:TPU:0, one launch (start us, length us, event | category | flops | bytes accessed | tf_op | source)
XLA Modules:
  0.0 36.9 jit_solution(1346558015422059101)
XLA Ops:
  0.0 1.8 %select.1 = (bf16[4,1,2,2,8,256]{5,4,3,2,1,0:T(8,128)(2,1)}, bf16[4,1,2,2,8,256]{5,4,3,2,1,0:T(8,128)(2,1)}, f32[4,16,320]{2,1,0:T(8,128)}) custom-call(s32[4,8]{1,0:T(4,128)} %clips_ref.1, s32[4,8]{1,0:T(4,128)} %offsets_ref.1, bf16[8,2,2,8,256]{4,3,2,1,0:T(8,128)(2,1)} %bitcast.27, bf16[320,128]{1,0:T(8,128)(2,1)} %bitcast.28, f32[320]{0:T(512)} %bias_ref.1), custom_call_target="tpu_custom_call" | custom-call | tf_op jit(solution)/shard_map/select/pallas_call | solution.py:320
  1.8 0.5 %collective-permute-start = (bf16[4,1,2,2,8,256]{5,4,3,2,1,0:T(8,128)(2,1)}, bf16[4,1,2,2,8,256]{5,4,3,2,1,0:T(8,128)(2,1)S(1)}, u32[]{:S(2)}, u32[]{:S(2)}) collective-permute-start(bf16[4,1,2,2,8,256]{5,4,3,2,1,0:T(8,128)(2,1)} %get-tuple-element.11), channel_id=1, source_target_pairs={{0,1},{1,0},{2,3},{3,2},{4,5},{5,4},{6,7},{7,6},{8,9},{9,8},{10,11... | collective-permute-start | bytes 196616 | tf_op jit(solution)/shard_map/ppermute | solution.py:355
  2.3 0.8 %fusion = (bf16[1,1,2,2,8,256]{5,4,3,2,1,0:T(8,128)(2,1)S(1)}, bf16[1,1,2,2,8,256]{5,4,3,2,1,0:T(8,128)(2,1)S(1)}, bf16[1,1,2,2,8,256]{5,4,3,2,1,0:T(8,128)(2,1)S(1)}, bf16[1,1,2,2,8,256]{5,4,3,2,1,0:T(8,128)(2,1)S(1)}) fusion(bf16[4,1,2,2,8,256]{5,4,3,2,1,0:T(8,128)(2,1)} %get-tuple-element.10), kind=kLoop, calls=%fused_computation.4 | loop fusion | bytes 131072 | tf_op jit(solution)/shard_map/slice | solution.py:328
  3.0 0.3 collective-permute-done.after_ref
  3.4 5.0 %collective-permute-start.1 = (bf16[2,1,2,2,8,256]{5,4,3,2,1,0:T(8,128)(2,1)S(1)}, bf16[2,1,2,2,8,256]{5,4,3,2,1,0:T(8,128)(2,1)S(1)}, u32[]{:S(2)}, u32[]{:S(2)}) collective-permute-start(bf16[2,1,2,2,8,256]{5,4,3,2,1,0:T(8,128)(2,1)S(1)} %pad_maximum_fusion), channel_id=1, source_target_pairs={{0,6},{1,7},{2,4},{3,5},{4,2},{5,3},{6,0},{7,1},{8,14},{9,15},{10,... | collective-permute-start | bytes 98312 | tf_op jit(solution)/shard_map/ppermute | solution.py:331
  8.4 0.0 copy-start.1
  8.4 0.0 copy-start.7
  8.5 0.7 %collective-permute-start.3 = (bf16[2,1,2,2,8,256]{5,4,3,2,1,0:T(8,128)(2,1)S(1)}, bf16[2,1,2,2,8,256]{5,4,3,2,1,0:T(8,128)(2,1)S(1)}, u32[]{:S(2)}, u32[]{:S(2)}) collective-permute-start(bf16[2,1,2,2,8,256]{5,4,3,2,1,0:T(8,128)(2,1)S(1)} %pad_maximum_fusion.2), channel_id=1, source_target_pairs={{0,2},{1,3},{2,0},{3,1},{4,6},{5,7},{6,4},{7,5},{8,10},{9,11},{10,... | collective-permute-start | bytes 98312 | tf_op jit(solution)/shard_map/ppermute | solution.py:331
  9.2 0.1 groups.1
  9.4 1.0 %collective-permute-done.1.refs_0_ = bf16[2,1,2,2,8,256]{5,4,3,2,1,0:T(8,128)(2,1)S(1)} collective-permute-done((bf16[2,1,2,2,8,256]{5,4,3,2,1,0:T(8,128)(2,1)S(1)}, bf16[2,1,2,2,8,256]{5,4,3,2,1,0:T(8,128)(2,1)S(1)}, u32[]{:S(2)}, u32[]{:S(2)}) %collective-permute-start.1) | collective-permute-done | bytes 32800 | tf_op jit(solution)/shard_map/ppermute | solution.py:331
  10.3 2.9 %collective-permute-done.2.refs_1_ = bf16[2,1,2,2,8,256]{5,4,3,2,1,0:T(8,128)(2,1)S(1)} collective-permute-done((bf16[2,1,2,2,8,256]{5,4,3,2,1,0:T(8,128)(2,1)S(1)}, bf16[2,1,2,2,8,256]{5,4,3,2,1,0:T(8,128)(2,1)S(1)}, u32[]{:S(2)}, u32[]{:S(2)}) %collective-permute-start.2) | collective-permute-done | bytes 32800 | tf_op jit(solution)/shard_map/ppermute | solution.py:331
  13.3 1.2 %encode.1 = bf16[1,64,16]{2,1,0:T(8,128)(2,1)S(1)} custom-call(bf16[2,1,2,2,8,256]{5,4,3,2,1,0:T(8,128)(2,1)S(1)} %collective-permute-done.1.refs_0_, bf16[2,1,2,2,8,256]{5,4,3,2,1,0:T(8,128)(2,1)S(1)} %collective-permute-done.2.refs_1_, bf16[2,1,2,2,8,256]{5,4,3,2,1,0:T(8,128)(2,1)S(1)} %collective-permute-done.3.refs_2_, ...), custom_call_target="tpu_custom_call" | custom-call | tf_op jit(solution)/shard_map/encode/pallas_call | solution.py:137
  14.5 0.3 collective-permute-start.10
  14.8 1.3 %collective-permute-start.9 = (bf16[1,64,16]{2,1,0:T(8,128)(2,1)S(1)}, bf16[1,64,16]{2,1,0:T(8,128)(2,1)S(1)}, u32[]{:S(2)}, u32[]{:S(2)}) collective-permute-start(bf16[1,64,16]{2,1,0:T(8,128)(2,1)S(1)} %encode.1), channel_id=1, source_target_pairs={{0,1},{1,0},{2,3},{3,2},{4,5},{5,4},{6,7},{7,6},{8,9},{9,8},{10,11... | collective-permute-start | bytes 6152 | tf_op jit(solution)/shard_map/ppermute | solution.py:355
  16.2 1.1 %collective-permute-start.5 = (bf16[1,64,16]{2,1,0:T(8,128)(2,1)S(1)}, bf16[1,64,16]{2,1,0:T(8,128)(2,1)S(1)}, u32[]{:S(2)}, u32[]{:S(2)}) collective-permute-start(bf16[1,64,16]{2,1,0:T(8,128)(2,1)S(1)} %encode.1), channel_id=1, source_target_pairs={{0,25},{1,24},{2,27},{3,26},{4,29},{5,28},{6,31},{7,30},{8,17},{9,... | collective-permute-start | bytes 6152 | tf_op jit(solution)/shard_map/ppermute | solution.py:351
  17.2 0.6 %collective-permute-start.4 = (bf16[1,64,16]{2,1,0:T(8,128)(2,1)S(1)}, bf16[1,64,16]{2,1,0:T(8,128)(2,1)S(1)}, u32[]{:S(2)}, u32[]{:S(2)}) collective-permute-start(bf16[1,64,16]{2,1,0:T(8,128)(2,1)S(1)} %encode.1), channel_id=1, source_target_pairs={{0,17},{1,16},{2,19},{3,18},{4,21},{5,20},{6,23},{7,22},{8,25},{9,... | collective-permute-start | bytes 6152 | tf_op jit(solution)/shard_map/ppermute | solution.py:351
  17.9 1.1 %first_block.3.kept_ref = bf16[128,320]{1,0:T(8,128)(2,1)S(1)} custom-call(bf16[1,64,16]{2,1,0:T(8,128)(2,1)S(1)} %collective-permute-done.9.refs_0_, bf16[1,64,16]{2,1,0:T(8,128)(2,1)S(1)} %collective-permute-done.10.refs_1_, f32[4,16,320]{2,1,0:T(8,128)S(1)} %copy-done.3, bf16[144,320]{1,0:T(8,128)(2,1)S(1)} %bitcast.20, ...), custom_call_target="tpu_custom_call" | custom-call | tf_op jit(solution)/shard_map/first_block/pallas_call | solution.py:429
  19.1 0.4 %collective-permute-start.11 = (bf16[128,320]{1,0:T(8,128)(2,1)S(1)}, bf16[128,320]{1,0:T(8,128)(2,1)S(1)}, u32[]{:S(2)}, u32[]{:S(2)}) collective-permute-start(bf16[128,320]{1,0:T(8,128)(2,1)S(1)} %first_block.3.kept_ref), channel_id=1, source_target_pairs={{0,8},{8,24},{24,16},{16,0},{1,9},{9,25},{25,17},{17,1},{2,10},{10... | collective-permute-start | bytes 245768 | tf_op jit(solution)/shard_map/ppermute | solution.py:348
  19.5 0.7 %collective-permute-done.5.refs_1_ = bf16[1,64,16]{2,1,0:T(8,128)(2,1)S(1)} collective-permute-done((bf16[1,64,16]{2,1,0:T(8,128)(2,1)S(1)}, bf16[1,64,16]{2,1,0:T(8,128)(2,1)S(1)}, u32[]{:S(2)}, u32[]{:S(2)}) %collective-permute-start.5) | collective-permute-done | bytes 2080 | tf_op jit(solution)/shard_map/ppermute | solution.py:351
  20.2 0.4 collective-permute-done.4.refs_0_
  20.6 1.1 %first_block.2.kept_ref = bf16[128,320]{1,0:T(8,128)(2,1)S(1)} custom-call(bf16[1,64,16]{2,1,0:T(8,128)(2,1)S(1)} %collective-permute-done.4.refs_0_, bf16[1,64,16]{2,1,0:T(8,128)(2,1)S(1)} %collective-permute-done.5.refs_1_, f32[4,16,320]{2,1,0:T(8,128)S(1)} %copy-done.3, bf16[144,320]{1,0:T(8,128)(2,1)S(1)} %bitcast.21, ...), custom_call_target="tpu_custom_call" | custom-call | tf_op jit(solution)/shard_map/first_block/pallas_call | solution.py:429
  21.7 0.2 collective-permute-start.6
  21.9 2.0 %collective-permute-done.11.before_ref = bf16[128,320]{1,0:T(8,128)(2,1)S(1)} collective-permute-done((bf16[128,320]{1,0:T(8,128)(2,1)S(1)}, bf16[128,320]{1,0:T(8,128)(2,1)S(1)}, u32[]{:S(2)}, u32[]{:S(2)}) %collective-permute-start.11) | collective-permute-done | bytes 81952 | tf_op jit(solution)/shard_map/ppermute | solution.py:348
  23.9 0.0 collective-permute-start.12
  23.9 2.9 %collective-permute-done.6.before_ref = bf16[128,320]{1,0:T(8,128)(2,1)S(1)} collective-permute-done((bf16[128,320]{1,0:T(8,128)(2,1)S(1)}, bf16[128,320]{1,0:T(8,128)(2,1)S(1)}, u32[]{:S(2)}, u32[]{:S(2)}) %collective-permute-start.6) | collective-permute-done | bytes 81952 | tf_op jit(solution)/shard_map/ppermute | solution.py:348
  26.8 2.1 %collective-permute-done.12.before_ref = bf16[128,320]{1,0:T(8,128)(2,1)S(1)} collective-permute-done((bf16[128,320]{1,0:T(8,128)(2,1)S(1)}, bf16[128,320]{1,0:T(8,128)(2,1)S(1)}, u32[]{:S(2)}, u32[]{:S(2)}) %collective-permute-start.12) | collective-permute-done | bytes 81952 | tf_op jit(solution)/shard_map/ppermute | solution.py:351
  28.9 0.7 %collective-permute-start.13 = (bf16[128,320]{1,0:T(8,128)(2,1)S(1)}, bf16[128,320]{1,0:T(8,128)(2,1)S(1)}, u32[]{:S(2)}, u32[]{:S(2)}) collective-permute-start(bf16[128,320]{1,0:T(8,128)(2,1)S(1)} %later_block.7.refs_0_), channel_id=1, source_target_pairs={{0,8},{8,0},{16,24},{24,16},{1,9},{9,1},{17,25},{25,17},{2,10},{10... | collective-permute-start | bytes 245768 | tf_op jit(solution)/shard_map/ppermute | solution.py:348
  29.6 2.0 %collective-permute-done.7.before_ref = bf16[128,320]{1,0:T(8,128)(2,1)S(1)} collective-permute-done((bf16[128,320]{1,0:T(8,128)(2,1)S(1)}, bf16[128,320]{1,0:T(8,128)(2,1)S(1)}, u32[]{:S(2)}, u32[]{:S(2)}) %collective-permute-start.7) | collective-permute-done | bytes 81952 | tf_op jit(solution)/shard_map/ppermute | solution.py:351
  31.6 1.4 %collective-permute-start.8 = (bf16[128,320]{1,0:T(8,128)(2,1)S(1)}, bf16[128,320]{1,0:T(8,128)(2,1)S(1)}, u32[]{:S(2)}, u32[]{:S(2)}) collective-permute-start(bf16[128,320]{1,0:T(8,128)(2,1)S(1)} %later_block.5.refs_1_), channel_id=1, source_target_pairs={{0,8},{8,0},{16,24},{24,16},{1,9},{9,1},{17,25},{25,17},{2,10},{10... | collective-permute-start | bytes 245768 | tf_op jit(solution)/shard_map/ppermute | solution.py:348
  33.1 1.1 %collective-permute-done.13.before_ref = bf16[128,320]{1,0:T(8,128)(2,1)S(1)} collective-permute-done((bf16[128,320]{1,0:T(8,128)(2,1)S(1)}, bf16[128,320]{1,0:T(8,128)(2,1)S(1)}, u32[]{:S(2)}, u32[]{:S(2)}) %collective-permute-start.13) | collective-permute-done | bytes 81952 | tf_op jit(solution)/shard_map/ppermute | solution.py:348
  34.1 1.5 %last_block.2.refs_0_ = bf16[4,8,2,1280]{3,2,1,0:T(2,128)(2,1)} custom-call(bf16[128,320]{1,0:T(8,128)(2,1)S(1)} %collective-permute-done.13.before_ref, bf16[128,320]{1,0:T(8,128)(2,1)S(1)} %later_block.7.refs_0_, bf16[128,320]{1,0:T(8,128)(2,1)S(1)} %later_block.5.refs_1_, bf16[128,320]{1,0:T(8,128)(2,1)S(1)} %collective-permute-done.14.refs_2_, ...), custom_call_target="tpu_custom_call" | custom-call | tf_op jit(solution)/shard_map/last_block/pallas_call | solution.py:459
  35.6 1.2 %collective-permute-done.8.before_ref = bf16[128,320]{1,0:T(8,128)(2,1)S(1)} collective-permute-done((bf16[128,320]{1,0:T(8,128)(2,1)S(1)}, bf16[128,320]{1,0:T(8,128)(2,1)S(1)}, u32[]{:S(2)}, u32[]{:S(2)}) %collective-permute-start.8) | collective-permute-done | bytes 81952 | tf_op jit(solution)/shard_map/ppermute | solution.py:348
  (41 shorter events, 0.1 us)
Async XLA Ops:
  1.8 1.6 %collective-permute-start = (bf16[4,1,2,2,8,256]{5,4,3,2,1,0:T(8,128)(2,1)}, bf16[4,1,2,2,8,256]{5,4,3,2,1,0:T(8,128)(2,1)S(1)}, u32[]{:S(2)}, u32[]{:S(2)}) collective-permute-start(bf16[4,1,2,2,8,256]{5,4,3,2,1,0:T(8,128)(2,1)} %get-tuple-element.11), channel_id=1, source_target_pairs={{0,1},{1,0},{2,3},{3,2},{4,5},{5,4},{6,7},{7,6},{8,9},{9,8},{10,11... | collective-permute-start | bytes 196616 | tf_op jit(solution)/shard_map/ppermute | solution.py:355
  3.4 6.9 %collective-permute-start.1 = (bf16[2,1,2,2,8,256]{5,4,3,2,1,0:T(8,128)(2,1)S(1)}, bf16[2,1,2,2,8,256]{5,4,3,2,1,0:T(8,128)(2,1)S(1)}, u32[]{:S(2)}, u32[]{:S(2)}) collective-permute-start(bf16[2,1,2,2,8,256]{5,4,3,2,1,0:T(8,128)(2,1)S(1)} %pad_maximum_fusion), channel_id=1, source_target_pairs={{0,6},{1,7},{2,4},{3,5},{4,2},{5,3},{6,0},{7,1},{8,14},{9,15},{10,... | collective-permute-start | bytes 98312 | tf_op jit(solution)/shard_map/ppermute | solution.py:331
  8.4 4.8 %collective-permute-start.2 = (bf16[2,1,2,2,8,256]{5,4,3,2,1,0:T(8,128)(2,1)S(1)}, bf16[2,1,2,2,8,256]{5,4,3,2,1,0:T(8,128)(2,1)S(1)}, u32[]{:S(2)}, u32[]{:S(2)}) collective-permute-start(bf16[2,1,2,2,8,256]{5,4,3,2,1,0:T(8,128)(2,1)S(1)} %pad_maximum_fusion.1), channel_id=1, source_target_pairs={{0,4},{1,5},{2,6},{3,7},{4,0},{5,1},{6,2},{7,3},{8,12},{9,13},{10,... | collective-permute-start | bytes 98312 | tf_op jit(solution)/shard_map/ppermute | solution.py:331
  8.4 4.8 %copy-start.1 = (bf16[3,3,3,256,256]{4,3,2,1,0:T(8,128)(2,1)S(1)}, bf16[3,3,3,256,256]{4,3,2,1,0:T(8,128)(2,1)}, u32[]{:S(2)}) copy-start(bf16[3,3,3,256,256]{4,3,2,1,0:T(8,128)(2,1)} %refs_4_.2) | copy-start | bytes 10616836
  8.4 4.8 %copy-start.7 = (bf16[256,16]{0,1:T(8,128)(2,1)S(1)}, bf16[256,16]{0,1:T(8,128)(2,1)}, u32[]{:S(2)}) copy-start(bf16[256,16]{0,1:T(8,128)(2,1)} %param.21) | copy-start | bytes 24580
  8.5 4.8 %copy-start.8 = (f32[256]{0:T(256)S(1)}, f32[256]{0:T(256)}, u32[]{:S(2)}) copy-start(f32[256]{0:T(256)} %param.18) | copy-start | bytes 3076
  8.5 4.8 %copy-start.9 = (f32[256]{0:T(256)S(1)}, f32[256]{0:T(256)}, u32[]{:S(2)}) copy-start(f32[256]{0:T(256)} %param.19) | copy-start | bytes 3076
  8.5 4.8 %copy-start.10 = (f32[256]{0:T(256)S(1)}, f32[256]{0:T(256)}, u32[]{:S(2)}) copy-start(f32[256]{0:T(256)} %param.20) | copy-start | bytes 3076
  8.5 4.8 %copy-start.11 = (f32[16]{0:T(128)S(1)}, f32[16]{0:T(128)}, u32[]{:S(2)}) copy-start(f32[16]{0:T(128)} %param.22) | copy-start | bytes 196
  8.5 4.7 %collective-permute-start.3 = (bf16[2,1,2,2,8,256]{5,4,3,2,1,0:T(8,128)(2,1)S(1)}, bf16[2,1,2,2,8,256]{5,4,3,2,1,0:T(8,128)(2,1)S(1)}, u32[]{:S(2)}, u32[]{:S(2)}) collective-permute-start(bf16[2,1,2,2,8,256]{5,4,3,2,1,0:T(8,128)(2,1)S(1)} %pad_maximum_fusion.2), channel_id=1, source_target_pairs={{0,2},{1,3},{2,0},{3,1},{4,6},{5,7},{6,4},{7,5},{8,10},{9,11},{10,... | collective-permute-start | bytes 98312 | tf_op jit(solution)/shard_map/ppermute | solution.py:331
  9.3 8.6 %copy-start = (bf16[1,3,3,320,320]{4,3,2,1,0:T(8,128)(2,1)S(1)}, bf16[1,3,3,320,320]{4,3,2,1,0:T(8,128)(2,1)}, u32[]{:S(2)}) copy-start(bf16[1,3,3,320,320]{4,3,2,1,0:T(8,128)(2,1)} %param.30) | copy-start | bytes 5529604
  9.3 8.6 %copy-start.2 = (bf16[3,3,16,320]{3,2,1,0:T(8,128)(2,1)S(1)}, bf16[3,3,16,320]{3,2,1,0:T(8,128)(2,1)}, u32[]{:S(2)}) copy-start(bf16[3,3,16,320]{3,2,1,0:T(8,128)(2,1)} %param.25) | copy-start | bytes 276484
  9.3 8.6 %copy-start.3 = (f32[4,16,320]{2,1,0:T(8,128)S(1)}, f32[4,16,320]{2,1,0:T(8,128)}, u32[]{:S(2)}) copy-start(f32[4,16,320]{2,1,0:T(8,128)} %get-tuple-element.13.refs_2_) | copy-start | bytes 245764
  9.3 8.6 %copy-start.4 = (f32[1,320]{1,0:T(1,128)S(1)}, f32[1,320]{1,0:T(1,128)}, u32[]{:S(2)}) copy-start(f32[1,320]{1,0:T(1,128)} %refs_2_.9) | copy-start | bytes 3844
  9.4 8.6 %copy-start.5 = (f32[1,320]{1,0:T(1,128)S(1)}, f32[1,320]{1,0:T(1,128)}, u32[]{:S(2)}) copy-start(f32[1,320]{1,0:T(1,128)} %refs_3_.9) | copy-start | bytes 3844
  9.4 8.6 %copy-start.6 = (f32[1,320]{1,0:T(1,128)S(1)}, f32[1,320]{1,0:T(1,128)}, u32[]{:S(2)}) copy-start(f32[1,320]{1,0:T(1,128)} %refs_4_.3) | copy-start | bytes 3844
  14.5 3.4 %collective-permute-start.10 = (bf16[1,64,16]{2,1,0:T(8,128)(2,1)S(1)}, bf16[1,64,16]{2,1,0:T(8,128)(2,1)S(1)}, u32[]{:S(2)}, u32[]{:S(2)}) collective-permute-start(bf16[1,64,16]{2,1,0:T(8,128)(2,1)S(1)} %encode.1), channel_id=1, source_target_pairs={{0,9},{1,8},{2,11},{3,10},{4,13},{5,12},{6,15},{7,14},{8,1},{9,0},... | collective-permute-start | bytes 6152 | tf_op jit(solution)/shard_map/ppermute | solution.py:351
  14.8 3.1 %collective-permute-start.9 = (bf16[1,64,16]{2,1,0:T(8,128)(2,1)S(1)}, bf16[1,64,16]{2,1,0:T(8,128)(2,1)S(1)}, u32[]{:S(2)}, u32[]{:S(2)}) collective-permute-start(bf16[1,64,16]{2,1,0:T(8,128)(2,1)S(1)} %encode.1), channel_id=1, source_target_pairs={{0,1},{1,0},{2,3},{3,2},{4,5},{5,4},{6,7},{7,6},{8,9},{9,8},{10,11... | collective-permute-start | bytes 6152 | tf_op jit(solution)/shard_map/ppermute | solution.py:355
  16.2 4.1 %collective-permute-start.5 = (bf16[1,64,16]{2,1,0:T(8,128)(2,1)S(1)}, bf16[1,64,16]{2,1,0:T(8,128)(2,1)S(1)}, u32[]{:S(2)}, u32[]{:S(2)}) collective-permute-start(bf16[1,64,16]{2,1,0:T(8,128)(2,1)S(1)} %encode.1), channel_id=1, source_target_pairs={{0,25},{1,24},{2,27},{3,26},{4,29},{5,28},{6,31},{7,30},{8,17},{9,... | collective-permute-start | bytes 6152 | tf_op jit(solution)/shard_map/ppermute | solution.py:351
  17.2 3.3 %collective-permute-start.4 = (bf16[1,64,16]{2,1,0:T(8,128)(2,1)S(1)}, bf16[1,64,16]{2,1,0:T(8,128)(2,1)S(1)}, u32[]{:S(2)}, u32[]{:S(2)}) collective-permute-start(bf16[1,64,16]{2,1,0:T(8,128)(2,1)S(1)} %encode.1), channel_id=1, source_target_pairs={{0,17},{1,16},{2,19},{3,18},{4,21},{5,20},{6,23},{7,22},{8,25},{9,... | collective-permute-start | bytes 6152 | tf_op jit(solution)/shard_map/ppermute | solution.py:351
  19.1 4.8 %collective-permute-start.11 = (bf16[128,320]{1,0:T(8,128)(2,1)S(1)}, bf16[128,320]{1,0:T(8,128)(2,1)S(1)}, u32[]{:S(2)}, u32[]{:S(2)}) collective-permute-start(bf16[128,320]{1,0:T(8,128)(2,1)S(1)} %first_block.3.kept_ref), channel_id=1, source_target_pairs={{0,8},{8,24},{24,16},{16,0},{1,9},{9,25},{25,17},{17,1},{2,10},{10... | collective-permute-start | bytes 245768 | tf_op jit(solution)/shard_map/ppermute | solution.py:348
  21.7 5.1 %collective-permute-start.6 = (bf16[128,320]{1,0:T(8,128)(2,1)S(1)}, bf16[128,320]{1,0:T(8,128)(2,1)S(1)}, u32[]{:S(2)}, u32[]{:S(2)}) collective-permute-start(bf16[128,320]{1,0:T(8,128)(2,1)S(1)} %first_block.2.kept_ref), channel_id=1, source_target_pairs={{0,8},{8,24},{24,16},{16,0},{1,9},{9,25},{25,17},{17,1},{2,10},{10... | collective-permute-start | bytes 245768 | tf_op jit(solution)/shard_map/ppermute | solution.py:348
  23.9 5.0 %collective-permute-start.12 = (bf16[128,320]{1,0:T(8,128)(2,1)S(1)}, bf16[128,320]{1,0:T(8,128)(2,1)S(1)}, u32[]{:S(2)}, u32[]{:S(2)}) collective-permute-start(bf16[128,320]{1,0:T(8,128)(2,1)S(1)} %later_block.6.kept_ref), channel_id=1, source_target_pairs={{8,17},{9,16},{10,19},{11,18},{12,21},{13,20},{14,23},{15,22},{16,... | collective-permute-start | bytes 245768 | tf_op jit(solution)/shard_map/ppermute | solution.py:351
  26.8 4.8 %collective-permute-start.7 = (bf16[128,320]{1,0:T(8,128)(2,1)S(1)}, bf16[128,320]{1,0:T(8,128)(2,1)S(1)}, u32[]{:S(2)}, u32[]{:S(2)}) collective-permute-start(bf16[128,320]{1,0:T(8,128)(2,1)S(1)} %later_block.4.kept_ref), channel_id=1, source_target_pairs={{8,17},{9,16},{10,19},{11,18},{12,21},{13,20},{14,23},{15,22},{16,... | collective-permute-start | bytes 245768 | tf_op jit(solution)/shard_map/ppermute | solution.py:351
  28.9 4.2 %collective-permute-start.14 = (bf16[128,320]{1,0:T(8,128)(2,1)S(1)}, bf16[128,320]{1,0:T(8,128)(2,1)S(1)}, u32[]{:S(2)}, u32[]{:S(2)}) collective-permute-start(bf16[128,320]{1,0:T(8,128)(2,1)S(1)} %later_block.7.refs_0_), channel_id=1, source_target_pairs={{0,1},{1,0},{2,3},{3,2},{4,5},{5,4},{6,7},{7,6},{8,9},{9,8},{10,11... | collective-permute-start | bytes 245768 | tf_op jit(solution)/shard_map/ppermute | solution.py:355
  28.9 5.2 %collective-permute-start.13 = (bf16[128,320]{1,0:T(8,128)(2,1)S(1)}, bf16[128,320]{1,0:T(8,128)(2,1)S(1)}, u32[]{:S(2)}, u32[]{:S(2)}) collective-permute-start(bf16[128,320]{1,0:T(8,128)(2,1)S(1)} %later_block.7.refs_0_), channel_id=1, source_target_pairs={{0,8},{8,0},{16,24},{24,16},{1,9},{9,1},{17,25},{25,17},{2,10},{10... | collective-permute-start | bytes 245768 | tf_op jit(solution)/shard_map/ppermute | solution.py:348
  31.6 2.5 %collective-permute-start.15 = (bf16[128,320]{1,0:T(8,128)(2,1)S(1)}, bf16[128,320]{1,0:T(8,128)(2,1)S(1)}, u32[]{:S(2)}, u32[]{:S(2)}) collective-permute-start(bf16[128,320]{1,0:T(8,128)(2,1)S(1)} %later_block.5.refs_1_), channel_id=1, source_target_pairs={{0,1},{1,0},{2,3},{3,2},{4,5},{5,4},{6,7},{7,6},{8,9},{9,8},{10,11... | collective-permute-start | bytes 245768 | tf_op jit(solution)/shard_map/ppermute | solution.py:355
  31.6 5.2 %collective-permute-start.8 = (bf16[128,320]{1,0:T(8,128)(2,1)S(1)}, bf16[128,320]{1,0:T(8,128)(2,1)S(1)}, u32[]{:S(2)}, u32[]{:S(2)}) collective-permute-start(bf16[128,320]{1,0:T(8,128)(2,1)S(1)} %later_block.5.refs_1_), channel_id=1, source_target_pairs={{0,8},{8,0},{16,24},{24,16},{1,9},{9,1},{17,25},{25,17},{2,10},{10... | collective-permute-start | bytes 245768 | tf_op jit(solution)/shard_map/ppermute | solution.py:348

commit v6 on v5

--- a/solution.py
+++ b/solution.py
@@ -265,36 +265,28 @@
         state_ref[...] = unet_layer(before_ref[...].astype(F32), operands, block, frames)
 
 
-def last_kernel(block, frames, chunk, chunks, before_ref, *refs):
+def last_kernel(block, frames, chunk, crossed, before_ref, kept_ref, *refs):
     streams = block[0]
-    count = 2 * chunks if chunk == 0 else 1
-    kept, operands = refs[:count], refs[count:-4]
-    out_ref, wide_ref, store_sem, _ = refs[-4:]
-    last = lax.axis_index("section") == lax.axis_size("section") - 1
-
-    def store(part, sem):
-        rows = pl.ds(part * streams, streams)
-        return pltpu.make_async_copy(wide_ref.at[rows], out_ref.at[rows], sem)
+    operands = refs[1:-3] if chunk else refs[:-3]
+    out_ref, wide_ref, sem = refs[-3:]
+    section = lax.axis_index("section")
+    last = section == lax.axis_size("section") - 1
 
     @pl.when(last)
     def _():
         state = unet_layer(before_ref[...].astype(F32), operands, block, frames)
-        write_output(wide_ref, state, chunk * streams, block, frames)
-        copy = store(chunk, store_sem)
-        copy.start()
-        copy.wait()
-
-    if chunk == 0:
-
-        @pl.when(jnp.logical_not(last))
-        def _():
-            early = lax.axis_index("section") < 2
-            for part in range(chunks):
-                state = jnp.where(early, kept[chunks + part][...].astype(F32), kept[part][...].astype(F32))
-                write_output(wide_ref, state, part * streams, block, frames)
-                copy = store(part, store_sem)
-                copy.start()
-                copy.wait()
+        write_output(wide_ref, state, 0, block, frames)
+
+    @pl.when(jnp.logical_not(last))
+    def _():
+        state = kept_ref[...].astype(F32)
+        if crossed:
+            state = jnp.where(section < 2, before_ref[...].astype(F32), state)
+        write_output(wide_ref, state, 0, block, frames)
+
+    copy = pltpu.make_async_copy(wide_ref, out_ref.at[pl.ds(chunk * streams, streams)], sem)
+    copy.start()
+    copy.wait()
 
 
 def select_kernel(
@@ -332,10 +324,10 @@
     return pieces, got, place
 
 
-CYCLES = {
-    (0, 1): ((0, 1), (1, 3), (3, 2), (2, 0)),
-    (1, 2): ((1, 2), (2, 0), (0, 3), (3, 1)),
-    (2, 3): ((0, 1), (1, 0), (2, 3), (3, 2)),
+ROUTES = {
+    (0, 1): ((1, False), (3, False), (0, False), (2, False)),
+    (1, 2): ((3, True), (2, True), (0, True), (1, True)),
+    (2, 3): ((0, True), (1, True), (3, False), (2, False)),
 }
 
 
@@ -343,12 +335,14 @@
     return lax.axis_size("section") == 4 and lax.axis_size("slab") % 2 == 0
 
 
-def send(value, pairs, cross):
-    if not cross:
-        return lax.ppermute(value, "section", pairs)
+def send(value, routes):
+    if not any(cross for _, cross in routes):
+        return lax.ppermute(value, "section", [(s, target) for s, (target, _) in enumerate(routes)])
     slabs = lax.axis_size("slab")
-    joint = [(s * slabs + slab, t * slabs + (slab ^ 1)) for s, t in pairs for slab in range(slabs)]
-    return lax.ppermute(value, ("section", "slab"), joint)
+    pairs = []
+    for s, (target, cross) in enumerate(routes):
+        pairs += [(s * slabs + slab, target * slabs + (slab ^ 1 if cross else slab)) for slab in range(slabs)]
+    return lax.ppermute(value, ("section", "slab"), pairs)
 
 
 def swap_cores(value):
@@ -357,8 +351,8 @@
 
 def hop(value, source, target):
     count = lax.axis_size("section")
-    if count == 4 and (source, target) in CYCLES:
-        return send(value, CYCLES[source, target], crosses() and source == 1)
+    if crosses():
+        return send(value, ROUTES[source, target])
     if count & (count - 1):
         return lax.ppermute(value, "section", [(source, target)])
     return lax.ppermute(value, "section", [(s, s ^ source ^ target) for s in range(count)])
@@ -370,7 +364,7 @@
         return [value] + [hop(value, other, 0) for other in range(1, count)]
     if count == 4:
         own = swap_cores(value) if crosses() else value
-        return [own] + [send(value, [(s, s ^ k) for s in range(4)], crosses()) for k in (1, 2, 3)]
+        return [own] + [send(value, [(s ^ k, crosses()) for s in range(4)]) for k in (1, 2, 3)]
     parts = [value]
     step = 1
     while step < count:
@@ -450,23 +444,18 @@
     hbm = pl.BlockSpec(memory_space=pltpu.HBM)
     out_shape = jax.ShapeDtypeStruct((section_count * owned, lat_rows, frames, lat_cols * width), BF16)
     out = None
-    early = [swap_cores(state) if crosses() else state for state in states]
     for chunk in range(chunks):
-        operands = [arrived[chunk]] + (states + early if chunk == 0 else [out]) + layer
+        operands = [arrived[chunk], states[chunk]] + ([out] if chunk else []) + layer
         specs = [vmem()] * len(operands)
         if chunk:
-            specs[1] = hbm
+            specs[2] = hbm
         out = pl.pallas_call(
-            functools.partial(last_kernel, block, frames, chunk, chunks),
+            functools.partial(last_kernel, block, frames, chunk, crosses()),
             out_shape=out_shape,
             in_specs=specs,
             out_specs=hbm,
-            scratch_shapes=[
-                pltpu.VMEM(out_shape.shape, BF16),
-                pltpu.SemaphoreType.DMA,
-                pltpu.SemaphoreType.DMA,
-            ],
-            input_output_aliases={1: 0} if chunk else {},
+            scratch_shapes=[pltpu.VMEM((streams,) + out_shape.shape[1:], BF16), pltpu.SemaphoreType.DMA],
+            input_output_aliases={2: 0} if chunk else {},
             compiler_params=params(),
             name="last_block",
         )(*operands)

time: 37.2 us -> 36.2 us (0.973)
  the two profiles are of different devices: /device:TPU:0 before, /device:TPU:4 now
where the time goes in v6:
time: 36.2 us; the launch traced here: 35.9 us
  starting transfers between devices  14.4 us (40%)
  waiting for transfers between devices  14 us (39%)
  Pallas kernels  6.38 us (18%)
  local copies, waits for them, and re-layouts  0.86 us (2%)
    ppermute x7, waiting for transfers between devices, send(): return lax.ppermute(value, ('section', 'slab'), pairs)  7.3 us
    ppermute x7, starting transfers between devices, send(): return lax.ppermute(value, ('section', 'slab'), pairs)  4.86 us
    ppermute x3, starting transfers between devices, exchange(): pieces[step] = lax.ppermute(pieces[step], 'slab', pairs)  4.49 us
    ppermute x3, waiting for transfers between devices, exchange(): pieces[step] = lax.ppermute(pieces[step], 'slab', pairs)  3.7 us
    ppermute x2, starting transfers between devices, send(): lax.ppermute(value, 'section', [(s, target) for s, (target, _) in enumera...  3.69 us
    ppermute x2, waiting for transfers between devices, send(): lax.ppermute(value, 'section', [(s, target) for s, (target, _) in enumera...  2.29 us
    pallas_call x1, Pallas kernels, exchange(): pl.pallas_call(functools.partial(select_kernel, 'section', 'slab', owned,...  1.81 us
    pallas_call x4, Pallas kernels, per_device(): pl.pallas_call(functools.partial(later_kernel, index, block, frames), out...  1.76 us
  transfers between devices with their start and end apart: 14, of which 10 were waited for; matrix products, arithmetic and copies ran while one was open for 2% of the time, Pallas kernels for 7%

profile of v6, /device:TPU:4, one launch (start us, length us, event | category | flops | bytes accessed | tf_op | source)
XLA Modules:
  0.0 35.9 jit_solution(4590374533778353059)
XLA Ops:
  0.0 1.8 %select.1 = (bf16[4,1,2,2,8,256]{5,4,3,2,1,0:T(8,128)(2,1)}, bf16[4,1,2,2,8,256]{5,4,3,2,1,0:T(8,128)(2,1)}, f32[4,16,320]{2,1,0:T(8,128)}) custom-call(s32[4,8]{1,0:T(4,128)} %clips_ref.1, s32[4,8]{1,0:T(4,128)} %offsets_ref.1, bf16[8,2,2,8,256]{4,3,2,1,0:T(8,128)(2,1)} %bitcast.27, bf16[320,128]{1,0:T(8,128)(2,1)} %bitcast.28, f32[320]{0:T(512)} %bias_ref.1), custom_call_target="tpu_custom_call" | custom-call | tf_op jit(solution)/shard_map/select/pallas_call | solution.py:312
  1.8 0.8 %fusion = (bf16[1,1,2,2,8,256]{5,4,3,2,1,0:T(8,128)(2,1)S(1)}, bf16[1,1,2,2,8,256]{5,4,3,2,1,0:T(8,128)(2,1)S(1)}, bf16[1,1,2,2,8,256]{5,4,3,2,1,0:T(8,128)(2,1)S(1)}, bf16[1,1,2,2,8,256]{5,4,3,2,1,0:T(8,128)(2,1)S(1)}) fusion(bf16[4,1,2,2,8,256]{5,4,3,2,1,0:T(8,128)(2,1)} %get-tuple-element.10), kind=kLoop, calls=%fused_computation.4 | loop fusion | bytes 131072 | tf_op jit(solution)/shard_map/slice | solution.py:320
  2.6 0.7 %collective-permute-done.after_ref = bf16[4,1,2,2,8,256]{5,4,3,2,1,0:T(8,128)(2,1)S(1)} collective-permute-done((bf16[4,1,2,2,8,256]{5,4,3,2,1,0:T(8,128)(2,1)}, bf16[4,1,2,2,8,256]{5,4,3,2,1,0:T(8,128)(2,1)S(1)}, u32[]{:S(2)}, u32[]{:S(2)}) %collective-permute-start) | collective-permute-done | bytes 65568 | tf_op jit(solution)/shard_map/ppermute | solution.py:349
  3.3 3.7 %collective-permute-start.1 = (bf16[2,1,2,2,8,256]{5,4,3,2,1,0:T(8,128)(2,1)S(1)}, bf16[2,1,2,2,8,256]{5,4,3,2,1,0:T(8,128)(2,1)S(1)}, u32[]{:S(2)}, u32[]{:S(2)}) collective-permute-start(bf16[2,1,2,2,8,256]{5,4,3,2,1,0:T(8,128)(2,1)S(1)} %pad_maximum_fusion), channel_id=1, source_target_pairs={{0,6},{1,7},{2,4},{3,5},{4,2},{5,3},{6,0},{7,1},{8,14},{9,15},{10,... | collective-permute-start | bytes 98312 | tf_op jit(solution)/shard_map/ppermute | solution.py:323
  7.0 0.0 copy-start.1
  7.0 0.0 copy-start.9
  7.1 0.8 %collective-permute-start.3 = (bf16[2,1,2,2,8,256]{5,4,3,2,1,0:T(8,128)(2,1)S(1)}, bf16[2,1,2,2,8,256]{5,4,3,2,1,0:T(8,128)(2,1)S(1)}, u32[]{:S(2)}, u32[]{:S(2)}) collective-permute-start(bf16[2,1,2,2,8,256]{5,4,3,2,1,0:T(8,128)(2,1)S(1)} %pad_maximum_fusion.2), channel_id=1, source_target_pairs={{0,2},{1,3},{2,0},{3,1},{4,6},{5,7},{6,4},{7,5},{8,10},{9,11},{10,... | collective-permute-start | bytes 98312 | tf_op jit(solution)/shard_map/ppermute | solution.py:323
  7.9 0.1 groups.1
  8.1 1.0 %collective-permute-done.1.refs_0_ = bf16[2,1,2,2,8,256]{5,4,3,2,1,0:T(8,128)(2,1)S(1)} collective-permute-done((bf16[2,1,2,2,8,256]{5,4,3,2,1,0:T(8,128)(2,1)S(1)}, bf16[2,1,2,2,8,256]{5,4,3,2,1,0:T(8,128)(2,1)S(1)}, u32[]{:S(2)}, u32[]{:S(2)}) %collective-permute-start.1) | collective-permute-done | bytes 32800 | tf_op jit(solution)/shard_map/ppermute | solution.py:323
  9.1 2.7 %collective-permute-done.2.refs_1_ = bf16[2,1,2,2,8,256]{5,4,3,2,1,0:T(8,128)(2,1)S(1)} collective-permute-done((bf16[2,1,2,2,8,256]{5,4,3,2,1,0:T(8,128)(2,1)S(1)}, bf16[2,1,2,2,8,256]{5,4,3,2,1,0:T(8,128)(2,1)S(1)}, u32[]{:S(2)}, u32[]{:S(2)}) %collective-permute-start.2) | collective-permute-done | bytes 32800 | tf_op jit(solution)/shard_map/ppermute | solution.py:323
  11.8 1.2 %encode.1 = bf16[1,64,16]{2,1,0:T(8,128)(2,1)S(1)} custom-call(bf16[2,1,2,2,8,256]{5,4,3,2,1,0:T(8,128)(2,1)S(1)} %collective-permute-done.1.refs_0_, bf16[2,1,2,2,8,256]{5,4,3,2,1,0:T(8,128)(2,1)S(1)} %collective-permute-done.2.refs_1_, bf16[2,1,2,2,8,256]{5,4,3,2,1,0:T(8,128)(2,1)S(1)} %collective-permute-done.3.refs_2_, ...), custom_call_target="tpu_custom_call" | custom-call | tf_op jit(solution)/shard_map/encode/pallas_call | solution.py:137
  13.0 0.3 collective-permute-start.10
  13.4 1.3 %collective-permute-start.9 = (bf16[1,64,16]{2,1,0:T(8,128)(2,1)S(1)}, bf16[1,64,16]{2,1,0:T(8,128)(2,1)S(1)}, u32[]{:S(2)}, u32[]{:S(2)}) collective-permute-start(bf16[1,64,16]{2,1,0:T(8,128)(2,1)S(1)} %encode.1), channel_id=1, source_target_pairs={{0,1},{1,0},{2,3},{3,2},{4,5},{5,4},{6,7},{7,6},{8,9},{9,8},{10,11... | collective-permute-start | bytes 6152 | tf_op jit(solution)/shard_map/ppermute | solution.py:349
  14.7 0.1 collective-permute-start.5
  14.8 1.6 %collective-permute-start.4 = (bf16[1,64,16]{2,1,0:T(8,128)(2,1)S(1)}, bf16[1,64,16]{2,1,0:T(8,128)(2,1)S(1)}, u32[]{:S(2)}, u32[]{:S(2)}) collective-permute-start(bf16[1,64,16]{2,1,0:T(8,128)(2,1)S(1)} %encode.1), channel_id=1, source_target_pairs={{0,17},{1,16},{2,19},{3,18},{4,21},{5,20},{6,23},{7,22},{8,25},{9,... | collective-permute-start | bytes 6152 | tf_op jit(solution)/shard_map/ppermute | solution.py:345
  16.5 1.7 %collective-permute-start.11 = (bf16[128,320]{1,0:T(8,128)(2,1)S(1)}, bf16[128,320]{1,0:T(8,128)(2,1)S(1)}, u32[]{:S(2)}, u32[]{:S(2)}) collective-permute-start(bf16[128,320]{1,0:T(8,128)(2,1)S(1)} %first_block.3.kept_ref), channel_id=1, source_target_pairs={{0,8},{8,24},{16,0},{24,16},{1,9},{9,25},{17,1},{25,17},{2,10},{10... | collective-permute-start | bytes 245768 | tf_op jit(solution)/shard_map/ppermute | solution.py:340
  18.2 0.6 %collective-permute-done.5.refs_1_ = bf16[1,64,16]{2,1,0:T(8,128)(2,1)S(1)} collective-permute-done((bf16[1,64,16]{2,1,0:T(8,128)(2,1)S(1)}, bf16[1,64,16]{2,1,0:T(8,128)(2,1)S(1)}, u32[]{:S(2)}, u32[]{:S(2)}) %collective-permute-start.5) | collective-permute-done | bytes 2080 | tf_op jit(solution)/shard_map/ppermute | solution.py:345
  18.8 2.0 %collective-permute-start.6 = (bf16[128,320]{1,0:T(8,128)(2,1)S(1)}, bf16[128,320]{1,0:T(8,128)(2,1)S(1)}, u32[]{:S(2)}, u32[]{:S(2)}) collective-permute-start(bf16[128,320]{1,0:T(8,128)(2,1)S(1)} %first_block.2.kept_ref), channel_id=1, source_target_pairs={{0,8},{8,24},{16,0},{24,16},{1,9},{9,25},{17,1},{25,17},{2,10},{10... | collective-permute-start | bytes 245768 | tf_op jit(solution)/shard_map/ppermute | solution.py:340
  20.8 0.5 %collective-permute-done.11.before_ref = bf16[128,320]{1,0:T(8,128)(2,1)S(1)} collective-permute-done((bf16[128,320]{1,0:T(8,128)(2,1)S(1)}, bf16[128,320]{1,0:T(8,128)(2,1)S(1)}, u32[]{:S(2)}, u32[]{:S(2)}) %collective-permute-start.11) | collective-permute-done | bytes 81952 | tf_op jit(solution)/shard_map/ppermute | solution.py:340
  21.3 0.5 %collective-permute-start.12 = (bf16[128,320]{1,0:T(8,128)(2,1)S(1)}, bf16[128,320]{1,0:T(8,128)(2,1)S(1)}, u32[]{:S(2)}, u32[]{:S(2)}) collective-permute-start(bf16[128,320]{1,0:T(8,128)(2,1)S(1)} %later_block.6.kept_ref), channel_id=1, source_target_pairs={{0,25},{1,24},{2,27},{3,26},{4,29},{5,28},{6,31},{7,30},{8,17},{9,... | collective-permute-start | bytes 245768 | tf_op jit(solution)/shard_map/ppermute | solution.py:345
  21.8 1.8 %collective-permute-done.6.before_ref = bf16[128,320]{1,0:T(8,128)(2,1)S(1)} collective-permute-done((bf16[128,320]{1,0:T(8,128)(2,1)S(1)}, bf16[128,320]{1,0:T(8,128)(2,1)S(1)}, u32[]{:S(2)}, u32[]{:S(2)}) %collective-permute-start.6) | collective-permute-done | bytes 81952 | tf_op jit(solution)/shard_map/ppermute | solution.py:340
  23.6 1.4 %collective-permute-start.7 = (bf16[128,320]{1,0:T(8,128)(2,1)S(1)}, bf16[128,320]{1,0:T(8,128)(2,1)S(1)}, u32[]{:S(2)}, u32[]{:S(2)}) collective-permute-start(bf16[128,320]{1,0:T(8,128)(2,1)S(1)} %later_block.4.kept_ref), channel_id=1, source_target_pairs={{0,25},{1,24},{2,27},{3,26},{4,29},{5,28},{6,31},{7,30},{8,17},{9,... | collective-permute-start | bytes 245768 | tf_op jit(solution)/shard_map/ppermute | solution.py:345
  25.0 2.3 %collective-permute-done.12.before_ref = bf16[128,320]{1,0:T(8,128)(2,1)S(1)} collective-permute-done((bf16[128,320]{1,0:T(8,128)(2,1)S(1)}, bf16[128,320]{1,0:T(8,128)(2,1)S(1)}, u32[]{:S(2)}, u32[]{:S(2)}) %collective-permute-start.12) | collective-permute-done | bytes 81952 | tf_op jit(solution)/shard_map/ppermute | solution.py:345
  27.3 0.9 %later_block.7.kept_ref = bf16[128,320]{1,0:T(8,128)(2,1)S(1)} custom-call(bf16[128,320]{1,0:T(8,128)(2,1)S(1)} %collective-permute-done.12.before_ref, bf16[128,320]{1,0:T(8,128)(2,1)S(1)} %later_block.6.kept_ref, bf16[3,3,320,320]{3,2,1,0:T(8,128)(2,1)S(1)} %bitcast.16, f32[1,320]{1,0:T(1,128)S(1)} %copy-done.4, ...), custom_call_target="tpu_custom_call", output_to_operand_aliasing={{}: (1, {})} | custom-call | tf_op jit(solution)/shard_map/later_block/pallas_call | solution.py:434
  28.2 0.1 collective-permute-start.13
  28.3 0.8 %collective-permute-done.7.before_ref = bf16[128,320]{1,0:T(8,128)(2,1)S(1)} collective-permute-done((bf16[128,320]{1,0:T(8,128)(2,1)S(1)}, bf16[128,320]{1,0:T(8,128)(2,1)S(1)}, u32[]{:S(2)}, u32[]{:S(2)}) %collective-permute-start.7) | collective-permute-done | bytes 81952 | tf_op jit(solution)/shard_map/ppermute | solution.py:345
  29.0 0.9 %later_block.5.kept_ref = bf16[128,320]{1,0:T(8,128)(2,1)S(1)} custom-call(bf16[128,320]{1,0:T(8,128)(2,1)S(1)} %collective-permute-done.7.before_ref, bf16[128,320]{1,0:T(8,128)(2,1)S(1)} %later_block.4.kept_ref, bf16[3,3,320,320]{3,2,1,0:T(8,128)(2,1)S(1)} %bitcast.17, f32[1,320]{1,0:T(1,128)S(1)} %copy-done.4, ...), custom_call_target="tpu_custom_call", output_to_operand_aliasing={{}: (1, {})} | custom-call | tf_op jit(solution)/shard_map/later_block/pallas_call | solution.py:434
  29.9 0.8 %collective-permute-start.8 = (bf16[128,320]{1,0:T(8,128)(2,1)S(1)}, bf16[128,320]{1,0:T(8,128)(2,1)S(1)}, u32[]{:S(2)}, u32[]{:S(2)}) collective-permute-start(bf16[128,320]{1,0:T(8,128)(2,1)S(1)} %later_block.5.kept_ref), channel_id=1, source_target_pairs={{0,1},{1,0},{2,3},{3,2},{4,5},{5,4},{6,7},{7,6},{8,9},{9,8},{10,11... | collective-permute-start | bytes 245768 | tf_op jit(solution)/shard_map/ppermute | solution.py:345
  30.7 2.3 %collective-permute-done.13.before_ref = bf16[128,320]{1,0:T(8,128)(2,1)S(1)} collective-permute-done((bf16[128,320]{1,0:T(8,128)(2,1)S(1)}, bf16[128,320]{1,0:T(8,128)(2,1)S(1)}, u32[]{:S(2)}, u32[]{:S(2)}) %collective-permute-start.13) | collective-permute-done | bytes 81952 | tf_op jit(solution)/shard_map/ppermute | solution.py:345
  33.1 0.7 %last_block.2.refs_0_ = bf16[4,8,2,1280]{3,2,1,0:T(2,128)(2,1)} custom-call(bf16[128,320]{1,0:T(8,128)(2,1)S(1)} %collective-permute-done.13.before_ref, bf16[128,320]{1,0:T(8,128)(2,1)S(1)} %later_block.7.kept_ref, bf16[3,3,320,320]{3,2,1,0:T(8,128)(2,1)S(1)} %bitcast.18, f32[1,320]{1,0:T(1,128)S(1)} %copy-done.4, f32[1,320]{1,0:T(1,128)S(1)} %copy-done.5, ...), custom_call_target="tpu_custom_call" | custom-call | tf_op jit(solution)/shard_map/last_block/pallas_call | solution.py:452
  33.8 1.3 %collective-permute-done.8.before_ref = bf16[128,320]{1,0:T(8,128)(2,1)S(1)} collective-permute-done((bf16[128,320]{1,0:T(8,128)(2,1)S(1)}, bf16[128,320]{1,0:T(8,128)(2,1)S(1)}, u32[]{:S(2)}, u32[]{:S(2)}) %collective-permute-start.8) | collective-permute-done | bytes 81952 | tf_op jit(solution)/shard_map/ppermute | solution.py:345
  35.1 0.7 %last_block.3 = bf16[4,8,2,1280]{3,2,1,0:T(2,128)(2,1)} custom-call(bf16[128,320]{1,0:T(8,128)(2,1)S(1)} %collective-permute-done.8.before_ref, bf16[128,320]{1,0:T(8,128)(2,1)S(1)} %later_block.5.kept_ref, bf16[4,8,2,1280]{3,2,1,0:T(2,128)(2,1)} %last_block.2.refs_0_, bf16[3,3,320,320]{3,2,1,0:T(8,128)(2,1)S(1)} %bitcast.19, ...), custom_call_target="tpu_custom_call", output_to_operand_aliasing={{}: (2, {})} | custom-call | tf_op jit(solution)/shard_map/last_block/pallas_call | solution.py:452
  (37 shorter events, 0.1 us)
Async XLA Ops:
  1.8 1.5 %collective-permute-start = (bf16[4,1,2,2,8,256]{5,4,3,2,1,0:T(8,128)(2,1)}, bf16[4,1,2,2,8,256]{5,4,3,2,1,0:T(8,128)(2,1)S(1)}, u32[]{:S(2)}, u32[]{:S(2)}) collective-permute-start(bf16[4,1,2,2,8,256]{5,4,3,2,1,0:T(8,128)(2,1)} %get-tuple-element.11), channel_id=1, source_target_pairs={{0,1},{1,0},{2,3},{3,2},{4,5},{5,4},{6,7},{7,6},{8,9},{9,8},{10,11... | collective-permute-start | bytes 196616 | tf_op jit(solution)/shard_map/ppermute | solution.py:349
  3.3 5.8 %collective-permute-start.1 = (bf16[2,1,2,2,8,256]{5,4,3,2,1,0:T(8,128)(2,1)S(1)}, bf16[2,1,2,2,8,256]{5,4,3,2,1,0:T(8,128)(2,1)S(1)}, u32[]{:S(2)}, u32[]{:S(2)}) collective-permute-start(bf16[2,1,2,2,8,256]{5,4,3,2,1,0:T(8,128)(2,1)S(1)} %pad_maximum_fusion), channel_id=1, source_target_pairs={{0,6},{1,7},{2,4},{3,5},{4,2},{5,3},{6,0},{7,1},{8,14},{9,15},{10,... | collective-permute-start | bytes 98312 | tf_op jit(solution)/shard_map/ppermute | solution.py:323
  7.0 4.8 %collective-permute-start.2 = (bf16[2,1,2,2,8,256]{5,4,3,2,1,0:T(8,128)(2,1)S(1)}, bf16[2,1,2,2,8,256]{5,4,3,2,1,0:T(8,128)(2,1)S(1)}, u32[]{:S(2)}, u32[]{:S(2)}) collective-permute-start(bf16[2,1,2,2,8,256]{5,4,3,2,1,0:T(8,128)(2,1)S(1)} %pad_maximum_fusion.1), channel_id=1, source_target_pairs={{0,4},{1,5},{2,6},{3,7},{4,0},{5,1},{6,2},{7,3},{8,12},{9,13},{10,... | collective-permute-start | bytes 98312 | tf_op jit(solution)/shard_map/ppermute | solution.py:323
  7.0 4.8 %copy-start.1 = (bf16[3,3,3,256,256]{4,3,2,1,0:T(8,128)(2,1)S(1)}, bf16[3,3,3,256,256]{4,3,2,1,0:T(8,128)(2,1)}, u32[]{:S(2)}) copy-start(bf16[3,3,3,256,256]{4,3,2,1,0:T(8,128)(2,1)} %refs_4_.2) | copy-start | bytes 10616836
  7.0 4.8 %copy-start.7 = (bf16[256,16]{0,1:T(8,128)(2,1)S(1)}, bf16[256,16]{0,1:T(8,128)(2,1)}, u32[]{:S(2)}) copy-start(bf16[256,16]{0,1:T(8,128)(2,1)} %param.21) | copy-start | bytes 24580
  7.0 4.8 %copy-start.8 = (f32[256]{0:T(256)S(1)}, f32[256]{0:T(256)}, u32[]{:S(2)}) copy-start(f32[256]{0:T(256)} %param.18) | copy-start | bytes 3076
  7.0 4.8 %copy-start.9 = (f32[256]{0:T(256)S(1)}, f32[256]{0:T(256)}, u32[]{:S(2)}) copy-start(f32[256]{0:T(256)} %param.19) | copy-start | bytes 3076
  7.0 4.8 %copy-start.10 = (f32[256]{0:T(256)S(1)}, f32[256]{0:T(256)}, u32[]{:S(2)}) copy-start(f32[256]{0:T(256)} %param.20) | copy-start | bytes 3076
  7.0 4.8 %copy-start.11 = (f32[16]{0:T(128)S(1)}, f32[16]{0:T(128)}, u32[]{:S(2)}) copy-start(f32[16]{0:T(128)} %param.22) | copy-start | bytes 196
  7.1 4.7 %collective-permute-start.3 = (bf16[2,1,2,2,8,256]{5,4,3,2,1,0:T(8,128)(2,1)S(1)}, bf16[2,1,2,2,8,256]{5,4,3,2,1,0:T(8,128)(2,1)S(1)}, u32[]{:S(2)}, u32[]{:S(2)}) collective-permute-start(bf16[2,1,2,2,8,256]{5,4,3,2,1,0:T(8,128)(2,1)S(1)} %pad_maximum_fusion.2), channel_id=1, source_target_pairs={{0,2},{1,3},{2,0},{3,1},{4,6},{5,7},{6,4},{7,5},{8,10},{9,11},{10,... | collective-permute-start | bytes 98312 | tf_op jit(solution)/shard_map/ppermute | solution.py:323
  8.0 8.4 %copy-start = (bf16[1,3,3,320,320]{4,3,2,1,0:T(8,128)(2,1)S(1)}, bf16[1,3,3,320,320]{4,3,2,1,0:T(8,128)(2,1)}, u32[]{:S(2)}) copy-start(bf16[1,3,3,320,320]{4,3,2,1,0:T(8,128)(2,1)} %param.30) | copy-start | bytes 5529604
  8.0 8.4 %copy-start.2 = (bf16[3,3,16,320]{3,2,1,0:T(8,128)(2,1)S(1)}, bf16[3,3,16,320]{3,2,1,0:T(8,128)(2,1)}, u32[]{:S(2)}) copy-start(bf16[3,3,16,320]{3,2,1,0:T(8,128)(2,1)} %param.25) | copy-start | bytes 276484
  8.0 8.4 %copy-start.3 = (f32[4,16,320]{2,1,0:T(8,128)S(1)}, f32[4,16,320]{2,1,0:T(8,128)}, u32[]{:S(2)}) copy-start(f32[4,16,320]{2,1,0:T(8,128)} %get-tuple-element.13.refs_2_) | copy-start | bytes 245764
  8.0 8.4 %copy-start.4 = (f32[1,320]{1,0:T(1,128)S(1)}, f32[1,320]{1,0:T(1,128)}, u32[]{:S(2)}) copy-start(f32[1,320]{1,0:T(1,128)} %refs_2_.11) | copy-start | bytes 3844
  8.0 8.4 %copy-start.5 = (f32[1,320]{1,0:T(1,128)S(1)}, f32[1,320]{1,0:T(1,128)}, u32[]{:S(2)}) copy-start(f32[1,320]{1,0:T(1,128)} %refs_3_.11) | copy-start | bytes 3844
  8.1 8.4 %copy-start.6 = (f32[1,320]{1,0:T(1,128)S(1)}, f32[1,320]{1,0:T(1,128)}, u32[]{:S(2)}) copy-start(f32[1,320]{1,0:T(1,128)} %refs_4_.3) | copy-start | bytes 3844
  13.0 3.4 %collective-permute-start.10 = (bf16[1,64,16]{2,1,0:T(8,128)(2,1)S(1)}, bf16[1,64,16]{2,1,0:T(8,128)(2,1)S(1)}, u32[]{:S(2)}, u32[]{:S(2)}) collective-permute-start(bf16[1,64,16]{2,1,0:T(8,128)(2,1)S(1)} %encode.1), channel_id=1, source_target_pairs={{0,9},{1,8},{2,11},{3,10},{4,13},{5,12},{6,15},{7,14},{8,1},{9,0},... | collective-permute-start | bytes 6152 | tf_op jit(solution)/shard_map/ppermute | solution.py:345
  13.4 3.1 %collective-permute-start.9 = (bf16[1,64,16]{2,1,0:T(8,128)(2,1)S(1)}, bf16[1,64,16]{2,1,0:T(8,128)(2,1)S(1)}, u32[]{:S(2)}, u32[]{:S(2)}) collective-permute-start(bf16[1,64,16]{2,1,0:T(8,128)(2,1)S(1)} %encode.1), channel_id=1, source_target_pairs={{0,1},{1,0},{2,3},{3,2},{4,5},{5,4},{6,7},{7,6},{8,9},{9,8},{10,11... | collective-permute-start | bytes 6152 | tf_op jit(solution)/shard_map/ppermute | solution.py:349
  14.7 4.1 %collective-permute-start.5 = (bf16[1,64,16]{2,1,0:T(8,128)(2,1)S(1)}, bf16[1,64,16]{2,1,0:T(8,128)(2,1)S(1)}, u32[]{:S(2)}, u32[]{:S(2)}) collective-permute-start(bf16[1,64,16]{2,1,0:T(8,128)(2,1)S(1)} %encode.1), channel_id=1, source_target_pairs={{0,25},{1,24},{2,27},{3,26},{4,29},{5,28},{6,31},{7,30},{8,17},{9,... | collective-permute-start | bytes 6152 | tf_op jit(solution)/shard_map/ppermute | solution.py:345
  14.8 4.0 %collective-permute-start.4 = (bf16[1,64,16]{2,1,0:T(8,128)(2,1)S(1)}, bf16[1,64,16]{2,1,0:T(8,128)(2,1)S(1)}, u32[]{:S(2)}, u32[]{:S(2)}) collective-permute-start(bf16[1,64,16]{2,1,0:T(8,128)(2,1)S(1)} %encode.1), channel_id=1, source_target_pairs={{0,17},{1,16},{2,19},{3,18},{4,21},{5,20},{6,23},{7,22},{8,25},{9,... | collective-permute-start | bytes 6152 | tf_op jit(solution)/shard_map/ppermute | solution.py:345
  16.5 4.8 %collective-permute-start.11 = (bf16[128,320]{1,0:T(8,128)(2,1)S(1)}, bf16[128,320]{1,0:T(8,128)(2,1)S(1)}, u32[]{:S(2)}, u32[]{:S(2)}) collective-permute-start(bf16[128,320]{1,0:T(8,128)(2,1)S(1)} %first_block.3.kept_ref), channel_id=1, source_target_pairs={{0,8},{8,24},{16,0},{24,16},{1,9},{9,25},{17,1},{25,17},{2,10},{10... | collective-permute-start | bytes 245768 | tf_op jit(solution)/shard_map/ppermute | solution.py:340
  18.8 4.8 %collective-permute-start.6 = (bf16[128,320]{1,0:T(8,128)(2,1)S(1)}, bf16[128,320]{1,0:T(8,128)(2,1)S(1)}, u32[]{:S(2)}, u32[]{:S(2)}) collective-permute-start(bf16[128,320]{1,0:T(8,128)(2,1)S(1)} %first_block.2.kept_ref), channel_id=1, source_target_pairs={{0,8},{8,24},{16,0},{24,16},{1,9},{9,25},{17,1},{25,17},{2,10},{10... | collective-permute-start | bytes 245768 | tf_op jit(solution)/shard_map/ppermute | solution.py:340
  21.3 6.0 %collective-permute-start.12 = (bf16[128,320]{1,0:T(8,128)(2,1)S(1)}, bf16[128,320]{1,0:T(8,128)(2,1)S(1)}, u32[]{:S(2)}, u32[]{:S(2)}) collective-permute-start(bf16[128,320]{1,0:T(8,128)(2,1)S(1)} %later_block.6.kept_ref), channel_id=1, source_target_pairs={{0,25},{1,24},{2,27},{3,26},{4,29},{5,28},{6,31},{7,30},{8,17},{9,... | collective-permute-start | bytes 245768 | tf_op jit(solution)/shard_map/ppermute | solution.py:345
  23.6 5.4 %collective-permute-start.7 = (bf16[128,320]{1,0:T(8,128)(2,1)S(1)}, bf16[128,320]{1,0:T(8,128)(2,1)S(1)}, u32[]{:S(2)}, u32[]{:S(2)}) collective-permute-start(bf16[128,320]{1,0:T(8,128)(2,1)S(1)} %later_block.4.kept_ref), channel_id=1, source_target_pairs={{0,25},{1,24},{2,27},{3,26},{4,29},{5,28},{6,31},{7,30},{8,17},{9,... | collective-permute-start | bytes 245768 | tf_op jit(solution)/shard_map/ppermute | solution.py:345
  28.2 4.9 %collective-permute-start.13 = (bf16[128,320]{1,0:T(8,128)(2,1)S(1)}, bf16[128,320]{1,0:T(8,128)(2,1)S(1)}, u32[]{:S(2)}, u32[]{:S(2)}) collective-permute-start(bf16[128,320]{1,0:T(8,128)(2,1)S(1)} %later_block.7.kept_ref), channel_id=1, source_target_pairs={{0,1},{1,0},{2,3},{3,2},{4,5},{5,4},{6,7},{7,6},{8,9},{9,8},{10,11... | collective-permute-start | bytes 245768 | tf_op jit(solution)/shard_map/ppermute | solution.py:345
  29.9 5.2 %collective-permute-start.8 = (bf16[128,320]{1,0:T(8,128)(2,1)S(1)}, bf16[128,320]{1,0:T(8,128)(2,1)S(1)}, u32[]{:S(2)}, u32[]{:S(2)}) collective-permute-start(bf16[128,320]{1,0:T(8,128)(2,1)S(1)} %later_block.5.kept_ref), channel_id=1, source_target_pairs={{0,1},{1,0},{2,3},{3,2},{4,5},{5,4},{6,7},{7,6},{8,9},{9,8},{10,11... | collective-permute-start | bytes 245768 | tf_op jit(solution)/shard_map/ppermute | solution.py:345

commit v7 on v6

--- a/solution.py
+++ b/solution.py
@@ -9,6 +9,7 @@
 
 GROUPS = 32
 LANES = 128
+CUTS = (2,)
 EPS = 1e-06
 VMEM_LIMIT = 32 * 1024 * 1024
 GROUPS_VMEM = 4 * 1024 * 1024
@@ -72,7 +73,7 @@
     pieces = refs[:-10]
     slab_rows = pieces[0].shape[2]
     items, frames, row_count, cols, channels = x_ref.shape
-    for step, piece_ref in enumerate(pieces[::-1]):
+    for step, piece_ref in zip(piece_order(len(pieces)), pieces):
         for half in range(2):
             source = lax.axis_index(slab_axis) ^ (2 * step + half)
             for item in range(items):
@@ -130,6 +131,10 @@
         out_ref[item] = (latent + lat_bias_ref[...]).astype(BF16)
 
 
+def piece_order(steps):
+    return (2, 3, 1, 0) if steps == 4 else tuple(range(steps))[::-1]
+
+
 def encode(pieces, *operands):
     _, items, slab_rows, frames, cols, channels = pieces[0].shape
     row_count = 2 * len(pieces) * slab_rows
@@ -145,7 +150,7 @@
         ],
         compiler_params=params(),
         name="encode",
-    )(*pieces[::-1], *operands)
+    )(*[pieces[step] for step in piece_order(len(pieces))], *operands)
 
 
 def shifted(value, unit, frames):
@@ -233,7 +238,7 @@
         out_ref[stream] = dot_last(hot, table) + bias
 
 
-def first_kernel(block, frames, count, chunk, *refs):
+def first_kernel(block, frames, count, first, *refs):
     streams, unit = block
     latent_refs = refs[:count]
     place_ref, in_weight_ref, *operands = refs[count:-1]
@@ -249,7 +254,7 @@
                 for item in range(ref.shape[0]):
                     parts.append(ref[item, pl.ds(col * unit, unit), :].astype(F32))
         total = conv3_narrow(jnp.concatenate(parts, axis=0), in_weight_ref[...], block, frames)
-        placed = place_ref[pl.ds(chunk * streams, streams)]
+        placed = place_ref[pl.ds(first, streams)]
         placed = placed.reshape(1, streams * unit, width)
         total = (total.reshape(cols, streams * unit, width) + placed).reshape(size, width)
         state = total.astype(BF16).astype(F32)
@@ -265,9 +270,9 @@
         state_ref[...] = unet_layer(before_ref[...].astype(F32), operands, block, frames)
 
 
-def last_kernel(block, frames, chunk, crossed, before_ref, kept_ref, *refs):
+def last_kernel(block, frames, first, crossed, before_ref, kept_ref, *refs):
     streams = block[0]
-    operands = refs[1:-3] if chunk else refs[:-3]
+    operands = refs[1:-3] if first else refs[:-3]
     out_ref, wide_ref, sem = refs[-3:]
     section = lax.axis_index("section")
     last = section == lax.axis_size("section") - 1
@@ -284,7 +289,7 @@
             state = jnp.where(section < 2, before_ref[...].astype(F32), state)
         write_output(wide_ref, state, 0, block, frames)
 
-    copy = pltpu.make_async_copy(wide_ref, out_ref.at[pl.ds(chunk * streams, streams)], sem)
+    copy = pltpu.make_async_copy(wide_ref, out_ref.at[pl.ds(first, streams)], sem)
     copy.start()
     copy.wait()
 
@@ -325,8 +330,8 @@
 
 
 ROUTES = {
-    (0, 1): ((1, False), (3, False), (0, False), (2, False)),
-    (1, 2): ((3, True), (2, True), (0, True), (1, True)),
+    (0, 1): ((1, False), (3, False), (2, True), (0, False)),
+    (1, 2): ((1, True), (2, True), (0, True), (3, True)),
     (2, 3): ((0, True), (1, True), (3, False), (2, False)),
 }
 
@@ -406,34 +411,34 @@
     )
     latents = gather_first(latent)
 
-    chunks = 2 if section_count % 2 == 0 else 1
-    per_chunk = section_count // chunks
-    streams = per_chunk * owned
-    block = (streams, unit)
-    state_shape = jax.ShapeDtypeStruct((lat_cols * streams * unit, width), BF16)
+    if section_count == 4:
+        parts = [latents[first:last] for first, last in zip((0,) + CUTS, CUTS + (4,))]
+    elif section_count & (section_count - 1):
+        parts = [latents]
+    else:
+        parts = [latents[:-1], latents[-1:]]
     layer = [unet_weight[0], unet_gain, unet_shift, unet_bias, unet_same]
-    states = [None] * chunks
-    arrived = [None] * chunks
-    for chunk in range(chunks):
-        mine = latents
-        if chunks == 2:
-            cut = len(latents) // 2 if section_count == 4 else -1
-            mine = latents[cut:] if chunk else latents[:cut]
-        operands = mine + [place, in_weight.reshape(-1, width)] + layer
-        states[chunk] = pl.pallas_call(
-            functools.partial(first_kernel, block, frames, len(mine), chunk),
-            out_shape=state_shape,
+    blocks, firsts, states, arrived = [], [], [], []
+    for part in parts:
+        streams = sum(array.shape[0] for array in part)
+        firsts.append(sum(block[0] for block in blocks))
+        blocks.append((streams, unit))
+        operands = part + [place, in_weight.reshape(-1, width)] + layer
+        state = pl.pallas_call(
+            functools.partial(first_kernel, blocks[-1], frames, len(part), firsts[-1]),
+            out_shape=jax.ShapeDtypeStruct((lat_cols * streams * unit, width), BF16),
             in_specs=[vmem()] * len(operands),
             out_specs=vmem(),
             compiler_params=params(),
             name="first_block",
         )(*operands)
-        arrived[chunk] = hop(states[chunk], 0, 1)
+        states.append(state)
+        arrived.append(hop(state, 0, 1))
     for index in range(1, section_count - 1):
-        for chunk in range(chunks):
+        for chunk, block in enumerate(blocks):
             states[chunk] = pl.pallas_call(
                 functools.partial(later_kernel, index, block, frames),
-                out_shape=state_shape,
+                out_shape=jax.ShapeDtypeStruct(states[chunk].shape, BF16),
                 in_specs=[vmem()] * (2 + len(layer)),
                 out_specs=vmem(),
                 input_output_aliases={1: 0},
@@ -444,17 +449,17 @@
     hbm = pl.BlockSpec(memory_space=pltpu.HBM)
     out_shape = jax.ShapeDtypeStruct((section_count * owned, lat_rows, frames, lat_cols * width), BF16)
     out = None
-    for chunk in range(chunks):
+    for chunk, block in enumerate(blocks):
         operands = [arrived[chunk], states[chunk]] + ([out] if chunk else []) + layer
         specs = [vmem()] * len(operands)
         if chunk:
             specs[2] = hbm
         out = pl.pallas_call(
-            functools.partial(last_kernel, block, frames, chunk, crosses()),
+            functools.partial(last_kernel, block, frames, firsts[chunk], crosses()),
             out_shape=out_shape,
             in_specs=specs,
             out_specs=hbm,
-            scratch_shapes=[pltpu.VMEM((streams,) + out_shape.shape[1:], BF16), pltpu.SemaphoreType.DMA],
+            scratch_shapes=[pltpu.VMEM((block[0],) + out_shape.shape[1:], BF16), pltpu.SemaphoreType.DMA],
             input_output_aliases={2: 0} if chunk else {},
             compiler_params=params(),
             name="last_block",

time: 36.2 us -> 35.8 us (0.989)
  waiting for transfers between devices: 14 us -> 13 us
  starting transfers between devices: 14.4 us -> 15.1 us
    ppermute x7 -> x9, starting transfers between devices: 4.86 us -> 9.16 us  [send(): return lax.ppermute(value, ('section', 'slab'), pairs)]
    ppermute x2 -> x0, starting transfers between devices: 3.69 us -> none  [send(): lax.ppermute(value, 'section', [(s, target) for s, (target, _) in enumera...]
    ppermute x2 -> x0, waiting for transfers between devices: 2.29 us -> none  [send(): lax.ppermute(value, 'section', [(s, target) for s, (target, _) in enumera...]
    ppermute x7 -> x9, waiting for transfers between devices: 7.3 us -> 8.47 us  [send(): return lax.ppermute(value, ('section', 'slab'), pairs)]
  transfers between devices with their start and end apart: 14 -> 14, of which waited for: 10 -> 8; matrix products, arithmetic and copies ran while one was open for 2% -> 2% of each run, Pallas kernels for 7% -> 7%
where the time goes in v7:
time: 35.8 us; the launch traced here: 35.5 us
  starting transfers between devices  15.1 us (42%)
  waiting for transfers between devices  13 us (36%)
  Pallas kernels  6.37 us (18%)
  local copies, waits for them, and re-layouts  0.85 us (2%)
    ppermute x9, starting transfers between devices, send(): return lax.ppermute(value, ('section', 'slab'), pairs)  9.16 us
    ppermute x9, waiting for transfers between devices, send(): return lax.ppermute(value, ('section', 'slab'), pairs)  8.47 us
    ppermute x3, starting transfers between devices, exchange(): pieces[step] = lax.ppermute(pieces[step], 'slab', pairs)  4.32 us
    ppermute x3, waiting for transfers between devices, exchange(): pieces[step] = lax.ppermute(pieces[step], 'slab', pairs)  3.81 us
    pallas_call x1, Pallas kernels, exchange(): pl.pallas_call(functools.partial(select_kernel, 'section', 'slab', owned,...  1.81 us
    pallas_call x4, Pallas kernels, per_device(): pl.pallas_call(functools.partial(later_kernel, index, block, frames), out...  1.75 us
    ppermute x2, starting transfers between devices, swap_cores(): lax.ppermute(value, 'slab', [(slab, slab ^ 1) for slab in range(lax.axis_...  1.59 us
    pallas_call x2, Pallas kernels, per_device(): pl.pallas_call(functools.partial(last_kernel, block, frames, firsts[chunk...  1.49 us
  transfers between devices with their start and end apart: 14, of which 8 were waited for; matrix products, arithmetic and copies ran while one was open for 2% of the time, Pallas kernels for 7%

profile of v7, /device:TPU:4, one launch (start us, length us, event | category | flops | bytes accessed | tf_op | source)
XLA Modules:
  0.0 35.5 jit_solution(12847171687983017036)
XLA Ops:
  0.0 1.8 %select.1 = (bf16[4,1,2,2,8,256]{5,4,3,2,1,0:T(8,128)(2,1)}, bf16[4,1,2,2,8,256]{5,4,3,2,1,0:T(8,128)(2,1)}, f32[4,16,320]{2,1,0:T(8,128)}) custom-call(s32[4,8]{1,0:T(4,128)} %clips_ref.1, s32[4,8]{1,0:T(4,128)} %offsets_ref.1, bf16[8,2,2,8,256]{4,3,2,1,0:T(8,128)(2,1)} %bitcast.27, bf16[320,128]{1,0:T(8,128)(2,1)} %bitcast.28, f32[320]{0:T(512)} %bias_ref.1), custom_call_target="tpu_custom_call" | custom-call | tf_op jit(solution)/shard_map/select/pallas_call | solution.py:317
  1.8 0.8 %fusion = (bf16[1,1,2,2,8,256]{5,4,3,2,1,0:T(8,128)(2,1)S(1)}, bf16[1,1,2,2,8,256]{5,4,3,2,1,0:T(8,128)(2,1)S(1)}, bf16[1,1,2,2,8,256]{5,4,3,2,1,0:T(8,128)(2,1)S(1)}, bf16[1,1,2,2,8,256]{5,4,3,2,1,0:T(8,128)(2,1)S(1)}) fusion(bf16[4,1,2,2,8,256]{5,4,3,2,1,0:T(8,128)(2,1)} %get-tuple-element.10), kind=kLoop, calls=%fused_computation.4 | loop fusion | bytes 131072 | tf_op jit(solution)/shard_map/slice | solution.py:325
  2.6 0.7 %collective-permute-done.after_ref = bf16[4,1,2,2,8,256]{5,4,3,2,1,0:T(8,128)(2,1)S(1)} collective-permute-done((bf16[4,1,2,2,8,256]{5,4,3,2,1,0:T(8,128)(2,1)}, bf16[4,1,2,2,8,256]{5,4,3,2,1,0:T(8,128)(2,1)S(1)}, u32[]{:S(2)}, u32[]{:S(2)}) %collective-permute-start) | collective-permute-done | bytes 65568 | tf_op jit(solution)/shard_map/ppermute | solution.py:354
  3.3 2.7 %collective-permute-start.1 = (bf16[2,1,2,2,8,256]{5,4,3,2,1,0:T(8,128)(2,1)S(1)}, bf16[2,1,2,2,8,256]{5,4,3,2,1,0:T(8,128)(2,1)S(1)}, u32[]{:S(2)}, u32[]{:S(2)}) collective-permute-start(bf16[2,1,2,2,8,256]{5,4,3,2,1,0:T(8,128)(2,1)S(1)} %pad_maximum_fusion), channel_id=1, source_target_pairs={{0,4},{1,5},{2,6},{3,7},{4,0},{5,1},{6,2},{7,3},{8,12},{9,13},{10,... | collective-permute-start | bytes 98312 | tf_op jit(solution)/shard_map/ppermute | solution.py:328
  6.0 1.3 %collective-permute-start.2 = (bf16[2,1,2,2,8,256]{5,4,3,2,1,0:T(8,128)(2,1)S(1)}, bf16[2,1,2,2,8,256]{5,4,3,2,1,0:T(8,128)(2,1)S(1)}, u32[]{:S(2)}, u32[]{:S(2)}) collective-permute-start(bf16[2,1,2,2,8,256]{5,4,3,2,1,0:T(8,128)(2,1)S(1)} %pad_maximum_fusion.1), channel_id=1, source_target_pairs={{0,6},{1,7},{2,4},{3,5},{4,2},{5,3},{6,0},{7,1},{8,14},{9,15},{10,... | collective-permute-start | bytes 98312 | tf_op jit(solution)/shard_map/ppermute | solution.py:328
  7.3 0.0 copy-start.10
  7.4 0.0 copy-start.11
  7.4 0.3 collective-permute-start.3
  7.7 0.1 groups.1
  7.8 0.0 copy-start
  7.9 0.6 %collective-permute-done.1.refs_0_ = bf16[2,1,2,2,8,256]{5,4,3,2,1,0:T(8,128)(2,1)S(1)} collective-permute-done((bf16[2,1,2,2,8,256]{5,4,3,2,1,0:T(8,128)(2,1)S(1)}, bf16[2,1,2,2,8,256]{5,4,3,2,1,0:T(8,128)(2,1)S(1)}, u32[]{:S(2)}, u32[]{:S(2)}) %collective-permute-start.1) | collective-permute-done | bytes 32800 | tf_op jit(solution)/shard_map/ppermute | solution.py:328
  8.5 3.2 %collective-permute-done.2.refs_1_ = bf16[2,1,2,2,8,256]{5,4,3,2,1,0:T(8,128)(2,1)S(1)} collective-permute-done((bf16[2,1,2,2,8,256]{5,4,3,2,1,0:T(8,128)(2,1)S(1)}, bf16[2,1,2,2,8,256]{5,4,3,2,1,0:T(8,128)(2,1)S(1)}, u32[]{:S(2)}, u32[]{:S(2)}) %collective-permute-start.2) | collective-permute-done | bytes 32800 | tf_op jit(solution)/shard_map/ppermute | solution.py:328
  11.8 1.2 %encode.1 = bf16[1,64,16]{2,1,0:T(8,128)(2,1)S(1)} custom-call(bf16[2,1,2,2,8,256]{5,4,3,2,1,0:T(8,128)(2,1)S(1)} %collective-permute-done.1.refs_0_, bf16[2,1,2,2,8,256]{5,4,3,2,1,0:T(8,128)(2,1)S(1)} %collective-permute-done.2.refs_1_, bf16[2,1,2,2,8,256]{5,4,3,2,1,0:T(8,128)(2,1)S(1)} %collective-permute-done.3.refs_2_, ...), custom_call_target="tpu_custom_call" | custom-call | tf_op jit(solution)/shard_map/encode/pallas_call | solution.py:142
  12.9 0.1 collective-permute-start.10
  13.0 1.6 %collective-permute-start.9 = (bf16[1,64,16]{2,1,0:T(8,128)(2,1)S(1)}, bf16[1,64,16]{2,1,0:T(8,128)(2,1)S(1)}, u32[]{:S(2)}, u32[]{:S(2)}) collective-permute-start(bf16[1,64,16]{2,1,0:T(8,128)(2,1)S(1)} %encode.1), channel_id=1, source_target_pairs={{0,1},{1,0},{2,3},{3,2},{4,5},{5,4},{6,7},{7,6},{8,9},{9,8},{10,11... | collective-permute-start | bytes 6152 | tf_op jit(solution)/shard_map/ppermute | solution.py:354
  14.6 0.1 collective-permute-start.5
  14.7 1.6 %collective-permute-start.4 = (bf16[1,64,16]{2,1,0:T(8,128)(2,1)S(1)}, bf16[1,64,16]{2,1,0:T(8,128)(2,1)S(1)}, u32[]{:S(2)}, u32[]{:S(2)}) collective-permute-start(bf16[1,64,16]{2,1,0:T(8,128)(2,1)S(1)} %encode.1), channel_id=1, source_target_pairs={{0,17},{1,16},{2,19},{3,18},{4,21},{5,20},{6,23},{7,22},{8,25},{9,... | collective-permute-start | bytes 6152 | tf_op jit(solution)/shard_map/ppermute | solution.py:350
  16.4 0.1 collective-permute-start.11
  16.6 2.2 %collective-permute-done.5.refs_1_ = bf16[1,64,16]{2,1,0:T(8,128)(2,1)S(1)} collective-permute-done((bf16[1,64,16]{2,1,0:T(8,128)(2,1)S(1)}, bf16[1,64,16]{2,1,0:T(8,128)(2,1)S(1)}, u32[]{:S(2)}, u32[]{:S(2)}) %collective-permute-start.5) | collective-permute-done | bytes 2080 | tf_op jit(solution)/shard_map/ppermute | solution.py:350
  18.7 0.1 collective-permute-start.6
  18.8 3.8 %collective-permute-start.12 = (bf16[128,320]{1,0:T(8,128)(2,1)S(1)}, bf16[128,320]{1,0:T(8,128)(2,1)S(1)}, u32[]{:S(2)}, u32[]{:S(2)}) collective-permute-start(bf16[128,320]{1,0:T(8,128)(2,1)S(1)} %later_block.6.kept_ref), channel_id=1, source_target_pairs={{0,9},{1,8},{2,11},{3,10},{4,13},{5,12},{6,15},{7,14},{8,17},{9,16... | collective-permute-start | bytes 245768 | tf_op jit(solution)/shard_map/ppermute | solution.py:350
  22.6 3.2 %collective-permute-start.7 = (bf16[128,320]{1,0:T(8,128)(2,1)S(1)}, bf16[128,320]{1,0:T(8,128)(2,1)S(1)}, u32[]{:S(2)}, u32[]{:S(2)}) collective-permute-start(bf16[128,320]{1,0:T(8,128)(2,1)S(1)} %later_block.4.kept_ref), channel_id=1, source_target_pairs={{0,9},{1,8},{2,11},{3,10},{4,13},{5,12},{6,15},{7,14},{8,17},{9,16... | collective-permute-start | bytes 245768 | tf_op jit(solution)/shard_map/ppermute | solution.py:350
  25.8 0.4 %collective-permute-done.12.before_ref = bf16[128,320]{1,0:T(8,128)(2,1)S(1)} collective-permute-done((bf16[128,320]{1,0:T(8,128)(2,1)S(1)}, bf16[128,320]{1,0:T(8,128)(2,1)S(1)}, u32[]{:S(2)}, u32[]{:S(2)}) %collective-permute-start.12) | collective-permute-done | bytes 81952 | tf_op jit(solution)/shard_map/ppermute | solution.py:350
  26.2 0.9 %later_block.7.kept_ref = bf16[128,320]{1,0:T(8,128)(2,1)S(1)} custom-call(bf16[128,320]{1,0:T(8,128)(2,1)S(1)} %collective-permute-done.12.before_ref, bf16[128,320]{1,0:T(8,128)(2,1)S(1)} %later_block.6.kept_ref, bf16[3,3,320,320]{3,2,1,0:T(8,128)(2,1)S(1)} %bitcast.16, f32[1,320]{1,0:T(1,128)S(1)} %copy-done.4, ...), custom_call_target="tpu_custom_call", output_to_operand_aliasing={{}: (1, {})} | custom-call | tf_op jit(solution)/shard_map/later_block/pallas_call | solution.py:439
  27.1 0.1 collective-permute-start.13
  27.2 1.5 %collective-permute-done.7.before_ref = bf16[128,320]{1,0:T(8,128)(2,1)S(1)} collective-permute-done((bf16[128,320]{1,0:T(8,128)(2,1)S(1)}, bf16[128,320]{1,0:T(8,128)(2,1)S(1)}, u32[]{:S(2)}, u32[]{:S(2)}) %collective-permute-start.7) | collective-permute-done | bytes 81952 | tf_op jit(solution)/shard_map/ppermute | solution.py:350
  28.7 0.9 %later_block.5.kept_ref = bf16[128,320]{1,0:T(8,128)(2,1)S(1)} custom-call(bf16[128,320]{1,0:T(8,128)(2,1)S(1)} %collective-permute-done.7.before_ref, bf16[128,320]{1,0:T(8,128)(2,1)S(1)} %later_block.4.kept_ref, bf16[3,3,320,320]{3,2,1,0:T(8,128)(2,1)S(1)} %bitcast.17, f32[1,320]{1,0:T(1,128)S(1)} %copy-done.4, ...), custom_call_target="tpu_custom_call", output_to_operand_aliasing={{}: (1, {})} | custom-call | tf_op jit(solution)/shard_map/later_block/pallas_call | solution.py:439
  29.6 0.1 collective-permute-start.8
  29.7 2.8 %collective-permute-done.13.before_ref = bf16[128,320]{1,0:T(8,128)(2,1)S(1)} collective-permute-done((bf16[128,320]{1,0:T(8,128)(2,1)S(1)}, bf16[128,320]{1,0:T(8,128)(2,1)S(1)}, u32[]{:S(2)}, u32[]{:S(2)}) %collective-permute-start.13) | collective-permute-done | bytes 81952 | tf_op jit(solution)/shard_map/ppermute | solution.py:350
  32.5 0.7 %last_block.2.refs_0_ = bf16[4,8,2,1280]{3,2,1,0:T(2,128)(2,1)} custom-call(bf16[128,320]{1,0:T(8,128)(2,1)S(1)} %collective-permute-done.13.before_ref, bf16[128,320]{1,0:T(8,128)(2,1)S(1)} %later_block.7.kept_ref, bf16[3,3,320,320]{3,2,1,0:T(8,128)(2,1)S(1)} %bitcast.18, f32[1,320]{1,0:T(1,128)S(1)} %copy-done.4, f32[1,320]{1,0:T(1,128)S(1)} %copy-done.5, ...), custom_call_target="tpu_custom_call" | custom-call | tf_op jit(solution)/shard_map/last_block/pallas_call | solution.py:457
  33.3 1.5 %collective-permute-done.8.before_ref = bf16[128,320]{1,0:T(8,128)(2,1)S(1)} collective-permute-done((bf16[128,320]{1,0:T(8,128)(2,1)S(1)}, bf16[128,320]{1,0:T(8,128)(2,1)S(1)}, u32[]{:S(2)}, u32[]{:S(2)}) %collective-permute-start.8) | collective-permute-done | bytes 81952 | tf_op jit(solution)/shard_map/ppermute | solution.py:350
  34.8 0.7 %last_block.3 = bf16[4,8,2,1280]{3,2,1,0:T(2,128)(2,1)} custom-call(bf16[128,320]{1,0:T(8,128)(2,1)S(1)} %collective-permute-done.8.before_ref, bf16[128,320]{1,0:T(8,128)(2,1)S(1)} %later_block.5.kept_ref, bf16[4,8,2,1280]{3,2,1,0:T(2,128)(2,1)} %last_block.2.refs_0_, bf16[3,3,320,320]{3,2,1,0:T(8,128)(2,1)S(1)} %bitcast.19, ...), custom_call_target="tpu_custom_call", output_to_operand_aliasing={{}: (2, {})} | custom-call | tf_op jit(solution)/shard_map/last_block/pallas_call | solution.py:457
  (37 shorter events, 0.1 us)
Async XLA Ops:
  1.8 1.5 %collective-permute-start = (bf16[4,1,2,2,8,256]{5,4,3,2,1,0:T(8,128)(2,1)}, bf16[4,1,2,2,8,256]{5,4,3,2,1,0:T(8,128)(2,1)S(1)}, u32[]{:S(2)}, u32[]{:S(2)}) collective-permute-start(bf16[4,1,2,2,8,256]{5,4,3,2,1,0:T(8,128)(2,1)} %get-tuple-element.11), channel_id=1, source_target_pairs={{0,1},{1,0},{2,3},{3,2},{4,5},{5,4},{6,7},{7,6},{8,9},{9,8},{10,11... | collective-permute-start | bytes 196616 | tf_op jit(solution)/shard_map/ppermute | solution.py:354
  3.3 5.2 %collective-permute-start.1 = (bf16[2,1,2,2,8,256]{5,4,3,2,1,0:T(8,128)(2,1)S(1)}, bf16[2,1,2,2,8,256]{5,4,3,2,1,0:T(8,128)(2,1)S(1)}, u32[]{:S(2)}, u32[]{:S(2)}) collective-permute-start(bf16[2,1,2,2,8,256]{5,4,3,2,1,0:T(8,128)(2,1)S(1)} %pad_maximum_fusion), channel_id=1, source_target_pairs={{0,4},{1,5},{2,6},{3,7},{4,0},{5,1},{6,2},{7,3},{8,12},{9,13},{10,... | collective-permute-start | bytes 98312 | tf_op jit(solution)/shard_map/ppermute | solution.py:328
  6.0 5.7 %collective-permute-start.2 = (bf16[2,1,2,2,8,256]{5,4,3,2,1,0:T(8,128)(2,1)S(1)}, bf16[2,1,2,2,8,256]{5,4,3,2,1,0:T(8,128)(2,1)S(1)}, u32[]{:S(2)}, u32[]{:S(2)}) collective-permute-start(bf16[2,1,2,2,8,256]{5,4,3,2,1,0:T(8,128)(2,1)S(1)} %pad_maximum_fusion.1), channel_id=1, source_target_pairs={{0,6},{1,7},{2,4},{3,5},{4,2},{5,3},{6,0},{7,1},{8,14},{9,15},{10,... | collective-permute-start | bytes 98312 | tf_op jit(solution)/shard_map/ppermute | solution.py:328
  7.3 4.4 %copy-start.1 = (bf16[3,3,3,256,256]{4,3,2,1,0:T(8,128)(2,1)S(1)}, bf16[3,3,3,256,256]{4,3,2,1,0:T(8,128)(2,1)}, u32[]{:S(2)}) copy-start(bf16[3,3,3,256,256]{4,3,2,1,0:T(8,128)(2,1)} %refs_4_.2) | copy-start | bytes 10616836
  7.3 4.4 %copy-start.7 = (bf16[256,16]{0,1:T(8,128)(2,1)S(1)}, bf16[256,16]{0,1:T(8,128)(2,1)}, u32[]{:S(2)}) copy-start(bf16[256,16]{0,1:T(8,128)(2,1)} %param.21) | copy-start | bytes 24580
  7.3 4.4 %copy-start.8 = (f32[256]{0:T(256)S(1)}, f32[256]{0:T(256)}, u32[]{:S(2)}) copy-start(f32[256]{0:T(256)} %param.18) | copy-start | bytes 3076
  7.3 4.4 %copy-start.9 = (f32[256]{0:T(256)S(1)}, f32[256]{0:T(256)}, u32[]{:S(2)}) copy-start(f32[256]{0:T(256)} %param.19) | copy-start | bytes 3076
  7.3 4.4 %copy-start.10 = (f32[256]{0:T(256)S(1)}, f32[256]{0:T(256)}, u32[]{:S(2)}) copy-start(f32[256]{0:T(256)} %param.20) | copy-start | bytes 3076
  7.4 4.4 %copy-start.11 = (f32[16]{0:T(128)S(1)}, f32[16]{0:T(128)}, u32[]{:S(2)}) copy-start(f32[16]{0:T(128)} %param.22) | copy-start | bytes 196
  7.4 4.3 %collective-permute-start.3 = (bf16[2,1,2,2,8,256]{5,4,3,2,1,0:T(8,128)(2,1)S(1)}, bf16[2,1,2,2,8,256]{5,4,3,2,1,0:T(8,128)(2,1)S(1)}, u32[]{:S(2)}, u32[]{:S(2)}) collective-permute-start(bf16[2,1,2,2,8,256]{5,4,3,2,1,0:T(8,128)(2,1)S(1)} %pad_maximum_fusion.2), channel_id=1, source_target_pairs={{0,2},{1,3},{2,0},{3,1},{4,6},{5,7},{6,4},{7,5},{8,10},{9,11},{10,... | collective-permute-start | bytes 98312 | tf_op jit(solution)/shard_map/ppermute | solution.py:328
  7.8 8.5 %copy-start = (bf16[1,3,3,320,320]{4,3,2,1,0:T(8,128)(2,1)S(1)}, bf16[1,3,3,320,320]{4,3,2,1,0:T(8,128)(2,1)}, u32[]{:S(2)}) copy-start(bf16[1,3,3,320,320]{4,3,2,1,0:T(8,128)(2,1)} %param.30) | copy-start | bytes 5529604
  7.8 8.5 %copy-start.2 = (bf16[3,3,16,320]{3,2,1,0:T(8,128)(2,1)S(1)}, bf16[3,3,16,320]{3,2,1,0:T(8,128)(2,1)}, u32[]{:S(2)}) copy-start(bf16[3,3,16,320]{3,2,1,0:T(8,128)(2,1)} %param.25) | copy-start | bytes 276484
  7.8 8.5 %copy-start.3 = (f32[4,16,320]{2,1,0:T(8,128)S(1)}, f32[4,16,320]{2,1,0:T(8,128)}, u32[]{:S(2)}) copy-start(f32[4,16,320]{2,1,0:T(8,128)} %get-tuple-element.13.refs_2_) | copy-start | bytes 245764
  7.8 8.5 %copy-start.4 = (f32[1,320]{1,0:T(1,128)S(1)}, f32[1,320]{1,0:T(1,128)}, u32[]{:S(2)}) copy-start(f32[1,320]{1,0:T(1,128)} %refs_2_.11) | copy-start | bytes 3844
  7.8 8.5 %copy-start.5 = (f32[1,320]{1,0:T(1,128)S(1)}, f32[1,320]{1,0:T(1,128)}, u32[]{:S(2)}) copy-start(f32[1,320]{1,0:T(1,128)} %refs_3_.11) | copy-start | bytes 3844
  7.9 8.5 %copy-start.6 = (f32[1,320]{1,0:T(1,128)S(1)}, f32[1,320]{1,0:T(1,128)}, u32[]{:S(2)}) copy-start(f32[1,320]{1,0:T(1,128)} %refs_4_.3) | copy-start | bytes 3844
  12.9 3.4 %collective-permute-start.10 = (bf16[1,64,16]{2,1,0:T(8,128)(2,1)S(1)}, bf16[1,64,16]{2,1,0:T(8,128)(2,1)S(1)}, u32[]{:S(2)}, u32[]{:S(2)}) collective-permute-start(bf16[1,64,16]{2,1,0:T(8,128)(2,1)S(1)} %encode.1), channel_id=1, source_target_pairs={{0,9},{1,8},{2,11},{3,10},{4,13},{5,12},{6,15},{7,14},{8,1},{9,0},... | collective-permute-start | bytes 6152 | tf_op jit(solution)/shard_map/ppermute | solution.py:350
  13.0 3.3 %collective-permute-start.9 = (bf16[1,64,16]{2,1,0:T(8,128)(2,1)S(1)}, bf16[1,64,16]{2,1,0:T(8,128)(2,1)S(1)}, u32[]{:S(2)}, u32[]{:S(2)}) collective-permute-start(bf16[1,64,16]{2,1,0:T(8,128)(2,1)S(1)} %encode.1), channel_id=1, source_target_pairs={{0,1},{1,0},{2,3},{3,2},{4,5},{5,4},{6,7},{7,6},{8,9},{9,8},{10,11... | collective-permute-start | bytes 6152 | tf_op jit(solution)/shard_map/ppermute | solution.py:354
  14.6 4.1 %collective-permute-start.5 = (bf16[1,64,16]{2,1,0:T(8,128)(2,1)S(1)}, bf16[1,64,16]{2,1,0:T(8,128)(2,1)S(1)}, u32[]{:S(2)}, u32[]{:S(2)}) collective-permute-start(bf16[1,64,16]{2,1,0:T(8,128)(2,1)S(1)} %encode.1), channel_id=1, source_target_pairs={{0,25},{1,24},{2,27},{3,26},{4,29},{5,28},{6,31},{7,30},{8,17},{9,... | collective-permute-start | bytes 6152 | tf_op jit(solution)/shard_map/ppermute | solution.py:350
  14.7 4.0 %collective-permute-start.4 = (bf16[1,64,16]{2,1,0:T(8,128)(2,1)S(1)}, bf16[1,64,16]{2,1,0:T(8,128)(2,1)S(1)}, u32[]{:S(2)}, u32[]{:S(2)}) collective-permute-start(bf16[1,64,16]{2,1,0:T(8,128)(2,1)S(1)} %encode.1), channel_id=1, source_target_pairs={{0,17},{1,16},{2,19},{3,18},{4,21},{5,20},{6,23},{7,22},{8,25},{9,... | collective-permute-start | bytes 6152 | tf_op jit(solution)/shard_map/ppermute | solution.py:350
  16.4 2.4 %collective-permute-start.11 = (bf16[128,320]{1,0:T(8,128)(2,1)S(1)}, bf16[128,320]{1,0:T(8,128)(2,1)S(1)}, u32[]{:S(2)}, u32[]{:S(2)}) collective-permute-start(bf16[128,320]{1,0:T(8,128)(2,1)S(1)} %first_block.3.kept_ref), channel_id=1, source_target_pairs={{0,8},{1,9},{2,10},{3,11},{4,12},{5,13},{6,14},{7,15},{8,24},{9,25... | collective-permute-start | bytes 245768 | tf_op jit(solution)/shard_map/ppermute | solution.py:350
  18.7 3.9 %collective-permute-start.6 = (bf16[128,320]{1,0:T(8,128)(2,1)S(1)}, bf16[128,320]{1,0:T(8,128)(2,1)S(1)}, u32[]{:S(2)}, u32[]{:S(2)}) collective-permute-start(bf16[128,320]{1,0:T(8,128)(2,1)S(1)} %first_block.2.kept_ref), channel_id=1, source_target_pairs={{0,8},{1,9},{2,10},{3,11},{4,12},{5,13},{6,14},{7,15},{8,24},{9,25... | collective-permute-start | bytes 245768 | tf_op jit(solution)/shard_map/ppermute | solution.py:350
  18.8 7.4 %collective-permute-start.12 = (bf16[128,320]{1,0:T(8,128)(2,1)S(1)}, bf16[128,320]{1,0:T(8,128)(2,1)S(1)}, u32[]{:S(2)}, u32[]{:S(2)}) collective-permute-start(bf16[128,320]{1,0:T(8,128)(2,1)S(1)} %later_block.6.kept_ref), channel_id=1, source_target_pairs={{0,9},{1,8},{2,11},{3,10},{4,13},{5,12},{6,15},{7,14},{8,17},{9,16... | collective-permute-start | bytes 245768 | tf_op jit(solution)/shard_map/ppermute | solution.py:350
  22.6 6.1 %collective-permute-start.7 = (bf16[128,320]{1,0:T(8,128)(2,1)S(1)}, bf16[128,320]{1,0:T(8,128)(2,1)S(1)}, u32[]{:S(2)}, u32[]{:S(2)}) collective-permute-start(bf16[128,320]{1,0:T(8,128)(2,1)S(1)} %later_block.4.kept_ref), channel_id=1, source_target_pairs={{0,9},{1,8},{2,11},{3,10},{4,13},{5,12},{6,15},{7,14},{8,17},{9,16... | collective-permute-start | bytes 245768 | tf_op jit(solution)/shard_map/ppermute | solution.py:350
  27.1 5.4 %collective-permute-start.13 = (bf16[128,320]{1,0:T(8,128)(2,1)S(1)}, bf16[128,320]{1,0:T(8,128)(2,1)S(1)}, u32[]{:S(2)}, u32[]{:S(2)}) collective-permute-start(bf16[128,320]{1,0:T(8,128)(2,1)S(1)} %later_block.7.kept_ref), channel_id=1, source_target_pairs={{0,1},{1,0},{2,3},{3,2},{4,5},{5,4},{6,7},{7,6},{8,9},{9,8},{10,11... | collective-permute-start | bytes 245768 | tf_op jit(solution)/shard_map/ppermute | solution.py:350
  29.6 5.2 %collective-permute-start.8 = (bf16[128,320]{1,0:T(8,128)(2,1)S(1)}, bf16[128,320]{1,0:T(8,128)(2,1)S(1)}, u32[]{:S(2)}, u32[]{:S(2)}) collective-permute-start(bf16[128,320]{1,0:T(8,128)(2,1)S(1)} %later_block.5.kept_ref), channel_id=1, source_target_pairs={{0,1},{1,0},{2,3},{3,2},{4,5},{5,4},{6,7},{7,6},{8,9},{9,8},{10,11... | collective-permute-start | bytes 245768 | tf_op jit(solution)/shard_map/ppermute | solution.py:350

commit v8 on v7

--- a/solution.py
+++ b/solution.py
@@ -75,7 +75,7 @@
     items, frames, row_count, cols, channels = x_ref.shape
     for step, piece_ref in zip(piece_order(len(pieces)), pieces):
         for half in range(2):
-            source = lax.axis_index(slab_axis) ^ (2 * step + half)
+            source = lax.axis_index(slab_axis) ^ (2 * step + (half if step == 0 else 1 - half))
             for item in range(items):
                 for frame in range(frames):
                     piece = piece_ref[half, item, :, frame].astype(F32)
@@ -303,7 +303,8 @@
     for step in range(keep_ref.shape[0]):
         for half, out_ref in enumerate((keep_ref, give_ref)):
             for item in range(owned):
-                slot = (slab ^ (2 * step + half)) * owned + item
+                other = half if step == 0 else 1 - half
+                slot = (slab ^ (2 * step + other)) * owned + item
                 out_ref[step, item] = features_ref[clips_ref[section, slot]]
     bias = bias_ref[...].reshape(1, -1)
     frames = features_ref.shape[2]
@@ -324,7 +325,7 @@
     got = swap_cores(give)
     pieces = [jnp.stack([keep[step], got[step]]) for step in range(steps)]
     for step in range(1, steps):
-        pairs = [(slab, slab ^ (2 * step)) for slab in range(slab_count)]
+        pairs = [(slab, slab ^ (2 * step + 1)) for slab in range(slab_count)]
         pieces[step] = lax.ppermute(pieces[step], "slab", pairs)
     return pieces, got, place
 

time: 35.8 us -> 35.2 us (0.983)
  waiting for transfers between devices: 13 us -> 12.4 us
    ppermute x9, starting transfers between devices: 9.16 us -> 10.7 us  [send(): return lax.ppermute(value, ('section', 'slab'), pairs)]
    ppermute x2, starting transfers between devices: 1.59 us -> 0.17 us  [swap_cores(): lax.ppermute(value, 'slab', [(slab, slab ^ 1) for slab in range(lax.axis_...]
    ppermute x3, waiting for transfers between devices: 3.81 us -> 3.39 us  [exchange(): pieces[step] = lax.ppermute(pieces[step], 'slab', pairs)]
  transfers between devices with their start and end apart: 14 -> 14, of which waited for: 8 -> 7; matrix products, arithmetic and copies ran while one was open for 2% -> 2% of each run, Pallas kernels for 7% -> 8%
where the time goes in v8:
time: 35.2 us; the launch traced here: 34.8 us
  starting transfers between devices  14.9 us (42%)
  waiting for transfers between devices  12.4 us (35%)
  Pallas kernels  6.37 us (18%)
  local copies, waits for them, and re-layouts  0.85 us (2%)
    ppermute x9, starting transfers between devices, send(): return lax.ppermute(value, ('section', 'slab'), pairs)  10.7 us
    ppermute x9, waiting for transfers between devices, send(): return lax.ppermute(value, ('section', 'slab'), pairs)  8.33 us
    ppermute x3, starting transfers between devices, exchange(): pieces[step] = lax.ppermute(pieces[step], 'slab', pairs)  4.04 us
    ppermute x3, waiting for transfers between devices, exchange(): pieces[step] = lax.ppermute(pieces[step], 'slab', pairs)  3.39 us
    pallas_call x1, Pallas kernels, exchange(): pl.pallas_call(functools.partial(select_kernel, 'section', 'slab', owned,...  1.81 us
    pallas_call x4, Pallas kernels, per_device(): pl.pallas_call(functools.partial(later_kernel, index, block, frames), out...  1.75 us
    pallas_call x2, Pallas kernels, per_device(): pl.pallas_call(functools.partial(last_kernel, block, frames, firsts[chunk...  1.49 us
    pallas_call x1, Pallas kernels, encode(): pl.pallas_call(functools.partial(encode_kernel, 'slab'), out_shape=jax.Sh...  1.19 us
  transfers between devices with their start and end apart: 14, of which 7 were waited for; matrix products, arithmetic and copies ran while one was open for 2% of the time, Pallas kernels for 8%

profile of v8, /device:TPU:4, one launch (start us, length us, event | category | flops | bytes accessed | tf_op | source)
XLA Modules:
  0.0 34.8 jit_solution(15964234664961787267)
XLA Ops:
  0.0 1.8 %select.1 = (bf16[4,1,2,2,8,256]{5,4,3,2,1,0:T(8,128)(2,1)}, bf16[4,1,2,2,8,256]{5,4,3,2,1,0:T(8,128)(2,1)}, f32[4,16,320]{2,1,0:T(8,128)}) custom-call(s32[4,8]{1,0:T(4,128)} %clips_ref.1, s32[4,8]{1,0:T(4,128)} %offsets_ref.1, bf16[8,2,2,8,256]{4,3,2,1,0:T(8,128)(2,1)} %bitcast.27, bf16[320,128]{1,0:T(8,128)(2,1)} %bitcast.28, f32[320]{0:T(512)} %bias_ref.1), custom_call_target="tpu_custom_call" | custom-call | tf_op jit(solution)/shard_map/select/pallas_call | solution.py:318
  1.8 0.8 %fusion = (bf16[1,1,2,2,8,256]{5,4,3,2,1,0:T(8,128)(2,1)S(1)}, bf16[1,1,2,2,8,256]{5,4,3,2,1,0:T(8,128)(2,1)S(1)}, bf16[1,1,2,2,8,256]{5,4,3,2,1,0:T(8,128)(2,1)S(1)}, bf16[1,1,2,2,8,256]{5,4,3,2,1,0:T(8,128)(2,1)S(1)}) fusion(bf16[4,1,2,2,8,256]{5,4,3,2,1,0:T(8,128)(2,1)} %get-tuple-element.10), kind=kLoop, calls=%fused_computation.4 | loop fusion | bytes 131072 | tf_op jit(solution)/shard_map/slice | solution.py:326
  2.6 0.7 %collective-permute-done.after_ref = bf16[4,1,2,2,8,256]{5,4,3,2,1,0:T(8,128)(2,1)S(1)} collective-permute-done((bf16[4,1,2,2,8,256]{5,4,3,2,1,0:T(8,128)(2,1)}, bf16[4,1,2,2,8,256]{5,4,3,2,1,0:T(8,128)(2,1)S(1)}, u32[]{:S(2)}, u32[]{:S(2)}) %collective-permute-start) | collective-permute-done | bytes 65568 | tf_op jit(solution)/shard_map/ppermute | solution.py:355
  3.3 2.4 %collective-permute-start.1 = (bf16[2,1,2,2,8,256]{5,4,3,2,1,0:T(8,128)(2,1)S(1)}, bf16[2,1,2,2,8,256]{5,4,3,2,1,0:T(8,128)(2,1)S(1)}, u32[]{:S(2)}, u32[]{:S(2)}) collective-permute-start(bf16[2,1,2,2,8,256]{5,4,3,2,1,0:T(8,128)(2,1)S(1)} %pad_maximum_fusion), channel_id=1, source_target_pairs={{0,5},{1,4},{2,7},{3,6},{4,1},{5,0},{6,3},{7,2},{8,13},{9,12},{10,... | collective-permute-start | bytes 98312 | tf_op jit(solution)/shard_map/ppermute | solution.py:329
  5.7 1.3 %collective-permute-start.2 = (bf16[2,1,2,2,8,256]{5,4,3,2,1,0:T(8,128)(2,1)S(1)}, bf16[2,1,2,2,8,256]{5,4,3,2,1,0:T(8,128)(2,1)S(1)}, u32[]{:S(2)}, u32[]{:S(2)}) collective-permute-start(bf16[2,1,2,2,8,256]{5,4,3,2,1,0:T(8,128)(2,1)S(1)} %pad_maximum_fusion.1), channel_id=1, source_target_pairs={{0,7},{1,6},{2,5},{3,4},{4,3},{5,2},{6,1},{7,0},{8,15},{9,14},{10,... | collective-permute-start | bytes 98312 | tf_op jit(solution)/shard_map/ppermute | solution.py:329
  7.1 0.0 copy-start.9
  7.1 0.0 copy-start.10
  7.1 0.3 collective-permute-start.3
  7.4 0.1 groups.1
  7.5 0.0 copy-start
  7.6 0.0 copy-start.4
  7.6 3.4 %collective-permute-done.2.refs_1_ = bf16[2,1,2,2,8,256]{5,4,3,2,1,0:T(8,128)(2,1)S(1)} collective-permute-done((bf16[2,1,2,2,8,256]{5,4,3,2,1,0:T(8,128)(2,1)S(1)}, bf16[2,1,2,2,8,256]{5,4,3,2,1,0:T(8,128)(2,1)S(1)}, u32[]{:S(2)}, u32[]{:S(2)}) %collective-permute-start.2) | collective-permute-done | bytes 32800 | tf_op jit(solution)/shard_map/ppermute | solution.py:329
  11.0 1.2 %encode.1 = bf16[1,64,16]{2,1,0:T(8,128)(2,1)S(1)} custom-call(bf16[2,1,2,2,8,256]{5,4,3,2,1,0:T(8,128)(2,1)S(1)} %collective-permute-done.1.refs_0_, bf16[2,1,2,2,8,256]{5,4,3,2,1,0:T(8,128)(2,1)S(1)} %collective-permute-done.2.refs_1_, bf16[2,1,2,2,8,256]{5,4,3,2,1,0:T(8,128)(2,1)S(1)} %collective-permute-done.3.refs_2_, ...), custom_call_target="tpu_custom_call" | custom-call | tf_op jit(solution)/shard_map/encode/pallas_call | solution.py:142
  12.2 1.5 %collective-permute-start.10 = (bf16[1,64,16]{2,1,0:T(8,128)(2,1)S(1)}, bf16[1,64,16]{2,1,0:T(8,128)(2,1)S(1)}, u32[]{:S(2)}, u32[]{:S(2)}) collective-permute-start(bf16[1,64,16]{2,1,0:T(8,128)(2,1)S(1)} %encode.1), channel_id=1, source_target_pairs={{0,9},{1,8},{2,11},{3,10},{4,13},{5,12},{6,15},{7,14},{8,1},{9,0},... | collective-permute-start | bytes 6152 | tf_op jit(solution)/shard_map/ppermute | solution.py:351
  13.8 0.2 collective-permute-start.9
  13.9 0.4 %collective-permute-start.5 = (bf16[1,64,16]{2,1,0:T(8,128)(2,1)S(1)}, bf16[1,64,16]{2,1,0:T(8,128)(2,1)S(1)}, u32[]{:S(2)}, u32[]{:S(2)}) collective-permute-start(bf16[1,64,16]{2,1,0:T(8,128)(2,1)S(1)} %encode.1), channel_id=1, source_target_pairs={{0,25},{1,24},{2,27},{3,26},{4,29},{5,28},{6,31},{7,30},{8,17},{9,... | collective-permute-start | bytes 6152 | tf_op jit(solution)/shard_map/ppermute | solution.py:351
  14.4 1.3 %collective-permute-start.4 = (bf16[1,64,16]{2,1,0:T(8,128)(2,1)S(1)}, bf16[1,64,16]{2,1,0:T(8,128)(2,1)S(1)}, u32[]{:S(2)}, u32[]{:S(2)}) collective-permute-start(bf16[1,64,16]{2,1,0:T(8,128)(2,1)S(1)} %encode.1), channel_id=1, source_target_pairs={{0,17},{1,16},{2,19},{3,18},{4,21},{5,20},{6,23},{7,22},{8,25},{9,... | collective-permute-start | bytes 6152 | tf_op jit(solution)/shard_map/ppermute | solution.py:351
  15.7 0.4 %collective-permute-start.11 = (bf16[128,320]{1,0:T(8,128)(2,1)S(1)}, bf16[128,320]{1,0:T(8,128)(2,1)S(1)}, u32[]{:S(2)}, u32[]{:S(2)}) collective-permute-start(bf16[128,320]{1,0:T(8,128)(2,1)S(1)} %first_block.3.kept_ref), channel_id=1, source_target_pairs={{0,8},{1,9},{2,10},{3,11},{4,12},{5,13},{6,14},{7,15},{8,24},{9,25... | collective-permute-start | bytes 245768 | tf_op jit(solution)/shard_map/ppermute | solution.py:351
  16.1 1.9 %collective-permute-done.5.refs_1_ = bf16[1,64,16]{2,1,0:T(8,128)(2,1)S(1)} collective-permute-done((bf16[1,64,16]{2,1,0:T(8,128)(2,1)S(1)}, bf16[1,64,16]{2,1,0:T(8,128)(2,1)S(1)}, u32[]{:S(2)}, u32[]{:S(2)}) %collective-permute-start.5) | collective-permute-done | bytes 2080 | tf_op jit(solution)/shard_map/ppermute | solution.py:351
  18.0 0.3 collective-permute-start.6
  18.3 4.2 %collective-permute-start.12 = (bf16[128,320]{1,0:T(8,128)(2,1)S(1)}, bf16[128,320]{1,0:T(8,128)(2,1)S(1)}, u32[]{:S(2)}, u32[]{:S(2)}) collective-permute-start(bf16[128,320]{1,0:T(8,128)(2,1)S(1)} %later_block.6.kept_ref), channel_id=1, source_target_pairs={{0,9},{1,8},{2,11},{3,10},{4,13},{5,12},{6,15},{7,14},{8,17},{9,16... | collective-permute-start | bytes 245768 | tf_op jit(solution)/shard_map/ppermute | solution.py:351
  22.5 2.5 %collective-permute-start.7 = (bf16[128,320]{1,0:T(8,128)(2,1)S(1)}, bf16[128,320]{1,0:T(8,128)(2,1)S(1)}, u32[]{:S(2)}, u32[]{:S(2)}) collective-permute-start(bf16[128,320]{1,0:T(8,128)(2,1)S(1)} %later_block.4.kept_ref), channel_id=1, source_target_pairs={{0,9},{1,8},{2,11},{3,10},{4,13},{5,12},{6,15},{7,14},{8,17},{9,16... | collective-permute-start | bytes 245768 | tf_op jit(solution)/shard_map/ppermute | solution.py:351
  25.0 0.5 %collective-permute-done.12.before_ref = bf16[128,320]{1,0:T(8,128)(2,1)S(1)} collective-permute-done((bf16[128,320]{1,0:T(8,128)(2,1)S(1)}, bf16[128,320]{1,0:T(8,128)(2,1)S(1)}, u32[]{:S(2)}, u32[]{:S(2)}) %collective-permute-start.12) | collective-permute-done | bytes 81952 | tf_op jit(solution)/shard_map/ppermute | solution.py:351
  25.5 0.9 %later_block.7.kept_ref = bf16[128,320]{1,0:T(8,128)(2,1)S(1)} custom-call(bf16[128,320]{1,0:T(8,128)(2,1)S(1)} %collective-permute-done.12.before_ref, bf16[128,320]{1,0:T(8,128)(2,1)S(1)} %later_block.6.kept_ref, bf16[3,3,320,320]{3,2,1,0:T(8,128)(2,1)S(1)} %bitcast.16, f32[1,320]{1,0:T(1,128)S(1)} %copy-done.4, ...), custom_call_target="tpu_custom_call", output_to_operand_aliasing={{}: (1, {})} | custom-call | tf_op jit(solution)/shard_map/later_block/pallas_call | solution.py:440
  26.4 0.1 collective-permute-start.13
  26.4 1.3 %collective-permute-done.7.before_ref = bf16[128,320]{1,0:T(8,128)(2,1)S(1)} collective-permute-done((bf16[128,320]{1,0:T(8,128)(2,1)S(1)}, bf16[128,320]{1,0:T(8,128)(2,1)S(1)}, u32[]{:S(2)}, u32[]{:S(2)}) %collective-permute-start.7) | collective-permute-done | bytes 81952 | tf_op jit(solution)/shard_map/ppermute | solution.py:351
  27.7 0.9 %later_block.5.kept_ref = bf16[128,320]{1,0:T(8,128)(2,1)S(1)} custom-call(bf16[128,320]{1,0:T(8,128)(2,1)S(1)} %collective-permute-done.7.before_ref, bf16[128,320]{1,0:T(8,128)(2,1)S(1)} %later_block.4.kept_ref, bf16[3,3,320,320]{3,2,1,0:T(8,128)(2,1)S(1)} %bitcast.17, f32[1,320]{1,0:T(1,128)S(1)} %copy-done.4, ...), custom_call_target="tpu_custom_call", output_to_operand_aliasing={{}: (1, {})} | custom-call | tf_op jit(solution)/shard_map/later_block/pallas_call | solution.py:440
  28.6 0.1 collective-permute-start.8
  28.7 3.2 %collective-permute-done.13.before_ref = bf16[128,320]{1,0:T(8,128)(2,1)S(1)} collective-permute-done((bf16[128,320]{1,0:T(8,128)(2,1)S(1)}, bf16[128,320]{1,0:T(8,128)(2,1)S(1)}, u32[]{:S(2)}, u32[]{:S(2)}) %collective-permute-start.13) | collective-permute-done | bytes 81952 | tf_op jit(solution)/shard_map/ppermute | solution.py:351
  31.9 0.7 %last_block.2.refs_0_ = bf16[4,8,2,1280]{3,2,1,0:T(2,128)(2,1)} custom-call(bf16[128,320]{1,0:T(8,128)(2,1)S(1)} %collective-permute-done.13.before_ref, bf16[128,320]{1,0:T(8,128)(2,1)S(1)} %later_block.7.kept_ref, bf16[3,3,320,320]{3,2,1,0:T(8,128)(2,1)S(1)} %bitcast.18, f32[1,320]{1,0:T(1,128)S(1)} %copy-done.4, f32[1,320]{1,0:T(1,128)S(1)} %copy-done.5, ...), custom_call_target="tpu_custom_call" | custom-call | tf_op jit(solution)/shard_map/last_block/pallas_call | solution.py:458
  32.6 1.4 %collective-permute-done.8.before_ref = bf16[128,320]{1,0:T(8,128)(2,1)S(1)} collective-permute-done((bf16[128,320]{1,0:T(8,128)(2,1)S(1)}, bf16[128,320]{1,0:T(8,128)(2,1)S(1)}, u32[]{:S(2)}, u32[]{:S(2)}) %collective-permute-start.8) | collective-permute-done | bytes 81952 | tf_op jit(solution)/shard_map/ppermute | solution.py:351
  34.1 0.7 %last_block.3 = bf16[4,8,2,1280]{3,2,1,0:T(2,128)(2,1)} custom-call(bf16[128,320]{1,0:T(8,128)(2,1)S(1)} %collective-permute-done.8.before_ref, bf16[128,320]{1,0:T(8,128)(2,1)S(1)} %later_block.5.kept_ref, bf16[4,8,2,1280]{3,2,1,0:T(2,128)(2,1)} %last_block.2.refs_0_, bf16[3,3,320,320]{3,2,1,0:T(8,128)(2,1)S(1)} %bitcast.19, ...), custom_call_target="tpu_custom_call", output_to_operand_aliasing={{}: (2, {})} | custom-call | tf_op jit(solution)/shard_map/last_block/pallas_call | solution.py:458
  (37 shorter events, 0.1 us)
Async XLA Ops:
  1.8 1.5 %collective-permute-start = (bf16[4,1,2,2,8,256]{5,4,3,2,1,0:T(8,128)(2,1)}, bf16[4,1,2,2,8,256]{5,4,3,2,1,0:T(8,128)(2,1)S(1)}, u32[]{:S(2)}, u32[]{:S(2)}) collective-permute-start(bf16[4,1,2,2,8,256]{5,4,3,2,1,0:T(8,128)(2,1)} %get-tuple-element.11), channel_id=1, source_target_pairs={{0,1},{1,0},{2,3},{3,2},{4,5},{5,4},{6,7},{7,6},{8,9},{9,8},{10,11... | collective-permute-start | bytes 196616 | tf_op jit(solution)/shard_map/ppermute | solution.py:355
  3.3 4.3 %collective-permute-start.1 = (bf16[2,1,2,2,8,256]{5,4,3,2,1,0:T(8,128)(2,1)S(1)}, bf16[2,1,2,2,8,256]{5,4,3,2,1,0:T(8,128)(2,1)S(1)}, u32[]{:S(2)}, u32[]{:S(2)}) collective-permute-start(bf16[2,1,2,2,8,256]{5,4,3,2,1,0:T(8,128)(2,1)S(1)} %pad_maximum_fusion), channel_id=1, source_target_pairs={{0,5},{1,4},{2,7},{3,6},{4,1},{5,0},{6,3},{7,2},{8,13},{9,12},{10,... | collective-permute-start | bytes 98312 | tf_op jit(solution)/shard_map/ppermute | solution.py:329
  5.7 5.3 %collective-permute-start.2 = (bf16[2,1,2,2,8,256]{5,4,3,2,1,0:T(8,128)(2,1)S(1)}, bf16[2,1,2,2,8,256]{5,4,3,2,1,0:T(8,128)(2,1)S(1)}, u32[]{:S(2)}, u32[]{:S(2)}) collective-permute-start(bf16[2,1,2,2,8,256]{5,4,3,2,1,0:T(8,128)(2,1)S(1)} %pad_maximum_fusion.1), channel_id=1, source_target_pairs={{0,7},{1,6},{2,5},{3,4},{4,3},{5,2},{6,1},{7,0},{8,15},{9,14},{10,... | collective-permute-start | bytes 98312 | tf_op jit(solution)/shard_map/ppermute | solution.py:329
  7.0 4.0 %copy-start.1 = (bf16[3,3,3,256,256]{4,3,2,1,0:T(8,128)(2,1)S(1)}, bf16[3,3,3,256,256]{4,3,2,1,0:T(8,128)(2,1)}, u32[]{:S(2)}) copy-start(bf16[3,3,3,256,256]{4,3,2,1,0:T(8,128)(2,1)} %refs_4_.2) | copy-start | bytes 10616836
  7.0 4.0 %copy-start.7 = (bf16[256,16]{0,1:T(8,128)(2,1)S(1)}, bf16[256,16]{0,1:T(8,128)(2,1)}, u32[]{:S(2)}) copy-start(bf16[256,16]{0,1:T(8,128)(2,1)} %param.21) | copy-start | bytes 24580
  7.0 4.0 %copy-start.8 = (f32[256]{0:T(256)S(1)}, f32[256]{0:T(256)}, u32[]{:S(2)}) copy-start(f32[256]{0:T(256)} %param.18) | copy-start | bytes 3076
  7.1 4.0 %copy-start.9 = (f32[256]{0:T(256)S(1)}, f32[256]{0:T(256)}, u32[]{:S(2)}) copy-start(f32[256]{0:T(256)} %param.19) | copy-start | bytes 3076
  7.1 4.0 %copy-start.10 = (f32[256]{0:T(256)S(1)}, f32[256]{0:T(256)}, u32[]{:S(2)}) copy-start(f32[256]{0:T(256)} %param.20) | copy-start | bytes 3076
  7.1 4.0 %copy-start.11 = (f32[16]{0:T(128)S(1)}, f32[16]{0:T(128)}, u32[]{:S(2)}) copy-start(f32[16]{0:T(128)} %param.22) | copy-start | bytes 196
  7.1 3.9 %collective-permute-start.3 = (bf16[2,1,2,2,8,256]{5,4,3,2,1,0:T(8,128)(2,1)S(1)}, bf16[2,1,2,2,8,256]{5,4,3,2,1,0:T(8,128)(2,1)S(1)}, u32[]{:S(2)}, u32[]{:S(2)}) collective-permute-start(bf16[2,1,2,2,8,256]{5,4,3,2,1,0:T(8,128)(2,1)S(1)} %pad_maximum_fusion.2), channel_id=1, source_target_pairs={{0,3},{1,2},{2,1},{3,0},{4,7},{5,6},{6,5},{7,4},{8,11},{9,10},{10,... | collective-permute-start | bytes 98312 | tf_op jit(solution)/shard_map/ppermute | solution.py:329
  7.5 8.1 %copy-start = (bf16[1,3,3,320,320]{4,3,2,1,0:T(8,128)(2,1)S(1)}, bf16[1,3,3,320,320]{4,3,2,1,0:T(8,128)(2,1)}, u32[]{:S(2)}) copy-start(bf16[1,3,3,320,320]{4,3,2,1,0:T(8,128)(2,1)} %param.30) | copy-start | bytes 5529604
  7.5 8.1 %copy-start.2 = (bf16[3,3,16,320]{3,2,1,0:T(8,128)(2,1)S(1)}, bf16[3,3,16,320]{3,2,1,0:T(8,128)(2,1)}, u32[]{:S(2)}) copy-start(bf16[3,3,16,320]{3,2,1,0:T(8,128)(2,1)} %param.25) | copy-start | bytes 276484
  7.5 8.1 %copy-start.3 = (f32[4,16,320]{2,1,0:T(8,128)S(1)}, f32[4,16,320]{2,1,0:T(8,128)}, u32[]{:S(2)}) copy-start(f32[4,16,320]{2,1,0:T(8,128)} %get-tuple-element.13.refs_2_) | copy-start | bytes 245764
  7.6 8.1 %copy-start.4 = (f32[1,320]{1,0:T(1,128)S(1)}, f32[1,320]{1,0:T(1,128)}, u32[]{:S(2)}) copy-start(f32[1,320]{1,0:T(1,128)} %refs_2_.11) | copy-start | bytes 3844
  7.6 8.1 %copy-start.5 = (f32[1,320]{1,0:T(1,128)S(1)}, f32[1,320]{1,0:T(1,128)}, u32[]{:S(2)}) copy-start(f32[1,320]{1,0:T(1,128)} %refs_3_.11) | copy-start | bytes 3844
  7.6 8.1 %copy-start.6 = (f32[1,320]{1,0:T(1,128)S(1)}, f32[1,320]{1,0:T(1,128)}, u32[]{:S(2)}) copy-start(f32[1,320]{1,0:T(1,128)} %refs_4_.3) | copy-start | bytes 3844
  12.2 3.4 %collective-permute-start.10 = (bf16[1,64,16]{2,1,0:T(8,128)(2,1)S(1)}, bf16[1,64,16]{2,1,0:T(8,128)(2,1)S(1)}, u32[]{:S(2)}, u32[]{:S(2)}) collective-permute-start(bf16[1,64,16]{2,1,0:T(8,128)(2,1)S(1)} %encode.1), channel_id=1, source_target_pairs={{0,9},{1,8},{2,11},{3,10},{4,13},{5,12},{6,15},{7,14},{8,1},{9,0},... | collective-permute-start | bytes 6152 | tf_op jit(solution)/shard_map/ppermute | solution.py:351
  13.8 1.9 %collective-permute-start.9 = (bf16[1,64,16]{2,1,0:T(8,128)(2,1)S(1)}, bf16[1,64,16]{2,1,0:T(8,128)(2,1)S(1)}, u32[]{:S(2)}, u32[]{:S(2)}) collective-permute-start(bf16[1,64,16]{2,1,0:T(8,128)(2,1)S(1)} %encode.1), channel_id=1, source_target_pairs={{0,1},{1,0},{2,3},{3,2},{4,5},{5,4},{6,7},{7,6},{8,9},{9,8},{10,11... | collective-permute-start | bytes 6152 | tf_op jit(solution)/shard_map/ppermute | solution.py:355
  13.9 4.1 %collective-permute-start.5 = (bf16[1,64,16]{2,1,0:T(8,128)(2,1)S(1)}, bf16[1,64,16]{2,1,0:T(8,128)(2,1)S(1)}, u32[]{:S(2)}, u32[]{:S(2)}) collective-permute-start(bf16[1,64,16]{2,1,0:T(8,128)(2,1)S(1)} %encode.1), channel_id=1, source_target_pairs={{0,25},{1,24},{2,27},{3,26},{4,29},{5,28},{6,31},{7,30},{8,17},{9,... | collective-permute-start | bytes 6152 | tf_op jit(solution)/shard_map/ppermute | solution.py:351
  14.4 3.7 %collective-permute-start.4 = (bf16[1,64,16]{2,1,0:T(8,128)(2,1)S(1)}, bf16[1,64,16]{2,1,0:T(8,128)(2,1)S(1)}, u32[]{:S(2)}, u32[]{:S(2)}) collective-permute-start(bf16[1,64,16]{2,1,0:T(8,128)(2,1)S(1)} %encode.1), channel_id=1, source_target_pairs={{0,17},{1,16},{2,19},{3,18},{4,21},{5,20},{6,23},{7,22},{8,25},{9,... | collective-permute-start | bytes 6152 | tf_op jit(solution)/shard_map/ppermute | solution.py:351
  15.7 2.6 %collective-permute-start.11 = (bf16[128,320]{1,0:T(8,128)(2,1)S(1)}, bf16[128,320]{1,0:T(8,128)(2,1)S(1)}, u32[]{:S(2)}, u32[]{:S(2)}) collective-permute-start(bf16[128,320]{1,0:T(8,128)(2,1)S(1)} %first_block.3.kept_ref), channel_id=1, source_target_pairs={{0,8},{1,9},{2,10},{3,11},{4,12},{5,13},{6,14},{7,15},{8,24},{9,25... | collective-permute-start | bytes 245768 | tf_op jit(solution)/shard_map/ppermute | solution.py:351
  18.0 4.5 %collective-permute-start.6 = (bf16[128,320]{1,0:T(8,128)(2,1)S(1)}, bf16[128,320]{1,0:T(8,128)(2,1)S(1)}, u32[]{:S(2)}, u32[]{:S(2)}) collective-permute-start(bf16[128,320]{1,0:T(8,128)(2,1)S(1)} %first_block.2.kept_ref), channel_id=1, source_target_pairs={{0,8},{1,9},{2,10},{3,11},{4,12},{5,13},{6,14},{7,15},{8,24},{9,25... | collective-permute-start | bytes 245768 | tf_op jit(solution)/shard_map/ppermute | solution.py:351
  18.3 7.1 %collective-permute-start.12 = (bf16[128,320]{1,0:T(8,128)(2,1)S(1)}, bf16[128,320]{1,0:T(8,128)(2,1)S(1)}, u32[]{:S(2)}, u32[]{:S(2)}) collective-permute-start(bf16[128,320]{1,0:T(8,128)(2,1)S(1)} %later_block.6.kept_ref), channel_id=1, source_target_pairs={{0,9},{1,8},{2,11},{3,10},{4,13},{5,12},{6,15},{7,14},{8,17},{9,16... | collective-permute-start | bytes 245768 | tf_op jit(solution)/shard_map/ppermute | solution.py:351
  22.5 5.2 %collective-permute-start.7 = (bf16[128,320]{1,0:T(8,128)(2,1)S(1)}, bf16[128,320]{1,0:T(8,128)(2,1)S(1)}, u32[]{:S(2)}, u32[]{:S(2)}) collective-permute-start(bf16[128,320]{1,0:T(8,128)(2,1)S(1)} %later_block.4.kept_ref), channel_id=1, source_target_pairs={{0,9},{1,8},{2,11},{3,10},{4,13},{5,12},{6,15},{7,14},{8,17},{9,16... | collective-permute-start | bytes 245768 | tf_op jit(solution)/shard_map/ppermute | solution.py:351
  26.4 5.5 %collective-permute-start.13 = (bf16[128,320]{1,0:T(8,128)(2,1)S(1)}, bf16[128,320]{1,0:T(8,128)(2,1)S(1)}, u32[]{:S(2)}, u32[]{:S(2)}) collective-permute-start(bf16[128,320]{1,0:T(8,128)(2,1)S(1)} %later_block.7.kept_ref), channel_id=1, source_target_pairs={{0,1},{1,0},{2,3},{3,2},{4,5},{5,4},{6,7},{7,6},{8,9},{9,8},{10,11... | collective-permute-start | bytes 245768 | tf_op jit(solution)/shard_map/ppermute | solution.py:351
  28.6 5.5 %collective-permute-start.8 = (bf16[128,320]{1,0:T(8,128)(2,1)S(1)}, bf16[128,320]{1,0:T(8,128)(2,1)S(1)}, u32[]{:S(2)}, u32[]{:S(2)}) collective-permute-start(bf16[128,320]{1,0:T(8,128)(2,1)S(1)} %later_block.5.kept_ref), channel_id=1, source_target_pairs={{0,1},{1,0},{2,3},{3,2},{4,5},{5,4},{6,7},{7,6},{8,9},{9,8},{10,11... | collective-permute-start | bytes 245768 | tf_op jit(solution)/shard_map/ppermute | solution.py:351

commit v9 on v8

--- a/solution.py
+++ b/solution.py
@@ -332,7 +332,7 @@
 
 ROUTES = {
     (0, 1): ((1, False), (3, False), (2, True), (0, False)),
-    (1, 2): ((1, True), (2, True), (0, True), (3, True)),
+    (1, 2): ((0, True), (2, True), (3, True), (1, True)),
     (2, 3): ((0, True), (1, True), (3, False), (2, False)),
 }
 

time: 35.2 us -> 35 us (level)
  waiting for transfers between devices: 12.4 us -> 10.6 us
  starting transfers between devices: 14.9 us -> 16.4 us
    ppermute x9, waiting for transfers between devices: 8.33 us -> 6.5 us  [send(): return lax.ppermute(value, ('section', 'slab'), pairs)]
    ppermute x9, starting transfers between devices: 10.7 us -> 12.2 us  [send(): return lax.ppermute(value, ('section', 'slab'), pairs)]
where the time goes in v9:
time: 35 us; the launch traced here: 34.5 us
  starting transfers between devices  16.4 us (47%)
  waiting for transfers between devices  10.6 us (30%)
  Pallas kernels  6.37 us (18%)
  local copies, waits for them, and re-layouts  0.85 us (2%)
    ppermute x9, starting transfers between devices, send(): return lax.ppermute(value, ('section', 'slab'), pairs)  12.2 us
    ppermute x9, waiting for transfers between devices, send(): return lax.ppermute(value, ('section', 'slab'), pairs)  6.5 us
    ppermute x3, starting transfers between devices, exchange(): pieces[step] = lax.ppermute(pieces[step], 'slab', pairs)  4.04 us
    ppermute x3, waiting for transfers between devices, exchange(): pieces[step] = lax.ppermute(pieces[step], 'slab', pairs)  3.39 us
    pallas_call x1, Pallas kernels, exchange(): pl.pallas_call(functools.partial(select_kernel, 'section', 'slab', owned,...  1.81 us
    pallas_call x4, Pallas kernels, per_device(): pl.pallas_call(functools.partial(later_kernel, index, block, frames), out...  1.75 us
    pallas_call x2, Pallas kernels, per_device(): pl.pallas_call(functools.partial(last_kernel, block, frames, firsts[chunk...  1.49 us
    pallas_call x1, Pallas kernels, encode(): pl.pallas_call(functools.partial(encode_kernel, 'slab'), out_shape=jax.Sh...  1.19 us
  transfers between devices with their start and end apart: 14, of which 7 were waited for; matrix products, arithmetic and copies ran while one was open for 2% of the time, Pallas kernels for 8%

profile of v9, /device:TPU:4, one launch (start us, length us, event | category | flops | bytes accessed | tf_op | source)
XLA Modules:
  0.0 34.5 jit_solution(10372085965005311550)
XLA Ops:
  0.0 1.8 %select.1 = (bf16[4,1,2,2,8,256]{5,4,3,2,1,0:T(8,128)(2,1)}, bf16[4,1,2,2,8,256]{5,4,3,2,1,0:T(8,128)(2,1)}, f32[4,16,320]{2,1,0:T(8,128)}) custom-call(s32[4,8]{1,0:T(4,128)} %clips_ref.1, s32[4,8]{1,0:T(4,128)} %offsets_ref.1, bf16[8,2,2,8,256]{4,3,2,1,0:T(8,128)(2,1)} %bitcast.27, bf16[320,128]{1,0:T(8,128)(2,1)} %bitcast.28, f32[320]{0:T(512)} %bias_ref.1), custom_call_target="tpu_custom_call" | custom-call | tf_op jit(solution)/shard_map/select/pallas_call | solution.py:318
  1.8 0.8 %fusion = (bf16[1,1,2,2,8,256]{5,4,3,2,1,0:T(8,128)(2,1)S(1)}, bf16[1,1,2,2,8,256]{5,4,3,2,1,0:T(8,128)(2,1)S(1)}, bf16[1,1,2,2,8,256]{5,4,3,2,1,0:T(8,128)(2,1)S(1)}, bf16[1,1,2,2,8,256]{5,4,3,2,1,0:T(8,128)(2,1)S(1)}) fusion(bf16[4,1,2,2,8,256]{5,4,3,2,1,0:T(8,128)(2,1)} %get-tuple-element.10), kind=kLoop, calls=%fused_computation.4 | loop fusion | bytes 131072 | tf_op jit(solution)/shard_map/slice | solution.py:326
  2.6 0.7 %collective-permute-done.after_ref = bf16[4,1,2,2,8,256]{5,4,3,2,1,0:T(8,128)(2,1)S(1)} collective-permute-done((bf16[4,1,2,2,8,256]{5,4,3,2,1,0:T(8,128)(2,1)}, bf16[4,1,2,2,8,256]{5,4,3,2,1,0:T(8,128)(2,1)S(1)}, u32[]{:S(2)}, u32[]{:S(2)}) %collective-permute-start) | collective-permute-done | bytes 65568 | tf_op jit(solution)/shard_map/ppermute | solution.py:355
  3.3 2.4 %collective-permute-start.1 = (bf16[2,1,2,2,8,256]{5,4,3,2,1,0:T(8,128)(2,1)S(1)}, bf16[2,1,2,2,8,256]{5,4,3,2,1,0:T(8,128)(2,1)S(1)}, u32[]{:S(2)}, u32[]{:S(2)}) collective-permute-start(bf16[2,1,2,2,8,256]{5,4,3,2,1,0:T(8,128)(2,1)S(1)} %pad_maximum_fusion), channel_id=1, source_target_pairs={{0,5},{1,4},{2,7},{3,6},{4,1},{5,0},{6,3},{7,2},{8,13},{9,12},{10,... | collective-permute-start | bytes 98312 | tf_op jit(solution)/shard_map/ppermute | solution.py:329
  5.7 1.3 %collective-permute-start.2 = (bf16[2,1,2,2,8,256]{5,4,3,2,1,0:T(8,128)(2,1)S(1)}, bf16[2,1,2,2,8,256]{5,4,3,2,1,0:T(8,128)(2,1)S(1)}, u32[]{:S(2)}, u32[]{:S(2)}) collective-permute-start(bf16[2,1,2,2,8,256]{5,4,3,2,1,0:T(8,128)(2,1)S(1)} %pad_maximum_fusion.1), channel_id=1, source_target_pairs={{0,7},{1,6},{2,5},{3,4},{4,3},{5,2},{6,1},{7,0},{8,15},{9,14},{10,... | collective-permute-start | bytes 98312 | tf_op jit(solution)/shard_map/ppermute | solution.py:329
  7.0 0.0 copy-start.8
  7.1 0.0 copy-start.11
  7.1 0.3 collective-permute-start.3
  7.4 0.1 groups.1
  7.5 0.0 copy-start
  7.5 0.0 copy-start.2
  7.6 3.4 %collective-permute-done.2.refs_1_ = bf16[2,1,2,2,8,256]{5,4,3,2,1,0:T(8,128)(2,1)S(1)} collective-permute-done((bf16[2,1,2,2,8,256]{5,4,3,2,1,0:T(8,128)(2,1)S(1)}, bf16[2,1,2,2,8,256]{5,4,3,2,1,0:T(8,128)(2,1)S(1)}, u32[]{:S(2)}, u32[]{:S(2)}) %collective-permute-start.2) | collective-permute-done | bytes 32800 | tf_op jit(solution)/shard_map/ppermute | solution.py:329
  11.0 1.2 %encode.1 = bf16[1,64,16]{2,1,0:T(8,128)(2,1)S(1)} custom-call(bf16[2,1,2,2,8,256]{5,4,3,2,1,0:T(8,128)(2,1)S(1)} %collective-permute-done.1.refs_0_, bf16[2,1,2,2,8,256]{5,4,3,2,1,0:T(8,128)(2,1)S(1)} %collective-permute-done.2.refs_1_, bf16[2,1,2,2,8,256]{5,4,3,2,1,0:T(8,128)(2,1)S(1)} %collective-permute-done.3.refs_2_, ...), custom_call_target="tpu_custom_call" | custom-call | tf_op jit(solution)/shard_map/encode/pallas_call | solution.py:142
  12.2 1.5 %collective-permute-start.10 = (bf16[1,64,16]{2,1,0:T(8,128)(2,1)S(1)}, bf16[1,64,16]{2,1,0:T(8,128)(2,1)S(1)}, u32[]{:S(2)}, u32[]{:S(2)}) collective-permute-start(bf16[1,64,16]{2,1,0:T(8,128)(2,1)S(1)} %encode.1), channel_id=1, source_target_pairs={{0,9},{1,8},{2,11},{3,10},{4,13},{5,12},{6,15},{7,14},{8,1},{9,0},... | collective-permute-start | bytes 6152 | tf_op jit(solution)/shard_map/ppermute | solution.py:351
  13.8 0.2 collective-permute-start.9
  13.9 0.4 %collective-permute-start.5 = (bf16[1,64,16]{2,1,0:T(8,128)(2,1)S(1)}, bf16[1,64,16]{2,1,0:T(8,128)(2,1)S(1)}, u32[]{:S(2)}, u32[]{:S(2)}) collective-permute-start(bf16[1,64,16]{2,1,0:T(8,128)(2,1)S(1)} %encode.1), channel_id=1, source_target_pairs={{0,25},{1,24},{2,27},{3,26},{4,29},{5,28},{6,31},{7,30},{8,17},{9,... | collective-permute-start | bytes 6152 | tf_op jit(solution)/shard_map/ppermute | solution.py:351
  14.4 1.3 %collective-permute-start.4 = (bf16[1,64,16]{2,1,0:T(8,128)(2,1)S(1)}, bf16[1,64,16]{2,1,0:T(8,128)(2,1)S(1)}, u32[]{:S(2)}, u32[]{:S(2)}) collective-permute-start(bf16[1,64,16]{2,1,0:T(8,128)(2,1)S(1)} %encode.1), channel_id=1, source_target_pairs={{0,17},{1,16},{2,19},{3,18},{4,21},{5,20},{6,23},{7,22},{8,25},{9,... | collective-permute-start | bytes 6152 | tf_op jit(solution)/shard_map/ppermute | solution.py:351
  15.7 0.4 %collective-permute-start.11 = (bf16[128,320]{1,0:T(8,128)(2,1)S(1)}, bf16[128,320]{1,0:T(8,128)(2,1)S(1)}, u32[]{:S(2)}, u32[]{:S(2)}) collective-permute-start(bf16[128,320]{1,0:T(8,128)(2,1)S(1)} %first_block.3.kept_ref), channel_id=1, source_target_pairs={{0,8},{1,9},{2,10},{3,11},{4,12},{5,13},{6,14},{7,15},{8,24},{9,25... | collective-permute-start | bytes 245768 | tf_op jit(solution)/shard_map/ppermute | solution.py:351
  16.1 1.9 %collective-permute-done.5.refs_1_ = bf16[1,64,16]{2,1,0:T(8,128)(2,1)S(1)} collective-permute-done((bf16[1,64,16]{2,1,0:T(8,128)(2,1)S(1)}, bf16[1,64,16]{2,1,0:T(8,128)(2,1)S(1)}, u32[]{:S(2)}, u32[]{:S(2)}) %collective-permute-start.5) | collective-permute-done | bytes 2080 | tf_op jit(solution)/shard_map/ppermute | solution.py:351
  18.0 0.3 collective-permute-start.6
  18.3 3.1 %collective-permute-start.12 = (bf16[128,320]{1,0:T(8,128)(2,1)S(1)}, bf16[128,320]{1,0:T(8,128)(2,1)S(1)}, u32[]{:S(2)}, u32[]{:S(2)}) collective-permute-start(bf16[128,320]{1,0:T(8,128)(2,1)S(1)} %later_block.6.kept_ref), channel_id=1, source_target_pairs={{0,1},{1,0},{2,3},{3,2},{4,5},{5,4},{6,7},{7,6},{8,17},{9,16},{10,... | collective-permute-start | bytes 245768 | tf_op jit(solution)/shard_map/ppermute | solution.py:351
  21.5 2.3 %collective-permute-start.7 = (bf16[128,320]{1,0:T(8,128)(2,1)S(1)}, bf16[128,320]{1,0:T(8,128)(2,1)S(1)}, u32[]{:S(2)}, u32[]{:S(2)}) collective-permute-start(bf16[128,320]{1,0:T(8,128)(2,1)S(1)} %later_block.4.kept_ref), channel_id=1, source_target_pairs={{0,1},{1,0},{2,3},{3,2},{4,5},{5,4},{6,7},{7,6},{8,17},{9,16},{10,... | collective-permute-start | bytes 245768 | tf_op jit(solution)/shard_map/ppermute | solution.py:351
  23.7 0.9 %collective-permute-done.12.before_ref = bf16[128,320]{1,0:T(8,128)(2,1)S(1)} collective-permute-done((bf16[128,320]{1,0:T(8,128)(2,1)S(1)}, bf16[128,320]{1,0:T(8,128)(2,1)S(1)}, u32[]{:S(2)}, u32[]{:S(2)}) %collective-permute-start.12) | collective-permute-done | bytes 81952 | tf_op jit(solution)/shard_map/ppermute | solution.py:351
  24.7 0.9 %later_block.7.kept_ref = bf16[128,320]{1,0:T(8,128)(2,1)S(1)} custom-call(bf16[128,320]{1,0:T(8,128)(2,1)S(1)} %collective-permute-done.12.before_ref, bf16[128,320]{1,0:T(8,128)(2,1)S(1)} %later_block.6.kept_ref, bf16[3,3,320,320]{3,2,1,0:T(8,128)(2,1)S(1)} %bitcast.16, f32[1,320]{1,0:T(1,128)S(1)} %copy-done.4, ...), custom_call_target="tpu_custom_call", output_to_operand_aliasing={{}: (1, {})} | custom-call | tf_op jit(solution)/shard_map/later_block/pallas_call | solution.py:440
  25.5 1.6 %collective-permute-start.13 = (bf16[128,320]{1,0:T(8,128)(2,1)S(1)}, bf16[128,320]{1,0:T(8,128)(2,1)S(1)}, u32[]{:S(2)}, u32[]{:S(2)}) collective-permute-start(bf16[128,320]{1,0:T(8,128)(2,1)S(1)} %later_block.7.kept_ref), channel_id=1, source_target_pairs={{0,1},{1,0},{2,3},{3,2},{4,5},{5,4},{6,7},{7,6},{8,9},{9,8},{10,11... | collective-permute-start | bytes 245768 | tf_op jit(solution)/shard_map/ppermute | solution.py:351
  27.1 0.1 collective-permute-done.7.before_ref
  27.2 0.9 %later_block.5.kept_ref = bf16[128,320]{1,0:T(8,128)(2,1)S(1)} custom-call(bf16[128,320]{1,0:T(8,128)(2,1)S(1)} %collective-permute-done.7.before_ref, bf16[128,320]{1,0:T(8,128)(2,1)S(1)} %later_block.4.kept_ref, bf16[3,3,320,320]{3,2,1,0:T(8,128)(2,1)S(1)} %bitcast.17, f32[1,320]{1,0:T(1,128)S(1)} %copy-done.4, ...), custom_call_target="tpu_custom_call", output_to_operand_aliasing={{}: (1, {})} | custom-call | tf_op jit(solution)/shard_map/later_block/pallas_call | solution.py:440
  28.1 1.3 %collective-permute-start.8 = (bf16[128,320]{1,0:T(8,128)(2,1)S(1)}, bf16[128,320]{1,0:T(8,128)(2,1)S(1)}, u32[]{:S(2)}, u32[]{:S(2)}) collective-permute-start(bf16[128,320]{1,0:T(8,128)(2,1)S(1)} %later_block.5.kept_ref), channel_id=1, source_target_pairs={{0,1},{1,0},{2,3},{3,2},{4,5},{5,4},{6,7},{7,6},{8,9},{9,8},{10,11... | collective-permute-start | bytes 245768 | tf_op jit(solution)/shard_map/ppermute | solution.py:351
  29.4 1.9 %collective-permute-done.13.before_ref = bf16[128,320]{1,0:T(8,128)(2,1)S(1)} collective-permute-done((bf16[128,320]{1,0:T(8,128)(2,1)S(1)}, bf16[128,320]{1,0:T(8,128)(2,1)S(1)}, u32[]{:S(2)}, u32[]{:S(2)}) %collective-permute-start.13) | collective-permute-done | bytes 81952 | tf_op jit(solution)/shard_map/ppermute | solution.py:351
  31.3 0.7 %last_block.2.refs_0_ = bf16[4,8,2,1280]{3,2,1,0:T(2,128)(2,1)} custom-call(bf16[128,320]{1,0:T(8,128)(2,1)S(1)} %collective-permute-done.13.before_ref, bf16[128,320]{1,0:T(8,128)(2,1)S(1)} %later_block.7.kept_ref, bf16[3,3,320,320]{3,2,1,0:T(8,128)(2,1)S(1)} %bitcast.18, f32[1,320]{1,0:T(1,128)S(1)} %copy-done.4, f32[1,320]{1,0:T(1,128)S(1)} %copy-done.5, ...), custom_call_target="tpu_custom_call" | custom-call | tf_op jit(solution)/shard_map/last_block/pallas_call | solution.py:458
  32.0 1.7 %collective-permute-done.8.before_ref = bf16[128,320]{1,0:T(8,128)(2,1)S(1)} collective-permute-done((bf16[128,320]{1,0:T(8,128)(2,1)S(1)}, bf16[128,320]{1,0:T(8,128)(2,1)S(1)}, u32[]{:S(2)}, u32[]{:S(2)}) %collective-permute-start.8) | collective-permute-done | bytes 81952 | tf_op jit(solution)/shard_map/ppermute | solution.py:351
  33.7 0.7 %last_block.3 = bf16[4,8,2,1280]{3,2,1,0:T(2,128)(2,1)} custom-call(bf16[128,320]{1,0:T(8,128)(2,1)S(1)} %collective-permute-done.8.before_ref, bf16[128,320]{1,0:T(8,128)(2,1)S(1)} %later_block.5.kept_ref, bf16[4,8,2,1280]{3,2,1,0:T(2,128)(2,1)} %last_block.2.refs_0_, bf16[3,3,320,320]{3,2,1,0:T(8,128)(2,1)S(1)} %bitcast.19, ...), custom_call_target="tpu_custom_call", output_to_operand_aliasing={{}: (2, {})} | custom-call | tf_op jit(solution)/shard_map/last_block/pallas_call | solution.py:458
  (37 shorter events, 0.1 us)
Async XLA Ops:
  1.8 1.5 %collective-permute-start = (bf16[4,1,2,2,8,256]{5,4,3,2,1,0:T(8,128)(2,1)}, bf16[4,1,2,2,8,256]{5,4,3,2,1,0:T(8,128)(2,1)S(1)}, u32[]{:S(2)}, u32[]{:S(2)}) collective-permute-start(bf16[4,1,2,2,8,256]{5,4,3,2,1,0:T(8,128)(2,1)} %get-tuple-element.11), channel_id=1, source_target_pairs={{0,1},{1,0},{2,3},{3,2},{4,5},{5,4},{6,7},{7,6},{8,9},{9,8},{10,11... | collective-permute-start | bytes 196616 | tf_op jit(solution)/shard_map/ppermute | solution.py:355
  3.3 4.3 %collective-permute-start.1 = (bf16[2,1,2,2,8,256]{5,4,3,2,1,0:T(8,128)(2,1)S(1)}, bf16[2,1,2,2,8,256]{5,4,3,2,1,0:T(8,128)(2,1)S(1)}, u32[]{:S(2)}, u32[]{:S(2)}) collective-permute-start(bf16[2,1,2,2,8,256]{5,4,3,2,1,0:T(8,128)(2,1)S(1)} %pad_maximum_fusion), channel_id=1, source_target_pairs={{0,5},{1,4},{2,7},{3,6},{4,1},{5,0},{6,3},{7,2},{8,13},{9,12},{10,... | collective-permute-start | bytes 98312 | tf_op jit(solution)/shard_map/ppermute | solution.py:329
  5.7 5.3 %collective-permute-start.2 = (bf16[2,1,2,2,8,256]{5,4,3,2,1,0:T(8,128)(2,1)S(1)}, bf16[2,1,2,2,8,256]{5,4,3,2,1,0:T(8,128)(2,1)S(1)}, u32[]{:S(2)}, u32[]{:S(2)}) collective-permute-start(bf16[2,1,2,2,8,256]{5,4,3,2,1,0:T(8,128)(2,1)S(1)} %pad_maximum_fusion.1), channel_id=1, source_target_pairs={{0,7},{1,6},{2,5},{3,4},{4,3},{5,2},{6,1},{7,0},{8,15},{9,14},{10,... | collective-permute-start | bytes 98312 | tf_op jit(solution)/shard_map/ppermute | solution.py:329
  7.0 4.0 %copy-start.1 = (bf16[3,3,3,256,256]{4,3,2,1,0:T(8,128)(2,1)S(1)}, bf16[3,3,3,256,256]{4,3,2,1,0:T(8,128)(2,1)}, u32[]{:S(2)}) copy-start(bf16[3,3,3,256,256]{4,3,2,1,0:T(8,128)(2,1)} %refs_4_.2) | copy-start | bytes 10616836
  7.0 4.0 %copy-start.7 = (bf16[256,16]{0,1:T(8,128)(2,1)S(1)}, bf16[256,16]{0,1:T(8,128)(2,1)}, u32[]{:S(2)}) copy-start(bf16[256,16]{0,1:T(8,128)(2,1)} %param.21) | copy-start | bytes 24580
  7.0 4.0 %copy-start.8 = (f32[256]{0:T(256)S(1)}, f32[256]{0:T(256)}, u32[]{:S(2)}) copy-start(f32[256]{0:T(256)} %param.18) | copy-start | bytes 3076
  7.1 4.0 %copy-start.9 = (f32[256]{0:T(256)S(1)}, f32[256]{0:T(256)}, u32[]{:S(2)}) copy-start(f32[256]{0:T(256)} %param.19) | copy-start | bytes 3076
  7.1 4.0 %copy-start.10 = (f32[256]{0:T(256)S(1)}, f32[256]{0:T(256)}, u32[]{:S(2)}) copy-start(f32[256]{0:T(256)} %param.20) | copy-start | bytes 3076
  7.1 4.0 %copy-start.11 = (f32[16]{0:T(128)S(1)}, f32[16]{0:T(128)}, u32[]{:S(2)}) copy-start(f32[16]{0:T(128)} %param.22) | copy-start | bytes 196
  7.1 3.9 %collective-permute-start.3 = (bf16[2,1,2,2,8,256]{5,4,3,2,1,0:T(8,128)(2,1)S(1)}, bf16[2,1,2,2,8,256]{5,4,3,2,1,0:T(8,128)(2,1)S(1)}, u32[]{:S(2)}, u32[]{:S(2)}) collective-permute-start(bf16[2,1,2,2,8,256]{5,4,3,2,1,0:T(8,128)(2,1)S(1)} %pad_maximum_fusion.2), channel_id=1, source_target_pairs={{0,3},{1,2},{2,1},{3,0},{4,7},{5,6},{6,5},{7,4},{8,11},{9,10},{10,... | collective-permute-start | bytes 98312 | tf_op jit(solution)/shard_map/ppermute | solution.py:329
  7.5 8.1 %copy-start = (bf16[1,3,3,320,320]{4,3,2,1,0:T(8,128)(2,1)S(1)}, bf16[1,3,3,320,320]{4,3,2,1,0:T(8,128)(2,1)}, u32[]{:S(2)}) copy-start(bf16[1,3,3,320,320]{4,3,2,1,0:T(8,128)(2,1)} %param.30) | copy-start | bytes 5529604
  7.5 8.1 %copy-start.2 = (bf16[3,3,16,320]{3,2,1,0:T(8,128)(2,1)S(1)}, bf16[3,3,16,320]{3,2,1,0:T(8,128)(2,1)}, u32[]{:S(2)}) copy-start(bf16[3,3,16,320]{3,2,1,0:T(8,128)(2,1)} %param.25) | copy-start | bytes 276484
  7.5 8.1 %copy-start.3 = (f32[4,16,320]{2,1,0:T(8,128)S(1)}, f32[4,16,320]{2,1,0:T(8,128)}, u32[]{:S(2)}) copy-start(f32[4,16,320]{2,1,0:T(8,128)} %get-tuple-element.13.refs_2_) | copy-start | bytes 245764
  7.6 8.1 %copy-start.4 = (f32[1,320]{1,0:T(1,128)S(1)}, f32[1,320]{1,0:T(1,128)}, u32[]{:S(2)}) copy-start(f32[1,320]{1,0:T(1,128)} %refs_2_.11) | copy-start | bytes 3844
  7.6 8.1 %copy-start.5 = (f32[1,320]{1,0:T(1,128)S(1)}, f32[1,320]{1,0:T(1,128)}, u32[]{:S(2)}) copy-start(f32[1,320]{1,0:T(1,128)} %refs_3_.11) | copy-start | bytes 3844
  7.6 8.1 %copy-start.6 = (f32[1,320]{1,0:T(1,128)S(1)}, f32[1,320]{1,0:T(1,128)}, u32[]{:S(2)}) copy-start(f32[1,320]{1,0:T(1,128)} %refs_4_.3) | copy-start | bytes 3844
  12.2 3.4 %collective-permute-start.10 = (bf16[1,64,16]{2,1,0:T(8,128)(2,1)S(1)}, bf16[1,64,16]{2,1,0:T(8,128)(2,1)S(1)}, u32[]{:S(2)}, u32[]{:S(2)}) collective-permute-start(bf16[1,64,16]{2,1,0:T(8,128)(2,1)S(1)} %encode.1), channel_id=1, source_target_pairs={{0,9},{1,8},{2,11},{3,10},{4,13},{5,12},{6,15},{7,14},{8,1},{9,0},... | collective-permute-start | bytes 6152 | tf_op jit(solution)/shard_map/ppermute | solution.py:351
  13.8 1.9 %collective-permute-start.9 = (bf16[1,64,16]{2,1,0:T(8,128)(2,1)S(1)}, bf16[1,64,16]{2,1,0:T(8,128)(2,1)S(1)}, u32[]{:S(2)}, u32[]{:S(2)}) collective-permute-start(bf16[1,64,16]{2,1,0:T(8,128)(2,1)S(1)} %encode.1), channel_id=1, source_target_pairs={{0,1},{1,0},{2,3},{3,2},{4,5},{5,4},{6,7},{7,6},{8,9},{9,8},{10,11... | collective-permute-start | bytes 6152 | tf_op jit(solution)/shard_map/ppermute | solution.py:355
  13.9 4.1 %collective-permute-start.5 = (bf16[1,64,16]{2,1,0:T(8,128)(2,1)S(1)}, bf16[1,64,16]{2,1,0:T(8,128)(2,1)S(1)}, u32[]{:S(2)}, u32[]{:S(2)}) collective-permute-start(bf16[1,64,16]{2,1,0:T(8,128)(2,1)S(1)} %encode.1), channel_id=1, source_target_pairs={{0,25},{1,24},{2,27},{3,26},{4,29},{5,28},{6,31},{7,30},{8,17},{9,... | collective-permute-start | bytes 6152 | tf_op jit(solution)/shard_map/ppermute | solution.py:351
  14.4 3.7 %collective-permute-start.4 = (bf16[1,64,16]{2,1,0:T(8,128)(2,1)S(1)}, bf16[1,64,16]{2,1,0:T(8,128)(2,1)S(1)}, u32[]{:S(2)}, u32[]{:S(2)}) collective-permute-start(bf16[1,64,16]{2,1,0:T(8,128)(2,1)S(1)} %encode.1), channel_id=1, source_target_pairs={{0,17},{1,16},{2,19},{3,18},{4,21},{5,20},{6,23},{7,22},{8,25},{9,... | collective-permute-start | bytes 6152 | tf_op jit(solution)/shard_map/ppermute | solution.py:351
  15.7 2.6 %collective-permute-start.11 = (bf16[128,320]{1,0:T(8,128)(2,1)S(1)}, bf16[128,320]{1,0:T(8,128)(2,1)S(1)}, u32[]{:S(2)}, u32[]{:S(2)}) collective-permute-start(bf16[128,320]{1,0:T(8,128)(2,1)S(1)} %first_block.3.kept_ref), channel_id=1, source_target_pairs={{0,8},{1,9},{2,10},{3,11},{4,12},{5,13},{6,14},{7,15},{8,24},{9,25... | collective-permute-start | bytes 245768 | tf_op jit(solution)/shard_map/ppermute | solution.py:351
  18.0 3.4 %collective-permute-start.6 = (bf16[128,320]{1,0:T(8,128)(2,1)S(1)}, bf16[128,320]{1,0:T(8,128)(2,1)S(1)}, u32[]{:S(2)}, u32[]{:S(2)}) collective-permute-start(bf16[128,320]{1,0:T(8,128)(2,1)S(1)} %first_block.2.kept_ref), channel_id=1, source_target_pairs={{0,8},{1,9},{2,10},{3,11},{4,12},{5,13},{6,14},{7,15},{8,24},{9,25... | collective-permute-start | bytes 245768 | tf_op jit(solution)/shard_map/ppermute | solution.py:351
  18.3 6.3 %collective-permute-start.12 = (bf16[128,320]{1,0:T(8,128)(2,1)S(1)}, bf16[128,320]{1,0:T(8,128)(2,1)S(1)}, u32[]{:S(2)}, u32[]{:S(2)}) collective-permute-start(bf16[128,320]{1,0:T(8,128)(2,1)S(1)} %later_block.6.kept_ref), channel_id=1, source_target_pairs={{0,1},{1,0},{2,3},{3,2},{4,5},{5,4},{6,7},{7,6},{8,17},{9,16},{10,... | collective-permute-start | bytes 245768 | tf_op jit(solution)/shard_map/ppermute | solution.py:351
  21.5 5.7 %collective-permute-start.7 = (bf16[128,320]{1,0:T(8,128)(2,1)S(1)}, bf16[128,320]{1,0:T(8,128)(2,1)S(1)}, u32[]{:S(2)}, u32[]{:S(2)}) collective-permute-start(bf16[128,320]{1,0:T(8,128)(2,1)S(1)} %later_block.4.kept_ref), channel_id=1, source_target_pairs={{0,1},{1,0},{2,3},{3,2},{4,5},{5,4},{6,7},{7,6},{8,17},{9,16},{10,... | collective-permute-start | bytes 245768 | tf_op jit(solution)/shard_map/ppermute | solution.py:351
  25.5 5.7 %collective-permute-start.13 = (bf16[128,320]{1,0:T(8,128)(2,1)S(1)}, bf16[128,320]{1,0:T(8,128)(2,1)S(1)}, u32[]{:S(2)}, u32[]{:S(2)}) collective-permute-start(bf16[128,320]{1,0:T(8,128)(2,1)S(1)} %later_block.7.kept_ref), channel_id=1, source_target_pairs={{0,1},{1,0},{2,3},{3,2},{4,5},{5,4},{6,7},{7,6},{8,9},{9,8},{10,11... | collective-permute-start | bytes 245768 | tf_op jit(solution)/shard_map/ppermute | solution.py:351
  28.1 5.6 %collective-permute-start.8 = (bf16[128,320]{1,0:T(8,128)(2,1)S(1)}, bf16[128,320]{1,0:T(8,128)(2,1)S(1)}, u32[]{:S(2)}, u32[]{:S(2)}) collective-permute-start(bf16[128,320]{1,0:T(8,128)(2,1)S(1)} %later_block.5.kept_ref), channel_id=1, source_target_pairs={{0,1},{1,0},{2,3},{3,2},{4,5},{5,4},{6,7},{7,6},{8,9},{9,8},{10,11... | collective-permute-start | bytes 245768 | tf_op jit(solution)/shard_map/ppermute | solution.py:351

commit v10 on v9

--- a/solution.py
+++ b/solution.py
@@ -93,7 +93,7 @@
         sums = group_sums(sums, same_ref[...]) * (1.0 / (size * (channels // GROUPS)))
         mean = sums[0:1]
         inverse = lax.rsqrt(sums[1:2] - mean * mean + EPS)
-        act = silu((x - mean) * inverse * gain_ref[...] + shift_ref[...])
+        act = silu((x - mean) * (inverse * gain_ref[...]) + shift_ref[...])
         column = lax.broadcasted_iota(jnp.int32, (size, 1), 0) & (cols - 1)
         taps = [
             jnp.where(column == 0, 0.0, pltpu.roll(act, 1, 0)),
@@ -208,8 +208,8 @@
     for item in range(streams):
         mean = sums[2 * item : 2 * item + 1]
         inverse = lax.rsqrt(sums[2 * item + 1 : 2 * item + 2] - mean * mean + EPS)
-        scaled = (values[:, item : item + 1] - mean) * inverse * gain_ref[...]
-        normed.append(scaled + shift_ref[...])
+        factor = inverse * gain_ref[...]
+        normed.append((values[:, item : item + 1] - mean) * factor + shift_ref[...])
     act = silu(jnp.concatenate(normed, axis=1).reshape(size, channels))
     total = conv3(act, weight_ref, block, frames)
     return (state + total + bias_ref[...]).astype(BF16)

time: 35 us -> 35 us (level)
  transfers between devices with their start and end apart: 14 -> 14, of which waited for: 7 -> 6; matrix products, arithmetic and copies ran while one was open for 2% -> 2% of each run, Pallas kernels for 8% -> 8%
where the time goes in v10:
time: 35 us; the launch traced here: 34.4 us
  starting transfers between devices  16.5 us (47%)
  waiting for transfers between devices  10.4 us (30%)
  Pallas kernels  6.35 us (18%)
  local copies, waits for them, and re-layouts  0.85 us (2%)
    ppermute x9, starting transfers between devices, send(): return lax.ppermute(value, ('section', 'slab'), pairs)  12.3 us
    ppermute x9, waiting for transfers between devices, send(): return lax.ppermute(value, ('section', 'slab'), pairs)  6.34 us
    ppermute x3, starting transfers between devices, exchange(): pieces[step] = lax.ppermute(pieces[step], 'slab', pairs)  4.04 us
    ppermute x3, waiting for transfers between devices, exchange(): pieces[step] = lax.ppermute(pieces[step], 'slab', pairs)  3.39 us
    pallas_call x1, Pallas kernels, exchange(): pl.pallas_call(functools.partial(select_kernel, 'section', 'slab', owned,...  1.81 us
    pallas_call x4, Pallas kernels, per_device(): pl.pallas_call(functools.partial(later_kernel, index, block, frames), out...  1.75 us
    pallas_call x2, Pallas kernels, per_device(): pl.pallas_call(functools.partial(last_kernel, block, frames, firsts[chunk...  1.49 us
    pallas_call x1, Pallas kernels, encode(): pl.pallas_call(functools.partial(encode_kernel, 'slab'), out_shape=jax.Sh...  1.17 us
  transfers between devices with their start and end apart: 14, of which 6 were waited for; matrix products, arithmetic and copies ran while one was open for 2% of the time, Pallas kernels for 8%

profile of v10, /device:TPU:4, one launch (start us, length us, event | category | flops | bytes accessed | tf_op | source)
XLA Modules:
  0.0 34.4 jit_solution(1218020082855769005)
XLA Ops:
  0.0 1.8 %select.1 = (bf16[4,1,2,2,8,256]{5,4,3,2,1,0:T(8,128)(2,1)}, bf16[4,1,2,2,8,256]{5,4,3,2,1,0:T(8,128)(2,1)}, f32[4,16,320]{2,1,0:T(8,128)}) custom-call(s32[4,8]{1,0:T(4,128)} %clips_ref.1, s32[4,8]{1,0:T(4,128)} %offsets_ref.1, bf16[8,2,2,8,256]{4,3,2,1,0:T(8,128)(2,1)} %bitcast.27, bf16[320,128]{1,0:T(8,128)(2,1)} %bitcast.28, f32[320]{0:T(512)} %bias_ref.1), custom_call_target="tpu_custom_call" | custom-call | tf_op jit(solution)/shard_map/select/pallas_call | solution.py:318
  1.8 0.8 %fusion = (bf16[1,1,2,2,8,256]{5,4,3,2,1,0:T(8,128)(2,1)S(1)}, bf16[1,1,2,2,8,256]{5,4,3,2,1,0:T(8,128)(2,1)S(1)}, bf16[1,1,2,2,8,256]{5,4,3,2,1,0:T(8,128)(2,1)S(1)}, bf16[1,1,2,2,8,256]{5,4,3,2,1,0:T(8,128)(2,1)S(1)}) fusion(bf16[4,1,2,2,8,256]{5,4,3,2,1,0:T(8,128)(2,1)} %get-tuple-element.10), kind=kLoop, calls=%fused_computation.4 | loop fusion | bytes 131072 | tf_op jit(solution)/shard_map/slice | solution.py:326
  2.6 0.7 %collective-permute-done.after_ref = bf16[4,1,2,2,8,256]{5,4,3,2,1,0:T(8,128)(2,1)S(1)} collective-permute-done((bf16[4,1,2,2,8,256]{5,4,3,2,1,0:T(8,128)(2,1)}, bf16[4,1,2,2,8,256]{5,4,3,2,1,0:T(8,128)(2,1)S(1)}, u32[]{:S(2)}, u32[]{:S(2)}) %collective-permute-start) | collective-permute-done | bytes 65568 | tf_op jit(solution)/shard_map/ppermute | solution.py:355
  3.3 2.4 %collective-permute-start.1 = (bf16[2,1,2,2,8,256]{5,4,3,2,1,0:T(8,128)(2,1)S(1)}, bf16[2,1,2,2,8,256]{5,4,3,2,1,0:T(8,128)(2,1)S(1)}, u32[]{:S(2)}, u32[]{:S(2)}) collective-permute-start(bf16[2,1,2,2,8,256]{5,4,3,2,1,0:T(8,128)(2,1)S(1)} %pad_maximum_fusion), channel_id=1, source_target_pairs={{0,5},{1,4},{2,7},{3,6},{4,1},{5,0},{6,3},{7,2},{8,13},{9,12},{10,... | collective-permute-start | bytes 98312 | tf_op jit(solution)/shard_map/ppermute | solution.py:329
  5.7 1.3 %collective-permute-start.2 = (bf16[2,1,2,2,8,256]{5,4,3,2,1,0:T(8,128)(2,1)S(1)}, bf16[2,1,2,2,8,256]{5,4,3,2,1,0:T(8,128)(2,1)S(1)}, u32[]{:S(2)}, u32[]{:S(2)}) collective-permute-start(bf16[2,1,2,2,8,256]{5,4,3,2,1,0:T(8,128)(2,1)S(1)} %pad_maximum_fusion.1), channel_id=1, source_target_pairs={{0,7},{1,6},{2,5},{3,4},{4,3},{5,2},{6,1},{7,0},{8,15},{9,14},{10,... | collective-permute-start | bytes 98312 | tf_op jit(solution)/shard_map/ppermute | solution.py:329
  7.0 0.0 copy-start.8
  7.1 0.0 copy-start.11
  7.1 0.3 collective-permute-start.3
  7.4 0.1 groups.1
  7.5 0.0 copy-start.2
  7.5 0.0 copy-start.3
  7.6 3.4 %collective-permute-done.2.refs_1_ = bf16[2,1,2,2,8,256]{5,4,3,2,1,0:T(8,128)(2,1)S(1)} collective-permute-done((bf16[2,1,2,2,8,256]{5,4,3,2,1,0:T(8,128)(2,1)S(1)}, bf16[2,1,2,2,8,256]{5,4,3,2,1,0:T(8,128)(2,1)S(1)}, u32[]{:S(2)}, u32[]{:S(2)}) %collective-permute-start.2) | collective-permute-done | bytes 32800 | tf_op jit(solution)/shard_map/ppermute | solution.py:329
  11.0 1.2 %encode.1 = bf16[1,64,16]{2,1,0:T(8,128)(2,1)S(1)} custom-call(bf16[2,1,2,2,8,256]{5,4,3,2,1,0:T(8,128)(2,1)S(1)} %collective-permute-done.1.refs_0_, bf16[2,1,2,2,8,256]{5,4,3,2,1,0:T(8,128)(2,1)S(1)} %collective-permute-done.2.refs_1_, bf16[2,1,2,2,8,256]{5,4,3,2,1,0:T(8,128)(2,1)S(1)} %collective-permute-done.3.refs_2_, ...), custom_call_target="tpu_custom_call" | custom-call | tf_op jit(solution)/shard_map/encode/pallas_call | solution.py:142
  12.2 1.5 %collective-permute-start.10 = (bf16[1,64,16]{2,1,0:T(8,128)(2,1)S(1)}, bf16[1,64,16]{2,1,0:T(8,128)(2,1)S(1)}, u32[]{:S(2)}, u32[]{:S(2)}) collective-permute-start(bf16[1,64,16]{2,1,0:T(8,128)(2,1)S(1)} %encode.1), channel_id=1, source_target_pairs={{0,9},{1,8},{2,11},{3,10},{4,13},{5,12},{6,15},{7,14},{8,1},{9,0},... | collective-permute-start | bytes 6152 | tf_op jit(solution)/shard_map/ppermute | solution.py:351
  13.8 0.2 collective-permute-start.9
  13.9 0.4 %collective-permute-start.5 = (bf16[1,64,16]{2,1,0:T(8,128)(2,1)S(1)}, bf16[1,64,16]{2,1,0:T(8,128)(2,1)S(1)}, u32[]{:S(2)}, u32[]{:S(2)}) collective-permute-start(bf16[1,64,16]{2,1,0:T(8,128)(2,1)S(1)} %encode.1), channel_id=1, source_target_pairs={{0,25},{1,24},{2,27},{3,26},{4,29},{5,28},{6,31},{7,30},{8,17},{9,... | collective-permute-start | bytes 6152 | tf_op jit(solution)/shard_map/ppermute | solution.py:351
  14.3 1.3 %collective-permute-start.4 = (bf16[1,64,16]{2,1,0:T(8,128)(2,1)S(1)}, bf16[1,64,16]{2,1,0:T(8,128)(2,1)S(1)}, u32[]{:S(2)}, u32[]{:S(2)}) collective-permute-start(bf16[1,64,16]{2,1,0:T(8,128)(2,1)S(1)} %encode.1), channel_id=1, source_target_pairs={{0,17},{1,16},{2,19},{3,18},{4,21},{5,20},{6,23},{7,22},{8,25},{9,... | collective-permute-start | bytes 6152 | tf_op jit(solution)/shard_map/ppermute | solution.py:351
  15.7 0.4 %collective-permute-start.11 = (bf16[128,320]{1,0:T(8,128)(2,1)S(1)}, bf16[128,320]{1,0:T(8,128)(2,1)S(1)}, u32[]{:S(2)}, u32[]{:S(2)}) collective-permute-start(bf16[128,320]{1,0:T(8,128)(2,1)S(1)} %first_block.3.kept_ref), channel_id=1, source_target_pairs={{0,8},{1,9},{2,10},{3,11},{4,12},{5,13},{6,14},{7,15},{8,24},{9,25... | collective-permute-start | bytes 245768 | tf_op jit(solution)/shard_map/ppermute | solution.py:351
  16.1 1.9 %collective-permute-done.5.refs_1_ = bf16[1,64,16]{2,1,0:T(8,128)(2,1)S(1)} collective-permute-done((bf16[1,64,16]{2,1,0:T(8,128)(2,1)S(1)}, bf16[1,64,16]{2,1,0:T(8,128)(2,1)S(1)}, u32[]{:S(2)}, u32[]{:S(2)}) %collective-permute-start.5) | collective-permute-done | bytes 2080 | tf_op jit(solution)/shard_map/ppermute | solution.py:351
  18.0 0.3 collective-permute-start.6
  18.3 3.1 %collective-permute-start.12 = (bf16[128,320]{1,0:T(8,128)(2,1)S(1)}, bf16[128,320]{1,0:T(8,128)(2,1)S(1)}, u32[]{:S(2)}, u32[]{:S(2)}) collective-permute-start(bf16[128,320]{1,0:T(8,128)(2,1)S(1)} %later_block.6.kept_ref), channel_id=1, source_target_pairs={{0,1},{1,0},{2,3},{3,2},{4,5},{5,4},{6,7},{7,6},{8,17},{9,16},{10,... | collective-permute-start | bytes 245768 | tf_op jit(solution)/shard_map/ppermute | solution.py:351
  21.5 2.3 %collective-permute-start.7 = (bf16[128,320]{1,0:T(8,128)(2,1)S(1)}, bf16[128,320]{1,0:T(8,128)(2,1)S(1)}, u32[]{:S(2)}, u32[]{:S(2)}) collective-permute-start(bf16[128,320]{1,0:T(8,128)(2,1)S(1)} %later_block.4.kept_ref), channel_id=1, source_target_pairs={{0,1},{1,0},{2,3},{3,2},{4,5},{5,4},{6,7},{7,6},{8,17},{9,16},{10,... | collective-permute-start | bytes 245768 | tf_op jit(solution)/shard_map/ppermute | solution.py:351
  23.7 0.9 %collective-permute-done.12.before_ref = bf16[128,320]{1,0:T(8,128)(2,1)S(1)} collective-permute-done((bf16[128,320]{1,0:T(8,128)(2,1)S(1)}, bf16[128,320]{1,0:T(8,128)(2,1)S(1)}, u32[]{:S(2)}, u32[]{:S(2)}) %collective-permute-start.12) | collective-permute-done | bytes 81952 | tf_op jit(solution)/shard_map/ppermute | solution.py:351
  24.6 0.9 %later_block.7.kept_ref = bf16[128,320]{1,0:T(8,128)(2,1)S(1)} custom-call(bf16[128,320]{1,0:T(8,128)(2,1)S(1)} %collective-permute-done.12.before_ref, bf16[128,320]{1,0:T(8,128)(2,1)S(1)} %later_block.6.kept_ref, bf16[3,3,320,320]{3,2,1,0:T(8,128)(2,1)S(1)} %bitcast.16, f32[1,320]{1,0:T(1,128)S(1)} %copy-done.4, ...), custom_call_target="tpu_custom_call", output_to_operand_aliasing={{}: (1, {})} | custom-call | tf_op jit(solution)/shard_map/later_block/pallas_call | solution.py:440
  25.5 1.6 %collective-permute-start.13 = (bf16[128,320]{1,0:T(8,128)(2,1)S(1)}, bf16[128,320]{1,0:T(8,128)(2,1)S(1)}, u32[]{:S(2)}, u32[]{:S(2)}) collective-permute-start(bf16[128,320]{1,0:T(8,128)(2,1)S(1)} %later_block.7.kept_ref), channel_id=1, source_target_pairs={{0,1},{1,0},{2,3},{3,2},{4,5},{5,4},{6,7},{7,6},{8,9},{9,8},{10,11... | collective-permute-start | bytes 245768 | tf_op jit(solution)/shard_map/ppermute | solution.py:351
  27.1 0.0 collective-permute-done.7.before_ref
  27.2 0.9 %later_block.5.kept_ref = bf16[128,320]{1,0:T(8,128)(2,1)S(1)} custom-call(bf16[128,320]{1,0:T(8,128)(2,1)S(1)} %collective-permute-done.7.before_ref, bf16[128,320]{1,0:T(8,128)(2,1)S(1)} %later_block.4.kept_ref, bf16[3,3,320,320]{3,2,1,0:T(8,128)(2,1)S(1)} %bitcast.17, f32[1,320]{1,0:T(1,128)S(1)} %copy-done.4, ...), custom_call_target="tpu_custom_call", output_to_operand_aliasing={{}: (1, {})} | custom-call | tf_op jit(solution)/shard_map/later_block/pallas_call | solution.py:440
  28.0 1.4 %collective-permute-start.8 = (bf16[128,320]{1,0:T(8,128)(2,1)S(1)}, bf16[128,320]{1,0:T(8,128)(2,1)S(1)}, u32[]{:S(2)}, u32[]{:S(2)}) collective-permute-start(bf16[128,320]{1,0:T(8,128)(2,1)S(1)} %later_block.5.kept_ref), channel_id=1, source_target_pairs={{0,1},{1,0},{2,3},{3,2},{4,5},{5,4},{6,7},{7,6},{8,9},{9,8},{10,11... | collective-permute-start | bytes 245768 | tf_op jit(solution)/shard_map/ppermute | solution.py:351
  29.4 1.8 %collective-permute-done.13.before_ref = bf16[128,320]{1,0:T(8,128)(2,1)S(1)} collective-permute-done((bf16[128,320]{1,0:T(8,128)(2,1)S(1)}, bf16[128,320]{1,0:T(8,128)(2,1)S(1)}, u32[]{:S(2)}, u32[]{:S(2)}) %collective-permute-start.13) | collective-permute-done | bytes 81952 | tf_op jit(solution)/shard_map/ppermute | solution.py:351
  31.2 0.7 %last_block.2.refs_0_ = bf16[4,8,2,1280]{3,2,1,0:T(2,128)(2,1)} custom-call(bf16[128,320]{1,0:T(8,128)(2,1)S(1)} %collective-permute-done.13.before_ref, bf16[128,320]{1,0:T(8,128)(2,1)S(1)} %later_block.7.kept_ref, bf16[3,3,320,320]{3,2,1,0:T(8,128)(2,1)S(1)} %bitcast.18, f32[1,320]{1,0:T(1,128)S(1)} %copy-done.4, f32[1,320]{1,0:T(1,128)S(1)} %copy-done.5, ...), custom_call_target="tpu_custom_call" | custom-call | tf_op jit(solution)/shard_map/last_block/pallas_call | solution.py:458
  32.0 1.6 %collective-permute-done.8.before_ref = bf16[128,320]{1,0:T(8,128)(2,1)S(1)} collective-permute-done((bf16[128,320]{1,0:T(8,128)(2,1)S(1)}, bf16[128,320]{1,0:T(8,128)(2,1)S(1)}, u32[]{:S(2)}, u32[]{:S(2)}) %collective-permute-start.8) | collective-permute-done | bytes 81952 | tf_op jit(solution)/shard_map/ppermute | solution.py:351
  33.6 0.7 %last_block.3 = bf16[4,8,2,1280]{3,2,1,0:T(2,128)(2,1)} custom-call(bf16[128,320]{1,0:T(8,128)(2,1)S(1)} %collective-permute-done.8.before_ref, bf16[128,320]{1,0:T(8,128)(2,1)S(1)} %later_block.5.kept_ref, bf16[4,8,2,1280]{3,2,1,0:T(2,128)(2,1)} %last_block.2.refs_0_, bf16[3,3,320,320]{3,2,1,0:T(8,128)(2,1)S(1)} %bitcast.19, ...), custom_call_target="tpu_custom_call", output_to_operand_aliasing={{}: (2, {})} | custom-call | tf_op jit(solution)/shard_map/last_block/pallas_call | solution.py:458
  (37 shorter events, 0.1 us)
Async XLA Ops:
  1.8 1.5 %collective-permute-start = (bf16[4,1,2,2,8,256]{5,4,3,2,1,0:T(8,128)(2,1)}, bf16[4,1,2,2,8,256]{5,4,3,2,1,0:T(8,128)(2,1)S(1)}, u32[]{:S(2)}, u32[]{:S(2)}) collective-permute-start(bf16[4,1,2,2,8,256]{5,4,3,2,1,0:T(8,128)(2,1)} %get-tuple-element.11), channel_id=1, source_target_pairs={{0,1},{1,0},{2,3},{3,2},{4,5},{5,4},{6,7},{7,6},{8,9},{9,8},{10,11... | collective-permute-start | bytes 196616 | tf_op jit(solution)/shard_map/ppermute | solution.py:355
  3.3 4.3 %collective-permute-start.1 = (bf16[2,1,2,2,8,256]{5,4,3,2,1,0:T(8,128)(2,1)S(1)}, bf16[2,1,2,2,8,256]{5,4,3,2,1,0:T(8,128)(2,1)S(1)}, u32[]{:S(2)}, u32[]{:S(2)}) collective-permute-start(bf16[2,1,2,2,8,256]{5,4,3,2,1,0:T(8,128)(2,1)S(1)} %pad_maximum_fusion), channel_id=1, source_target_pairs={{0,5},{1,4},{2,7},{3,6},{4,1},{5,0},{6,3},{7,2},{8,13},{9,12},{10,... | collective-permute-start | bytes 98312 | tf_op jit(solution)/shard_map/ppermute | solution.py:329
  5.7 5.3 %collective-permute-start.2 = (bf16[2,1,2,2,8,256]{5,4,3,2,1,0:T(8,128)(2,1)S(1)}, bf16[2,1,2,2,8,256]{5,4,3,2,1,0:T(8,128)(2,1)S(1)}, u32[]{:S(2)}, u32[]{:S(2)}) collective-permute-start(bf16[2,1,2,2,8,256]{5,4,3,2,1,0:T(8,128)(2,1)S(1)} %pad_maximum_fusion.1), channel_id=1, source_target_pairs={{0,7},{1,6},{2,5},{3,4},{4,3},{5,2},{6,1},{7,0},{8,15},{9,14},{10,... | collective-permute-start | bytes 98312 | tf_op jit(solution)/shard_map/ppermute | solution.py:329
  7.0 4.0 %copy-start.1 = (bf16[3,3,3,256,256]{4,3,2,1,0:T(8,128)(2,1)S(1)}, bf16[3,3,3,256,256]{4,3,2,1,0:T(8,128)(2,1)}, u32[]{:S(2)}) copy-start(bf16[3,3,3,256,256]{4,3,2,1,0:T(8,128)(2,1)} %refs_4_.2) | copy-start | bytes 10616836
  7.0 4.0 %copy-start.7 = (bf16[256,16]{0,1:T(8,128)(2,1)S(1)}, bf16[256,16]{0,1:T(8,128)(2,1)}, u32[]{:S(2)}) copy-start(bf16[256,16]{0,1:T(8,128)(2,1)} %param.21) | copy-start | bytes 24580
  7.0 4.0 %copy-start.8 = (f32[256]{0:T(256)S(1)}, f32[256]{0:T(256)}, u32[]{:S(2)}) copy-start(f32[256]{0:T(256)} %param.18) | copy-start | bytes 3076
  7.1 4.0 %copy-start.9 = (f32[256]{0:T(256)S(1)}, f32[256]{0:T(256)}, u32[]{:S(2)}) copy-start(f32[256]{0:T(256)} %param.19) | copy-start | bytes 3076
  7.1 4.0 %copy-start.10 = (f32[256]{0:T(256)S(1)}, f32[256]{0:T(256)}, u32[]{:S(2)}) copy-start(f32[256]{0:T(256)} %param.20) | copy-start | bytes 3076
  7.1 4.0 %copy-start.11 = (f32[16]{0:T(128)S(1)}, f32[16]{0:T(128)}, u32[]{:S(2)}) copy-start(f32[16]{0:T(128)} %param.22) | copy-start | bytes 196
  7.1 3.9 %collective-permute-start.3 = (bf16[2,1,2,2,8,256]{5,4,3,2,1,0:T(8,128)(2,1)S(1)}, bf16[2,1,2,2,8,256]{5,4,3,2,1,0:T(8,128)(2,1)S(1)}, u32[]{:S(2)}, u32[]{:S(2)}) collective-permute-start(bf16[2,1,2,2,8,256]{5,4,3,2,1,0:T(8,128)(2,1)S(1)} %pad_maximum_fusion.2), channel_id=1, source_target_pairs={{0,3},{1,2},{2,1},{3,0},{4,7},{5,6},{6,5},{7,4},{8,11},{9,10},{10,... | collective-permute-start | bytes 98312 | tf_op jit(solution)/shard_map/ppermute | solution.py:329
  7.5 8.1 %copy-start = (bf16[1,3,3,320,320]{4,3,2,1,0:T(8,128)(2,1)S(1)}, bf16[1,3,3,320,320]{4,3,2,1,0:T(8,128)(2,1)}, u32[]{:S(2)}) copy-start(bf16[1,3,3,320,320]{4,3,2,1,0:T(8,128)(2,1)} %param.30) | copy-start | bytes 5529604
  7.5 8.1 %copy-start.2 = (bf16[3,3,16,320]{3,2,1,0:T(8,128)(2,1)S(1)}, bf16[3,3,16,320]{3,2,1,0:T(8,128)(2,1)}, u32[]{:S(2)}) copy-start(bf16[3,3,16,320]{3,2,1,0:T(8,128)(2,1)} %param.25) | copy-start | bytes 276484
  7.5 8.1 %copy-start.3 = (f32[4,16,320]{2,1,0:T(8,128)S(1)}, f32[4,16,320]{2,1,0:T(8,128)}, u32[]{:S(2)}) copy-start(f32[4,16,320]{2,1,0:T(8,128)} %get-tuple-element.13.refs_2_) | copy-start | bytes 245764
  7.6 8.1 %copy-start.4 = (f32[1,320]{1,0:T(1,128)S(1)}, f32[1,320]{1,0:T(1,128)}, u32[]{:S(2)}) copy-start(f32[1,320]{1,0:T(1,128)} %refs_2_.11) | copy-start | bytes 3844
  7.6 8.1 %copy-start.5 = (f32[1,320]{1,0:T(1,128)S(1)}, f32[1,320]{1,0:T(1,128)}, u32[]{:S(2)}) copy-start(f32[1,320]{1,0:T(1,128)} %refs_3_.11) | copy-start | bytes 3844
  7.6 8.1 %copy-start.6 = (f32[1,320]{1,0:T(1,128)S(1)}, f32[1,320]{1,0:T(1,128)}, u32[]{:S(2)}) copy-start(f32[1,320]{1,0:T(1,128)} %refs_4_.3) | copy-start | bytes 3844
  12.2 3.4 %collective-permute-start.10 = (bf16[1,64,16]{2,1,0:T(8,128)(2,1)S(1)}, bf16[1,64,16]{2,1,0:T(8,128)(2,1)S(1)}, u32[]{:S(2)}, u32[]{:S(2)}) collective-permute-start(bf16[1,64,16]{2,1,0:T(8,128)(2,1)S(1)} %encode.1), channel_id=1, source_target_pairs={{0,9},{1,8},{2,11},{3,10},{4,13},{5,12},{6,15},{7,14},{8,1},{9,0},... | collective-permute-start | bytes 6152 | tf_op jit(solution)/shard_map/ppermute | solution.py:351
  13.8 1.9 %collective-permute-start.9 = (bf16[1,64,16]{2,1,0:T(8,128)(2,1)S(1)}, bf16[1,64,16]{2,1,0:T(8,128)(2,1)S(1)}, u32[]{:S(2)}, u32[]{:S(2)}) collective-permute-start(bf16[1,64,16]{2,1,0:T(8,128)(2,1)S(1)} %encode.1), channel_id=1, source_target_pairs={{0,1},{1,0},{2,3},{3,2},{4,5},{5,4},{6,7},{7,6},{8,9},{9,8},{10,11... | collective-permute-start | bytes 6152 | tf_op jit(solution)/shard_map/ppermute | solution.py:355
  13.9 4.1 %collective-permute-start.5 = (bf16[1,64,16]{2,1,0:T(8,128)(2,1)S(1)}, bf16[1,64,16]{2,1,0:T(8,128)(2,1)S(1)}, u32[]{:S(2)}, u32[]{:S(2)}) collective-permute-start(bf16[1,64,16]{2,1,0:T(8,128)(2,1)S(1)} %encode.1), channel_id=1, source_target_pairs={{0,25},{1,24},{2,27},{3,26},{4,29},{5,28},{6,31},{7,30},{8,17},{9,... | collective-permute-start | bytes 6152 | tf_op jit(solution)/shard_map/ppermute | solution.py:351
  14.3 3.7 %collective-permute-start.4 = (bf16[1,64,16]{2,1,0:T(8,128)(2,1)S(1)}, bf16[1,64,16]{2,1,0:T(8,128)(2,1)S(1)}, u32[]{:S(2)}, u32[]{:S(2)}) collective-permute-start(bf16[1,64,16]{2,1,0:T(8,128)(2,1)S(1)} %encode.1), channel_id=1, source_target_pairs={{0,17},{1,16},{2,19},{3,18},{4,21},{5,20},{6,23},{7,22},{8,25},{9,... | collective-permute-start | bytes 6152 | tf_op jit(solution)/shard_map/ppermute | solution.py:351
  15.7 2.6 %collective-permute-start.11 = (bf16[128,320]{1,0:T(8,128)(2,1)S(1)}, bf16[128,320]{1,0:T(8,128)(2,1)S(1)}, u32[]{:S(2)}, u32[]{:S(2)}) collective-permute-start(bf16[128,320]{1,0:T(8,128)(2,1)S(1)} %first_block.3.kept_ref), channel_id=1, source_target_pairs={{0,8},{1,9},{2,10},{3,11},{4,12},{5,13},{6,14},{7,15},{8,24},{9,25... | collective-permute-start | bytes 245768 | tf_op jit(solution)/shard_map/ppermute | solution.py:351
  18.0 3.4 %collective-permute-start.6 = (bf16[128,320]{1,0:T(8,128)(2,1)S(1)}, bf16[128,320]{1,0:T(8,128)(2,1)S(1)}, u32[]{:S(2)}, u32[]{:S(2)}) collective-permute-start(bf16[128,320]{1,0:T(8,128)(2,1)S(1)} %first_block.2.kept_ref), channel_id=1, source_target_pairs={{0,8},{1,9},{2,10},{3,11},{4,12},{5,13},{6,14},{7,15},{8,24},{9,25... | collective-permute-start | bytes 245768 | tf_op jit(solution)/shard_map/ppermute | solution.py:351
  18.3 6.3 %collective-permute-start.12 = (bf16[128,320]{1,0:T(8,128)(2,1)S(1)}, bf16[128,320]{1,0:T(8,128)(2,1)S(1)}, u32[]{:S(2)}, u32[]{:S(2)}) collective-permute-start(bf16[128,320]{1,0:T(8,128)(2,1)S(1)} %later_block.6.kept_ref), channel_id=1, source_target_pairs={{0,1},{1,0},{2,3},{3,2},{4,5},{5,4},{6,7},{7,6},{8,17},{9,16},{10,... | collective-permute-start | bytes 245768 | tf_op jit(solution)/shard_map/ppermute | solution.py:351
  21.5 5.7 %collective-permute-start.7 = (bf16[128,320]{1,0:T(8,128)(2,1)S(1)}, bf16[128,320]{1,0:T(8,128)(2,1)S(1)}, u32[]{:S(2)}, u32[]{:S(2)}) collective-permute-start(bf16[128,320]{1,0:T(8,128)(2,1)S(1)} %later_block.4.kept_ref), channel_id=1, source_target_pairs={{0,1},{1,0},{2,3},{3,2},{4,5},{5,4},{6,7},{7,6},{8,17},{9,16},{10,... | collective-permute-start | bytes 245768 | tf_op jit(solution)/shard_map/ppermute | solution.py:351
  25.5 5.7 %collective-permute-start.13 = (bf16[128,320]{1,0:T(8,128)(2,1)S(1)}, bf16[128,320]{1,0:T(8,128)(2,1)S(1)}, u32[]{:S(2)}, u32[]{:S(2)}) collective-permute-start(bf16[128,320]{1,0:T(8,128)(2,1)S(1)} %later_block.7.kept_ref), channel_id=1, source_target_pairs={{0,1},{1,0},{2,3},{3,2},{4,5},{5,4},{6,7},{7,6},{8,9},{9,8},{10,11... | collective-permute-start | bytes 245768 | tf_op jit(solution)/shard_map/ppermute | solution.py:351
  28.0 5.6 %collective-permute-start.8 = (bf16[128,320]{1,0:T(8,128)(2,1)S(1)}, bf16[128,320]{1,0:T(8,128)(2,1)S(1)}, u32[]{:S(2)}, u32[]{:S(2)}) collective-permute-start(bf16[128,320]{1,0:T(8,128)(2,1)S(1)} %later_block.5.kept_ref), channel_id=1, source_target_pairs={{0,1},{1,0},{2,3},{3,2},{4,5},{5,4},{6,7},{7,6},{8,9},{9,8},{10,11... | collective-permute-start | bytes 245768 | tf_op jit(solution)/shard_map/ppermute | solution.py:351
